TPU v7x, 32 devices: a whole 2x2x4 slice. The times are simulated.
32 devices in a mesh: pix: 8 (over y, x, core), ion: 4 (over z).
Axes of the slice: x: 2, y: 2, z: 4, core: 2. Of those that a mesh axis runs over, the one named last changes fastest.
Arguments:
- images: bfloat16 [20480, 16384], P('ion', 'pix')
- stencil: float32 [5, 16384], P(None, 'pix'), may hold values from 0.05 to 0.4
- pairs: int32 [192, 2], P('ion'), may hold values from 0 to 159, as said below
- live: int32 [4], P('ion'), may hold values from 16 to 48, as said below
- rule_of_block: int32 [160], replicated, may hold values from 0 to 63
- adduct: bfloat16 [64, 128, 128], P('ion'), may hold values from -6 to 6
Outputs:
- smoothed: bfloat16 [20480, 16384], P('ion', 'pix')
- scores: bfloat16 [192, 128, 128], P('ion', 'pix')
Inputs may be any that keep to these rules, and one draw needn't show every extreme that they name: Slot s belongs to ion block range of index s // 48 of ion: a lies in that index's own 20480 // (128 * 4) blocks, and |a - b| <= 3. Entries of unused slots are valid pairs too. `live`: some index of ion uses all its slots.
All inputs are finite; a program needn't handle non-finite values.
Results may differ from a plain program's by a relative error of at most 0.0053.
Values may be sent and summed in bfloat16 or wider, within the bound.
No kernel may reach another device: no remote copies, remote signals or barrier semaphores. Data moves between devices by JAX's collectives and lax.ppermute only.
A program may use at most 192 MiB of HBM per device.

v0:
```python
import jax
import jax.numpy as jnp
from jax import lax
from jax.sharding import PartitionSpec as P

REACH = 3


slot_group = 16


def extended_2(array, sides, width):
    for axis, dim in sides:
        size, length = (lax.axis_size(axis), array.shape[dim])
        up = [(i, (i + 1) % size) for i in range(size - 1)]
        down = [(j, i) for i, j in up]
        last = lax.slice_in_dim(array, length - width, length, axis=dim)
        first = lax.slice_in_dim(array, 0, width, axis=dim)
        before = lax.ppermute(last, axis, up)
        after = lax.ppermute(first, axis, down)
        array = jnp.concatenate([before, array, after], axis=dim)
    return array


def on_device(images, stencil, pairs, live, rule_of_block, adduct):
    local_rows, pix_local = images.shape
    block = adduct.shape[1]
    local_blocks = local_rows // block
    padded = extended_2(images, (("pix", 1),), 2)
    total = jnp.zeros((local_rows, pix_local), jnp.float32)
    for tap in range(5):
        total = total + stencil[tap][None, :] * padded[:, tap : tap + pix_local].astype(jnp.float32)
    smoothed = total.astype(jnp.bfloat16)
    extended = extended_2(smoothed, (("ion", 0),), REACH * block)
    values = extended.astype(jnp.float32)
    squares = jnp.sum(values * values, axis=1)
    pixel_count = pix_local * lax.axis_size("pix")
    energy = lax.psum(squares, "pix") / pixel_count
    inverse = 1.0 / jnp.sqrt(energy + 1e-06)
    lookup_tables = lax.all_gather(adduct, "ion", axis=0, tiled=True)
    first = lax.axis_index("ion") * local_blocks
    ext_blocks = extended.reshape(local_blocks + 2 * REACH, block, pix_local)
    inv_blocks = inverse.reshape(local_blocks + 2 * REACH, block)
    slots = pairs.shape[0]
    relative = pairs - first + REACH

    def group_gram(start):
        chosen = lax.dynamic_slice_in_dim(relative, start, slot_group, 0)
        left_operand = jnp.take(ext_blocks, chosen[:, 0], axis=0)
        right_operand = jnp.take(ext_blocks, chosen[:, 1], axis=0)
        return jnp.einsum(
            "uwf,uvf->uwv", left_operand, right_operand, preferred_element_type=jnp.float32
        )

    grams = jnp.concatenate(
        [group_gram(step * slot_group) for step in range(slots // slot_group)], axis=0
    )
    inv_left = jnp.take(inv_blocks, relative[:, 0], axis=0)
    inv_right = jnp.take(inv_blocks, relative[:, 1], axis=0)
    rules = jnp.take(rule_of_block, pairs[:, 1], axis=0)
    matrices = jnp.take(lookup_tables, rules, axis=0)
    share = block // lax.axis_size("pix")
    offset = lax.axis_index("pix") * share
    gram = lax.psum(grams, "pix")
    coloc = (gram * inv_left[:, :, None] * inv_right[:, None, :] / pixel_count).astype(jnp.bfloat16)
    complete_scores = jnp.einsum(
        "src,scd->srd", coloc, matrices, preferred_element_type=jnp.float32
    )
    scores = lax.dynamic_slice_in_dim(complete_scores, offset, share, 1)
    used = jnp.arange(slots, dtype=jnp.int32) < live[0]
    scores = jnp.where(used[:, None, None], scores, 0.0).astype(jnp.bfloat16)
    return (smoothed, scores)


def solution(mesh):
    return jax.shard_map(
        on_device,
        mesh=mesh,
        in_specs=(
            P("ion", "pix"),
            P(None, "pix"),
            P("ion", None),
            P("ion"),
            P(),
            P("ion", None, None),
        ),
        out_specs=(P("ion", "pix"), P("ion", "pix", None)),
        check_vma=False,
    )
```

profile of v0, /device:TPU:8, one launch (start us, length us, event | category | flops | bytes accessed | tf_op | source)
XLA Modules:
  0.0 376.6 jit_solution(16916569274455860241)
XLA Ops:
  8.1 2.2 fusion.34
  10.7 1.3 collective-permute-start.1
  12.5 3.0 collective-permute-start
  15.6 1.1 fusion.35
  16.6 0.6 copy.11
  17.3 0.6 copy.9
  17.9 72.7 %add_convert_fusion = bf16[5120,2048]{1,0:T(8,128)(2,1)S(1)} fusion(bf16[5120,2048]{1,0:T(8,128)(2,1)} %param.10, bf16[5120,2]{1,0:T(8,128)(2,1)S(1)} %copy.11, bf16[5120,2]{1,0:T(8,128)(2,1)S(1)} %copy.9, f32[2048]{0:T(1024)S(1)} %bitcast.53, f32[2048]{0:T(1024)S(1)} %bitcast.54, f32[2048]{0:T(1024)S(1)} %bitcast.51, f32[2048]{0:T(1024)S(1)} %bitcast.52, ...), kind=kLoop, calls=%fused_computation.11 | loop fusion | flops 283115520 | bytes 42024960 | tf_op jit(solution)/shard_map/convert_element_type | solution.py:33
  90.6 7.5 %copy-done.1 = bf16[5120,2048]{1,0:T(8,128)(2,1)} copy-done((bf16[5120,2048]{1,0:T(8,128)(2,1)}, bf16[5120,2048]{1,0:T(8,128)(2,1)S(1)}, u32[]{:S(2)}) %copy-start.1) | copy-done | bytes 20971544
  98.1 1.9 fusion.33
  100.0 1.9 collective-permute-start.3
  101.9 3.9 %collective-permute-start.2 = (bf16[384,2048]{1,0:T(8,128)(2,1)}, bf16[384,2048]{1,0:T(8,128)(2,1)S(1)}, u32[]{:S(2)}, u32[]{:S(2)}) collective-permute-start(bf16[384,2048]{1,0:T(8,128)(2,1)} %get-tuple-element.24), channel_id=1, source_target_pairs={{0,1},{1,2},{2,3},{4,5},{5,6},{6,7},{8,9},{9,10},{10,11},{12,13},{... | collective-permute-start | bytes 4718600 | tf_op jit(solution)/shard_map/ppermute | solution.py:19
  106.2 66.7 %collective-permute-done.3 = bf16[384,2048]{1,0:T(8,128)(2,1)S(1)} collective-permute-done((bf16[384,2048]{1,0:T(8,128)(2,1)}, bf16[384,2048]{1,0:T(8,128)(2,1)S(1)}, u32[]{:S(2)}, u32[]{:S(2)}) %collective-permute-start.3) | collective-permute-done | bytes 1572896 | tf_op jit(solution)/shard_map/ppermute | solution.py:20
  172.9 1.6 collective-permute-done.2
  174.5 16.5 %multiply_reduce_fusion = (f32[5888]{0:T(1024)S(1)}, bf16[5888,2048]{1,0:T(8,128)(2,1)}) fusion(bf16[384,2048]{1,0:T(8,128)(2,1)S(1)} %collective-permute-done.3, bf16[5120,2048]{1,0:T(8,128)(2,1)} %copy-done.1, bf16[384,2048]{1,0:T(8,128)(2,1)S(1)} %collective-permute-done.2), kind=kLoop, calls=%fused_computation.10 | loop fusion | flops 108521728 | bytes 48258048 | tf_op jit(solution)/shard_map/reduce_sum | solution.py:36
  190.9 12.7 %gather_fusion.7 = bf16[16,128,2048]{2,1,0:T(8,128)(2,1)} fusion(bf16[46,128,2048]{2,1,0:T(8,128)(2,1)} %bitcast.44, s32[1024]{0:T(1024)S(1)} %get-tuple-element.45), kind=kCustom, calls=%fused_computation.6.clone | custom fusion | bytes 16777280 | tf_op jit(solution)/shard_map/jit(_take)/gather | solution.py:50
  203.7 12.6 %gather_fusion.6 = bf16[16,128,2048]{2,1,0:T(8,128)(2,1)} fusion(bf16[46,128,2048]{2,1,0:T(8,128)(2,1)} %bitcast.45, s32[1024]{0:T(1024)S(1)} %get-tuple-element.46), kind=kCustom, calls=%fused_computation.5.clone | custom fusion | bytes 16777280 | tf_op jit(solution)/shard_map/jit(_take)/gather | solution.py:49
  216.2 8.4 %fusion.2 = f32[16,128,128]{2,1,0:T(8,128)S(1)} fusion(bf16[16,128,2048]{2,1,0:T(8,128)(2,1)} %gather_fusion.7, bf16[16,128,2048]{2,1,0:T(8,128)(2,1)} %gather_fusion.6, pred[16]{0:T(512)(128)(4,1)S(1)} %get-tuple-element.35, pred[16]{0:T(512)(128)(4,1)S(1)} %get-tuple-element.37), kind=kOutput, calls=%fused_computation.21 | convolution fusion | flops 1082130432 | bytes 17825824 | tf_op jit(solution)/shard_map/uwf,uvf->uwv/dot_general | solution.py:51
  224.6 12.7 %gather_fusion.5 = bf16[16,128,2048]{2,1,0:T(8,128)(2,1)} fusion(bf16[46,128,2048]{2,1,0:T(8,128)(2,1)} %bitcast.46, s32[1024]{0:T(1024)S(1)} %get-tuple-element.47), kind=kCustom, calls=%fused_computation.4.clone | custom fusion | bytes 16777280 | tf_op jit(solution)/shard_map/jit(_take)/gather | solution.py:50
  237.3 12.6 %gather_fusion.4 = bf16[16,128,2048]{2,1,0:T(8,128)(2,1)} fusion(bf16[46,128,2048]{2,1,0:T(8,128)(2,1)} %bitcast.47, s32[1024]{0:T(1024)S(1)} %get-tuple-element.48), kind=kCustom, calls=%fused_computation.3.clone | custom fusion | bytes 16777280 | tf_op jit(solution)/shard_map/jit(_take)/gather | solution.py:49
  249.9 12.6 %gather_fusion.3 = bf16[16,128,2048]{2,1,0:T(8,128)(2,1)} fusion(bf16[46,128,2048]{2,1,0:T(8,128)(2,1)} %bitcast.48, s32[1024]{0:T(1024)S(1)} %get-tuple-element.49), kind=kCustom, calls=%fused_computation.2.clone | custom fusion | bytes 16777280 | tf_op jit(solution)/shard_map/jit(_take)/gather | solution.py:50
  262.6 12.6 %gather_fusion.2 = bf16[16,128,2048]{2,1,0:T(8,128)(2,1)} fusion(bf16[46,128,2048]{2,1,0:T(8,128)(2,1)} %bitcast.49, s32[1024]{0:T(1024)S(1)} %get-tuple-element.50), kind=kCustom, calls=%fused_computation.clone | custom fusion | bytes 16777280 | tf_op jit(solution)/shard_map/jit(_take)/gather | solution.py:49
  275.2 8.4 %fusion.5 = f32[16,128,128]{2,1,0:T(8,128)S(1)} fusion(bf16[16,128,2048]{2,1,0:T(8,128)(2,1)} %gather_fusion.5, bf16[16,128,2048]{2,1,0:T(8,128)(2,1)} %gather_fusion.4, pred[16]{0:T(512)(128)(4,1)S(1)} %get-tuple-element.39, pred[16]{0:T(512)(128)(4,1)S(1)} %get-tuple-element.41), kind=kOutput, calls=%fused_computation.24 | convolution fusion | flops 1082130432 | bytes 17825824 | tf_op jit(solution)/shard_map/uwf,uvf->uwv/dot_general | solution.py:51
  283.5 8.4 %fusion.8 = f32[16,128,128]{2,1,0:T(8,128)S(1)} fusion(bf16[16,128,2048]{2,1,0:T(8,128)(2,1)} %gather_fusion.3, bf16[16,128,2048]{2,1,0:T(8,128)(2,1)} %gather_fusion.2, pred[16]{0:T(512)(128)(4,1)S(1)} %get-tuple-element.43, pred[16]{0:T(512)(128)(4,1)S(1)} %get-tuple-element.12), kind=kOutput, calls=%fused_computation.27 | convolution fusion | flops 1082130432 | bytes 17825824 | tf_op jit(solution)/shard_map/uwf,uvf->uwv/dot_general | solution.py:51
  291.9 1.9 pad_maximum_fusion.3
  294.6 0.8 gather_fusion
  295.4 22.9 %psum.15 = f32[5888]{0:T(1024)S(1)} all-reduce(f32[5888]{0:T(1024)S(1)} %get-tuple-element.10), channel_id=1, replica_groups=mesh['pix'=8,'ion'=4] {'pix'}, use_global_device_ids=true, to_apply=%region_2.0 | all-reduce | flops 5888 | bytes 47104 | tf_op jit(solution)/shard_map/psum | solution.py:38
  318.4 0.6 gather_fusion.9
  318.9 0.6 gather_fusion.8
  319.6 2.4 gather_fusion.1
  322.1 43.3 %all-reduce.2.cloned.1.call-done = f32[48,128,128]{2,1,0:T(8,128)} async-done(((f32[48,128,128]{2,1,0:T(8,128)}), f32[48,128,128]{2,1,0:T(8,128)}) %all-reduce.2.cloned.1.call-update) | async-done | bytes 3145744 | tf_op jit(solution)/shard_map/psum | solution.py:64
  365.4 3.0 fusion.20
  368.4 0.8 select_convert_fusion
  (29 shorter events, 1.6 us)
Async XLA Ops:
  8.0 286.6 %copy-start = (s32[160]{0:T(256)S(1)}, s32[160]{0:T(256)}, u32[]{:S(2)}) copy-start(s32[160]{0:T(256)} %param.14) | copy-start | bytes 1924
  8.0 311.6 %all-gather.2.cloned.1.call-start = ((), (), s32[]{:S(2)}) async-start(), calls=%async_computation.1 | async-start | bytes 2621440 | tf_op jit(solution)/shard_map/all_gather | solution.py:40
  10.7 5.9 %collective-permute-start.1 = (bf16[5120,2]{0,1:T(2,128)(2,1)S(1)}, bf16[5120,2]{0,1:T(2,128)(2,1)S(1)}, u32[]{:S(2)}, u32[]{:S(2)}) collective-permute-start(bf16[5120,2]{0,1:T(2,128)(2,1)S(1)} %copy.13), channel_id=1, source_target_pairs={{4,0},{8,4},{12,8},{16,12},{20,16},{24,20},{28,24},{5,1},{9,5},{13... | collective-permute-start | bytes 61448 | tf_op jit(solution)/shard_map/ppermute | solution.py:20
  12.5 4.7 %collective-permute-start = (bf16[5120,2]{0,1:T(2,128)(2,1)S(1)}, bf16[5120,2]{0,1:T(2,128)(2,1)S(1)}, u32[]{:S(2)}, u32[]{:S(2)}) collective-permute-start(bf16[5120,2]{0,1:T(2,128)(2,1)S(1)} %copy.12), channel_id=1, source_target_pairs={{0,4},{4,8},{8,12},{12,16},{16,20},{20,24},{24,28},{1,5},{5,9},{9,... | collective-permute-start | bytes 61448 | tf_op jit(solution)/shard_map/ppermute | solution.py:19
  17.9 88.2 %copy-start.2 = (s32[48,2]{0,1:T(2,128)S(1)}, s32[48,2]{0,1:T(2,128)}, u32[]{:S(2)}) copy-start(s32[48,2]{0,1:T(2,128)} %param.12) | copy-start | bytes 1156
  90.6 7.5 %copy-start.1 = (bf16[5120,2048]{1,0:T(8,128)(2,1)}, bf16[5120,2048]{1,0:T(8,128)(2,1)S(1)}, u32[]{:S(2)}) copy-start(bf16[5120,2048]{1,0:T(8,128)(2,1)S(1)} %add_convert_fusion) | copy-start | bytes 62914564
  100.0 72.9 %collective-permute-start.3 = (bf16[384,2048]{1,0:T(8,128)(2,1)}, bf16[384,2048]{1,0:T(8,128)(2,1)S(1)}, u32[]{:S(2)}, u32[]{:S(2)}) collective-permute-start(bf16[384,2048]{1,0:T(8,128)(2,1)} %get-tuple-element.25), channel_id=1, source_target_pairs={{1,0},{2,1},{3,2},{5,4},{6,5},{7,6},{9,8},{10,9},{11,10},{13,12},{... | collective-permute-start | bytes 4718600 | tf_op jit(solution)/shard_map/ppermute | solution.py:20
  101.9 72.6 %collective-permute-start.2 = (bf16[384,2048]{1,0:T(8,128)(2,1)}, bf16[384,2048]{1,0:T(8,128)(2,1)S(1)}, u32[]{:S(2)}, u32[]{:S(2)}) collective-permute-start(bf16[384,2048]{1,0:T(8,128)(2,1)} %get-tuple-element.24), channel_id=1, source_target_pairs={{0,1},{1,2},{2,3},{4,5},{5,6},{6,7},{8,9},{9,10},{10,11},{12,13},{... | collective-permute-start | bytes 4718600 | tf_op jit(solution)/shard_map/ppermute | solution.py:19
  105.9 259.6 %all-reduce.2.cloned.1.call-start = ((), (), s32[]{:S(2)}) async-start(), calls=%async_computation | async-start | bytes 6291456 | tf_op jit(solution)/shard_map/psum | solution.py:64
Sparse Core Ops, SparseCore 0:
  106.0 69.4 all-gather.1
Sparse Core Ops, SparseCore 1:
  294.0 71.4 all-reduce.1
where the time goes:
time: 379 us; the launch traced here: 377 us
  waiting for transfers between devices  112 us (30%)
  local copies, waits for them, and re-layouts  95.1 us (25%)
  other arithmetic  92.2 us (24%)
  matrix products  28.1 us (7%)
  blocking collectives  22.9 us (6%)
  between operations  16.4 us (4%)
  starting transfers between devices  10.4 us (3%)
    convert_element_type x1, other arithmetic, on_device(): smoothed = total.astype(jnp.bfloat16)  72.7 us
    ppermute x2, waiting for transfers between devices, extended_2(): after = lax.ppermute(first, axis, down)  66.7 us
    psum x1, waiting for transfers between devices, on_device(): gram = lax.psum(grams, 'pix')  43.3 us
    gather x3, local copies, waits for them, and re-layouts, group_gram(): right_operand = jnp.take(ext_blocks, chosen[:, 1], axis=0)  38 us
    gather x3, local copies, waits for them, and re-layouts, group_gram(): left_operand = jnp.take(ext_blocks, chosen[:, 0], axis=0)  37.8 us
    dot_general x3, matrix products, group_gram(): jnp.einsum('uwf,uvf->uwv', left_operand, right_operand, preferred_element...  25.1 us
    psum x1, blocking collectives, on_device(): energy = lax.psum(squares, 'pix') / pixel_count  22.9 us
    reduce_sum x1, other arithmetic, on_device(): squares = jnp.sum(values * values, axis=1)  16.5 us
  transfers between devices with their start and end apart: 6, of which 3 were waited for; matrix products, arithmetic and copies ran while one was open for 33% of the time, Pallas kernels for 0%

commit v1 on v0

v1 whole, which is shorter than its diff:
```python
import functools

import jax
import jax.numpy as jnp
from jax import lax
from jax.experimental import pallas as pl
from jax.experimental.pallas import tpu as pltpu
from jax.sharding import PartitionSpec as P

REACH = 3
TAPS = 5
LANES = 128
HALF = LANES // 2
TILE = 2 * LANES
DEPTH = 6 * LANES
VMEM_BYTES = 58 * 1024 * 1024


def params():
    return pltpu.CompilerParams(vmem_limit_bytes=VMEM_BYTES)


def cost(flops, moved):
    return pl.CostEstimate(flops=flops, bytes_accessed=moved, transcendentals=0)


def whole(shape):
    return pl.BlockSpec(shape, lambda *_: (0,) * len(shape))


def split(values):
    high = values.astype(jnp.bfloat16)
    return high, (values - high.astype(jnp.float32)).astype(jnp.bfloat16)


def weights_kernel(stencil_ref, out_ref):
    k = lax.broadcasted_iota(jnp.int32, (TILE, TILE), 0)
    n = lax.broadcasted_iota(jnp.int32, (TILE, TILE), 1)
    inner = k - n + 2
    k, n = k[:LANES], n[:LANES]
    outer = k - n + jnp.where(k < HALF, TILE + 2, 2 - LANES)
    for j in range(out_ref.shape[0]):
        taps = stencil_ref[:, j * TILE : (j + 1) * TILE]
        main = jnp.zeros((TILE, TILE), jnp.float32)
        edge = jnp.zeros((LANES, TILE), jnp.float32)
        for t in range(TAPS):
            main = jnp.where(inner == t, taps[t : t + 1, :], main)
            edge = jnp.where(outer == t, taps[t : t + 1, :], edge)
        out_ref[j, :TILE], out_ref[j, TILE : 2 * TILE] = split(main)
        out_ref[j, 2 * TILE : 2 * TILE + LANES], out_ref[j, 2 * TILE + LANES :] = split(edge)


def smooth_rows(x_ref, halo_ref, w_ref, store):
    rows, width = x_ref.shape
    tiles = width // TILE
    first = lax.broadcasted_iota(jnp.int32, (rows, LANES), 1) < HALF
    for j in range(tiles):
        own = x_ref[:, j * TILE : (j + 1) * TILE]
        before = halo_ref[...] if j == 0 else x_ref[:, j * TILE - LANES : j * TILE]
        after = halo_ref[...] if j == tiles - 1 else x_ref[:, (j + 1) * TILE : (j + 1) * TILE + LANES]
        edge = jnp.where(first, after, before)
        window = jnp.concatenate([own, own, edge, edge], axis=1)
        store(j, jnp.dot(window, w_ref[j], preferred_element_type=jnp.float32))


def lane_pairs(values):
    squares = values * values
    return squares[:, :LANES] + squares[:, LANES:]


def row_sums(part):
    return jnp.sum(part.T, axis=0, keepdims=True)


def gram_of(left, right):
    return lax.dot_general(
        left, right, (((1,), (1,)), ((), ())), preferred_element_type=jnp.float32
    )


def by_core(gram, chips, core):
    parts = gram.reshape(chips, 2, gram.shape[0] // (2 * chips), gram.shape[1])
    return jnp.where(core == 0, parts[:, 0], parts[:, 1]), jnp.where(core == 0, parts[:, 1], parts[:, 0])


def main_kernel(steps, group, block, info_ref, rel_ref, x_ref, halo_ref, w_ref,
                out_ref, energy_ref, keep_ref, give_ref, held, wide):
    step = pl.program_id(0)
    blocks = steps * group
    slots, chips = wide.shape[:2]

    @pl.when(step < steps)
    def smooth():
        total = [None]

        def store(j, values):
            columns = slice(j * TILE, (j + 1) * TILE)
            rounded = values.astype(jnp.bfloat16)
            out_ref[:, columns] = rounded
            held[pl.ds(step * group, group), :, columns] = rounded.reshape(group, block, TILE)
            squares = lane_pairs(values)
            total[0] = squares if j == 0 else total[0] + squares

        smooth_rows(x_ref, halo_ref, w_ref, store)
        for g in range(group):
            energy_ref[pl.ds(step * group + g, 1), :] = row_sums(total[0][g * block : (g + 1) * block, :])

    @pl.when(step == steps)
    def grams():
        core = info_ref[0]

        def one(s, carry):
            a = rel_ref[2 * s]
            b = jnp.clip(rel_ref[2 * s + 1], 0, blocks - 1)
            keep_ref[s], wide[s] = by_core(gram_of(held[a], held[b]), chips, core)
            return carry

        lax.fori_loop(0, slots, one, 0, unroll=4)
        give_ref[:slots] = wide[...].astype(jnp.bfloat16)


def cross_kernel(blocks, block, info_ref, rel_ref, slots, down_ref, up_ref, down_halo_ref, up_halo_ref, w_ref, energy_ref,
                 smoothed_ref, keep_in, give_in, keep_ref, give_ref, near, own, table, keep_part, give_part, sems):
    del keep_in, give_in
    core = info_ref[0]
    chips, share = keep_part.shape[1:3]
    units = 2 * table.shape[0] // block
    edge = REACH * block
    rows = blocks * block
    copies = [
        pltpu.make_async_copy(smoothed_ref.at[pl.ds(0, edge)], own.at[0], sems.at[0]),
        pltpu.make_async_copy(smoothed_ref.at[pl.ds(rows - edge, edge)], own.at[1], sems.at[1]),
    ]
    for copy in copies:
        copy.start()

    table[...] = jnp.zeros_like(table)
    table[REACH : REACH + blocks, :] = energy_ref[...]
    for side, (x_ref, halo_ref) in enumerate(((down_ref, down_halo_ref), (up_ref, up_halo_ref))):
        total = [None]

        def store(j, values):
            near[side, :, j * TILE : (j + 1) * TILE] = values.astype(jnp.bfloat16)
            squares = lane_pairs(values)
            total[0] = squares if j == 0 else total[0] + squares

        smooth_rows(x_ref, halo_ref, w_ref, store)
        for k in range(REACH):
            row = side * (REACH + blocks) + k
            table[row : row + 1, :] = row_sums(total[0][k * block : (k + 1) * block, :])
    for copy in copies:
        copy.wait()

    high, low = split(table[...])
    shape = (units, chips, share, LANES)
    keep_part[:units] = table[...].reshape(shape)
    give_part[:units] = high.reshape(shape)
    give_part[units:] = low.reshape(shape)
    copies = [
        pltpu.make_async_copy(keep_part.at[pl.ds(0, units)], keep_ref.at[pl.ds(slots, units)], sems.at[0]),
        pltpu.make_async_copy(give_part, give_ref.at[pl.ds(slots, 2 * units)], sems.at[1]),
    ]
    for copy in copies:
        copy.start()
    for copy in copies:
        copy.wait()

    def one(s, carry):
        a, b = rel_ref[2 * s], rel_ref[2 * s + 1]

        @pl.when((b < 0) | (b >= blocks))
        def crossing():
            side = (b >= 0).astype(jnp.int32)
            a_row = pl.multiple_of((a - side * (blocks - REACH)) * block, block)
            b_row = pl.multiple_of((b + REACH - side * (blocks + REACH)) * block, block)
            gram = gram_of(own[side, pl.ds(a_row, block), :], near[side, pl.ds(b_row, block), :])
            mine, other = by_core(gram, chips, core)
            keep_part[0] = mine
            give_part[0] = other.astype(jnp.bfloat16)
            first = pltpu.make_async_copy(keep_part.at[0], keep_ref.at[s], sems.at[0])
            second = pltpu.make_async_copy(give_part.at[0], give_ref.at[s], sems.at[1])
            first.start()
            second.start()
            first.wait()
            second.wait()

        return carry

    lax.fori_loop(0, slots, one, 0)


def chip_kernel(slots, units, info_ref, keep_ref, got_ref, own_ref, *out_refs):
    chip = info_ref[1]
    chips, share = keep_ref.shape[1:3]
    shape = (units * chips, share, LANES)
    energies = keep_ref[slots:] + (
        got_ref[slots : slots + units].astype(jnp.float32) + got_ref[slots + units :].astype(jnp.float32)
    )
    high, low = split(energies)
    for d in range(chips):
        total = keep_ref[:slots, chip ^ d] + got_ref[:slots, chip ^ d].astype(jnp.float32)
        if d == 0:
            own_ref[:slots] = total
            own_ref[slots:] = energies.reshape(shape)
        else:
            out = out_refs[d - 1]
            out[:slots] = total.astype(jnp.bfloat16)
            out[slots : slots + units * chips] = high.reshape(shape)
            out[slots + units * chips :] = low.reshape(shape)


def score_kernel(slots, pixel_count, info_ref, rel_ref, place_ref, own_ref, *refs):
    got_refs, (table_ref, out_ref, gram, inverse) = refs[:-4], refs[-4:]
    share = gram.shape[1]
    block = table_ref.shape[1]
    e_units = inverse.shape[0] // share
    live, offset = info_ref[2], info_ref[3]
    total = own_ref[:slots]
    energies = own_ref[slots:]
    for got in got_refs:
        total = total + got[:slots].astype(jnp.float32)
        energies = energies + (
            got[slots : slots + e_units].astype(jnp.float32) + got[slots + e_units :].astype(jnp.float32)
        )
    gram[...] = total
    inverse[...] = (1.0 / jnp.sqrt(energies / pixel_count + 1e-06)).reshape(inverse.shape)
    lane = lax.broadcasted_iota(jnp.int32, (share, LANES), 1)
    mine = lane == lax.broadcasted_iota(jnp.int32, (share, LANES), 0) + offset

    def one(s, carry):
        inv_a = inverse[pl.ds(rel_ref[2 * s] + REACH, 1), :]
        inv_b = inverse[pl.ds(rel_ref[2 * s + 1] + REACH, 1), :]
        inv_a = jnp.sum(jnp.where(mine, inv_a, 0.0), axis=1, keepdims=True)
        coloc = (gram[s] * inv_a * inv_b / pixel_count).astype(jnp.bfloat16)
        matrix = table_ref[pl.ds(pl.multiple_of(place_ref[s], block), block), :]
        scores = jnp.dot(coloc, matrix, preferred_element_type=jnp.float32)
        out_ref[s] = jnp.where(s < live, scores, 0.0).astype(jnp.bfloat16)
        return carry

    lax.fori_loop(0, slots, one, 0, unroll=4)


def on_device(images, stencil, pairs, live, rule_of_block, adduct):
    rows, width = images.shape
    rules_here, block, _ = adduct.shape
    blocks = rows // block
    slots = pairs.shape[0]
    n_pix, n_ion = lax.axis_size("pix"), lax.axis_size("ion")
    pix, ion = lax.axis_index("pix"), lax.axis_index("ion")
    pixel_count = width * n_pix
    chips, share = n_pix // 2, block // n_pix
    core, chip = pix % 2, pix // 2
    edge = REACH * block

    def shifted(axis, size, up, value):
        steps = [(i, i + 1) if up else (i + 1, i) for i in range(size - 1)]
        return lax.ppermute(value, axis, steps)

    def to_neighbours(value):
        return (
            shifted("ion", n_ion, True, value[rows - edge :]),
            shifted("ion", n_ion, False, value[:edge]),
        )

    before = shifted("pix", n_pix, True, images[:, width - 2 :])
    after = shifted("pix", n_pix, False, images[:, :2])
    down, up = to_neighbours(images)
    halo = jnp.concatenate([after, jnp.zeros((rows, LANES - 4), images.dtype), before], axis=1)
    down_halo, up_halo = to_neighbours(halo)

    flat = adduct.reshape(rules_here * block, block)
    part = rules_here * block // n_pix
    flat = lax.dynamic_slice_in_dim(flat, pix * part, part, 0)
    table = lax.all_gather(flat, "ion", axis=0, tiled=True)
    table = lax.all_gather(table, "pix", axis=0, tiled=True)
    rules = jnp.take(rule_of_block, pairs[:, 1], axis=0)
    if part % block == 0:
        row = rules % rules_here * block
        place = (row // part * n_ion + rules // rules_here) * part + row % part
    else:
        table = table.reshape(n_pix, n_ion, part, block).swapaxes(0, 1).reshape(-1, block)
        place = rules * block

    weights = pl.pallas_call(
        weights_kernel,
        out_shape=jax.ShapeDtypeStruct((width // TILE, DEPTH, TILE), jnp.bfloat16),
        compiler_params=params(),
        cost_estimate=cost(0, width * DEPTH * 2),
        name="band_weights",
    )(stencil)

    info = jnp.stack([core, chip, live[0], pix * share]).astype(jnp.int32)
    relative = (pairs - ion * blocks).reshape(-1)
    group = next(g for g in (4, 2, 1) if blocks % g == 0)
    steps = blocks // group
    units = -(-2 * (blocks + 2 * REACH) // block)
    half = (chips, share, LANES)
    keep_shape = (slots + units, *half)
    give_shape = (slots + 2 * units, *half)

    def rows_at(columns):
        return pl.BlockSpec((group * block, columns), lambda i, *_: (jnp.minimum(i, steps - 1), 0))

    smoothed, energy, keep, give = pl.pallas_call(
        functools.partial(main_kernel, steps, group, block),
        grid_spec=pltpu.PrefetchScalarGridSpec(
            num_scalar_prefetch=2,
            grid=(steps + 1,),
            in_specs=[rows_at(width), rows_at(LANES), whole(weights.shape)],
            out_specs=[rows_at(width), whole((blocks, LANES)), whole(keep_shape), whole(give_shape)],
            scratch_shapes=[
                pltpu.VMEM((blocks, block, width), jnp.bfloat16),
                pltpu.VMEM((slots, *half), jnp.float32),
            ],
        ),
        out_shape=[
            jax.ShapeDtypeStruct((rows, width), jnp.bfloat16),
            jax.ShapeDtypeStruct((blocks, LANES), jnp.float32),
            jax.ShapeDtypeStruct(keep_shape, jnp.float32),
            jax.ShapeDtypeStruct(give_shape, jnp.bfloat16),
        ],
        compiler_params=params(),
        cost_estimate=cost(2 * rows * width * DEPTH + 2 * slots * block * block * width, 4 * rows * width),
        name="smooth_and_gram",
    )(info, relative, images, halo, weights)

    smem = pl.BlockSpec(memory_space=pltpu.SMEM)
    vmem = pl.BlockSpec(memory_space=pltpu.VMEM)
    hbm = pl.BlockSpec(memory_space=pl.ANY)

    def cross(info_ref, rel_ref, *refs):
        cross_kernel(blocks, block, info_ref, rel_ref, slots, *refs)

    keep, give = pl.pallas_call(
        cross,
        in_specs=[smem, smem] + [vmem] * 6 + [hbm] * 3,
        out_specs=[hbm, hbm],
        out_shape=[jax.ShapeDtypeStruct(keep_shape, jnp.float32), jax.ShapeDtypeStruct(give_shape, jnp.bfloat16)],
        input_output_aliases={9: 0, 10: 1},
        scratch_shapes=[
            pltpu.VMEM((2, edge, width), jnp.bfloat16),
            pltpu.VMEM((2, edge, width), jnp.bfloat16),
            pltpu.VMEM((units * block // 2, LANES), jnp.float32),
            pltpu.VMEM((units, *half), jnp.float32),
            pltpu.VMEM((2 * units, *half), jnp.bfloat16),
            pltpu.SemaphoreType.DMA((2,)),
        ],
        compiler_params=params(),
        cost_estimate=cost(4 * edge * width * DEPTH, 8 * edge * width),
        name="cross_grams",
    )(info, relative, down, up, down_halo, up_halo, weights, energy, smoothed, keep, give)

    got = lax.ppermute(give, "pix", [(i, i ^ 1) for i in range(n_pix)])
    message = jax.ShapeDtypeStruct((slots + 2 * units * chips, share, LANES), jnp.bfloat16)
    own, *messages = pl.pallas_call(
        functools.partial(chip_kernel, slots, units),
        in_specs=[smem, vmem, vmem],
        out_specs=[vmem] * chips,
        out_shape=[jax.ShapeDtypeStruct((slots + units * chips, share, LANES), jnp.float32)]
        + [message] * (chips - 1),
        compiler_params=params(),
        name="chip_sums",
    )(info, keep, got)
    received = [
        lax.ppermute(m, "pix", [(i, i ^ (2 * (d + 1))) for i in range(n_pix)]) for d, m in enumerate(messages)
    ]

    scores = pl.pallas_call(
        functools.partial(score_kernel, slots, pixel_count),
        in_specs=[smem, smem, smem] + [vmem] * (chips + 1),
        out_specs=vmem,
        out_shape=jax.ShapeDtypeStruct((slots, share, block), jnp.bfloat16),
        scratch_shapes=[
            pltpu.VMEM((slots, share, LANES), jnp.float32),
            pltpu.VMEM((units * block // 2, LANES), jnp.float32),
        ],
        compiler_params=params(),
        name="scores",
    )(info, relative, place, own, *received, table)
    return (smoothed, scores)


def solution(mesh):
    return jax.shard_map(
        on_device,
        mesh=mesh,
        in_specs=(
            P("ion", "pix"),
            P(None, "pix"),
            P("ion", None),
            P("ion"),
            P(),
            P("ion", None, None),
        ),
        out_specs=(P("ion", "pix"), P("ion", "pix", None)),
        check_vma=False,
    )
```

time: 379 us -> 165 us (0.44)
  waiting for transfers between devices: 112 us -> 11.7 us
  other arithmetic: 92.2 us -> 1.99 us
  local copies, waits for them, and re-layouts: 95.1 us -> 12.4 us
  Pallas kernels: 0 us -> 57.6 us
  matrix products: 28.1 us -> 0 us
  blocking collectives: 22.9 us -> 43.2 us
  starting transfers between devices: 10.4 us -> 22.7 us
    gather x9 -> x0, local copies, waits for them, and re-layouts: 79.5 us -> none  [the longest x3 38 us: group_gram(): right_operand = jnp.take(ext_blocks, chosen[:, 1], axis=0)]
    convert_element_type x2 -> x0, other arithmetic: 73.5 us -> none  [the longest x1 72.7 us: on_device(): smoothed = total.astype(jnp.bfloat16)]
    pallas_call x0 -> x5, Pallas kernels: none -> 57.6 us  [the longest x1 35.3 us: on_device(): pl.pallas_call(functools.partial(main_kernel, steps, group, block), grid_...]
    ppermute x4 -> x10, waiting for transfers between devices: 68.3 us -> 11.7 us  [the longest x3 9.12 us: on_device(): lax.ppermute(m, 'pix', [(i, i ^ 2 * (d + 1)) for i in range(n_pix)])]
    psum x1 -> x0, waiting for transfers between devices: 43.3 us -> none  [on_device(): gram = lax.psum(grams, 'pix')]
    all_gather x0 -> x1, blocking collectives: none -> 43.2 us  [on_device(): table = lax.all_gather(flat, 'ion', axis=0, tiled=True)]
    dot_general x4 -> x0, matrix products: 28.1 us -> none  [the longest x3 25.1 us: group_gram(): jnp.einsum('uwf,uvf->uwv', left_operand, right_operand, preferred_element...]
    psum x1 -> x0, blocking collectives: 22.9 us -> none  [on_device(): energy = lax.psum(squares, 'pix') / pixel_count]
  transfers between devices with their start and end apart: 6 -> 11, of which waited for: 3 -> 3; matrix products, arithmetic and copies ran while one was open for 33% -> 6% of each run, Pallas kernels for 0% -> 32%
where the time goes in v1:
time: 165 us; the launch traced here: 164 us
  Pallas kernels  57.6 us (35%)
  blocking collectives  43.2 us (26%)
  starting transfers between devices  22.7 us (14%)
  between operations  14.9 us (9%)
  local copies, waits for them, and re-layouts  12.4 us (8%)
  waiting for transfers between devices  11.7 us (7%)
  other arithmetic  1.99 us (1%)
    all_gather x1, blocking collectives, on_device(): table = lax.all_gather(flat, 'ion', axis=0, tiled=True)  43.2 us
    pallas_call x1, Pallas kernels, on_device(): pl.pallas_call(functools.partial(main_kernel, steps, group, block), grid_...  35.3 us
    ppermute x6, starting transfers between devices, shifted(): return lax.ppermute(value, axis, steps)  19.1 us
    pallas_call x1, Pallas kernels, on_device(): pl.pallas_call(cross, in_specs=[smem, smem] + [vmem] * 6 + [hbm] * 3, out...  10.9 us
    ppermute x3, waiting for transfers between devices, on_device(): lax.ppermute(m, 'pix', [(i, i ^ 2 * (d + 1)) for i in range(n_pix)])  9.12 us
    pallas_call x1, Pallas kernels, on_device(): pl.pallas_call(functools.partial(score_kernel, slots, pixel_count), in_sp...  5.46 us
    slice x2, local copies, waits for them, and re-layouts, to_neighbours(): value[:edge]  4.06 us
    ppermute x3, starting transfers between devices, on_device(): lax.ppermute(m, 'pix', [(i, i ^ 2 * (d + 1)) for i in range(n_pix)])  3.49 us
  transfers between devices with their start and end apart: 11, of which 3 were waited for; matrix products, arithmetic and copies ran while one was open for 6% of the time, Pallas kernels for 32%

profile of v1, /device:TPU:8, one launch (start us, length us, event | category | flops | bytes accessed | tf_op | source)
XLA Modules:
  0.0 164.4 jit_solution(3756371305850387672)
XLA Ops:
  7.2 2.2 %fusion.4 = (bf16[5120,2]{1,0:T(8,128)(2,1)S(1)}, bf16[5120,2]{1,0:T(8,128)(2,1)S(1)}) fusion(bf16[5120,2048]{1,0:T(8,128)(2,1)} %x_ref.1), kind=kLoop, calls=%fused_computation.22 | loop fusion | bytes 81920 | tf_op jit(solution)/shard_map/slice | solution.py:266
  9.5 0.5 copy.17
  9.9 1.3 collective-permute-start
  11.2 0.5 copy.18
  11.7 3.2 %collective-permute-start.1 = (bf16[5120,2]{0,1:T(2,128)(2,1)S(1)}, bf16[5120,2]{0,1:T(2,128)(2,1)S(1)}, u32[]{:S(2)}, u32[]{:S(2)}) collective-permute-start(bf16[5120,2]{0,1:T(2,128)(2,1)S(1)} %copy.18), channel_id=1, source_target_pairs={{0,4},{4,8},{8,12},{12,16},{16,20},{20,24},{24,28},{1,5},{5,9},{9,... | collective-permute-start | bytes 61448 | tf_op jit(solution)/shard_map/ppermute | solution.py:257
  14.9 4.0 %fusion.3 = (bf16[384,2048]{1,0:T(8,128)(2,1)}, bf16[384,2048]{1,0:T(8,128)(2,1)}) fusion(bf16[5120,2048]{1,0:T(8,128)(2,1)} %x_ref.1), kind=kLoop, calls=%fused_computation.21 | loop fusion | bytes 6291456 | tf_op jit(solution)/shard_map/slice | solution.py:262
  18.9 3.5 %collective-permute-start.2 = (bf16[384,2048]{1,0:T(8,128)(2,1)}, bf16[384,2048]{1,0:T(8,128)(2,1)}, u32[]{:S(2)}, u32[]{:S(2)}) collective-permute-start(bf16[384,2048]{1,0:T(8,128)(2,1)} %get-tuple-element.23), channel_id=1, source_target_pairs={{0,1},{1,2},{2,3},{4,5},{5,6},{6,7},{8,9},{9,10},{10,11},{12,13},{... | collective-permute-start | bytes 4718600 | tf_op jit(solution)/shard_map/ppermute | solution.py:257
  22.4 3.6 %collective-permute-start.3 = (bf16[384,2048]{1,0:T(8,128)(2,1)}, bf16[384,2048]{1,0:T(8,128)(2,1)}, u32[]{:S(2)}, u32[]{:S(2)}) collective-permute-start(bf16[384,2048]{1,0:T(8,128)(2,1)} %get-tuple-element.22), channel_id=1, source_target_pairs={{1,0},{2,1},{3,2},{5,4},{6,5},{7,6},{9,8},{10,9},{11,10},{13,12},{... | collective-permute-start | bytes 4718600 | tf_op jit(solution)/shard_map/ppermute | solution.py:257
  26.0 43.2 %all_gather.6 = bf16[1024,128]{1,0:T(8,128)(2,1)} all-gather(bf16[256,128]{1,0:T(8,128)(2,1)S(1)} %constant_dynamic-slice_fusion), channel_id=1, replica_groups=mesh['pix'=8,'ion'=4] {'ion'}, dimensions={0}, use_global_device_ids=true | all-gather | bytes 327680 | tf_op jit(solution)/shard_map/all_gather | solution.py:274
  69.9 0.7 pad_add_fusion.info_ref
  70.6 0.7 reshape.14.rel_ref
  71.3 3.1 %band_weights.1.w_ref.refs_4_ = bf16[8,768,256]{2,1,0:T(8,128)(2,1)} custom-call(f32[5,2048]{1,0:T(8,128)} %stencil_ref.1), custom_call_target="tpu_custom_call" | custom-call | bytes 3145728 | tf_op jit(solution)/shard_map/band_weights/pallas_call | solution.py:284
  74.5 0.6 copy.15
  75.2 0.6 copy.16
  75.8 0.8 pad_maximum_fusion.halo_ref
  76.6 5.5 %collective-permute-start.4 = (bf16[384,128]{1,0:T(8,128)(2,1)S(1)}, bf16[384,128]{1,0:T(8,128)(2,1)S(1)}, u32[]{:S(2)}, u32[]{:S(2)}) collective-permute-start(bf16[384,128]{1,0:T(8,128)(2,1)S(1)} %get-tuple-element.27), channel_id=1, source_target_pairs={{0,1},{1,2},{2,3},{4,5},{5,6},{6,7},{8,9},{9,10},{10,11},{12,13},{... | collective-permute-start | bytes 294920 | tf_op jit(solution)/shard_map/ppermute | solution.py:257
  82.1 2.1 %collective-permute-start.5 = (bf16[384,128]{1,0:T(8,128)(2,1)S(1)}, bf16[384,128]{1,0:T(8,128)(2,1)S(1)}, u32[]{:S(2)}, u32[]{:S(2)}) collective-permute-start(bf16[384,128]{1,0:T(8,128)(2,1)S(1)} %get-tuple-element.26), channel_id=1, source_target_pairs={{1,0},{2,1},{3,2},{5,4},{6,5},{7,6},{9,8},{10,9},{11,10},{13,12},{... | collective-permute-start | bytes 294920 | tf_op jit(solution)/shard_map/ppermute | solution.py:257
  84.2 35.3 %smooth_and_gram.1 = (bf16[5120,2048]{1,0:T(8,128)(2,1)}, f32[40,128]{1,0:T(8,128)}, f32[49,4,16,128]{3,2,1,0:T(8,128)}, bf16[50,4,16,128]{3,2,1,0:T(8,128)(2,1)}) custom-call(s32[4]{0:T(128)} %pad_add_fusion.info_ref, s32[96]{0:T(128)} %reshape.14.rel_ref, bf16[5120,2048]{1,0:T(8,128)(2,1)} %x_ref.1, bf16[5120,128]{1,0:T(8,128)(2,1)} %copy-done.2, ...), custom_call_target="tpu_custom_call" | custom-call | flops 19327352832 | bytes 41943040 | tf_op jit(solution)/shard_map/smooth_and_gram/pallas_call | solution.py:304
  119.5 0.6 copy-done.7
  120.2 10.9 %cross_grams.1 = (f32[49,4,16,128]{3,2,1,0:T(8,128)}, bf16[50,4,16,128]{3,2,1,0:T(8,128)(2,1)}) custom-call(s32[4]{0:T(128)} %pad_add_fusion.info_ref, s32[96]{0:T(128)} %reshape.14.rel_ref, bf16[384,2048]{1,0:T(8,128)(2,1)} %collective-permute-done.2.refs_0_, ...), custom_call_target="tpu_custom_call", output_to_operand_aliasing={{0}: (9, {}), {1}: (10, {})} | custom-call | flops 2415919104 | bytes 6291456 | tf_op jit(solution)/shard_map/cross_grams/pallas_call | solution.py:334
  131.2 2.5 %collective-permute-done.6.got_ref = bf16[50,4,16,128]{3,2,1,0:T(8,128)(2,1)S(1)} collective-permute-done((bf16[50,4,16,128]{3,2,1,0:T(8,128)(2,1)}, bf16[50,4,16,128]{3,2,1,0:T(8,128)(2,1)S(1)}, u32[]{:S(2)}, u32[]{:S(2)}) %collective-permute-start.6) | collective-permute-done | bytes 819232 | tf_op jit(solution)/shard_map/ppermute | solution.py:353
  133.7 0.9 copy-done.3
  134.6 2.8 %chip_sums.1 = (f32[52,16,128]{2,1,0:T(8,128)}, bf16[56,16,128]{2,1,0:T(8,128)(2,1)}, bf16[56,16,128]{2,1,0:T(8,128)(2,1)}, bf16[56,16,128]{2,1,0:T(8,128)(2,1)}) custom-call(s32[4]{0:T(128)} %pad_add_fusion.info_ref, f32[49,4,16,128]{3,2,1,0:T(8,128)} %get-tuple-element.16.keep_ref, bf16[50,4,16,128]{3,2,1,0:T(8,128)(2,1)} %copy-done.3), custom_call_target="tpu_custom_call" | custom-call | tf_op jit(solution)/shard_map/chip_sums/pallas_call | solution.py:355
  137.4 0.8 collective-permute-start.7
  138.3 1.1 collective-permute-start.8
  139.4 1.6 collective-permute-start.9
  141.0 0.8 gather_fusion
  141.7 0.5 fusion.place_ref
  142.3 3.8 %collective-permute-done.7.refs_0_ = bf16[56,16,128]{2,1,0:T(8,128)(2,1)S(1)} collective-permute-done((bf16[56,16,128]{2,1,0:T(8,128)(2,1)}, bf16[56,16,128]{2,1,0:T(8,128)(2,1)S(1)}, u32[]{:S(2)}, u32[]{:S(2)}) %collective-permute-start.7) | collective-permute-done | bytes 229408 | tf_op jit(solution)/shard_map/ppermute | solution.py:365
  146.1 5.3 %collective-permute-done.9.refs_2_ = bf16[56,16,128]{2,1,0:T(8,128)(2,1)S(1)} collective-permute-done((bf16[56,16,128]{2,1,0:T(8,128)(2,1)}, bf16[56,16,128]{2,1,0:T(8,128)(2,1)S(1)}, u32[]{:S(2)}, u32[]{:S(2)}) %collective-permute-start.9) | collective-permute-done | bytes 229408 | tf_op jit(solution)/shard_map/ppermute | solution.py:365
  151.4 0.7 copy-done.6
  152.1 5.5 %scores.1 = bf16[48,16,128]{2,1,0:T(8,128)(2,1)} custom-call(s32[4]{0:T(128)} %pad_add_fusion.info_ref, s32[96]{0:T(128)} %reshape.14.rel_ref, s32[48]{0:T(128)} %fusion.place_ref, f32[52,16,128]{2,1,0:T(8,128)} %get-tuple-element.18.own_ref, bf16[56,16,128]{2,1,0:T(8,128)(2,1)} %copy-done.4, bf16[56,16,128]{2,1,0:T(8,128)(2,1)} %copy-done.5, ...), custom_call_target="tpu_custom_call" | custom-call | tf_op jit(solution)/shard_map/scores/pallas_call | solution.py:368
  (36 shorter events, 0.4 us)
Async XLA Ops:
  7.2 18.8 %copy-start = (bf16[16,128,128]{2,1,0:T(8,128)(2,1)S(1)}, bf16[16,128,128]{2,1,0:T(8,128)(2,1)}, u32[]{:S(2)}) copy-start(bf16[16,128,128]{2,1,0:T(8,128)(2,1)} %param.11) | copy-start | bytes 1572868
  7.2 144.2 %all-gather.2.cloned.1.call-start = ((), (), s32[]{:S(2)}) async-start(), calls=%async_computation | async-start | bytes 2359296 | tf_op jit(solution)/shard_map/all_gather | solution.py:275
  9.9 64.6 %collective-permute-start = (bf16[5120,2]{0,1:T(2,128)(2,1)S(1)}, bf16[5120,2]{0,1:T(2,128)(2,1)S(1)}, u32[]{:S(2)}, u32[]{:S(2)}) collective-permute-start(bf16[5120,2]{0,1:T(2,128)(2,1)S(1)} %copy.17), channel_id=1, source_target_pairs={{4,0},{8,4},{12,8},{16,12},{20,16},{24,20},{28,24},{5,1},{9,5},{13... | collective-permute-start | bytes 61448 | tf_op jit(solution)/shard_map/ppermute | solution.py:257
  11.7 58.2 %copy-start.9 = (s32[48,2]{0,1:T(2,128)S(1)}, s32[48,2]{0,1:T(2,128)}, u32[]{:S(2)}) copy-start(s32[48,2]{0,1:T(2,128)} %param.8) | copy-start | bytes 1156
  11.7 63.5 %collective-permute-start.1 = (bf16[5120,2]{0,1:T(2,128)(2,1)S(1)}, bf16[5120,2]{0,1:T(2,128)(2,1)S(1)}, u32[]{:S(2)}, u32[]{:S(2)}) collective-permute-start(bf16[5120,2]{0,1:T(2,128)(2,1)S(1)} %copy.18), channel_id=1, source_target_pairs={{0,4},{4,8},{8,12},{12,16},{16,20},{20,24},{24,28},{1,5},{5,9},{9,... | collective-permute-start | bytes 61448 | tf_op jit(solution)/shard_map/ppermute | solution.py:257
  18.9 100.6 %collective-permute-start.2 = (bf16[384,2048]{1,0:T(8,128)(2,1)}, bf16[384,2048]{1,0:T(8,128)(2,1)}, u32[]{:S(2)}, u32[]{:S(2)}) collective-permute-start(bf16[384,2048]{1,0:T(8,128)(2,1)} %get-tuple-element.23), channel_id=1, source_target_pairs={{0,1},{1,2},{2,3},{4,5},{5,6},{6,7},{8,9},{9,10},{10,11},{12,13},{... | collective-permute-start | bytes 4718600 | tf_op jit(solution)/shard_map/ppermute | solution.py:257
  22.4 97.1 %collective-permute-start.3 = (bf16[384,2048]{1,0:T(8,128)(2,1)}, bf16[384,2048]{1,0:T(8,128)(2,1)}, u32[]{:S(2)}, u32[]{:S(2)}) collective-permute-start(bf16[384,2048]{1,0:T(8,128)(2,1)} %get-tuple-element.22), channel_id=1, source_target_pairs={{1,0},{2,1},{3,2},{5,4},{6,5},{7,6},{9,8},{10,9},{11,10},{13,12},{... | collective-permute-start | bytes 4718600 | tf_op jit(solution)/shard_map/ppermute | solution.py:257
  76.6 7.6 %copy-start.2 = (bf16[5120,128]{1,0:T(8,128)(2,1)}, bf16[5120,128]{1,0:T(8,128)(2,1)S(1)}, u32[]{:S(2)}) copy-start(bf16[5120,128]{1,0:T(8,128)(2,1)S(1)} %pad_maximum_fusion.halo_ref) | copy-start | bytes 3932164
  76.6 42.9 %collective-permute-start.4 = (bf16[384,128]{1,0:T(8,128)(2,1)S(1)}, bf16[384,128]{1,0:T(8,128)(2,1)S(1)}, u32[]{:S(2)}, u32[]{:S(2)}) collective-permute-start(bf16[384,128]{1,0:T(8,128)(2,1)S(1)} %get-tuple-element.27), channel_id=1, source_target_pairs={{0,1},{1,2},{2,3},{4,5},{5,6},{6,7},{8,9},{9,10},{10,11},{12,13},{... | collective-permute-start | bytes 294920 | tf_op jit(solution)/shard_map/ppermute | solution.py:257
  82.1 37.4 %collective-permute-start.5 = (bf16[384,128]{1,0:T(8,128)(2,1)S(1)}, bf16[384,128]{1,0:T(8,128)(2,1)S(1)}, u32[]{:S(2)}, u32[]{:S(2)}) collective-permute-start(bf16[384,128]{1,0:T(8,128)(2,1)S(1)} %get-tuple-element.26), channel_id=1, source_target_pairs={{1,0},{2,1},{3,2},{5,4},{6,5},{7,6},{9,8},{10,9},{11,10},{13,12},{... | collective-permute-start | bytes 294920 | tf_op jit(solution)/shard_map/ppermute | solution.py:257
  119.5 0.6 copy-start.7
  119.5 0.6 copy-start.8
  131.1 9.9 %copy-start.1 = (s32[160]{0:T(256)S(1)}, s32[160]{0:T(256)}, u32[]{:S(2)}) copy-start(s32[160]{0:T(256)} %param.10) | copy-start | bytes 1924
  131.1 2.6 %collective-permute-start.6 = (bf16[50,4,16,128]{3,2,1,0:T(8,128)(2,1)}, bf16[50,4,16,128]{3,2,1,0:T(8,128)(2,1)S(1)}, u32[]{:S(2)}, u32[]{:S(2)}) collective-permute-start(bf16[50,4,16,128]{3,2,1,0:T(8,128)(2,1)} %get-tuple-element.17), channel_id=1, source_target_pairs={{0,4},{4,0},{8,12},{12,8},{16,20},{20,16},{24,28},{28,24},{1,5},{5... | collective-permute-start | bytes 2457608 | tf_op jit(solution)/shard_map/ppermute | solution.py:353
  133.7 0.9 copy-start.3
  137.4 8.7 %collective-permute-start.7 = (bf16[56,16,128]{2,1,0:T(8,128)(2,1)}, bf16[56,16,128]{2,1,0:T(8,128)(2,1)S(1)}, u32[]{:S(2)}, u32[]{:S(2)}) collective-permute-start(bf16[56,16,128]{2,1,0:T(8,128)(2,1)} %get-tuple-element.19), channel_id=1, source_target_pairs={{0,8},{4,12},{8,0},{12,4},{16,24},{20,28},{24,16},{28,20},{1,9},{5... | collective-permute-start | bytes 688136 | tf_op jit(solution)/shard_map/ppermute | solution.py:365
  138.3 7.8 %collective-permute-start.8 = (bf16[56,16,128]{2,1,0:T(8,128)(2,1)}, bf16[56,16,128]{2,1,0:T(8,128)(2,1)S(1)}, u32[]{:S(2)}, u32[]{:S(2)}) collective-permute-start(bf16[56,16,128]{2,1,0:T(8,128)(2,1)} %get-tuple-element.20), channel_id=1, source_target_pairs={{0,16},{4,20},{8,24},{12,28},{16,0},{20,4},{24,8},{28,12},{1,17},{... | collective-permute-start | bytes 688136 | tf_op jit(solution)/shard_map/ppermute | solution.py:365
  139.4 12.0 %collective-permute-start.9 = (bf16[56,16,128]{2,1,0:T(8,128)(2,1)}, bf16[56,16,128]{2,1,0:T(8,128)(2,1)S(1)}, u32[]{:S(2)}, u32[]{:S(2)}) collective-permute-start(bf16[56,16,128]{2,1,0:T(8,128)(2,1)} %get-tuple-element.21), channel_id=1, source_target_pairs={{0,24},{4,28},{8,16},{12,20},{16,8},{20,12},{24,0},{28,4},{1,25},{... | collective-permute-start | bytes 688136 | tf_op jit(solution)/shard_map/ppermute | solution.py:365
  146.1 5.3 %copy-start.4 = (bf16[56,16,128]{2,1,0:T(8,128)(2,1)}, bf16[56,16,128]{2,1,0:T(8,128)(2,1)S(1)}, u32[]{:S(2)}) copy-start(bf16[56,16,128]{2,1,0:T(8,128)(2,1)S(1)} %collective-permute-done.7.refs_0_) | copy-start | bytes 688132
  146.1 5.3 %copy-start.5 = (bf16[56,16,128]{2,1,0:T(8,128)(2,1)}, bf16[56,16,128]{2,1,0:T(8,128)(2,1)S(1)}, u32[]{:S(2)}) copy-start(bf16[56,16,128]{2,1,0:T(8,128)(2,1)S(1)} %collective-permute-done.8.refs_1_) | copy-start | bytes 688132
  151.4 0.7 copy-start.6
Sparse Core Ops, SparseCore 0:
  69.3 29.3 all-gather.1

commit v2 on v1

v2 whole, which is shorter than its diff:
```python
import functools

import jax
import jax.numpy as jnp
from jax import lax
from jax.experimental import pallas as pl
from jax.experimental.pallas import tpu as pltpu
from jax.sharding import PartitionSpec as P

REACH = 3
TAPS = 5
LANES = 128
HALF = LANES // 2
TILE = 2 * LANES
DEPTH = 6 * LANES
VMEM_BYTES = 58 * 1024 * 1024


def params():
    return pltpu.CompilerParams(vmem_limit_bytes=VMEM_BYTES)


def cost(flops, moved):
    return pl.CostEstimate(flops=flops, bytes_accessed=moved, transcendentals=0)


def whole(shape):
    return pl.BlockSpec(shape, lambda *_: (0,) * len(shape))


def split(values):
    high = values.astype(jnp.bfloat16)
    return high, (values - high.astype(jnp.float32)).astype(jnp.bfloat16)


def weights_kernel(stencil_ref, out_ref):
    k = lax.broadcasted_iota(jnp.int32, (TILE, TILE), 0)
    n = lax.broadcasted_iota(jnp.int32, (TILE, TILE), 1)
    inner = k - n + 2
    k, n = k[:LANES], n[:LANES]
    outer = k - n + jnp.where(k < HALF, TILE + 2, 2 - LANES)
    for j in range(out_ref.shape[0]):
        taps = stencil_ref[:, j * TILE : (j + 1) * TILE]
        main = jnp.zeros((TILE, TILE), jnp.float32)
        edge = jnp.zeros((LANES, TILE), jnp.float32)
        for t in range(TAPS):
            main = jnp.where(inner == t, taps[t : t + 1, :], main)
            edge = jnp.where(outer == t, taps[t : t + 1, :], edge)
        out_ref[j, :TILE], out_ref[j, TILE : 2 * TILE] = split(main)
        out_ref[j, 2 * TILE : 2 * TILE + LANES], out_ref[j, 2 * TILE + LANES :] = split(edge)


def smooth_rows(x_ref, halo, w_ref, store):
    rows, width = x_ref.shape
    tiles = width // TILE
    first = lax.broadcasted_iota(jnp.int32, (rows, LANES), 1) < HALF
    for j in range(tiles):
        own = x_ref[:, j * TILE : (j + 1) * TILE]
        before = halo if j == 0 else x_ref[:, j * TILE - LANES : j * TILE]
        after = halo if j == tiles - 1 else x_ref[:, (j + 1) * TILE : (j + 1) * TILE + LANES]
        edge = jnp.where(first, after, before)
        window = jnp.concatenate([own, own, edge, edge], axis=1)
        store(j, jnp.dot(window, w_ref[j], preferred_element_type=jnp.float32))


def lane_pairs(values):
    squares = values * values
    return squares[:, :LANES] + squares[:, LANES:]


def row_sums(part):
    return jnp.sum(part.T, axis=0, keepdims=True)


def gram_of(left, right):
    return lax.dot_general(
        left, right, (((1,), (1,)), ((), ())), preferred_element_type=jnp.float32
    )


def by_core(gram, chips, core):
    parts = gram.reshape(chips, 2, gram.shape[0] // (2 * chips), gram.shape[1])
    return jnp.where(core == 0, parts[:, 0], parts[:, 1]), jnp.where(core == 0, parts[:, 1], parts[:, 0])


def cut_kernel(edge, images_ref, first_ref, last_ref, top_ref, bottom_ref, head_ref, tail_ref, sems):
    rows = images_ref.shape[0]
    copies = [
        pltpu.make_async_copy(images_ref.at[pl.ds(0, edge)], top_ref, sems.at[0]),
        pltpu.make_async_copy(images_ref.at[pl.ds(rows - edge, edge)], bottom_ref, sems.at[1]),
    ]
    for copy in copies:
        copy.start()
    row = lax.broadcasted_iota(jnp.int32, (8, LANES), 0)
    lane = lax.broadcasted_iota(jnp.int32, (8, LANES), 1)
    for source, out, shift in ((first_ref, head_ref, 0), (last_ref, tail_ref, LANES - 8)):
        pick = (lane == row + shift).astype(jnp.bfloat16)
        out[...] = gram_of(pick, source[...]).astype(jnp.bfloat16)
    for copy in copies:
        copy.wait()


def halo_tile(columns_ref):
    columns = columns_ref[...].astype(jnp.float32).T.astype(jnp.bfloat16)
    row = lax.broadcasted_iota(jnp.int32, (8, LANES), 0)
    lane = lax.broadcasted_iota(jnp.int32, (8, LANES), 1)
    place = (lane == row + jnp.where(row < 4, 0, LANES - 8)).astype(jnp.bfloat16)
    return jnp.dot(columns, place, preferred_element_type=jnp.float32).astype(jnp.bfloat16)


def smooth_kernel(group, block, x_ref, columns_ref, w_ref, out_ref, energy_ref):
    step = pl.program_id(0)
    total = [None]

    def store(j, values):
        out_ref[:, j * TILE : (j + 1) * TILE] = values.astype(jnp.bfloat16)
        squares = lane_pairs(values)
        total[0] = squares if j == 0 else total[0] + squares

    smooth_rows(x_ref, halo_tile(columns_ref), w_ref, store)
    for g in range(group):
        energy_ref[pl.ds(step * group + g, 1), :] = row_sums(total[0][g * block : (g + 1) * block, :])


def gram_kernel(blocks, block, info_ref, rel_ref, down_ref, up_ref, down_columns_ref, up_columns_ref, w_ref, energy_ref,
                smoothed_ref, keep_ref, give_ref, held, wide, table, sems):
    core = info_ref[0]
    slots, chips, share = wide.shape[:3]
    units = keep_ref.shape[0] - slots
    parts = sems.shape[0]
    count = blocks // parts
    copies = [
        pltpu.make_async_copy(
            smoothed_ref.at[pl.ds(p * count, count)], held.at[pl.ds(REACH + p * count, count)], sems.at[p]
        )
        for p in range(parts)
    ]
    for copy in copies:
        copy.start()

    table[...] = jnp.zeros_like(table)
    table[REACH : REACH + blocks, :] = energy_ref[...]
    for first, x_ref, columns_ref in ((0, down_ref, down_columns_ref), (REACH + blocks, up_ref, up_columns_ref)):
        total = [None]

        def store(j, values):
            rounded = values.astype(jnp.bfloat16).reshape(REACH, block, TILE)
            held[first : first + REACH, :, j * TILE : (j + 1) * TILE] = rounded
            squares = lane_pairs(values)
            total[0] = squares if j == 0 else total[0] + squares

        smooth_rows(x_ref, halo_tile(columns_ref), w_ref, store)
        for k in range(REACH):
            table[first + k : first + k + 1, :] = row_sums(total[0][k * block : (k + 1) * block, :])

    high, low = split(table[...])
    shape = (units, chips, share, LANES)
    keep_ref[slots:] = table[...].reshape(shape)
    give_ref[slots : slots + units] = high.reshape(shape)
    give_ref[slots + units :] = low.reshape(shape)
    for copy in copies:
        copy.wait()

    def one(s, carry):
        gram = gram_of(held[rel_ref[2 * s] + REACH], held[rel_ref[2 * s + 1] + REACH])
        keep_ref[s], wide[s] = by_core(gram, chips, core)
        return carry

    lax.fori_loop(0, slots, one, 0, unroll=4)
    give_ref[:slots] = wide[...].astype(jnp.bfloat16)


def chip_kernel(slots, units, info_ref, keep_ref, got_ref, own_ref, *out_refs):
    chip = info_ref[1]
    chips, share = keep_ref.shape[1:3]
    shape = (units * chips, share, LANES)
    energies = keep_ref[slots:] + (
        got_ref[slots : slots + units].astype(jnp.float32) + got_ref[slots + units :].astype(jnp.float32)
    )
    high, low = split(energies)
    for d in range(chips):
        total = keep_ref[:slots, chip ^ d] + got_ref[:slots, chip ^ d].astype(jnp.float32)
        if d == 0:
            own_ref[:slots] = total
            own_ref[slots:] = energies.reshape(shape)
        else:
            out = out_refs[d - 1]
            out[:slots] = total.astype(jnp.bfloat16)
            out[slots : slots + units * chips] = high.reshape(shape)
            out[slots + units * chips :] = low.reshape(shape)


def score_kernel(slots, pixel_count, info_ref, rel_ref, place_ref, own_ref, *refs):
    got_refs, (table_ref, out_ref, gram, inverse) = refs[:-4], refs[-4:]
    share = gram.shape[1]
    block = table_ref.shape[1]
    e_units = inverse.shape[0] // share
    live, offset = info_ref[2], info_ref[3]
    total = own_ref[:slots]
    energies = own_ref[slots:]
    for got in got_refs:
        total = total + got[:slots].astype(jnp.float32)
        energies = energies + (
            got[slots : slots + e_units].astype(jnp.float32) + got[slots + e_units :].astype(jnp.float32)
        )
    gram[...] = total
    inverse[...] = (1.0 / jnp.sqrt(energies / pixel_count + 1e-06)).reshape(inverse.shape)
    lane = lax.broadcasted_iota(jnp.int32, (share, LANES), 1)
    mine = lane == lax.broadcasted_iota(jnp.int32, (share, LANES), 0) + offset

    def one(s, carry):
        inv_a = inverse[pl.ds(rel_ref[2 * s] + REACH, 1), :]
        inv_b = inverse[pl.ds(rel_ref[2 * s + 1] + REACH, 1), :]
        inv_a = jnp.sum(jnp.where(mine, inv_a, 0.0), axis=1, keepdims=True)
        coloc = (gram[s] * inv_a * inv_b / pixel_count).astype(jnp.bfloat16)
        matrix = table_ref[pl.ds(pl.multiple_of(place_ref[s], block), block), :]
        scores = jnp.dot(coloc, matrix, preferred_element_type=jnp.float32)
        out_ref[s] = jnp.where(s < live, scores, 0.0).astype(jnp.bfloat16)
        return carry

    lax.fori_loop(0, slots, one, 0, unroll=4)


def on_device(images, stencil, pairs, live, rule_of_block, adduct):
    rows, width = images.shape
    rules_here, block, _ = adduct.shape
    blocks = rows // block
    slots = pairs.shape[0]
    n_pix, n_ion = lax.axis_size("pix"), lax.axis_size("ion")
    pix, ion = lax.axis_index("pix"), lax.axis_index("ion")
    pixel_count = width * n_pix
    chips, share = n_pix // 2, block // n_pix
    core, chip = pix % 2, pix // 2
    edge = REACH * block

    def shifted(axis, size, up, value):
        steps = [(i, i + 1) if up else (i + 1, i) for i in range(size - 1)]
        return lax.ppermute(value, axis, steps)

    vmem = pl.BlockSpec(memory_space=pltpu.VMEM)
    smem = pl.BlockSpec(memory_space=pltpu.SMEM)
    hbm = pl.BlockSpec(memory_space=pl.ANY)
    edge_rows = jax.ShapeDtypeStruct((edge, width), images.dtype)
    edge_columns = jax.ShapeDtypeStruct((8, rows), images.dtype)
    top, bottom, head, tail = pl.pallas_call(
        functools.partial(cut_kernel, edge),
        grid=(1,),
        in_specs=[
            hbm,
            pl.BlockSpec((rows, LANES), lambda i: (0, 0)),
            pl.BlockSpec((rows, LANES), lambda i: (0, width // LANES - 1)),
        ],
        out_specs=[hbm, hbm, whole((8, rows)), whole((8, rows))],
        out_shape=[edge_rows, edge_rows, edge_columns, edge_columns],
        scratch_shapes=[pltpu.SemaphoreType.DMA((2,))],
        compiler_params=params(),
        name="cut_edges",
    )(images, images, images)

    before = shifted("pix", n_pix, True, tail[6:])
    after = shifted("pix", n_pix, False, head[:2])
    down = shifted("ion", n_ion, True, bottom)
    up = shifted("ion", n_ion, False, top)
    columns = jnp.concatenate([after, jnp.zeros((4, rows), images.dtype), before], axis=0)
    down_columns = shifted("ion", n_ion, True, columns[:, rows - edge :])
    up_columns = shifted("ion", n_ion, False, columns[:, :edge])

    flat = adduct.reshape(rules_here * block, block)
    part = rules_here * block // n_pix
    flat = lax.dynamic_slice_in_dim(flat, pix * part, part, 0)
    table, distance = flat, 1
    while distance < n_ion:
        other = lax.ppermute(table, "ion", [(i, i ^ distance) for i in range(n_ion)])
        table, distance = jnp.concatenate([table, other], axis=0), 2 * distance
    table = lax.all_gather(table, "pix", axis=0, tiled=True)
    rules = jnp.take(rule_of_block, pairs[:, 1], axis=0)
    if part % block == 0:
        row = rules % rules_here * block
        place = (row // part * n_ion + ((rules // rules_here) ^ ion)) * part + row % part
    else:
        table = table.reshape(n_pix, n_ion, part, block).swapaxes(0, 1).reshape(-1, block)
        place = (((rules // rules_here) ^ ion) * rules_here + rules % rules_here) * block

    weights = pl.pallas_call(
        weights_kernel,
        out_shape=jax.ShapeDtypeStruct((width // TILE, DEPTH, TILE), jnp.bfloat16),
        compiler_params=params(),
        cost_estimate=cost(0, width * DEPTH * 2),
        name="band_weights",
    )(stencil)

    info = jnp.stack([core, chip, live[0], pix * share]).astype(jnp.int32)
    relative = (pairs - ion * blocks).reshape(-1)
    group = next(g for g in (4, 2, 1) if blocks % g == 0)
    steps = blocks // group
    units = -(-2 * (blocks + 2 * REACH) // block)
    half = (chips, share, LANES)
    keep_shape = (slots + units, *half)
    give_shape = (slots + 2 * units, *half)

    def rows_at(columns):
        return pl.BlockSpec((group * block, columns), lambda i: (i, 0))

    smoothed, energy = pl.pallas_call(
        functools.partial(smooth_kernel, group, block),
        grid=(steps,),
        in_specs=[rows_at(width), pl.BlockSpec((8, group * block), lambda i: (0, i)), whole(weights.shape)],
        out_specs=[rows_at(width), whole((blocks, LANES))],
        out_shape=[
            jax.ShapeDtypeStruct((rows, width), jnp.bfloat16),
            jax.ShapeDtypeStruct((blocks, LANES), jnp.float32),
        ],
        compiler_params=params(),
        cost_estimate=cost(2 * rows * width * DEPTH, 4 * rows * width),
        name="smooth",
    )(images, columns, weights)

    keep, give = pl.pallas_call(
        functools.partial(gram_kernel, blocks, block),
        in_specs=[smem, smem] + [vmem] * 6 + [hbm],
        out_specs=[vmem, vmem],
        out_shape=[jax.ShapeDtypeStruct(keep_shape, jnp.float32), jax.ShapeDtypeStruct(give_shape, jnp.bfloat16)],
        scratch_shapes=[
            pltpu.VMEM((blocks + 2 * REACH, block, width), jnp.bfloat16),
            pltpu.VMEM((slots, *half), jnp.float32),
            pltpu.VMEM((units * block // 2, LANES), jnp.float32),
            pltpu.SemaphoreType.DMA((2,)),
        ],
        compiler_params=params(),
        cost_estimate=cost(4 * edge * width * DEPTH + 2 * slots * block * block * width, 2 * rows * width),
        name="grams",
    )(info, relative, down, up, down_columns, up_columns, weights, energy, smoothed.reshape(blocks, block, width))

    got = lax.ppermute(give, "pix", [(i, i ^ 1) for i in range(n_pix)])
    message = jax.ShapeDtypeStruct((slots + 2 * units * chips, share, LANES), jnp.bfloat16)
    own, *messages = pl.pallas_call(
        functools.partial(chip_kernel, slots, units),
        in_specs=[smem, vmem, vmem],
        out_specs=[vmem] * chips,
        out_shape=[jax.ShapeDtypeStruct((slots + units * chips, share, LANES), jnp.float32)]
        + [message] * (chips - 1),
        compiler_params=params(),
        name="chip_sums",
    )(info, keep, got)
    received = [
        lax.ppermute(m, "pix", [(i, i ^ (2 * (d + 1))) for i in range(n_pix)]) for d, m in enumerate(messages)
    ]

    scores = pl.pallas_call(
        functools.partial(score_kernel, slots, pixel_count),
        in_specs=[smem, smem, smem] + [vmem] * (chips + 1),
        out_specs=vmem,
        out_shape=jax.ShapeDtypeStruct((slots, share, block), jnp.bfloat16),
        scratch_shapes=[
            pltpu.VMEM((slots, share, LANES), jnp.float32),
            pltpu.VMEM((units * block // 2, LANES), jnp.float32),
        ],
        compiler_params=params(),
        name="scores",
    )(info, relative, place, own, *received, table)
    return (smoothed, scores)


def solution(mesh):
    return jax.shard_map(
        on_device,
        mesh=mesh,
        in_specs=(
            P("ion", "pix"),
            P(None, "pix"),
            P("ion", None),
            P("ion"),
            P(),
            P("ion", None, None),
        ),
        out_specs=(P("ion", "pix"), P("ion", "pix", None)),
        check_vma=False,
    )
```

time: 165 us -> 249 us (1.51)
  Pallas kernels: 57.6 us -> 156 us
  blocking collectives: 43.2 us -> 0 us
  waiting for transfers between devices: 11.7 us -> 43.3 us
  local copies, waits for them, and re-layouts: 12.4 us -> 7.21 us
  starting transfers between devices: 22.7 us -> 25.6 us
    pallas_call x2 -> x3, Pallas kernels: 46.2 us -> 144 us  [the longest x1 98.8 us: on_device(): pl.pallas_call(functools.partial(cut_kernel, edge), grid=(1,), in_specs=[...]
    all_gather x1 -> x0, blocking collectives: 43.2 us -> none  [on_device(): table = lax.all_gather(flat, 'ion', axis=0, tiled=True)]
    ppermute x0 -> x2, waiting for transfers between devices: none -> 31.8 us  [on_device(): lax.ppermute(table, 'ion', [(i, i ^ distance) for i in range(n_ion)])]
    slice x3, local copies, waits for them, and re-layouts: 6.3 us -> 1.82 us  [the longest x1 0.91 us: on_device(): before = shifted('pix', n_pix, True, tail[6:])]
    ppermute x0 -> x2, starting transfers between devices: none -> 3.24 us  [on_device(): lax.ppermute(table, 'ion', [(i, i ^ distance) for i in range(n_ion)])]
  transfers between devices with their start and end apart: 11 -> 13, of which waited for: 3 -> 4; matrix products, arithmetic and copies ran while one was open for 6% -> 2% of each run, Pallas kernels for 32% -> 60%
where the time goes in v2:
time: 249 us
  Pallas kernels  156 us (63%)
  waiting for transfers between devices  43.3 us (17%)
  starting transfers between devices  25.6 us (10%)
  between operations  14.9 us (6%)
  local copies, waits for them, and re-layouts  7.21 us (3%)
    pallas_call x1, Pallas kernels, on_device(): pl.pallas_call(functools.partial(cut_kernel, edge), grid=(1,), in_specs=[...  98.8 us
    ppermute x2, waiting for transfers between devices, on_device(): lax.ppermute(table, 'ion', [(i, i ^ distance) for i in range(n_ion)])  31.8 us
    pallas_call x1, Pallas kernels, on_device(): pl.pallas_call(functools.partial(smooth_kernel, group, block), grid=(step...  25.4 us
    pallas_call x1, Pallas kernels, on_device(): pl.pallas_call(functools.partial(gram_kernel, blocks, block), in_specs=[s...  19.9 us
    ppermute x6, starting transfers between devices, shifted(): return lax.ppermute(value, axis, steps)  18.8 us
    ppermute x3, waiting for transfers between devices, on_device(): lax.ppermute(m, 'pix', [(i, i ^ 2 * (d + 1)) for i in range(n_pix)])  8.95 us
    pallas_call x1, Pallas kernels, on_device(): pl.pallas_call(functools.partial(score_kernel, slots, pixel_count), in_sp...  5.47 us
  transfers between devices with their start and end apart: 13, of which 4 were waited for; matrix products, arithmetic and copies ran while one was open for 2% of the time, Pallas kernels for 60%

profile of v2, /device:TPU:8, one launch (start us, length us, event | category | flops | bytes accessed | tf_op | source)
XLA Modules:
  0.0 248.6 jit_solution(13625403181156277598)
XLA Ops:
  7.2 1.0 copy-done
  8.3 98.8 %cut_edges.1 = (bf16[384,2048]{1,0:T(8,128)(2,1)}, bf16[384,2048]{1,0:T(8,128)(2,1)}, bf16[8,5120]{1,0:T(8,128)(2,1)}, bf16[8,5120]{1,0:T(8,128)(2,1)}) custom-call(bf16[5120,2048]{1,0:T(8,128)(2,1)} %x_ref.1, bf16[5120,2048]{1,0:T(8,128)(2,1)} %x_ref.1, bf16[5120,2048]{1,0:T(8,128)(2,1)} %x_ref.1), custom_call_target="tpu_custom_call" | custom-call | tf_op jit(solution)/shard_map/cut_edges/pallas_call | solution.py:245
  107.1 0.9 slice.15
  108.0 1.3 collective-permute-start
  109.3 0.9 slice.16
  110.2 3.0 %collective-permute-start.1 = (bf16[2,5120]{1,0:T(2,128)(2,1)S(1)}, bf16[2,5120]{1,0:T(2,128)(2,1)S(1)}, u32[]{:S(2)}, u32[]{:S(2)}) collective-permute-start(bf16[2,5120]{1,0:T(2,128)(2,1)S(1)} %slice.16), channel_id=1, source_target_pairs={{0,4},{4,8},{8,12},{12,16},{16,20},{20,24},{24,28},{1,5},{5,9},{9,... | collective-permute-start | bytes 61448 | tf_op jit(solution)/shard_map/ppermute | solution.py:238
  113.3 5.0 %collective-permute-start.2 = (bf16[384,2048]{1,0:T(8,128)(2,1)}, bf16[384,2048]{1,0:T(8,128)(2,1)S(1)}, u32[]{:S(2)}, u32[]{:S(2)}) collective-permute-start(bf16[384,2048]{1,0:T(8,128)(2,1)} %get-tuple-element.17), channel_id=1, source_target_pairs={{0,1},{1,2},{2,3},{4,5},{5,6},{6,7},{8,9},{9,10},{10,11},{12,13},{... | collective-permute-start | bytes 4718600 | tf_op jit(solution)/shard_map/ppermute | solution.py:238
  118.3 1.9 collective-permute-start.3
  120.3 3.2 %collective-permute-start.11 = (bf16[512,128]{1,0:T(8,128)(2,1)S(1)}, bf16[512,128]{1,0:T(8,128)(2,1)S(1)}, u32[]{:S(2)}, u32[]{:S(2)}) collective-permute-start(bf16[512,128]{1,0:T(8,128)(2,1)S(1)} %pad_maximum_fusion.1), channel_id=1, source_target_pairs={{0,2},{1,3},{2,0},{3,1},{4,6},{5,7},{6,4},{7,5},{8,10},{9,11},{10,... | collective-permute-start | bytes 393224 | tf_op jit(solution)/shard_map/ppermute | solution.py:273
  124.1 3.1 %band_weights.1.w_ref = bf16[8,768,256]{2,1,0:T(8,128)(2,1)} custom-call(f32[5,2048]{1,0:T(8,128)} %stencil_ref.1), custom_call_target="tpu_custom_call" | custom-call | bytes 3145728 | tf_op jit(solution)/shard_map/band_weights/pallas_call | solution.py:284
  127.3 0.6 reshape.17.rel_ref
  128.0 0.6 pad_add_fusion.info_ref
  128.6 31.7 %collective-permute-done.11 = bf16[512,128]{1,0:T(8,128)(2,1)S(1)} collective-permute-done((bf16[512,128]{1,0:T(8,128)(2,1)S(1)}, bf16[512,128]{1,0:T(8,128)(2,1)S(1)}, u32[]{:S(2)}, u32[]{:S(2)}) %collective-permute-start.11) | collective-permute-done | bytes 131104 | tf_op jit(solution)/shard_map/ppermute | solution.py:273
  160.4 0.7 pad_maximum_fusion
  161.2 4.3 %collective-permute-start.4 = (bf16[8,384]{1,0:T(8,128)(2,1)S(1)}, bf16[8,384]{1,0:T(8,128)(2,1)S(1)}, u32[]{:S(2)}, u32[]{:S(2)}) collective-permute-start(bf16[8,384]{1,0:T(8,128)(2,1)S(1)} %get-tuple-element.27), channel_id=1, source_target_pairs={{0,1},{1,2},{2,3},{4,5},{5,6},{6,7},{8,9},{9,10},{10,11},{12,13},{... | collective-permute-start | bytes 18440 | tf_op jit(solution)/shard_map/ppermute | solution.py:238
  165.5 3.2 %collective-permute-start.5 = (bf16[8,384]{1,0:T(8,128)(2,1)S(1)}, bf16[8,384]{1,0:T(8,128)(2,1)S(1)}, u32[]{:S(2)}, u32[]{:S(2)}) collective-permute-start(bf16[8,384]{1,0:T(8,128)(2,1)S(1)} %get-tuple-element.26), channel_id=1, source_target_pairs={{1,0},{2,1},{3,2},{5,4},{6,5},{7,6},{9,8},{10,9},{11,10},{13,12},{... | collective-permute-start | bytes 18440 | tf_op jit(solution)/shard_map/ppermute | solution.py:238
  168.7 25.4 %smooth.1 = (bf16[5120,2048]{1,0:T(8,128)(2,1)}, f32[40,128]{1,0:T(8,128)}) custom-call(bf16[5120,2048]{1,0:T(8,128)(2,1)} %x_ref.1, bf16[8,5120]{1,0:T(8,128)(2,1)} %copy-done.7, bf16[8,768,256]{2,1,0:T(8,128)(2,1)} %band_weights.1.w_ref), custom_call_target="tpu_custom_call" | custom-call | flops 16106127360 | bytes 41943040 | tf_op jit(solution)/shard_map/smooth/pallas_call | solution.py:304
  194.2 0.5 copy-done.8
  194.7 0.6 copy-done.2
  195.4 19.9 %grams.1 = (f32[49,4,16,128]{3,2,1,0:T(8,128)}, bf16[50,4,16,128]{3,2,1,0:T(8,128)(2,1)}) custom-call(s32[4]{0:T(128)} %pad_add_fusion.info_ref, s32[96]{0:T(128)} %reshape.17.rel_ref, bf16[384,2048]{1,0:T(8,128)(2,1)} %copy-done.2, bf16[384,2048]{1,0:T(8,128)(2,1)} %collective-permute-done.3.up_ref, bf16[8,384]{1,0:T(8,128)(2,1)} %copy-done.8, ...), custom_call_target="tpu_custom_call" | custom-call | flops 5637144576 | bytes 20971520 | tf_op jit(solution)/shard_map/grams/pallas_call | solution.py:318
  215.3 2.5 %collective-permute-done.6.got_ref = bf16[50,4,16,128]{3,2,1,0:T(8,128)(2,1)S(1)} collective-permute-done((bf16[50,4,16,128]{3,2,1,0:T(8,128)(2,1)}, bf16[50,4,16,128]{3,2,1,0:T(8,128)(2,1)S(1)}, u32[]{:S(2)}, u32[]{:S(2)}) %collective-permute-start.6) | collective-permute-done | bytes 819232 | tf_op jit(solution)/shard_map/ppermute | solution.py:334
  217.9 0.9 copy-done.3
  218.8 2.9 %chip_sums.1 = (f32[52,16,128]{2,1,0:T(8,128)}, bf16[56,16,128]{2,1,0:T(8,128)(2,1)}, bf16[56,16,128]{2,1,0:T(8,128)(2,1)}, bf16[56,16,128]{2,1,0:T(8,128)(2,1)}) custom-call(s32[4]{0:T(128)} %pad_add_fusion.info_ref, f32[49,4,16,128]{3,2,1,0:T(8,128)} %get-tuple-element.20.keep_ref, bf16[50,4,16,128]{3,2,1,0:T(8,128)(2,1)} %copy-done.3), custom_call_target="tpu_custom_call" | custom-call | tf_op jit(solution)/shard_map/chip_sums/pallas_call | solution.py:336
  221.6 1.4 collective-permute-start.7
  223.0 0.2 collective-permute-start.8
  223.2 2.0 collective-permute-start.9
  225.1 0.8 gather_fusion
  225.9 0.6 fusion.place_ref
  226.5 3.8 %collective-permute-done.7.refs_0_ = bf16[56,16,128]{2,1,0:T(8,128)(2,1)S(1)} collective-permute-done((bf16[56,16,128]{2,1,0:T(8,128)(2,1)}, bf16[56,16,128]{2,1,0:T(8,128)(2,1)S(1)}, u32[]{:S(2)}, u32[]{:S(2)}) %collective-permute-start.7) | collective-permute-done | bytes 229408 | tf_op jit(solution)/shard_map/ppermute | solution.py:346
  230.3 5.2 %collective-permute-done.8.refs_1_ = bf16[56,16,128]{2,1,0:T(8,128)(2,1)S(1)} collective-permute-done((bf16[56,16,128]{2,1,0:T(8,128)(2,1)}, bf16[56,16,128]{2,1,0:T(8,128)(2,1)S(1)}, u32[]{:S(2)}, u32[]{:S(2)}) %collective-permute-start.8) | collective-permute-done | bytes 229408 | tf_op jit(solution)/shard_map/ppermute | solution.py:346
  235.5 0.6 copy-done.5
  236.2 5.5 %scores.1 = bf16[48,16,128]{2,1,0:T(8,128)(2,1)} custom-call(s32[4]{0:T(128)} %pad_add_fusion.info_ref, s32[96]{0:T(128)} %reshape.17.rel_ref, s32[48]{0:T(128)} %fusion.place_ref, f32[52,16,128]{2,1,0:T(8,128)} %get-tuple-element.22.own_ref, bf16[56,16,128]{2,1,0:T(8,128)(2,1)} %copy-done.4, bf16[56,16,128]{2,1,0:T(8,128)(2,1)} %copy-done.5, ...), custom_call_target="tpu_custom_call" | custom-call | tf_op jit(solution)/shard_map/scores/pallas_call | solution.py:349
  (40 shorter events, 0.7 us)
Async XLA Ops:
  7.2 1.0 copy-start
  7.2 228.3 %all-gather.2.cloned.1.call-start = ((), (), s32[]{:S(2)}) async-start(), calls=%async_computation | async-start | bytes 2359296 | tf_op jit(solution)/shard_map/all_gather | solution.py:275
  8.2 115.2 %copy-start.10 = (s32[48,2]{0,1:T(2,128)S(1)}, s32[48,2]{0,1:T(2,128)}, u32[]{:S(2)}) copy-start(s32[48,2]{0,1:T(2,128)} %param.8) | copy-start | bytes 1156
  8.2 112.0 %collective-permute-start.10 = (bf16[256,128]{1,0:T(8,128)(2,1)S(1)}, bf16[256,128]{1,0:T(8,128)(2,1)S(1)}, u32[]{:S(2)}, u32[]{:S(2)}) collective-permute-start(bf16[256,128]{1,0:T(8,128)(2,1)S(1)} %constant_dynamic-slice_fusion), channel_id=1, source_target_pairs={{0,1},{1,0},{2,3},{3,2},{4,5},{5,4},{6,7},{7,6},{8,9},{9,8},{10,11... | collective-permute-start | bytes 196616 | tf_op jit(solution)/shard_map/ppermute | solution.py:273
  108.0 53.1 %collective-permute-start = (bf16[2,5120]{1,0:T(2,128)(2,1)S(1)}, bf16[2,5120]{1,0:T(2,128)(2,1)S(1)}, u32[]{:S(2)}, u32[]{:S(2)}) collective-permute-start(bf16[2,5120]{1,0:T(2,128)(2,1)S(1)} %slice.15), channel_id=1, source_target_pairs={{4,0},{8,4},{12,8},{16,12},{20,16},{24,20},{28,24},{5,1},{9,5},{13... | collective-permute-start | bytes 61448 | tf_op jit(solution)/shard_map/ppermute | solution.py:238
  110.2 50.9 %collective-permute-start.1 = (bf16[2,5120]{1,0:T(2,128)(2,1)S(1)}, bf16[2,5120]{1,0:T(2,128)(2,1)S(1)}, u32[]{:S(2)}, u32[]{:S(2)}) collective-permute-start(bf16[2,5120]{1,0:T(2,128)(2,1)S(1)} %slice.16), channel_id=1, source_target_pairs={{0,4},{4,8},{8,12},{12,16},{16,20},{20,24},{24,28},{1,5},{5,9},{9,... | collective-permute-start | bytes 61448 | tf_op jit(solution)/shard_map/ppermute | solution.py:238
  113.3 80.9 %collective-permute-start.2 = (bf16[384,2048]{1,0:T(8,128)(2,1)}, bf16[384,2048]{1,0:T(8,128)(2,1)S(1)}, u32[]{:S(2)}, u32[]{:S(2)}) collective-permute-start(bf16[384,2048]{1,0:T(8,128)(2,1)} %get-tuple-element.17), channel_id=1, source_target_pairs={{0,1},{1,2},{2,3},{4,5},{5,6},{6,7},{8,9},{9,10},{10,11},{12,13},{... | collective-permute-start | bytes 4718600 | tf_op jit(solution)/shard_map/ppermute | solution.py:238
  118.3 75.9 %collective-permute-start.3 = (bf16[384,2048]{1,0:T(8,128)(2,1)}, bf16[384,2048]{1,0:T(8,128)(2,1)}, u32[]{:S(2)}, u32[]{:S(2)}) collective-permute-start(bf16[384,2048]{1,0:T(8,128)(2,1)} %get-tuple-element.18), channel_id=1, source_target_pairs={{1,0},{2,1},{3,2},{5,4},{6,5},{7,6},{9,8},{10,9},{11,10},{13,12},{... | collective-permute-start | bytes 4718600 | tf_op jit(solution)/shard_map/ppermute | solution.py:238
  120.3 40.1 %collective-permute-start.11 = (bf16[512,128]{1,0:T(8,128)(2,1)S(1)}, bf16[512,128]{1,0:T(8,128)(2,1)S(1)}, u32[]{:S(2)}, u32[]{:S(2)}) collective-permute-start(bf16[512,128]{1,0:T(8,128)(2,1)S(1)} %pad_maximum_fusion.1), channel_id=1, source_target_pairs={{0,2},{1,3},{2,0},{3,1},{4,6},{5,7},{6,4},{7,5},{8,10},{9,11},{10,... | collective-permute-start | bytes 393224 | tf_op jit(solution)/shard_map/ppermute | solution.py:273
  161.2 7.5 %copy-start.7 = (bf16[8,5120]{1,0:T(8,128)(2,1)}, bf16[8,5120]{1,0:T(8,128)(2,1)S(1)}, u32[]{:S(2)}) copy-start(bf16[8,5120]{1,0:T(8,128)(2,1)S(1)} %pad_maximum_fusion.2.columns_ref) | copy-start | bytes 245764
  161.2 32.9 %collective-permute-start.4 = (bf16[8,384]{1,0:T(8,128)(2,1)S(1)}, bf16[8,384]{1,0:T(8,128)(2,1)S(1)}, u32[]{:S(2)}, u32[]{:S(2)}) collective-permute-start(bf16[8,384]{1,0:T(8,128)(2,1)S(1)} %get-tuple-element.27), channel_id=1, source_target_pairs={{0,1},{1,2},{2,3},{4,5},{5,6},{6,7},{8,9},{9,10},{10,11},{12,13},{... | collective-permute-start | bytes 18440 | tf_op jit(solution)/shard_map/ppermute | solution.py:238
  165.5 28.6 %collective-permute-start.5 = (bf16[8,384]{1,0:T(8,128)(2,1)S(1)}, bf16[8,384]{1,0:T(8,128)(2,1)S(1)}, u32[]{:S(2)}, u32[]{:S(2)}) collective-permute-start(bf16[8,384]{1,0:T(8,128)(2,1)S(1)} %get-tuple-element.26), channel_id=1, source_target_pairs={{1,0},{2,1},{3,2},{5,4},{6,5},{7,6},{9,8},{10,9},{11,10},{13,12},{... | collective-permute-start | bytes 18440 | tf_op jit(solution)/shard_map/ppermute | solution.py:238
  194.1 0.6 copy-start.8
  194.2 0.6 copy-start.9
  194.2 1.2 copy-start.2
  215.2 9.9 %copy-start.1 = (s32[160]{0:T(256)S(1)}, s32[160]{0:T(256)}, u32[]{:S(2)}) copy-start(s32[160]{0:T(256)} %param.10) | copy-start | bytes 1924
  215.3 2.6 %collective-permute-start.6 = (bf16[50,4,16,128]{3,2,1,0:T(8,128)(2,1)}, bf16[50,4,16,128]{3,2,1,0:T(8,128)(2,1)S(1)}, u32[]{:S(2)}, u32[]{:S(2)}) collective-permute-start(bf16[50,4,16,128]{3,2,1,0:T(8,128)(2,1)} %get-tuple-element.21), channel_id=1, source_target_pairs={{0,4},{4,0},{8,12},{12,8},{16,20},{20,16},{24,28},{28,24},{1,5},{5... | collective-permute-start | bytes 2457608 | tf_op jit(solution)/shard_map/ppermute | solution.py:334
  217.9 0.9 copy-start.3
  221.6 8.7 %collective-permute-start.7 = (bf16[56,16,128]{2,1,0:T(8,128)(2,1)}, bf16[56,16,128]{2,1,0:T(8,128)(2,1)S(1)}, u32[]{:S(2)}, u32[]{:S(2)}) collective-permute-start(bf16[56,16,128]{2,1,0:T(8,128)(2,1)} %get-tuple-element.23), channel_id=1, source_target_pairs={{0,8},{4,12},{8,0},{12,4},{16,24},{20,28},{24,16},{28,20},{1,9},{5... | collective-permute-start | bytes 688136 | tf_op jit(solution)/shard_map/ppermute | solution.py:346
  223.0 12.5 %collective-permute-start.8 = (bf16[56,16,128]{2,1,0:T(8,128)(2,1)}, bf16[56,16,128]{2,1,0:T(8,128)(2,1)S(1)}, u32[]{:S(2)}, u32[]{:S(2)}) collective-permute-start(bf16[56,16,128]{2,1,0:T(8,128)(2,1)} %get-tuple-element.24), channel_id=1, source_target_pairs={{0,16},{4,20},{8,24},{12,28},{16,0},{20,4},{24,8},{28,12},{1,17},{... | collective-permute-start | bytes 688136 | tf_op jit(solution)/shard_map/ppermute | solution.py:346
  223.2 12.3 %collective-permute-start.9 = (bf16[56,16,128]{2,1,0:T(8,128)(2,1)}, bf16[56,16,128]{2,1,0:T(8,128)(2,1)S(1)}, u32[]{:S(2)}, u32[]{:S(2)}) collective-permute-start(bf16[56,16,128]{2,1,0:T(8,128)(2,1)} %get-tuple-element.25), channel_id=1, source_target_pairs={{0,24},{4,28},{8,16},{12,20},{16,8},{20,12},{24,0},{28,4},{1,25},{... | collective-permute-start | bytes 688136 | tf_op jit(solution)/shard_map/ppermute | solution.py:346
  230.3 5.2 %copy-start.4 = (bf16[56,16,128]{2,1,0:T(8,128)(2,1)}, bf16[56,16,128]{2,1,0:T(8,128)(2,1)S(1)}, u32[]{:S(2)}) copy-start(bf16[56,16,128]{2,1,0:T(8,128)(2,1)S(1)} %collective-permute-done.7.refs_0_) | copy-start | bytes 688132
  235.5 0.7 copy-start.5
  235.5 0.8 copy-start.6
Sparse Core Ops, SparseCore 0:
  161.2 28.9 all-gather.1

commit v3 on v1

--- a/solution.py
+++ b/solution.py
@@ -50,14 +50,14 @@
         out_ref[j, 2 * TILE : 2 * TILE + LANES], out_ref[j, 2 * TILE + LANES :] = split(edge)
 
 
-def smooth_rows(x_ref, halo_ref, w_ref, store):
+def smooth_rows(x_ref, halo, w_ref, store):
     rows, width = x_ref.shape
     tiles = width // TILE
     first = lax.broadcasted_iota(jnp.int32, (rows, LANES), 1) < HALF
     for j in range(tiles):
         own = x_ref[:, j * TILE : (j + 1) * TILE]
-        before = halo_ref[...] if j == 0 else x_ref[:, j * TILE - LANES : j * TILE]
-        after = halo_ref[...] if j == tiles - 1 else x_ref[:, (j + 1) * TILE : (j + 1) * TILE + LANES]
+        before = halo if j == 0 else x_ref[:, j * TILE - LANES : j * TILE]
+        after = halo if j == tiles - 1 else x_ref[:, (j + 1) * TILE : (j + 1) * TILE + LANES]
         edge = jnp.where(first, after, before)
         window = jnp.concatenate([own, own, edge, edge], axis=1)
         store(j, jnp.dot(window, w_ref[j], preferred_element_type=jnp.float32))
@@ -83,7 +83,43 @@
     return jnp.where(core == 0, parts[:, 0], parts[:, 1]), jnp.where(core == 0, parts[:, 1], parts[:, 0])
 
 
-def main_kernel(steps, group, block, info_ref, rel_ref, x_ref, halo_ref, w_ref,
+def cut_kernel(images_ref, top_ref, bottom_ref, head_ref, tail_ref, strips, bands, sems):
+    rows, width = images_ref.shape
+    edge = top_ref.shape[0]
+    reads = [
+        pltpu.make_async_copy(images_ref.at[:, pl.ds(0, LANES)], strips.at[0], sems.at[0]),
+        pltpu.make_async_copy(images_ref.at[:, pl.ds(width - LANES, LANES)], strips.at[1], sems.at[1]),
+        pltpu.make_async_copy(images_ref.at[pl.ds(0, edge)], bands.at[0], sems.at[2]),
+        pltpu.make_async_copy(images_ref.at[pl.ds(rows - edge, edge)], bands.at[1], sems.at[3]),
+    ]
+    writes = [
+        pltpu.make_async_copy(bands.at[0], top_ref, sems.at[4]),
+        pltpu.make_async_copy(bands.at[1], bottom_ref, sems.at[5]),
+    ]
+    for copy in reads:
+        copy.start()
+    row = lax.broadcasted_iota(jnp.int32, (8, LANES), 0)
+    lane = lax.broadcasted_iota(jnp.int32, (8, LANES), 1)
+    for k, (out, shift) in enumerate(((head_ref, 0), (tail_ref, LANES - 8))):
+        reads[k].wait()
+        pick = (lane == row + shift).astype(jnp.bfloat16)
+        out[...] = gram_of(pick, strips[k]).astype(jnp.bfloat16)
+    for k in range(2):
+        reads[2 + k].wait()
+        writes[k].start()
+    for copy in writes:
+        copy.wait()
+
+
+def halo_tile(columns_ref):
+    columns = columns_ref[...].astype(jnp.float32).T.astype(jnp.bfloat16)
+    row = lax.broadcasted_iota(jnp.int32, (8, LANES), 0)
+    lane = lax.broadcasted_iota(jnp.int32, (8, LANES), 1)
+    place = (lane == row + jnp.where(row < 4, 0, LANES - 8)).astype(jnp.bfloat16)
+    return jnp.dot(columns, place, preferred_element_type=jnp.float32).astype(jnp.bfloat16)
+
+
+def main_kernel(steps, group, block, pairs_ref, x_ref, columns_ref, w_ref,
                 out_ref, energy_ref, keep_ref, give_ref, held, wide):
     step = pl.program_id(0)
     blocks = steps * group
@@ -101,17 +137,18 @@
             squares = lane_pairs(values)
             total[0] = squares if j == 0 else total[0] + squares
 
-        smooth_rows(x_ref, halo_ref, w_ref, store)
+        smooth_rows(x_ref, halo_tile(columns_ref), w_ref, store)
         for g in range(group):
             energy_ref[pl.ds(step * group + g, 1), :] = row_sums(total[0][g * block : (g + 1) * block, :])
 
     @pl.when(step == steps)
     def grams():
-        core = info_ref[0]
+        core = lax.axis_index("pix") % 2
+        first = lax.axis_index("ion") * blocks
 
         def one(s, carry):
-            a = rel_ref[2 * s]
-            b = jnp.clip(rel_ref[2 * s + 1], 0, blocks - 1)
+            a = pairs_ref[0, s] - first
+            b = jnp.clip(pairs_ref[1, s] - first, 0, blocks - 1)
             keep_ref[s], wide[s] = by_core(gram_of(held[a], held[b]), chips, core)
             return carry
 
@@ -119,10 +156,12 @@
         give_ref[:slots] = wide[...].astype(jnp.bfloat16)
 
 
-def cross_kernel(blocks, block, info_ref, rel_ref, slots, down_ref, up_ref, down_halo_ref, up_halo_ref, w_ref, energy_ref,
+def cross_kernel(blocks, block, pairs_ref, down_ref, up_ref, down_columns_ref, up_columns_ref, w_ref, energy_ref,
                  smoothed_ref, keep_in, give_in, keep_ref, give_ref, near, own, table, keep_part, give_part, sems):
     del keep_in, give_in
-    core = info_ref[0]
+    core = lax.axis_index("pix") % 2
+    first_block = lax.axis_index("ion") * blocks
+    slots = pairs_ref.shape[1]
     chips, share = keep_part.shape[1:3]
     units = 2 * table.shape[0] // block
     edge = REACH * block
@@ -136,7 +175,7 @@
 
     table[...] = jnp.zeros_like(table)
     table[REACH : REACH + blocks, :] = energy_ref[...]
-    for side, (x_ref, halo_ref) in enumerate(((down_ref, down_halo_ref), (up_ref, up_halo_ref))):
+    for side, (x_ref, columns_ref) in enumerate(((down_ref, down_columns_ref), (up_ref, up_columns_ref))):
         total = [None]
 
         def store(j, values):
@@ -144,7 +183,7 @@
             squares = lane_pairs(values)
             total[0] = squares if j == 0 else total[0] + squares
 
-        smooth_rows(x_ref, halo_ref, w_ref, store)
+        smooth_rows(x_ref, halo_tile(columns_ref), w_ref, store)
         for k in range(REACH):
             row = side * (REACH + blocks) + k
             table[row : row + 1, :] = row_sums(total[0][k * block : (k + 1) * block, :])
@@ -166,7 +205,7 @@
         copy.wait()
 
     def one(s, carry):
-        a, b = rel_ref[2 * s], rel_ref[2 * s + 1]
+        a, b = pairs_ref[0, s] - first_block, pairs_ref[1, s] - first_block
 
         @pl.when((b < 0) | (b >= blocks))
         def crossing():
@@ -189,10 +228,20 @@
     lax.fori_loop(0, slots, one, 0)
 
 
-def chip_kernel(slots, units, info_ref, keep_ref, got_ref, own_ref, *out_refs):
-    chip = info_ref[1]
+def fetch(sources, targets, sems):
+    copies = [pltpu.make_async_copy(x, y, sems.at[k]) for k, (x, y) in enumerate(zip(sources, targets))]
+    for copy in copies:
+        copy.start()
+    return copies
+
+
+def chip_kernel(slots, units, keep_hbm, got_hbm, own_ref, *refs):
+    out_refs, (keep_ref, got_ref, sems) = refs[:-3], refs[-3:]
+    chip = lax.axis_index("pix") // 2
     chips, share = keep_ref.shape[1:3]
     shape = (units * chips, share, LANES)
+    for copy in fetch((keep_hbm, got_hbm), (keep_ref, got_ref), sems):
+        copy.wait()
     energies = keep_ref[slots:] + (
         got_ref[slots : slots + units].astype(jnp.float32) + got_ref[slots + units :].astype(jnp.float32)
     )
@@ -209,12 +258,21 @@
             out[slots + units * chips :] = low.reshape(shape)
 
 
-def score_kernel(slots, pixel_count, info_ref, rel_ref, place_ref, own_ref, *refs):
-    got_refs, (table_ref, out_ref, gram, inverse) = refs[:-4], refs[-4:]
-    share = gram.shape[1]
-    block = table_ref.shape[1]
+def score_kernel(blocks, place_of, pixel_count, pairs_ref, live_ref, rules_ref, *refs):
+    chips = (len(refs) - 7) // 2
+    sources, refs = refs[: chips + 2], refs[chips + 2 :]
+    out_ref, own_ref, got_refs, table_ref, gram, inverse, sems = (
+        refs[0], refs[1], refs[2 : chips + 1], refs[-4], refs[-3], refs[-2], refs[-1]
+    )
+    slots, share = gram.shape[:2]
+    block = out_ref.shape[2]
     e_units = inverse.shape[0] // share
-    live, offset = info_ref[2], info_ref[3]
+    half = table_ref.shape[0] // 2
+    targets = (own_ref, *got_refs, table_ref.at[pl.ds(0, half)], table_ref.at[pl.ds(half, half)])
+    copies = fetch(sources, targets, sems)
+    pix, first = lax.axis_index("pix"), lax.axis_index("ion") * blocks
+    for copy in copies[:-2]:
+        copy.wait()
     total = own_ref[:slots]
     energies = own_ref[slots:]
     for got in got_refs:
@@ -225,19 +283,27 @@
     gram[...] = total
     inverse[...] = (1.0 / jnp.sqrt(energies / pixel_count + 1e-06)).reshape(inverse.shape)
     lane = lax.broadcasted_iota(jnp.int32, (share, LANES), 1)
-    mine = lane == lax.broadcasted_iota(jnp.int32, (share, LANES), 0) + offset
+    mine = lane == lax.broadcasted_iota(jnp.int32, (share, LANES), 0) + pix * share
+    for copy in copies[-2:]:
+        copy.wait()
 
     def one(s, carry):
-        inv_a = inverse[pl.ds(rel_ref[2 * s] + REACH, 1), :]
-        inv_b = inverse[pl.ds(rel_ref[2 * s + 1] + REACH, 1), :]
+        a, b = pairs_ref[0, s], pairs_ref[1, s]
+        inv_a = inverse[pl.ds(a - first + REACH, 1), :]
+        inv_b = inverse[pl.ds(b - first + REACH, 1), :]
         inv_a = jnp.sum(jnp.where(mine, inv_a, 0.0), axis=1, keepdims=True)
         coloc = (gram[s] * inv_a * inv_b / pixel_count).astype(jnp.bfloat16)
-        matrix = table_ref[pl.ds(pl.multiple_of(place_ref[s], block), block), :]
-        scores = jnp.dot(coloc, matrix, preferred_element_type=jnp.float32)
-        out_ref[s] = jnp.where(s < live, scores, 0.0).astype(jnp.bfloat16)
+        scores = jnp.zeros((share, block), jnp.float32)
+        pieces = place_of(rules_ref[b])
+        depth = block // len(pieces)
+        for k, at in enumerate(pieces):
+            matrix = table_ref[pl.ds(pl.multiple_of(at, depth), depth), :]
+            part = coloc[:, k * depth : (k + 1) * depth]
+            scores = scores + jnp.dot(part, matrix, preferred_element_type=jnp.float32)
+        out_ref[s] = jnp.where(s < live_ref[0], scores, 0.0).astype(jnp.bfloat16)
         return carry
 
-    lax.fori_loop(0, slots, one, 0, unroll=4)
+    lax.fori_loop(0, slots, one, 0, unroll=8)
 
 
 def on_device(images, stencil, pairs, live, rule_of_block, adduct):
@@ -256,30 +322,57 @@
         steps = [(i, i + 1) if up else (i + 1, i) for i in range(size - 1)]
         return lax.ppermute(value, axis, steps)
 
-    def to_neighbours(value):
-        return (
-            shifted("ion", n_ion, True, value[rows - edge :]),
-            shifted("ion", n_ion, False, value[:edge]),
-        )
-
-    before = shifted("pix", n_pix, True, images[:, width - 2 :])
-    after = shifted("pix", n_pix, False, images[:, :2])
-    down, up = to_neighbours(images)
-    halo = jnp.concatenate([after, jnp.zeros((rows, LANES - 4), images.dtype), before], axis=1)
-    down_halo, up_halo = to_neighbours(halo)
+    vmem = pl.BlockSpec(memory_space=pltpu.VMEM)
+    smem = pl.BlockSpec(memory_space=pltpu.SMEM)
+    hbm = pl.BlockSpec(memory_space=pl.ANY)
+    edge_rows = jax.ShapeDtypeStruct((edge, width), images.dtype)
+    edge_columns = jax.ShapeDtypeStruct((8, rows), images.dtype)
+    top, bottom, head, tail = pl.pallas_call(
+        cut_kernel,
+        in_specs=[hbm],
+        out_specs=[hbm, hbm, vmem, vmem],
+        out_shape=[edge_rows, edge_rows, edge_columns, edge_columns],
+        scratch_shapes=[
+            pltpu.VMEM((2, rows, LANES), images.dtype),
+            pltpu.VMEM((2, edge, width), images.dtype),
+            pltpu.SemaphoreType.DMA((6,)),
+        ],
+        compiler_params=params(),
+        cost_estimate=cost(0, 8 * edge * width),
+        name="cut_edges",
+    )(images)
+
+    before = shifted("pix", n_pix, True, tail[6:])
+    after = shifted("pix", n_pix, False, head[:2])
+    down = shifted("ion", n_ion, True, bottom)
+    up = shifted("ion", n_ion, False, top)
+    columns = jnp.concatenate([after, jnp.zeros((4, rows), images.dtype), before], axis=0)
+    down_columns = shifted("ion", n_ion, True, columns[:, rows - edge :])
+    up_columns = shifted("ion", n_ion, False, columns[:, :edge])
 
     flat = adduct.reshape(rules_here * block, block)
     part = rules_here * block // n_pix
-    flat = lax.dynamic_slice_in_dim(flat, pix * part, part, 0)
-    table = lax.all_gather(flat, "ion", axis=0, tiled=True)
-    table = lax.all_gather(table, "pix", axis=0, tiled=True)
-    rules = jnp.take(rule_of_block, pairs[:, 1], axis=0)
-    if part % block == 0:
-        row = rules % rules_here * block
-        place = (row // part * n_ion + rules // rules_here) * part + row % part
-    else:
-        table = table.reshape(n_pix, n_ion, part, block).swapaxes(0, 1).reshape(-1, block)
-        place = rules * block
+    mine = lax.dynamic_slice_in_dim(flat, pix * part, part, 0)
+    axes = []
+    for axis, size, index in (("ion", n_ion, ion), ("pix", n_pix, pix)):
+        distances = [2**k for k in range(size.bit_length() - 1)]
+        axes += [(axis, size, d) for d in (distances if axis == "ion" else distances[::-1])]
+    for k, (axis, size, distance) in enumerate(axes):
+        other = lax.ppermute(mine, axis, [(i, i ^ distance) for i in range(size)])
+        if k < len(axes) - 1:
+            mine = jnp.concatenate([mine, other], axis=0)
+
+    def place_of(rule):
+        here = {"ion": lax.axis_index("ion"), "pix": lax.axis_index("pix")}
+        row = rule % rules_here * block
+        pieces = []
+        for offset in range(0, block, min(part, block)):
+            from_ = {"ion": rule // rules_here, "pix": (row + offset) // part}
+            at = (row + offset) % part
+            for k, (axis, _, distance) in enumerate(axes):
+                at = at + (((from_[axis] ^ here[axis]) // distance) % 2) * (part << k)
+            pieces.append(at)
+        return pieces
 
     weights = pl.pallas_call(
         weights_kernel,
@@ -289,9 +382,8 @@
         name="band_weights",
     )(stencil)
 
-    info = jnp.stack([core, chip, live[0], pix * share]).astype(jnp.int32)
-    relative = (pairs - ion * blocks).reshape(-1)
-    group = next(g for g in (4, 2, 1) if blocks % g == 0)
+    table_pairs = pairs.T
+    group = next(g for g in (8, 5, 4, 2, 1) if blocks % g == 0)
     steps = blocks // group
     units = -(-2 * (blocks + 2 * REACH) // block)
     half = (chips, share, LANES)
@@ -304,9 +396,13 @@
     smoothed, energy, keep, give = pl.pallas_call(
         functools.partial(main_kernel, steps, group, block),
         grid_spec=pltpu.PrefetchScalarGridSpec(
-            num_scalar_prefetch=2,
+            num_scalar_prefetch=1,
             grid=(steps + 1,),
-            in_specs=[rows_at(width), rows_at(LANES), whole(weights.shape)],
+            in_specs=[
+                rows_at(width),
+                pl.BlockSpec((8, group * block), lambda i, *_: (0, jnp.minimum(i, steps - 1))),
+                whole(weights.shape),
+            ],
             out_specs=[rows_at(width), whole((blocks, LANES)), whole(keep_shape), whole(give_shape)],
             scratch_shapes=[
                 pltpu.VMEM((blocks, block, width), jnp.bfloat16),
@@ -322,21 +418,14 @@
         compiler_params=params(),
         cost_estimate=cost(2 * rows * width * DEPTH + 2 * slots * block * block * width, 4 * rows * width),
         name="smooth_and_gram",
-    )(info, relative, images, halo, weights)
-
-    smem = pl.BlockSpec(memory_space=pltpu.SMEM)
-    vmem = pl.BlockSpec(memory_space=pltpu.VMEM)
-    hbm = pl.BlockSpec(memory_space=pl.ANY)
-
-    def cross(info_ref, rel_ref, *refs):
-        cross_kernel(blocks, block, info_ref, rel_ref, slots, *refs)
+    )(table_pairs, images, columns, weights)
 
     keep, give = pl.pallas_call(
-        cross,
-        in_specs=[smem, smem] + [vmem] * 6 + [hbm] * 3,
+        functools.partial(cross_kernel, blocks, block),
+        in_specs=[smem] + [vmem] * 6 + [hbm] * 3,
         out_specs=[hbm, hbm],
         out_shape=[jax.ShapeDtypeStruct(keep_shape, jnp.float32), jax.ShapeDtypeStruct(give_shape, jnp.bfloat16)],
-        input_output_aliases={9: 0, 10: 1},
+        input_output_aliases={8: 0, 9: 1},
         scratch_shapes=[
             pltpu.VMEM((2, edge, width), jnp.bfloat16),
             pltpu.VMEM((2, edge, width), jnp.bfloat16),
@@ -348,35 +437,45 @@
         compiler_params=params(),
         cost_estimate=cost(4 * edge * width * DEPTH, 8 * edge * width),
         name="cross_grams",
-    )(info, relative, down, up, down_halo, up_halo, weights, energy, smoothed, keep, give)
+    )(table_pairs, down, up, down_columns, up_columns, weights, energy, smoothed, keep, give)
 
     got = lax.ppermute(give, "pix", [(i, i ^ 1) for i in range(n_pix)])
     message = jax.ShapeDtypeStruct((slots + 2 * units * chips, share, LANES), jnp.bfloat16)
+    own_rows = jax.ShapeDtypeStruct((slots + units * chips, share, LANES), jnp.float32)
+    small = pltpu.CompilerParams(vmem_limit_bytes=16 * 1024 * 1024)
     own, *messages = pl.pallas_call(
         functools.partial(chip_kernel, slots, units),
-        in_specs=[smem, vmem, vmem],
+        in_specs=[hbm, hbm],
         out_specs=[vmem] * chips,
-        out_shape=[jax.ShapeDtypeStruct((slots + units * chips, share, LANES), jnp.float32)]
-        + [message] * (chips - 1),
-        compiler_params=params(),
+        out_shape=[own_rows] + [message] * (chips - 1),
+        scratch_shapes=[
+            pltpu.VMEM(keep_shape, jnp.float32),
+            pltpu.VMEM(give_shape, jnp.bfloat16),
+            pltpu.SemaphoreType.DMA((2,)),
+        ],
+        compiler_params=small,
         name="chip_sums",
-    )(info, keep, got)
+    )(keep, got)
     received = [
         lax.ppermute(m, "pix", [(i, i ^ (2 * (d + 1))) for i in range(n_pix)]) for d, m in enumerate(messages)
     ]
 
     scores = pl.pallas_call(
-        functools.partial(score_kernel, slots, pixel_count),
-        in_specs=[smem, smem, smem] + [vmem] * (chips + 1),
+        functools.partial(score_kernel, blocks, place_of, pixel_count),
+        in_specs=[smem] * 3 + [hbm] * (chips + 2),
         out_specs=vmem,
         out_shape=jax.ShapeDtypeStruct((slots, share, block), jnp.bfloat16),
         scratch_shapes=[
+            pltpu.VMEM(own_rows.shape, jnp.float32),
+            *[pltpu.VMEM(message.shape, jnp.bfloat16)] * (chips - 1),
+            pltpu.VMEM((2 * mine.shape[0], block), jnp.bfloat16),
             pltpu.VMEM((slots, share, LANES), jnp.float32),
             pltpu.VMEM((units * block // 2, LANES), jnp.float32),
+            pltpu.SemaphoreType.DMA((chips + 2,)),
         ],
-        compiler_params=params(),
+        compiler_params=small,
         name="scores",
-    )(info, relative, place, own, *received, table)
+    )(table_pairs, live, rule_of_block, own, *received, mine, other)
     return (smoothed, scores)
 
 

time: 165 us -> 136 us (0.82); the launches traced: 164 us -> 133 us
  blocking collectives: 43.2 us -> 0 us
  waiting for transfers between devices: 11.7 us -> 43.6 us
  between operations: 14.9 us -> 1.55 us
  local copies, waits for them, and re-layouts: 12.4 us -> 5.98 us
  starting transfers between devices: 22.7 us -> 25 us
  other arithmetic: 1.99 us -> 0.15 us
    all_gather x1 -> x0, blocking collectives: 43.2 us -> none  [on_device(): table = lax.all_gather(flat, 'ion', axis=0, tiled=True)]
    ppermute x0 -> x5, waiting for transfers between devices: none -> 32.5 us  [on_device(): other = lax.ppermute(mine, axis, [(i, i ^ distance) for i in range(size)])]
    ppermute x0 -> x5, starting transfers between devices: none -> 5.28 us  [on_device(): other = lax.ppermute(mine, axis, [(i, i ^ distance) for i in range(size)])]
    slice x3, local copies, waits for them, and re-layouts: 6.3 us -> 1.82 us  [the longest x1 0.91 us: on_device(): before = shifted('pix', n_pix, True, tail[6:])]
    ppermute x6, starting transfers between devices: 19.1 us -> 16.1 us  [shifted(): return lax.ppermute(value, axis, steps)]
    unnamed x22 -> x20, local copies, waits for them, and re-layouts: 3.17 us -> 4.01 us
    pallas_call x3 -> x4, Pallas kernels: 19.2 us -> 19.8 us  [the longest x1 9.23 us: on_device(): pl.pallas_call(functools.partial(cross_kernel, blocks, block), in_specs=[...]
  transfers between devices with their start and end apart: 11 -> 15, of which waited for: 3 -> 5; matrix products, arithmetic and copies ran while one was open for 6% -> 2% of each run, Pallas kernels for 32% -> 35%
where the time goes in v3:
time: 136 us; the launch traced here: 133 us
  Pallas kernels  56.7 us (42%)
  waiting for transfers between devices  43.6 us (32%)
  starting transfers between devices  25 us (18%)
  local copies, waits for them, and re-layouts  5.98 us (4%)
  between operations  1.55 us (1%)
    pallas_call x1, Pallas kernels, on_device(): pl.pallas_call(functools.partial(main_kernel, steps, group, block), grid_...  33.8 us
    ppermute x5, waiting for transfers between devices, on_device(): other = lax.ppermute(mine, axis, [(i, i ^ distance) for i in range(size)])  32.5 us
    ppermute x6, starting transfers between devices, shifted(): return lax.ppermute(value, axis, steps)  16.1 us
    ppermute x3, waiting for transfers between devices, on_device(): lax.ppermute(m, 'pix', [(i, i ^ 2 * (d + 1)) for i in range(n_pix)])  9.27 us
    pallas_call x1, Pallas kernels, on_device(): pl.pallas_call(functools.partial(cross_kernel, blocks, block), in_specs=[...  9.23 us
    pallas_call x1, Pallas kernels, on_device(): pl.pallas_call(functools.partial(score_kernel, blocks, place_of, pixel_co...  5.4 us
    ppermute x5, starting transfers between devices, on_device(): other = lax.ppermute(mine, axis, [(i, i ^ distance) for i in range(size)])  5.28 us
    pallas_call x1, Pallas kernels, on_device(): pl.pallas_call(cut_kernel, in_specs=[hbm], out_specs=[hbm, hbm, vmem, vme...  4.65 us
  transfers between devices with their start and end apart: 15, of which 5 were waited for; matrix products, arithmetic and copies ran while one was open for 2% of the time, Pallas kernels for 35%

profile of v3, /device:TPU:8, one launch (start us, length us, event | category | flops | bytes accessed | tf_op | source)
XLA Modules:
  0.0 133.0 jit_solution(7737142932470307181)
XLA Ops:
  0.6 4.7 %cut_edges.1 = (bf16[384,2048]{1,0:T(8,128)(2,1)}, bf16[384,2048]{1,0:T(8,128)(2,1)}, bf16[8,5120]{1,0:T(8,128)(2,1)}, bf16[8,5120]{1,0:T(8,128)(2,1)}) custom-call(bf16[5120,2048]{1,0:T(8,128)(2,1)} %x_ref.1), custom_call_target="tpu_custom_call" | custom-call | bytes 6291456 | tf_op jit(solution)/shard_map/cut_edges/pallas_call | solution.py:330
  5.3 0.9 slice.12
  6.2 1.3 collective-permute-start
  7.5 0.9 slice.13
  8.4 3.0 %collective-permute-start.1 = (bf16[2,5120]{1,0:T(2,128)(2,1)S(1)}, bf16[2,5120]{1,0:T(2,128)(2,1)S(1)}, u32[]{:S(2)}, u32[]{:S(2)}) collective-permute-start(bf16[2,5120]{1,0:T(2,128)(2,1)S(1)} %slice.13), channel_id=1, source_target_pairs={{0,4},{4,8},{8,12},{12,16},{16,20},{20,24},{24,28},{1,5},{5,9},{9,... | collective-permute-start | bytes 61448 | tf_op jit(solution)/shard_map/ppermute | solution.py:323
  11.4 3.5 %collective-permute-start.2 = (bf16[384,2048]{1,0:T(8,128)(2,1)}, bf16[384,2048]{1,0:T(8,128)(2,1)S(1)}, u32[]{:S(2)}, u32[]{:S(2)}) collective-permute-start(bf16[384,2048]{1,0:T(8,128)(2,1)} %get-tuple-element.19), channel_id=1, source_target_pairs={{0,1},{1,2},{2,3},{4,5},{5,6},{6,7},{8,9},{9,10},{10,11},{12,13},{... | collective-permute-start | bytes 4718600 | tf_op jit(solution)/shard_map/ppermute | solution.py:323
  14.9 2.5 %collective-permute-start.3 = (bf16[384,2048]{1,0:T(8,128)(2,1)}, bf16[384,2048]{1,0:T(8,128)(2,1)S(1)}, u32[]{:S(2)}, u32[]{:S(2)}) collective-permute-start(bf16[384,2048]{1,0:T(8,128)(2,1)} %get-tuple-element.20), channel_id=1, source_target_pairs={{1,0},{2,1},{3,2},{5,4},{6,5},{7,6},{9,8},{10,9},{11,10},{13,12},{... | collective-permute-start | bytes 4718600 | tf_op jit(solution)/shard_map/ppermute | solution.py:323
  17.4 0.9 constant_dynamic-update-slice_fusion.4
  18.4 3.1 %band_weights.1.w_ref = bf16[8,768,256]{2,1,0:T(8,128)(2,1)} custom-call(f32[5,2048]{1,0:T(8,128)} %stencil_ref.1), custom_call_target="tpu_custom_call" | custom-call | bytes 3145728 | tf_op jit(solution)/shard_map/band_weights/pallas_call | solution.py:377
  21.5 0.1 pad_maximum_fusion.3.columns_ref
  21.6 32.0 %collective-permute-done.10 = bf16[256,128]{1,0:T(8,128)(2,1)S(1)} collective-permute-done((bf16[256,128]{1,0:T(8,128)(2,1)S(1)}, bf16[256,128]{1,0:T(8,128)(2,1)S(1)}, u32[]{:S(2)}, u32[]{:S(2)}) %collective-permute-start.10) | collective-permute-done | bytes 65568 | tf_op jit(solution)/shard_map/ppermute | solution.py:361
  53.7 2.6 %collective-permute-start.11 = (bf16[512,128]{1,0:T(8,128)(2,1)S(1)}, bf16[512,128]{1,0:T(8,128)(2,1)S(1)}, u32[]{:S(2)}, u32[]{:S(2)}) collective-permute-start(bf16[512,128]{1,0:T(8,128)(2,1)S(1)} %pad_maximum_fusion.2), channel_id=1, source_target_pairs={{0,2},{1,3},{2,0},{3,1},{4,6},{5,7},{6,4},{7,5},{8,10},{9,11},{10,... | collective-permute-start | bytes 393224 | tf_op jit(solution)/shard_map/ppermute | solution.py:361
  56.2 3.3 %collective-permute-start.4 = (bf16[8,384]{1,0:T(8,128)(2,1)S(1)}, bf16[8,384]{1,0:T(8,128)(2,1)S(1)}, u32[]{:S(2)}, u32[]{:S(2)}) collective-permute-start(bf16[8,384]{1,0:T(8,128)(2,1)S(1)} %get-tuple-element.33), channel_id=1, source_target_pairs={{0,1},{1,2},{2,3},{4,5},{5,6},{6,7},{8,9},{9,10},{10,11},{12,13},{... | collective-permute-start | bytes 18440 | tf_op jit(solution)/shard_map/ppermute | solution.py:323
  59.6 2.5 %collective-permute-start.5 = (bf16[8,384]{1,0:T(8,128)(2,1)S(1)}, bf16[8,384]{1,0:T(8,128)(2,1)S(1)}, u32[]{:S(2)}, u32[]{:S(2)}) collective-permute-start(bf16[8,384]{1,0:T(8,128)(2,1)S(1)} %get-tuple-element.32), channel_id=1, source_target_pairs={{1,0},{2,1},{3,2},{5,4},{6,5},{7,6},{9,8},{10,9},{11,10},{13,12},{... | collective-permute-start | bytes 18440 | tf_op jit(solution)/shard_map/ppermute | solution.py:323
  62.1 1.6 %collective-permute-start.12 = (bf16[1024,128]{1,0:T(8,128)(2,1)S(1)}, bf16[1024,128]{1,0:T(8,128)(2,1)S(1)}, u32[]{:S(2)}, u32[]{:S(2)}) collective-permute-start(bf16[1024,128]{1,0:T(8,128)(2,1)S(1)} %pad_maximum_fusion.1), channel_id=1, source_target_pairs={{0,16},{4,20},{8,24},{12,28},{16,0},{20,4},{24,8},{28,12},{1,17},{... | collective-permute-start | bytes 786440 | tf_op jit(solution)/shard_map/ppermute | solution.py:361
  63.7 33.8 %smooth_and_gram.1 = (bf16[5120,2048]{1,0:T(8,128)(2,1)}, f32[40,128]{1,0:T(8,128)}, f32[49,4,16,128]{3,2,1,0:T(8,128)}, bf16[50,4,16,128]{3,2,1,0:T(8,128)(2,1)}) custom-call(s32[2,48]{1,0:T(2,128)} %bitcast.2, bf16[5120,2048]{1,0:T(8,128)(2,1)} %x_ref.1, bf16[8,5120]{1,0:T(8,128)(2,1)} %copy-done.5, bf16[8,768,256]{2,1,0:T(8,128)(2,1)} %band_weights.1.w_ref), custom_call_target="tpu_custom_call" | custom-call | flops 19327352832 | bytes 41943040 | tf_op jit(solution)/shard_map/smooth_and_gram/pallas_call | solution.py:396
  97.6 1.0 collective-permute-start.13
  98.7 0.5 copy-done.6
  99.2 0.6 copy-done.3
  99.9 0.5 copy-done.4
  100.3 9.2 %cross_grams.1 = (f32[49,4,16,128]{3,2,1,0:T(8,128)}, bf16[50,4,16,128]{3,2,1,0:T(8,128)(2,1)}) custom-call(s32[2,48]{1,0:T(2,128)} %bitcast.3, bf16[384,2048]{1,0:T(8,128)(2,1)} %copy-done.3, bf16[384,2048]{1,0:T(8,128)(2,1)} %copy-done.4, bf16[8,384]{1,0:T(8,128)(2,1)} %copy-done.6, ...), custom_call_target="tpu_custom_call", output_to_operand_aliasing={{0}: (8, {}), {1}: (9, {})} | custom-call | flops 2415919104 | bytes 6291456 | tf_op jit(solution)/shard_map/cross_grams/pallas_call | solution.py:423
  109.7 0.5 collective-permute-done.13
  110.2 0.1 collective-permute-start.14
  110.3 1.9 %collective-permute-done.6.got_hbm = bf16[50,4,16,128]{3,2,1,0:T(8,128)(2,1)S(1)} collective-permute-done((bf16[50,4,16,128]{3,2,1,0:T(8,128)(2,1)}, bf16[50,4,16,128]{3,2,1,0:T(8,128)(2,1)S(1)}, u32[]{:S(2)}, u32[]{:S(2)}) %collective-permute-start.6) | collective-permute-done | bytes 819232 | tf_op jit(solution)/shard_map/ppermute | solution.py:442
  112.2 1.4 %copy-done = f32[49,4,16,128]{3,2,1,0:T(8,128)S(1)} copy-done((f32[49,4,16,128]{3,2,1,0:T(8,128)S(1)}, f32[49,4,16,128]{3,2,1,0:T(8,128)}, u32[]{:S(2)}) %copy-start) | copy-done | bytes 1605656
  113.6 0.5 chip_sums.1
  114.1 1.2 collective-permute-start.7
  115.3 0.5 collective-permute-start.8
  115.8 1.9 %collective-permute-start.9 = (bf16[56,16,128]{2,1,0:T(8,128)(2,1)S(1)}, bf16[56,16,128]{2,1,0:T(8,128)(2,1)S(1)}, u32[]{:S(2)}, u32[]{:S(2)}) collective-permute-start(bf16[56,16,128]{2,1,0:T(8,128)(2,1)S(1)} %get-tuple-element.29), channel_id=1, source_target_pairs={{0,24},{4,28},{8,16},{12,20},{16,8},{20,12},{24,0},{28,4},{1,25},{... | collective-permute-start | bytes 688136 | tf_op jit(solution)/shard_map/ppermute | solution.py:460
  118.3 4.3 %collective-permute-done.7.refs_1_ = bf16[56,16,128]{2,1,0:T(8,128)(2,1)S(1)} collective-permute-done((bf16[56,16,128]{2,1,0:T(8,128)(2,1)S(1)}, bf16[56,16,128]{2,1,0:T(8,128)(2,1)S(1)}, u32[]{:S(2)}, u32[]{:S(2)}) %collective-permute-start.7) | collective-permute-done | bytes 229408 | tf_op jit(solution)/shard_map/ppermute | solution.py:460
  122.6 5.0 %collective-permute-done.8.refs_2_ = bf16[56,16,128]{2,1,0:T(8,128)(2,1)S(1)} collective-permute-done((bf16[56,16,128]{2,1,0:T(8,128)(2,1)S(1)}, bf16[56,16,128]{2,1,0:T(8,128)(2,1)S(1)}, u32[]{:S(2)}, u32[]{:S(2)}) %collective-permute-start.8) | collective-permute-done | bytes 229408 | tf_op jit(solution)/shard_map/ppermute | solution.py:460
  127.6 5.4 %scores.1 = bf16[48,16,128]{2,1,0:T(8,128)(2,1)} custom-call(s32[2,48]{1,0:T(2,128)S(1)} %bitcast.4, s32[1]{0:T(128)S(6)} %copy.16.live_ref, s32[160]{0:T(256)S(1)} %copy-done.2, f32[52,16,128]{2,1,0:T(8,128)S(1)} %get-tuple-element.26.refs_0_, bf16[56,16,128]{2,1,0:T(8,128)(2,1)S(1)} %collective-permute-done.7.refs_1_, ...), custom_call_target="tpu_custom_call" | custom-call | tf_op jit(solution)/shard_map/scores/pallas_call | solution.py:463
  (34 shorter events, 0.5 us)
Async XLA Ops:
  6.2 15.3 %collective-permute-start = (bf16[2,5120]{1,0:T(2,128)(2,1)S(1)}, bf16[2,5120]{1,0:T(2,128)(2,1)S(1)}, u32[]{:S(2)}, u32[]{:S(2)}) collective-permute-start(bf16[2,5120]{1,0:T(2,128)(2,1)S(1)} %slice.12), channel_id=1, source_target_pairs={{4,0},{8,4},{12,8},{16,12},{20,16},{24,20},{28,24},{5,1},{9,5},{13... | collective-permute-start | bytes 61448 | tf_op jit(solution)/shard_map/ppermute | solution.py:323
  8.4 13.1 %collective-permute-start.1 = (bf16[2,5120]{1,0:T(2,128)(2,1)S(1)}, bf16[2,5120]{1,0:T(2,128)(2,1)S(1)}, u32[]{:S(2)}, u32[]{:S(2)}) collective-permute-start(bf16[2,5120]{1,0:T(2,128)(2,1)S(1)} %slice.13), channel_id=1, source_target_pairs={{0,4},{4,8},{8,12},{12,16},{16,20},{20,24},{24,28},{1,5},{5,9},{9,... | collective-permute-start | bytes 61448 | tf_op jit(solution)/shard_map/ppermute | solution.py:323
  11.4 87.2 %collective-permute-start.2 = (bf16[384,2048]{1,0:T(8,128)(2,1)}, bf16[384,2048]{1,0:T(8,128)(2,1)S(1)}, u32[]{:S(2)}, u32[]{:S(2)}) collective-permute-start(bf16[384,2048]{1,0:T(8,128)(2,1)} %get-tuple-element.19), channel_id=1, source_target_pairs={{0,1},{1,2},{2,3},{4,5},{5,6},{6,7},{8,9},{9,10},{10,11},{12,13},{... | collective-permute-start | bytes 4718600 | tf_op jit(solution)/shard_map/ppermute | solution.py:323
  14.9 83.7 %collective-permute-start.3 = (bf16[384,2048]{1,0:T(8,128)(2,1)}, bf16[384,2048]{1,0:T(8,128)(2,1)S(1)}, u32[]{:S(2)}, u32[]{:S(2)}) collective-permute-start(bf16[384,2048]{1,0:T(8,128)(2,1)} %get-tuple-element.20), channel_id=1, source_target_pairs={{1,0},{2,1},{3,2},{5,4},{6,5},{7,6},{9,8},{10,9},{11,10},{13,12},{... | collective-permute-start | bytes 4718600 | tf_op jit(solution)/shard_map/ppermute | solution.py:323
  18.3 35.4 %collective-permute-start.10 = (bf16[256,128]{1,0:T(8,128)(2,1)S(1)}, bf16[256,128]{1,0:T(8,128)(2,1)S(1)}, u32[]{:S(2)}, u32[]{:S(2)}) collective-permute-start(bf16[256,128]{1,0:T(8,128)(2,1)S(1)} %get-tuple-element.31), channel_id=1, source_target_pairs={{0,1},{1,0},{2,3},{3,2},{4,5},{5,4},{6,7},{7,6},{8,9},{9,8},{10,11... | collective-permute-start | bytes 196616 | tf_op jit(solution)/shard_map/ppermute | solution.py:361
  21.6 42.0 %copy-start.5 = (bf16[8,5120]{1,0:T(8,128)(2,1)}, bf16[8,5120]{1,0:T(8,128)(2,1)S(1)}, u32[]{:S(2)}) copy-start(bf16[8,5120]{1,0:T(8,128)(2,1)S(1)} %pad_maximum_fusion.3.columns_ref) | copy-start | bytes 245764
  53.7 8.4 %collective-permute-start.11 = (bf16[512,128]{1,0:T(8,128)(2,1)S(1)}, bf16[512,128]{1,0:T(8,128)(2,1)S(1)}, u32[]{:S(2)}, u32[]{:S(2)}) collective-permute-start(bf16[512,128]{1,0:T(8,128)(2,1)S(1)} %pad_maximum_fusion.2), channel_id=1, source_target_pairs={{0,2},{1,3},{2,0},{3,1},{4,6},{5,7},{6,4},{7,5},{8,10},{9,11},{10,... | collective-permute-start | bytes 393224 | tf_op jit(solution)/shard_map/ppermute | solution.py:361
  56.2 42.4 %collective-permute-start.4 = (bf16[8,384]{1,0:T(8,128)(2,1)S(1)}, bf16[8,384]{1,0:T(8,128)(2,1)S(1)}, u32[]{:S(2)}, u32[]{:S(2)}) collective-permute-start(bf16[8,384]{1,0:T(8,128)(2,1)S(1)} %get-tuple-element.33), channel_id=1, source_target_pairs={{0,1},{1,2},{2,3},{4,5},{5,6},{6,7},{8,9},{9,10},{10,11},{12,13},{... | collective-permute-start | bytes 18440 | tf_op jit(solution)/shard_map/ppermute | solution.py:323
  59.6 39.1 %collective-permute-start.5 = (bf16[8,384]{1,0:T(8,128)(2,1)S(1)}, bf16[8,384]{1,0:T(8,128)(2,1)S(1)}, u32[]{:S(2)}, u32[]{:S(2)}) collective-permute-start(bf16[8,384]{1,0:T(8,128)(2,1)S(1)} %get-tuple-element.32), channel_id=1, source_target_pairs={{1,0},{2,1},{3,2},{5,4},{6,5},{7,6},{9,8},{10,9},{11,10},{13,12},{... | collective-permute-start | bytes 18440 | tf_op jit(solution)/shard_map/ppermute | solution.py:323
  62.1 35.4 %collective-permute-start.12 = (bf16[1024,128]{1,0:T(8,128)(2,1)S(1)}, bf16[1024,128]{1,0:T(8,128)(2,1)S(1)}, u32[]{:S(2)}, u32[]{:S(2)}) collective-permute-start(bf16[1024,128]{1,0:T(8,128)(2,1)S(1)} %pad_maximum_fusion.1), channel_id=1, source_target_pairs={{0,16},{4,20},{8,24},{12,28},{16,0},{20,4},{24,8},{28,12},{1,17},{... | collective-permute-start | bytes 786440 | tf_op jit(solution)/shard_map/ppermute | solution.py:361
  97.6 12.6 %collective-permute-start.13 = (bf16[2048,128]{1,0:T(8,128)(2,1)S(1)}, bf16[2048,128]{1,0:T(8,128)(2,1)S(1)}, u32[]{:S(2)}, u32[]{:S(2)}) collective-permute-start(bf16[2048,128]{1,0:T(8,128)(2,1)S(1)} %pad_maximum_fusion), channel_id=1, source_target_pairs={{0,8},{4,12},{8,0},{12,4},{16,24},{20,28},{24,16},{28,20},{1,9},{5... | collective-permute-start | bytes 1572872 | tf_op jit(solution)/shard_map/ppermute | solution.py:361
  98.6 0.6 copy-start.6
  98.6 0.6 copy-start.7
  98.7 1.2 copy-start.3
  98.7 1.6 %copy-start.4 = (bf16[384,2048]{1,0:T(8,128)(2,1)}, bf16[384,2048]{1,0:T(8,128)(2,1)S(1)}, u32[]{:S(2)}) copy-start(bf16[384,2048]{1,0:T(8,128)(2,1)S(1)} %collective-permute-done.3.up_ref) | copy-start | bytes 4718596
  109.6 18.0 %copy-start.1 = (s32[48,2]{0,1:T(2,128)S(1)}, s32[48,2]{0,1:T(2,128)}, u32[]{:S(2)}) copy-start(s32[48,2]{0,1:T(2,128)} %param.8) | copy-start | bytes 1156
  109.6 18.0 %copy-start.2 = (s32[160]{0:T(256)S(1)}, s32[160]{0:T(256)}, u32[]{:S(2)}) copy-start(s32[160]{0:T(256)} %rules_ref.1) | copy-start | bytes 1924
  109.6 2.6 %collective-permute-start.6 = (bf16[50,4,16,128]{3,2,1,0:T(8,128)(2,1)}, bf16[50,4,16,128]{3,2,1,0:T(8,128)(2,1)S(1)}, u32[]{:S(2)}, u32[]{:S(2)}) collective-permute-start(bf16[50,4,16,128]{3,2,1,0:T(8,128)(2,1)} %get-tuple-element.25), channel_id=1, source_target_pairs={{0,4},{4,0},{8,12},{12,8},{16,20},{20,16},{24,28},{28,24},{1,5},{5... | collective-permute-start | bytes 2457608 | tf_op jit(solution)/shard_map/ppermute | solution.py:442
  110.2 8.1 %collective-permute-start.14 = (bf16[4096,128]{1,0:T(8,128)(2,1)S(1)}, bf16[4096,128]{1,0:T(8,128)(2,1)S(1)}, u32[]{:S(2)}, u32[]{:S(2)}) collective-permute-start(bf16[4096,128]{1,0:T(8,128)(2,1)S(1)} %constant_dynamic-update-slice_fusion.refs_4_), channel_id=1, source_target_pairs={{0,4},{4,0},{8,12},{12,8},{16,20},{20,16},{24,28},{28,24},{1,5},{5... | collective-permute-start | bytes 3145736 | tf_op jit(solution)/shard_map/ppermute | solution.py:361
  112.2 1.4 %copy-start = (f32[49,4,16,128]{3,2,1,0:T(8,128)S(1)}, f32[49,4,16,128]{3,2,1,0:T(8,128)}, u32[]{:S(2)}) copy-start(f32[49,4,16,128]{3,2,1,0:T(8,128)} %get-tuple-element.24.keep_hbm) | copy-start | bytes 4816900
  114.1 8.5 %collective-permute-start.7 = (bf16[56,16,128]{2,1,0:T(8,128)(2,1)S(1)}, bf16[56,16,128]{2,1,0:T(8,128)(2,1)S(1)}, u32[]{:S(2)}, u32[]{:S(2)}) collective-permute-start(bf16[56,16,128]{2,1,0:T(8,128)(2,1)S(1)} %get-tuple-element.27), channel_id=1, source_target_pairs={{0,8},{4,12},{8,0},{12,4},{16,24},{20,28},{24,16},{28,20},{1,9},{5... | collective-permute-start | bytes 688136 | tf_op jit(solution)/shard_map/ppermute | solution.py:460
  115.3 12.3 %collective-permute-start.8 = (bf16[56,16,128]{2,1,0:T(8,128)(2,1)S(1)}, bf16[56,16,128]{2,1,0:T(8,128)(2,1)S(1)}, u32[]{:S(2)}, u32[]{:S(2)}) collective-permute-start(bf16[56,16,128]{2,1,0:T(8,128)(2,1)S(1)} %get-tuple-element.28), channel_id=1, source_target_pairs={{0,16},{4,20},{8,24},{12,28},{16,0},{20,4},{24,8},{28,12},{1,17},{... | collective-permute-start | bytes 688136 | tf_op jit(solution)/shard_map/ppermute | solution.py:460
  115.8 11.8 %collective-permute-start.9 = (bf16[56,16,128]{2,1,0:T(8,128)(2,1)S(1)}, bf16[56,16,128]{2,1,0:T(8,128)(2,1)S(1)}, u32[]{:S(2)}, u32[]{:S(2)}) collective-permute-start(bf16[56,16,128]{2,1,0:T(8,128)(2,1)S(1)} %get-tuple-element.29), channel_id=1, source_target_pairs={{0,24},{4,28},{8,16},{12,20},{16,8},{20,12},{24,0},{28,4},{1,25},{... | collective-permute-start | bytes 688136 | tf_op jit(solution)/shard_map/ppermute | solution.py:460

commit v4 on v3

v4 whole, which is shorter than its diff:
```python
import functools

import jax
import jax.numpy as jnp
from jax import lax
from jax.experimental import pallas as pl
from jax.experimental.pallas import tpu as pltpu
from jax.sharding import PartitionSpec as P

REACH = 3
TAPS = 5
LANES = 128
HALF = LANES // 2
TILE = 2 * LANES
DEPTH = 6 * LANES
VMEM_BYTES = 58 * 1024 * 1024


def params():
    return pltpu.CompilerParams(vmem_limit_bytes=VMEM_BYTES)


def cost(flops, moved):
    return pl.CostEstimate(flops=flops, bytes_accessed=moved, transcendentals=0)


def whole(shape):
    return pl.BlockSpec(shape, lambda *_: (0,) * len(shape))


def split(values):
    high = values.astype(jnp.bfloat16)
    return high, (values - high.astype(jnp.float32)).astype(jnp.bfloat16)


def smooth_rows(x_ref, halo, w_ref, store):
    rows, width = x_ref.shape
    tiles = width // TILE
    first = lax.broadcasted_iota(jnp.int32, (rows, LANES), 1) < HALF
    for j in range(tiles):
        own = x_ref[:, j * TILE : (j + 1) * TILE]
        before = halo if j == 0 else x_ref[:, j * TILE - LANES : j * TILE]
        after = halo if j == tiles - 1 else x_ref[:, (j + 1) * TILE : (j + 1) * TILE + LANES]
        edge = jnp.where(first, after, before)
        window = jnp.concatenate([own, own, edge, edge], axis=1)
        store(j, jnp.dot(window, w_ref[j], preferred_element_type=jnp.float32))


def lane_pairs(values):
    squares = values * values
    return squares[:, :LANES] + squares[:, LANES:]


def row_sums(part):
    return jnp.sum(part.T, axis=0, keepdims=True)


def gram_of(left, right):
    return lax.dot_general(
        left, right, (((1,), (1,)), ((), ())), preferred_element_type=jnp.float32
    )


def by_core(gram, chips, core):
    parts = gram.reshape(chips, 2, gram.shape[0] // (2 * chips), gram.shape[1])
    return jnp.where(core == 0, parts[:, 0], parts[:, 1]), jnp.where(core == 0, parts[:, 1], parts[:, 0])


def write_weights(stencil_ref, out_ref):
    k = lax.broadcasted_iota(jnp.int32, (TILE, TILE), 0)
    n = lax.broadcasted_iota(jnp.int32, (TILE, TILE), 1)
    inner = k - n + 2
    k, n = k[:LANES], n[:LANES]
    outer = k - n + jnp.where(k < HALF, TILE + 2, 2 - LANES)
    for j in range(out_ref.shape[0]):
        taps = stencil_ref[:, j * TILE : (j + 1) * TILE]
        main = jnp.zeros((TILE, TILE), jnp.float32)
        edge = jnp.zeros((LANES, TILE), jnp.float32)
        for t in range(TAPS):
            main = jnp.where(inner == t, taps[t : t + 1, :], main)
            edge = jnp.where(outer == t, taps[t : t + 1, :], edge)
        out_ref[j, :TILE], out_ref[j, TILE : 2 * TILE] = split(main)
        out_ref[j, 2 * TILE : 2 * TILE + LANES], out_ref[j, 2 * TILE + LANES :] = split(edge)


def cut_kernel(images_ref, stencil_ref, top_ref, bottom_ref, head_ref, tail_ref, w_ref, strips, bands, sems):
    rows, width = images_ref.shape
    edge = top_ref.shape[0]
    reads = [
        pltpu.make_async_copy(images_ref.at[pl.ds(0, edge)], bands.at[0], sems.at[0]),
        pltpu.make_async_copy(images_ref.at[pl.ds(rows - edge, edge)], bands.at[1], sems.at[1]),
        pltpu.make_async_copy(images_ref.at[:, pl.ds(0, LANES)], strips.at[0], sems.at[2]),
        pltpu.make_async_copy(images_ref.at[:, pl.ds(width - LANES, LANES)], strips.at[1], sems.at[3]),
    ]
    writes = [
        pltpu.make_async_copy(bands.at[0], top_ref, sems.at[4]),
        pltpu.make_async_copy(bands.at[1], bottom_ref, sems.at[5]),
    ]
    for copy in reads:
        copy.start()
    write_weights(stencil_ref, w_ref)
    for k in range(2):
        reads[k].wait()
        writes[k].start()
    row = lax.broadcasted_iota(jnp.int32, (8, LANES), 0)
    lane = lax.broadcasted_iota(jnp.int32, (8, LANES), 1)
    for k, (out, shift) in enumerate(((head_ref, 0), (tail_ref, LANES - 2))):
        reads[2 + k].wait()
        pick = (lane == row + shift).astype(jnp.bfloat16)
        out[...] = gram_of(pick, strips[k])[:2].astype(jnp.bfloat16)
    for copy in writes:
        copy.wait()


def halo_tile(columns_ref):
    columns = columns_ref[...].astype(jnp.float32).T.astype(jnp.bfloat16)
    row = lax.broadcasted_iota(jnp.int32, (8, LANES), 0)
    lane = lax.broadcasted_iota(jnp.int32, (8, LANES), 1)
    place = (lane == row + jnp.where(row < 4, 0, LANES - 8)).astype(jnp.bfloat16)
    return jnp.dot(columns, place, preferred_element_type=jnp.float32).astype(jnp.bfloat16)


def main_kernel(steps, group, block, pairs_ref, x_ref, columns_ref, w_ref,
                out_ref, energy_ref, keep_ref, give_ref, held, wide):
    step = pl.program_id(0)
    blocks = steps * group
    slots, chips = wide.shape[:2]

    @pl.when(step < steps)
    def smooth():
        total = [None]

        def store(j, values):
            columns = slice(j * TILE, (j + 1) * TILE)
            rounded = values.astype(jnp.bfloat16)
            out_ref[:, columns] = rounded
            held[pl.ds(step * group, group), :, columns] = rounded.reshape(group, block, TILE)
            squares = lane_pairs(values)
            total[0] = squares if j == 0 else total[0] + squares

        smooth_rows(x_ref, halo_tile(columns_ref), w_ref, store)
        for g in range(group):
            energy_ref[pl.ds(step * group + g, 1), :] = row_sums(total[0][g * block : (g + 1) * block, :])

    @pl.when(step == steps)
    def grams():
        core = lax.axis_index("pix") % 2
        first = lax.axis_index("ion") * blocks

        def one(s, carry):
            a = pairs_ref[0, s] - first
            b = jnp.clip(pairs_ref[1, s] - first, 0, blocks - 1)
            keep_ref[s], wide[s] = by_core(gram_of(held[a], held[b]), chips, core)
            return carry

        lax.fori_loop(0, slots, one, 0, unroll=4)
        give_ref[:slots] = wide[...].astype(jnp.bfloat16)


def fetch(sources, targets, sems):
    copies = [pltpu.make_async_copy(x, y, sems.at[k]) for k, (x, y) in enumerate(zip(sources, targets))]
    for copy in copies:
        copy.start()
    return copies


def cross_kernel(blocks, block, pairs_ref, down_hbm, up_hbm, down_columns_hbm, up_columns_hbm, w_hbm, energy_hbm,
                 smoothed_hbm, keep_hbm, give_hbm, keep_ref, give_ref, x_ref, columns_ref, w_ref, energy_ref, own, near,
                 table, sems):
    core = lax.axis_index("pix") % 2
    first_block = lax.axis_index("ion") * blocks
    slots = pairs_ref.shape[1]
    chips, share = keep_ref.shape[1:3]
    units = keep_ref.shape[0] - slots
    edge = REACH * block
    rows = blocks * block
    low, high = pl.ds(0, edge), pl.ds(edge, edge)
    copies = fetch(
        (down_hbm, up_hbm, down_columns_hbm, up_columns_hbm, w_hbm, energy_hbm, smoothed_hbm.at[low],
         smoothed_hbm.at[pl.ds(rows - edge, edge)], keep_hbm, give_hbm),
        (x_ref.at[low], x_ref.at[high], columns_ref.at[:, low], columns_ref.at[:, high], w_ref, energy_ref, own.at[low],
         own.at[high], keep_ref, give_ref),
        sems,
    )
    for copy in copies[:6]:
        copy.wait()
    table[...] = jnp.zeros_like(table)
    table[REACH : REACH + blocks, :] = energy_ref[...]
    total = [None]

    def store(j, values):
        near[:, j * TILE : (j + 1) * TILE] = values.astype(jnp.bfloat16)
        squares = lane_pairs(values)
        total[0] = squares if j == 0 else total[0] + squares

    smooth_rows(x_ref, halo_tile(columns_ref), w_ref, store)
    for k in range(2 * REACH):
        row = k if k < REACH else k + blocks
        table[row : row + 1, :] = row_sums(total[0][k * block : (k + 1) * block, :])
    for copy in copies[6:]:
        copy.wait()

    upper, lower = split(table[...])
    shape = (units, chips, share, LANES)
    keep_ref[slots:] = table[...].reshape(shape)
    give_ref[slots : slots + units] = upper.reshape(shape)
    give_ref[slots + units :] = lower.reshape(shape)

    def one(s, carry):
        a, b = pairs_ref[0, s] - first_block, pairs_ref[1, s] - first_block

        @pl.when((b < 0) | (b >= blocks))
        def crossing():
            side = (b >= 0).astype(jnp.int32)
            a_row = pl.multiple_of((a - side * (blocks - 2 * REACH)) * block, block)
            b_row = pl.multiple_of((b + REACH - side * blocks) * block, block)
            gram = gram_of(own[pl.ds(a_row, block), :], near[pl.ds(b_row, block), :])
            mine, other = by_core(gram, chips, core)
            keep_ref[s] = mine
            give_ref[s] = other.astype(jnp.bfloat16)

        return carry

    lax.fori_loop(0, slots, one, 0)


def chip_kernel(slots, units, keep_hbm, got_hbm, own_ref, *refs):
    out_refs, (keep_ref, got_ref, sems) = refs[:-3], refs[-3:]
    chip = lax.axis_index("pix") // 2
    chips, share = keep_ref.shape[1:3]
    shape = (units * chips, share, LANES)
    for copy in fetch((keep_hbm, got_hbm), (keep_ref, got_ref), sems):
        copy.wait()
    energies = keep_ref[slots:] + (
        got_ref[slots : slots + units].astype(jnp.float32) + got_ref[slots + units :].astype(jnp.float32)
    )
    high, low = split(energies)
    for d in range(chips):
        total = keep_ref[:slots, chip ^ d] + got_ref[:slots, chip ^ d].astype(jnp.float32)
        if d == 0:
            own_ref[:slots] = total
            own_ref[slots:] = energies.reshape(shape)
        else:
            out = out_refs[d - 1]
            out[:slots] = total.astype(jnp.bfloat16)
            out[slots : slots + units * chips] = high.reshape(shape)
            out[slots + units * chips :] = low.reshape(shape)


def score_kernel(blocks, place_of, pixel_count, pairs_ref, live_ref, rules_ref, *refs):
    chips = (len(refs) - 9) // 2
    sources, out_ref, own_ref = refs[: chips + 2], refs[chips + 2], refs[chips + 3]
    got_refs, (table_ref, inverse, left, right, coloc, place, sems) = refs[chips + 4 : -7], refs[-7:]
    slots, share, block = out_ref.shape
    e_units = inverse.shape[0] // share
    half = table_ref.shape[0] // 2
    targets = (own_ref, *got_refs, table_ref.at[pl.ds(0, half)], table_ref.at[pl.ds(half, half)])
    copies = fetch(sources, targets, sems)
    pix, first = lax.axis_index("pix"), lax.axis_index("ion") * blocks
    pieces = place.shape[0]
    depth = block // pieces

    def find(s, carry):
        for k, at in enumerate(place_of(rules_ref[pairs_ref[1, s]])):
            place[k, s] = at
        return carry

    lax.fori_loop(0, slots, find, 0)
    for copy in copies[:-2]:
        copy.wait()
    gram = own_ref[:slots]
    energies = own_ref[slots:]
    for got in got_refs:
        gram = gram + got[:slots].astype(jnp.float32)
        energies = energies + (
            got[slots : slots + e_units].astype(jnp.float32) + got[slots + e_units :].astype(jnp.float32)
        )
    inverse[...] = (1.0 / jnp.sqrt(energies / pixel_count + 1e-06)).reshape(inverse.shape)

    def pick(s, carry):
        left[pl.ds(s, 1), :] = inverse[pl.ds(pairs_ref[0, s] - first + REACH, 1), :]
        right[pl.ds(s, 1), :] = inverse[pl.ds(pairs_ref[1, s] - first + REACH, 1), :]
        return carry

    lax.fori_loop(0, slots, pick, 0, unroll=8)
    lane = lax.broadcasted_iota(jnp.int32, (1, share, LANES), 2)
    mine = lane == lax.broadcasted_iota(jnp.int32, (1, share, LANES), 1) + pix * share
    inv_a = jnp.sum(jnp.where(mine, left[...][:, None, :], 0.0), axis=2, keepdims=True)
    coloc[...] = (gram * inv_a * right[...][:, None, :] / pixel_count).astype(jnp.bfloat16)
    for copy in copies[-2:]:
        copy.wait()

    def one(s, carry):
        scores = jnp.zeros((share, block), jnp.float32)
        for k in range(pieces):
            matrix = table_ref[pl.ds(pl.multiple_of(place[k, s], depth), depth), :]
            part = coloc[s, :, k * depth : (k + 1) * depth]
            scores = scores + jnp.dot(part, matrix, preferred_element_type=jnp.float32)
        out_ref[s] = jnp.where(s < live_ref[0], scores, 0.0).astype(jnp.bfloat16)
        return carry

    lax.fori_loop(0, slots, one, 0, unroll=16)


def on_device(images, stencil, pairs, live, rule_of_block, adduct):
    rows, width = images.shape
    rules_here, block, _ = adduct.shape
    blocks = rows // block
    slots = pairs.shape[0]
    n_pix, n_ion = lax.axis_size("pix"), lax.axis_size("ion")
    pix, ion = lax.axis_index("pix"), lax.axis_index("ion")
    pixel_count = width * n_pix
    chips, share = n_pix // 2, block // n_pix
    core, chip = pix % 2, pix // 2
    edge = REACH * block

    def shifted(axis, size, up, value):
        steps = [(i, i + 1) if up else (i + 1, i) for i in range(size - 1)]
        return lax.ppermute(value, axis, steps)

    vmem = pl.BlockSpec(memory_space=pltpu.VMEM)
    smem = pl.BlockSpec(memory_space=pltpu.SMEM)
    hbm = pl.BlockSpec(memory_space=pl.ANY)
    fixed = pl.BlockSpec(memory_space=pltpu.HBM)

    part = rules_here * block // n_pix
    mine = lax.dynamic_slice_in_dim(adduct.reshape(rules_here * block, block), pix * part, part, 0)
    turns = [lax.ppermute(mine, "ion", [(i, i ^ d) for i in range(n_ion)]) for d in range(1, n_ion)]

    edge_rows = jax.ShapeDtypeStruct((edge, width), images.dtype)
    edge_columns = jax.ShapeDtypeStruct((2, rows), images.dtype)
    top, bottom, head, tail, weights = pl.pallas_call(
        cut_kernel,
        in_specs=[hbm, vmem],
        out_specs=[hbm, hbm, vmem, vmem, vmem],
        out_shape=[
            edge_rows,
            edge_rows,
            edge_columns,
            edge_columns,
            jax.ShapeDtypeStruct((width // TILE, DEPTH, TILE), jnp.bfloat16),
        ],
        scratch_shapes=[
            pltpu.VMEM((2, rows, LANES), images.dtype),
            pltpu.VMEM((2, edge, width), images.dtype),
            pltpu.SemaphoreType.DMA((6,)),
        ],
        compiler_params=params(),
        cost_estimate=cost(0, 8 * edge * width),
        name="cut_edges",
    )(images, stencil)

    top, bottom, head, tail, *turns = lax.optimization_barrier((top, bottom, head, tail, *turns))
    mine = jnp.concatenate([mine, *turns], axis=0)

    before = shifted("pix", n_pix, True, tail)
    after = shifted("pix", n_pix, False, head)
    down = shifted("ion", n_ion, True, bottom)
    up = shifted("ion", n_ion, False, top)
    columns = jnp.concatenate([after, jnp.zeros((4, rows), images.dtype), before], axis=0)
    down_columns = shifted("ion", n_ion, True, columns[:, rows - edge :])
    up_columns = shifted("ion", n_ion, False, columns[:, :edge])

    distances = [n_pix >> k for k in range(1, n_pix.bit_length())]
    for distance in distances:
        other = lax.ppermute(mine, "pix", [(i, i ^ distance) for i in range(n_pix)])
        if distance > 1:
            mine = jnp.concatenate([mine, other], axis=0)

    def place_of(rule):
        row = rule % rules_here * block
        turn = (rule // rules_here) ^ lax.axis_index("ion")
        pieces = []
        for offset in range(0, block, min(part, block)):
            share_of = ((row + offset) // part) ^ lax.axis_index("pix")
            at = turn * part + (row + offset) % part
            for k, distance in enumerate(distances):
                at = at + (share_of // distance) % 2 * (n_ion * part << k)
            pieces.append(at)
        return pieces

    table_pairs = pairs.T
    group = next(g for g in (8, 5, 4, 2, 1) if blocks % g == 0)
    steps = blocks // group
    units = -(-2 * (blocks + 2 * REACH) // block)
    half = (chips, share, LANES)
    keep_shape = (slots + units, *half)
    give_shape = (slots + 2 * units, *half)

    def rows_at(columns):
        return pl.BlockSpec((group * block, columns), lambda i, *_: (jnp.minimum(i, steps - 1), 0))

    smoothed, energy, keep, give = pl.pallas_call(
        functools.partial(main_kernel, steps, group, block),
        grid_spec=pltpu.PrefetchScalarGridSpec(
            num_scalar_prefetch=1,
            grid=(steps + 1,),
            in_specs=[
                rows_at(width),
                pl.BlockSpec((8, group * block), lambda i, *_: (0, jnp.minimum(i, steps - 1))),
                whole(weights.shape),
            ],
            out_specs=[rows_at(width), whole((blocks, LANES)), whole(keep_shape), whole(give_shape)],
            scratch_shapes=[
                pltpu.VMEM((blocks, block, width), jnp.bfloat16),
                pltpu.VMEM((slots, *half), jnp.float32),
            ],
        ),
        out_shape=[
            jax.ShapeDtypeStruct((rows, width), jnp.bfloat16),
            jax.ShapeDtypeStruct((blocks, LANES), jnp.float32),
            jax.ShapeDtypeStruct(keep_shape, jnp.float32),
            jax.ShapeDtypeStruct(give_shape, jnp.bfloat16),
        ],
        compiler_params=params(),
        cost_estimate=cost(2 * rows * width * DEPTH + 2 * slots * block * block * width, 4 * rows * width),
        name="smooth_and_gram",
    )(table_pairs, images, columns, weights)

    keep, give = pl.pallas_call(
        functools.partial(cross_kernel, blocks, block),
        in_specs=[smem] + [hbm] * 4 + [fixed] * 5,
        out_specs=[vmem, vmem],
        out_shape=[jax.ShapeDtypeStruct(keep_shape, jnp.float32), jax.ShapeDtypeStruct(give_shape, jnp.bfloat16)],
        scratch_shapes=[
            pltpu.VMEM((2 * edge, width), jnp.bfloat16),
            pltpu.VMEM((8, 2 * edge), jnp.bfloat16),
            pltpu.VMEM(weights.shape, jnp.bfloat16),
            pltpu.VMEM((blocks, LANES), jnp.float32),
            pltpu.VMEM((2 * edge, width), jnp.bfloat16),
            pltpu.VMEM((2 * edge, width), jnp.bfloat16),
            pltpu.VMEM((units * block // 2, LANES), jnp.float32),
            pltpu.SemaphoreType.DMA((10,)),
        ],
        compiler_params=params(),
        cost_estimate=cost(4 * edge * width * DEPTH, 8 * edge * width),
        name="cross_grams",
    )(table_pairs, down, up, down_columns, up_columns, weights, energy, smoothed, keep, give)

    got = lax.ppermute(give, "pix", [(i, i ^ 1) for i in range(n_pix)])
    message = jax.ShapeDtypeStruct((slots + 2 * units * chips, share, LANES), jnp.bfloat16)
    own_rows = jax.ShapeDtypeStruct((slots + units * chips, share, LANES), jnp.float32)
    small = pltpu.CompilerParams(vmem_limit_bytes=16 * 1024 * 1024)
    own, *messages = pl.pallas_call(
        functools.partial(chip_kernel, slots, units),
        in_specs=[fixed, hbm],
        out_specs=[vmem] * chips,
        out_shape=[own_rows] + [message] * (chips - 1),
        scratch_shapes=[
            pltpu.VMEM(keep_shape, jnp.float32),
            pltpu.VMEM(give_shape, jnp.bfloat16),
            pltpu.SemaphoreType.DMA((2,)),
        ],
        compiler_params=small,
        name="chip_sums",
    )(keep, got)
    received = [
        lax.ppermute(m, "pix", [(i, i ^ (2 * (d + 1))) for i in range(n_pix)]) for d, m in enumerate(messages)
    ]

    scores = pl.pallas_call(
        functools.partial(score_kernel, blocks, place_of, pixel_count),
        in_specs=[smem] * 3 + [hbm] * (chips + 2),
        out_specs=vmem,
        out_shape=jax.ShapeDtypeStruct((slots, share, block), jnp.bfloat16),
        scratch_shapes=[
            pltpu.VMEM(own_rows.shape, jnp.float32),
            *[pltpu.VMEM(message.shape, jnp.bfloat16)] * (chips - 1),
            pltpu.VMEM((2 * mine.shape[0], block), jnp.bfloat16),
            pltpu.VMEM((units * block // 2, LANES), jnp.float32),
            pltpu.VMEM((slots, LANES), jnp.float32),
            pltpu.VMEM((slots, LANES), jnp.float32),
            pltpu.VMEM((slots, share, LANES), jnp.bfloat16),
            pltpu.SMEM((-(-block // part), slots), jnp.int32),
            pltpu.SemaphoreType.DMA((chips + 2,)),
        ],
        compiler_params=small,
        name="scores",
    )(table_pairs, live, rule_of_block, own, *received, mine, other)
    return (smoothed, scores)


def solution(mesh):
    return jax.shard_map(
        on_device,
        mesh=mesh,
        in_specs=(
            P("ion", "pix"),
            P(None, "pix"),
            P("ion", None),
            P("ion"),
            P(),
            P("ion", None, None),
        ),
        out_specs=(P("ion", "pix"), P("ion", "pix", None)),
        check_vma=False,
    )
```

time: 136 us -> 104 us (0.76)
  waiting for transfers between devices: 43.6 us -> 11.5 us
  starting transfers between devices: 25 us -> 28.2 us
  local copies, waits for them, and re-layouts: 5.98 us -> 4.32 us
    ppermute x5 -> x6, waiting for transfers between devices: 32.5 us -> 0.02 us  [the longest x3 0.01 us: on_device(): other = lax.ppermute(mine, 'pix', [(i, i ^ distance) for i in range(n_pix)])]
    ppermute x5 -> x6, starting transfers between devices: 5.28 us -> 10.2 us  [the longest x3 6.65 us: on_device(): other = lax.ppermute(mine, 'pix', [(i, i ^ distance) for i in range(n_pix)])]
    slice x2 -> x0, local copies, waits for them, and re-layouts: 1.82 us -> none  [the longest x1 0.91 us: on_device(): before = shifted('pix', n_pix, True, tail[6:])]
    ppermute x6, starting transfers between devices: 16.1 us -> 14.4 us  [shifted(): return lax.ppermute(value, axis, steps)]
    pallas_call x3 -> x2, Pallas kernels: 8.23 us -> 6.98 us  [the longest x1 6.5 us: on_device(): pl.pallas_call(cut_kernel, in_specs=[hbm, vmem], out_specs=[hbm, hbm, vme...]
    unnamed x20 -> x21, local copies, waits for them, and re-layouts: 4.01 us -> 4.09 us
  transfers between devices with their start and end apart: 15 -> 16, of which waited for: 5 -> 3; matrix products, arithmetic and copies ran while one was open for 2% -> 0% of each run, Pallas kernels for 35% -> 50%
where the time goes in v4:
time: 104 us; the launch traced here: 102 us
  Pallas kernels  56.5 us (54%)
  starting transfers between devices  28.2 us (27%)
  waiting for transfers between devices  11.5 us (11%)
  local copies, waits for them, and re-layouts  4.32 us (4%)
  between operations  1.58 us (2%)
    pallas_call x1, Pallas kernels, on_device(): pl.pallas_call(functools.partial(main_kernel, steps, group, block), grid_...  33.8 us
    ppermute x6, starting transfers between devices, shifted(): return lax.ppermute(value, axis, steps)  14.4 us
    pallas_call x1, Pallas kernels, on_device(): pl.pallas_call(functools.partial(cross_kernel, blocks, block), in_specs=[...  9.98 us
    ppermute x3, waiting for transfers between devices, on_device(): lax.ppermute(m, 'pix', [(i, i ^ 2 * (d + 1)) for i in range(n_pix)])  9.57 us
    ppermute x3, starting transfers between devices, on_device(): other = lax.ppermute(mine, 'pix', [(i, i ^ distance) for i in range(n_pix)])  6.65 us
    pallas_call x1, Pallas kernels, on_device(): pl.pallas_call(cut_kernel, in_specs=[hbm, vmem], out_specs=[hbm, hbm, vme...  6.5 us
    pallas_call x1, Pallas kernels, on_device(): pl.pallas_call(functools.partial(score_kernel, blocks, place_of, pixel_co...  5.71 us
    unnamed x21, local copies, waits for them, and re-layouts  4.09 us
  transfers between devices with their start and end apart: 16, of which 3 were waited for; matrix products, arithmetic and copies ran while one was open for 0% of the time, Pallas kernels for 50%

profile of v4, /device:TPU:8, one launch (start us, length us, event | category | flops | bytes accessed | tf_op | source)
XLA Modules:
  0.0 102.1 jit_solution(10353910604536890933)
XLA Ops:
  0.6 0.9 constant_dynamic-update-slice_fusion.4
  1.5 0.1 collective-permute-start
  1.6 3.0 %collective-permute-start.1 = (bf16[256,128]{1,0:T(8,128)(2,1)S(1)}, bf16[256,128]{1,0:T(8,128)(2,1)S(1)}, u32[]{:S(2)}, u32[]{:S(2)}) collective-permute-start(bf16[256,128]{1,0:T(8,128)(2,1)S(1)} %get-tuple-element.47), channel_id=1, source_target_pairs={{0,2},{1,3},{2,0},{3,1},{4,6},{5,7},{6,4},{7,5},{8,10},{9,11},{10,... | collective-permute-start | bytes 196616 | tf_op jit(solution)/shard_map/ppermute | solution.py:328
  4.6 0.5 collective-permute-start.2
  5.1 6.5 %cut_edges.1 = (bf16[384,2048]{1,0:T(8,128)(2,1)}, bf16[384,2048]{1,0:T(8,128)(2,1)}, bf16[2,5120]{1,0:T(2,128)(2,1)}, bf16[2,5120]{1,0:T(2,128)(2,1)}, bf16[8,768,256]{2,1,0:T(8,128)(2,1)}) custom-call(bf16[5120,2048]{1,0:T(8,128)(2,1)} %x_ref.1, f32[5,2048]{1,0:T(8,128)} %stencil_ref.1), custom_call_target="tpu_custom_call" | custom-call | bytes 6291456 | tf_op jit(solution)/shard_map/cut_edges/pallas_call | solution.py:332
  11.6 0.1 pad.5.clone
  11.7 1.3 %collective-permute-start.4 = (bf16[2,5120]{1,0:T(2,128)(2,1)}, bf16[2,5120]{1,0:T(2,128)(2,1)S(1)}, u32[]{:S(2)}, u32[]{:S(2)}) collective-permute-start(bf16[2,5120]{1,0:T(2,128)(2,1)} %get-tuple-element.29), channel_id=1, source_target_pairs={{0,4},{4,8},{8,12},{12,16},{16,20},{20,24},{24,28},{1,5},{5,9},{9,... | collective-permute-start | bytes 61448 | tf_op jit(solution)/shard_map/ppermute | solution.py:319
  13.0 1.3 %collective-permute-start.3 = (bf16[2,5120]{1,0:T(2,128)(2,1)}, bf16[2,5120]{1,0:T(2,128)(2,1)S(1)}, u32[]{:S(2)}, u32[]{:S(2)}) collective-permute-start(bf16[2,5120]{1,0:T(2,128)(2,1)} %get-tuple-element.28), channel_id=1, source_target_pairs={{4,0},{8,4},{12,8},{16,12},{20,16},{24,20},{28,24},{5,1},{9,5},{13... | collective-permute-start | bytes 61448 | tf_op jit(solution)/shard_map/ppermute | solution.py:319
  14.3 3.5 %collective-permute-start.5 = (bf16[384,2048]{1,0:T(8,128)(2,1)}, bf16[384,2048]{1,0:T(8,128)(2,1)S(1)}, u32[]{:S(2)}, u32[]{:S(2)}) collective-permute-start(bf16[384,2048]{1,0:T(8,128)(2,1)} %get-tuple-element.32), channel_id=1, source_target_pairs={{0,1},{1,2},{2,3},{4,5},{5,6},{6,7},{8,9},{9,10},{10,11},{12,13},{... | collective-permute-start | bytes 4718600 | tf_op jit(solution)/shard_map/ppermute | solution.py:319
  17.8 2.5 %collective-permute-start.6 = (bf16[384,2048]{1,0:T(8,128)(2,1)}, bf16[384,2048]{1,0:T(8,128)(2,1)S(1)}, u32[]{:S(2)}, u32[]{:S(2)}) collective-permute-start(bf16[384,2048]{1,0:T(8,128)(2,1)} %get-tuple-element.33), channel_id=1, source_target_pairs={{1,0},{2,1},{3,2},{5,4},{6,5},{7,6},{9,8},{10,9},{11,10},{13,12},{... | collective-permute-start | bytes 4718600 | tf_op jit(solution)/shard_map/ppermute | solution.py:319
  20.3 5.5 %collective-permute-start.13 = (bf16[1024,128]{1,0:T(8,128)(2,1)S(1)}, bf16[1024,128]{1,0:T(8,128)(2,1)S(1)}, u32[]{:S(2)}, u32[]{:S(2)}) collective-permute-start(bf16[1024,128]{1,0:T(8,128)(2,1)S(1)} %pad_maximum_fusion), channel_id=1, source_target_pairs={{0,16},{4,20},{8,24},{12,28},{16,0},{20,4},{24,8},{28,12},{1,17},{... | collective-permute-start | bytes 786440 | tf_op jit(solution)/shard_map/ppermute | solution.py:366
  25.8 0.1 pad_maximum_fusion.1.columns_ref
  25.9 3.9 %collective-permute-start.7 = (bf16[8,384]{1,0:T(8,128)(2,1)S(1)}, bf16[8,384]{1,0:T(8,128)(2,1)S(1)}, u32[]{:S(2)}, u32[]{:S(2)}) collective-permute-start(bf16[8,384]{1,0:T(8,128)(2,1)S(1)} %get-tuple-element.51), channel_id=1, source_target_pairs={{0,1},{1,2},{2,3},{4,5},{5,6},{6,7},{8,9},{9,10},{10,11},{12,13},{... | collective-permute-start | bytes 18440 | tf_op jit(solution)/shard_map/ppermute | solution.py:319
  29.8 2.0 %collective-permute-start.8 = (bf16[8,384]{1,0:T(8,128)(2,1)S(1)}, bf16[8,384]{1,0:T(8,128)(2,1)S(1)}, u32[]{:S(2)}, u32[]{:S(2)}) collective-permute-start(bf16[8,384]{1,0:T(8,128)(2,1)S(1)} %get-tuple-element.50), channel_id=1, source_target_pairs={{1,0},{2,1},{3,2},{5,4},{6,5},{7,6},{9,8},{10,9},{11,10},{13,12},{... | collective-permute-start | bytes 18440 | tf_op jit(solution)/shard_map/ppermute | solution.py:319
  31.8 0.1 constant_dynamic-update-slice_fusion
  31.9 0.7 collective-permute-start.14
  32.5 33.8 %smooth_and_gram.1 = (bf16[5120,2048]{1,0:T(8,128)(2,1)}, f32[40,128]{1,0:T(8,128)}, f32[49,4,16,128]{3,2,1,0:T(8,128)}, bf16[50,4,16,128]{3,2,1,0:T(8,128)(2,1)}) custom-call(s32[2,48]{1,0:T(2,128)} %bitcast.2, bf16[5120,2048]{1,0:T(8,128)(2,1)} %x_ref.1, bf16[8,5120]{1,0:T(8,128)(2,1)} %copy-done.5, bf16[8,768,256]{2,1,0:T(8,128)(2,1)} %get-tuple-element.30.w_ref.w_hbm), custom_call_target="tpu_custom_call" | custom-call | flops 19327352832 | bytes 41943040 | tf_op jit(solution)/shard_map/smooth_and_gram/pallas_call | solution.py:393
  66.4 0.5 copy-done.6
  67.0 0.6 copy-done.3
  67.6 0.6 copy-done.4
  68.1 10.0 %cross_grams.1 = (f32[49,4,16,128]{3,2,1,0:T(8,128)}, bf16[50,4,16,128]{3,2,1,0:T(8,128)(2,1)}) custom-call(s32[2,48]{1,0:T(2,128)} %bitcast.3, bf16[384,2048]{1,0:T(8,128)(2,1)} %copy-done.3, bf16[384,2048]{1,0:T(8,128)(2,1)} %copy-done.4, bf16[8,384]{1,0:T(8,128)(2,1)} %copy-done.6, bf16[8,384]{1,0:T(8,128)(2,1)} %copy-done.7, ...), custom_call_target="tpu_custom_call" | custom-call | flops 2415919104 | bytes 6291456 | tf_op jit(solution)/shard_map/cross_grams/pallas_call | solution.py:420
  78.1 0.1 collective-permute-start.9
  78.3 0.5 collective-permute-start.15
  78.8 1.9 %collective-permute-done.9.got_hbm = bf16[50,4,16,128]{3,2,1,0:T(8,128)(2,1)S(1)} collective-permute-done((bf16[50,4,16,128]{3,2,1,0:T(8,128)(2,1)}, bf16[50,4,16,128]{3,2,1,0:T(8,128)(2,1)S(1)}, u32[]{:S(2)}, u32[]{:S(2)}) %collective-permute-start.9) | collective-permute-done | bytes 819232 | tf_op jit(solution)/shard_map/ppermute | solution.py:440
  80.7 1.4 %copy-done = f32[49,4,16,128]{3,2,1,0:T(8,128)S(1)} copy-done((f32[49,4,16,128]{3,2,1,0:T(8,128)S(1)}, f32[49,4,16,128]{3,2,1,0:T(8,128)}, u32[]{:S(2)}) %copy-start) | copy-done | bytes 1605656
  82.1 0.5 chip_sums.1
  82.6 1.5 %collective-permute-start.10 = (bf16[56,16,128]{2,1,0:T(8,128)(2,1)S(1)}, bf16[56,16,128]{2,1,0:T(8,128)(2,1)S(1)}, u32[]{:S(2)}, u32[]{:S(2)}) collective-permute-start(bf16[56,16,128]{2,1,0:T(8,128)(2,1)S(1)} %get-tuple-element.40), channel_id=1, source_target_pairs={{0,8},{4,12},{8,0},{12,4},{16,24},{20,28},{24,16},{28,20},{1,9},{5... | collective-permute-start | bytes 688136 | tf_op jit(solution)/shard_map/ppermute | solution.py:458
  84.1 0.5 collective-permute-start.11
  84.7 1.5 %collective-permute-start.12 = (bf16[56,16,128]{2,1,0:T(8,128)(2,1)S(1)}, bf16[56,16,128]{2,1,0:T(8,128)(2,1)S(1)}, u32[]{:S(2)}, u32[]{:S(2)}) collective-permute-start(bf16[56,16,128]{2,1,0:T(8,128)(2,1)S(1)} %get-tuple-element.42), channel_id=1, source_target_pairs={{0,24},{4,28},{8,16},{12,20},{16,8},{20,12},{24,0},{28,4},{1,25},{... | collective-permute-start | bytes 688136 | tf_op jit(solution)/shard_map/ppermute | solution.py:458
  86.8 4.3 %collective-permute-done.10.refs_1_ = bf16[56,16,128]{2,1,0:T(8,128)(2,1)S(1)} collective-permute-done((bf16[56,16,128]{2,1,0:T(8,128)(2,1)S(1)}, bf16[56,16,128]{2,1,0:T(8,128)(2,1)S(1)}, u32[]{:S(2)}, u32[]{:S(2)}) %collective-permute-start.10) | collective-permute-done | bytes 229408 | tf_op jit(solution)/shard_map/ppermute | solution.py:458
  91.1 5.3 %collective-permute-done.11.refs_2_ = bf16[56,16,128]{2,1,0:T(8,128)(2,1)S(1)} collective-permute-done((bf16[56,16,128]{2,1,0:T(8,128)(2,1)S(1)}, bf16[56,16,128]{2,1,0:T(8,128)(2,1)S(1)}, u32[]{:S(2)}, u32[]{:S(2)}) %collective-permute-start.11) | collective-permute-done | bytes 229408 | tf_op jit(solution)/shard_map/ppermute | solution.py:458
  96.4 5.7 %scores.1 = bf16[48,16,128]{2,1,0:T(8,128)(2,1)} custom-call(s32[2,48]{1,0:T(2,128)S(1)} %bitcast.4, s32[1]{0:T(128)S(6)} %copy.17.live_ref, s32[160]{0:T(256)S(1)} %copy-done.2, f32[52,16,128]{2,1,0:T(8,128)S(1)} %get-tuple-element.39.refs_0_, bf16[56,16,128]{2,1,0:T(8,128)(2,1)S(1)} %collective-permute-done.10.refs_1_, ...), custom_call_target="tpu_custom_call" | custom-call | tf_op jit(solution)/shard_map/scores/pallas_call | solution.py:461
  (33 shorter events, 0.3 us)
Async XLA Ops:
  1.5 10.2 %collective-permute-start = (bf16[256,128]{1,0:T(8,128)(2,1)S(1)}, bf16[256,128]{1,0:T(8,128)(2,1)S(1)}, u32[]{:S(2)}, u32[]{:S(2)}) collective-permute-start(bf16[256,128]{1,0:T(8,128)(2,1)S(1)} %get-tuple-element.47), channel_id=1, source_target_pairs={{0,1},{1,0},{2,3},{3,2},{4,5},{5,4},{6,7},{7,6},{8,9},{9,8},{10,11... | collective-permute-start | bytes 196616 | tf_op jit(solution)/shard_map/ppermute | solution.py:328
  1.6 10.1 %collective-permute-start.1 = (bf16[256,128]{1,0:T(8,128)(2,1)S(1)}, bf16[256,128]{1,0:T(8,128)(2,1)S(1)}, u32[]{:S(2)}, u32[]{:S(2)}) collective-permute-start(bf16[256,128]{1,0:T(8,128)(2,1)S(1)} %get-tuple-element.47), channel_id=1, source_target_pairs={{0,2},{1,3},{2,0},{3,1},{4,6},{5,7},{6,4},{7,5},{8,10},{9,11},{10,... | collective-permute-start | bytes 196616 | tf_op jit(solution)/shard_map/ppermute | solution.py:328
  4.6 7.1 %collective-permute-start.2 = (bf16[256,128]{1,0:T(8,128)(2,1)S(1)}, bf16[256,128]{1,0:T(8,128)(2,1)S(1)}, u32[]{:S(2)}, u32[]{:S(2)}) collective-permute-start(bf16[256,128]{1,0:T(8,128)(2,1)S(1)} %get-tuple-element.47), channel_id=1, source_target_pairs={{0,3},{1,2},{2,1},{3,0},{4,7},{5,6},{6,5},{7,4},{8,11},{9,10},{10,... | collective-permute-start | bytes 196616 | tf_op jit(solution)/shard_map/ppermute | solution.py:328
  11.7 14.1 %collective-permute-start.4 = (bf16[2,5120]{1,0:T(2,128)(2,1)}, bf16[2,5120]{1,0:T(2,128)(2,1)S(1)}, u32[]{:S(2)}, u32[]{:S(2)}) collective-permute-start(bf16[2,5120]{1,0:T(2,128)(2,1)} %get-tuple-element.29), channel_id=1, source_target_pairs={{0,4},{4,8},{8,12},{12,16},{16,20},{20,24},{24,28},{1,5},{5,9},{9,... | collective-permute-start | bytes 61448 | tf_op jit(solution)/shard_map/ppermute | solution.py:319
  13.0 12.8 %collective-permute-start.3 = (bf16[2,5120]{1,0:T(2,128)(2,1)}, bf16[2,5120]{1,0:T(2,128)(2,1)S(1)}, u32[]{:S(2)}, u32[]{:S(2)}) collective-permute-start(bf16[2,5120]{1,0:T(2,128)(2,1)} %get-tuple-element.28), channel_id=1, source_target_pairs={{4,0},{8,4},{12,8},{16,12},{20,16},{24,20},{28,24},{5,1},{9,5},{13... | collective-permute-start | bytes 61448 | tf_op jit(solution)/shard_map/ppermute | solution.py:319
  14.3 52.1 %collective-permute-start.5 = (bf16[384,2048]{1,0:T(8,128)(2,1)}, bf16[384,2048]{1,0:T(8,128)(2,1)S(1)}, u32[]{:S(2)}, u32[]{:S(2)}) collective-permute-start(bf16[384,2048]{1,0:T(8,128)(2,1)} %get-tuple-element.32), channel_id=1, source_target_pairs={{0,1},{1,2},{2,3},{4,5},{5,6},{6,7},{8,9},{9,10},{10,11},{12,13},{... | collective-permute-start | bytes 4718600 | tf_op jit(solution)/shard_map/ppermute | solution.py:319
  17.8 48.6 %collective-permute-start.6 = (bf16[384,2048]{1,0:T(8,128)(2,1)}, bf16[384,2048]{1,0:T(8,128)(2,1)S(1)}, u32[]{:S(2)}, u32[]{:S(2)}) collective-permute-start(bf16[384,2048]{1,0:T(8,128)(2,1)} %get-tuple-element.33), channel_id=1, source_target_pairs={{1,0},{2,1},{3,2},{5,4},{6,5},{7,6},{9,8},{10,9},{11,10},{13,12},{... | collective-permute-start | bytes 4718600 | tf_op jit(solution)/shard_map/ppermute | solution.py:319
  20.3 11.5 %collective-permute-start.13 = (bf16[1024,128]{1,0:T(8,128)(2,1)S(1)}, bf16[1024,128]{1,0:T(8,128)(2,1)S(1)}, u32[]{:S(2)}, u32[]{:S(2)}) collective-permute-start(bf16[1024,128]{1,0:T(8,128)(2,1)S(1)} %pad_maximum_fusion), channel_id=1, source_target_pairs={{0,16},{4,20},{8,24},{12,28},{16,0},{20,4},{24,8},{28,12},{1,17},{... | collective-permute-start | bytes 786440 | tf_op jit(solution)/shard_map/ppermute | solution.py:366
  25.9 6.6 %copy-start.5 = (bf16[8,5120]{1,0:T(8,128)(2,1)}, bf16[8,5120]{1,0:T(8,128)(2,1)S(1)}, u32[]{:S(2)}) copy-start(bf16[8,5120]{1,0:T(8,128)(2,1)S(1)} %pad_maximum_fusion.1.columns_ref) | copy-start | bytes 245764
  25.9 40.4 %collective-permute-start.7 = (bf16[8,384]{1,0:T(8,128)(2,1)S(1)}, bf16[8,384]{1,0:T(8,128)(2,1)S(1)}, u32[]{:S(2)}, u32[]{:S(2)}) collective-permute-start(bf16[8,384]{1,0:T(8,128)(2,1)S(1)} %get-tuple-element.51), channel_id=1, source_target_pairs={{0,1},{1,2},{2,3},{4,5},{5,6},{6,7},{8,9},{9,10},{10,11},{12,13},{... | collective-permute-start | bytes 18440 | tf_op jit(solution)/shard_map/ppermute | solution.py:319
  29.8 36.6 %collective-permute-start.8 = (bf16[8,384]{1,0:T(8,128)(2,1)S(1)}, bf16[8,384]{1,0:T(8,128)(2,1)S(1)}, u32[]{:S(2)}, u32[]{:S(2)}) collective-permute-start(bf16[8,384]{1,0:T(8,128)(2,1)S(1)} %get-tuple-element.50), channel_id=1, source_target_pairs={{1,0},{2,1},{3,2},{5,4},{6,5},{7,6},{9,8},{10,9},{11,10},{13,12},{... | collective-permute-start | bytes 18440 | tf_op jit(solution)/shard_map/ppermute | solution.py:319
  31.9 46.3 %collective-permute-start.14 = (bf16[2048,128]{1,0:T(8,128)(2,1)S(1)}, bf16[2048,128]{1,0:T(8,128)(2,1)S(1)}, u32[]{:S(2)}, u32[]{:S(2)}) collective-permute-start(bf16[2048,128]{1,0:T(8,128)(2,1)S(1)} %get-tuple-element.48), channel_id=1, source_target_pairs={{0,8},{4,12},{8,0},{12,4},{16,24},{20,28},{24,16},{28,20},{1,9},{5... | collective-permute-start | bytes 1572872 | tf_op jit(solution)/shard_map/ppermute | solution.py:366
  66.3 0.6 copy-start.6
  66.4 0.6 copy-start.7
  66.4 1.2 %copy-start.3 = (bf16[384,2048]{1,0:T(8,128)(2,1)}, bf16[384,2048]{1,0:T(8,128)(2,1)S(1)}, u32[]{:S(2)}) copy-start(bf16[384,2048]{1,0:T(8,128)(2,1)S(1)} %collective-permute-done.5.down_hbm) | copy-start | bytes 4718596
  66.4 1.7 %copy-start.4 = (bf16[384,2048]{1,0:T(8,128)(2,1)}, bf16[384,2048]{1,0:T(8,128)(2,1)S(1)}, u32[]{:S(2)}) copy-start(bf16[384,2048]{1,0:T(8,128)(2,1)S(1)} %collective-permute-done.6.up_hbm) | copy-start | bytes 4718596
  78.1 2.6 %collective-permute-start.9 = (bf16[50,4,16,128]{3,2,1,0:T(8,128)(2,1)}, bf16[50,4,16,128]{3,2,1,0:T(8,128)(2,1)S(1)}, u32[]{:S(2)}, u32[]{:S(2)}) collective-permute-start(bf16[50,4,16,128]{3,2,1,0:T(8,128)(2,1)} %get-tuple-element.38), channel_id=1, source_target_pairs={{0,4},{4,0},{8,12},{12,8},{16,20},{20,16},{24,28},{28,24},{1,5},{5... | collective-permute-start | bytes 2457608 | tf_op jit(solution)/shard_map/ppermute | solution.py:440
  78.2 18.2 %copy-start.1 = (s32[48,2]{0,1:T(2,128)S(1)}, s32[48,2]{0,1:T(2,128)}, u32[]{:S(2)}) copy-start(s32[48,2]{0,1:T(2,128)} %param.8) | copy-start | bytes 1156
  78.2 18.2 %copy-start.2 = (s32[160]{0:T(256)S(1)}, s32[160]{0:T(256)}, u32[]{:S(2)}) copy-start(s32[160]{0:T(256)} %rules_ref.1) | copy-start | bytes 1924
  78.3 8.5 %collective-permute-start.15 = (bf16[4096,128]{1,0:T(8,128)(2,1)S(1)}, bf16[4096,128]{1,0:T(8,128)(2,1)S(1)}, u32[]{:S(2)}, u32[]{:S(2)}) collective-permute-start(bf16[4096,128]{1,0:T(8,128)(2,1)S(1)} %constant_dynamic-update-slice_fusion.5.refs_4_), channel_id=1, source_target_pairs={{0,4},{4,0},{8,12},{12,8},{16,20},{20,16},{24,28},{28,24},{1,5},{5... | collective-permute-start | bytes 3145736 | tf_op jit(solution)/shard_map/ppermute | solution.py:366
  80.7 1.4 %copy-start = (f32[49,4,16,128]{3,2,1,0:T(8,128)S(1)}, f32[49,4,16,128]{3,2,1,0:T(8,128)}, u32[]{:S(2)}) copy-start(f32[49,4,16,128]{3,2,1,0:T(8,128)} %get-tuple-element.37.keep_hbm) | copy-start | bytes 4816900
  82.6 8.5 %collective-permute-start.10 = (bf16[56,16,128]{2,1,0:T(8,128)(2,1)S(1)}, bf16[56,16,128]{2,1,0:T(8,128)(2,1)S(1)}, u32[]{:S(2)}, u32[]{:S(2)}) collective-permute-start(bf16[56,16,128]{2,1,0:T(8,128)(2,1)S(1)} %get-tuple-element.40), channel_id=1, source_target_pairs={{0,8},{4,12},{8,0},{12,4},{16,24},{20,28},{24,16},{28,20},{1,9},{5... | collective-permute-start | bytes 688136 | tf_op jit(solution)/shard_map/ppermute | solution.py:458
  84.1 12.3 %collective-permute-start.11 = (bf16[56,16,128]{2,1,0:T(8,128)(2,1)S(1)}, bf16[56,16,128]{2,1,0:T(8,128)(2,1)S(1)}, u32[]{:S(2)}, u32[]{:S(2)}) collective-permute-start(bf16[56,16,128]{2,1,0:T(8,128)(2,1)S(1)} %get-tuple-element.41), channel_id=1, source_target_pairs={{0,16},{4,20},{8,24},{12,28},{16,0},{20,4},{24,8},{28,12},{1,17},{... | collective-permute-start | bytes 688136 | tf_op jit(solution)/shard_map/ppermute | solution.py:458
  84.7 11.8 %collective-permute-start.12 = (bf16[56,16,128]{2,1,0:T(8,128)(2,1)S(1)}, bf16[56,16,128]{2,1,0:T(8,128)(2,1)S(1)}, u32[]{:S(2)}, u32[]{:S(2)}) collective-permute-start(bf16[56,16,128]{2,1,0:T(8,128)(2,1)S(1)} %get-tuple-element.42), channel_id=1, source_target_pairs={{0,24},{4,28},{8,16},{12,20},{16,8},{20,12},{24,0},{28,4},{1,25},{... | collective-permute-start | bytes 688136 | tf_op jit(solution)/shard_map/ppermute | solution.py:458

commit v5 on v4

--- a/solution.py
+++ b/solution.py
@@ -12,7 +12,7 @@
 LANES = 128
 HALF = LANES // 2
 TILE = 2 * LANES
-DEPTH = 6 * LANES
+DEPTH = 3 * LANES
 VMEM_BYTES = 58 * 1024 * 1024
 
 
@@ -42,7 +42,7 @@
         before = halo if j == 0 else x_ref[:, j * TILE - LANES : j * TILE]
         after = halo if j == tiles - 1 else x_ref[:, (j + 1) * TILE : (j + 1) * TILE + LANES]
         edge = jnp.where(first, after, before)
-        window = jnp.concatenate([own, own, edge, edge], axis=1)
+        window = jnp.concatenate([own, edge], axis=1)
         store(j, jnp.dot(window, w_ref[j], preferred_element_type=jnp.float32))
 
 
@@ -63,24 +63,25 @@
 
 def by_core(gram, chips, core):
     parts = gram.reshape(chips, 2, gram.shape[0] // (2 * chips), gram.shape[1])
-    return jnp.where(core == 0, parts[:, 0], parts[:, 1]), jnp.where(core == 0, parts[:, 1], parts[:, 0])
+    even, odd = parts[:, 0].astype(jnp.bfloat16), parts[:, 1].astype(jnp.bfloat16)
+    return jnp.where(core == 0, even, odd), jnp.where(core == 0, odd, even)
 
 
 def write_weights(stencil_ref, out_ref):
-    k = lax.broadcasted_iota(jnp.int32, (TILE, TILE), 0)
-    n = lax.broadcasted_iota(jnp.int32, (TILE, TILE), 1)
-    inner = k - n + 2
-    k, n = k[:LANES], n[:LANES]
-    outer = k - n + jnp.where(k < HALF, TILE + 2, 2 - LANES)
-    for j in range(out_ref.shape[0]):
-        taps = stencil_ref[:, j * TILE : (j + 1) * TILE]
-        main = jnp.zeros((TILE, TILE), jnp.float32)
-        edge = jnp.zeros((LANES, TILE), jnp.float32)
-        for t in range(TAPS):
-            main = jnp.where(inner == t, taps[t : t + 1, :], main)
-            edge = jnp.where(outer == t, taps[t : t + 1, :], edge)
-        out_ref[j, :TILE], out_ref[j, TILE : 2 * TILE] = split(main)
-        out_ref[j, 2 * TILE : 2 * TILE + LANES], out_ref[j, 2 * TILE + LANES :] = split(edge)
+    out_ref[...] = jnp.zeros_like(out_ref)
+    strip = 16
+    places = [(0, LANES, 0, 2), (LANES, LANES, LANES, 2)]
+    places += [(LANES - strip, strip, LANES, 2), (LANES, strip, 0, 2)]
+    places += [(TILE + LANES - strip, strip, 0, 2 - LANES - TILE), (TILE, strip, LANES, 2)]
+    for k0, rows, n0, shift in places:
+        k = lax.broadcasted_iota(jnp.int32, (rows, LANES), 0) + k0
+        tap = k - lax.broadcasted_iota(jnp.int32, (rows, LANES), 1) - n0 + shift
+        for j in range(out_ref.shape[0]):
+            taps = stencil_ref[:, j * TILE + n0 : j * TILE + n0 + LANES]
+            w = jnp.zeros((rows, LANES), jnp.float32)
+            for t in range(TAPS):
+                w = jnp.where(tap == t, taps[t : t + 1, :], w)
+            out_ref[j, k0 : k0 + rows, n0 : n0 + LANES] = w.astype(jnp.bfloat16)
 
 
 def cut_kernel(images_ref, stencil_ref, top_ref, bottom_ref, head_ref, tail_ref, w_ref, strips, bands, sems):
@@ -121,10 +122,11 @@
 
 
 def main_kernel(steps, group, block, pairs_ref, x_ref, columns_ref, w_ref,
-                out_ref, energy_ref, keep_ref, give_ref, held, wide):
+                out_ref, energy_ref, keep_ref, give_ref, held):
     step = pl.program_id(0)
     blocks = steps * group
-    slots, chips = wide.shape[:2]
+    chips = keep_ref.shape[1]
+    slots = pairs_ref.shape[1]
 
     @pl.when(step < steps)
     def smooth():
@@ -150,11 +152,10 @@
         def one(s, carry):
             a = pairs_ref[0, s] - first
             b = jnp.clip(pairs_ref[1, s] - first, 0, blocks - 1)
-            keep_ref[s], wide[s] = by_core(gram_of(held[a], held[b]), chips, core)
+            keep_ref[s], give_ref[s] = by_core(gram_of(held[a], held[b]), chips, core)
             return carry
 
         lax.fori_loop(0, slots, one, 0, unroll=4)
-        give_ref[:slots] = wide[...].astype(jnp.bfloat16)
 
 
 def fetch(sources, targets, sems):
@@ -171,7 +172,7 @@
     first_block = lax.axis_index("ion") * blocks
     slots = pairs_ref.shape[1]
     chips, share = keep_ref.shape[1:3]
-    units = keep_ref.shape[0] - slots
+    units = (keep_ref.shape[0] - slots) // 2
     edge = REACH * block
     rows = blocks * block
     low, high = pl.ds(0, edge), pl.ds(edge, edge)
@@ -200,11 +201,11 @@
     for copy in copies[6:]:
         copy.wait()
 
-    upper, lower = split(table[...])
     shape = (units, chips, share, LANES)
-    keep_ref[slots:] = table[...].reshape(shape)
-    give_ref[slots : slots + units] = upper.reshape(shape)
-    give_ref[slots + units :] = lower.reshape(shape)
+    upper, lower = split(table[...].reshape(shape))
+    for ref in (keep_ref, give_ref):
+        ref[slots : slots + units] = upper
+        ref[slots + units :] = lower
 
     def one(s, carry):
         a, b = pairs_ref[0, s] - first_block, pairs_ref[1, s] - first_block
@@ -215,9 +216,7 @@
             a_row = pl.multiple_of((a - side * (blocks - 2 * REACH)) * block, block)
             b_row = pl.multiple_of((b + REACH - side * blocks) * block, block)
             gram = gram_of(own[pl.ds(a_row, block), :], near[pl.ds(b_row, block), :])
-            mine, other = by_core(gram, chips, core)
-            keep_ref[s] = mine
-            give_ref[s] = other.astype(jnp.bfloat16)
+            keep_ref[s], give_ref[s] = by_core(gram, chips, core)
 
         return carry
 
@@ -231,12 +230,14 @@
     shape = (units * chips, share, LANES)
     for copy in fetch((keep_hbm, got_hbm), (keep_ref, got_ref), sems):
         copy.wait()
-    energies = keep_ref[slots:] + (
-        got_ref[slots : slots + units].astype(jnp.float32) + got_ref[slots + units :].astype(jnp.float32)
-    )
+    energies = 0.0
+    for ref in (keep_ref, got_ref):
+        energies = energies + (
+            ref[slots : slots + units].astype(jnp.float32) + ref[slots + units :].astype(jnp.float32)
+        )
     high, low = split(energies)
     for d in range(chips):
-        total = keep_ref[:slots, chip ^ d] + got_ref[:slots, chip ^ d].astype(jnp.float32)
+        total = keep_ref[:slots, chip ^ d].astype(jnp.float32) + got_ref[:slots, chip ^ d].astype(jnp.float32)
         if d == 0:
             own_ref[:slots] = total
             own_ref[slots:] = energies.reshape(shape)
@@ -353,10 +354,10 @@
     top, bottom, head, tail, *turns = lax.optimization_barrier((top, bottom, head, tail, *turns))
     mine = jnp.concatenate([mine, *turns], axis=0)
 
+    down = shifted("ion", n_ion, True, bottom)
+    up = shifted("ion", n_ion, False, top)
     before = shifted("pix", n_pix, True, tail)
     after = shifted("pix", n_pix, False, head)
-    down = shifted("ion", n_ion, True, bottom)
-    up = shifted("ion", n_ion, False, top)
     columns = jnp.concatenate([after, jnp.zeros((4, rows), images.dtype), before], axis=0)
     down_columns = shifted("ion", n_ion, True, columns[:, rows - edge :])
     up_columns = shifted("ion", n_ion, False, columns[:, :edge])
@@ -368,14 +369,14 @@
             mine = jnp.concatenate([mine, other], axis=0)
 
     def place_of(rule):
-        row = rule % rules_here * block
-        turn = (rule // rules_here) ^ lax.axis_index("ion")
+        row = (rule & (rules_here - 1)) * block
+        turn = (rule >> (rules_here.bit_length() - 1)) ^ lax.axis_index("ion")
         pieces = []
         for offset in range(0, block, min(part, block)):
-            share_of = ((row + offset) // part) ^ lax.axis_index("pix")
-            at = turn * part + (row + offset) % part
+            share_of = ((row + offset) >> (part.bit_length() - 1)) ^ lax.axis_index("pix")
+            at = turn * part + ((row + offset) & (part - 1))
             for k, distance in enumerate(distances):
-                at = at + (share_of // distance) % 2 * (n_ion * part << k)
+                at = at + jnp.where((share_of & distance) != 0, n_ion * part << k, 0)
             pieces.append(at)
         return pieces
 
@@ -384,8 +385,8 @@
     steps = blocks // group
     units = -(-2 * (blocks + 2 * REACH) // block)
     half = (chips, share, LANES)
-    keep_shape = (slots + units, *half)
-    give_shape = (slots + 2 * units, *half)
+    half_shape = (slots + 2 * units, *half)
+    both_halves = [jax.ShapeDtypeStruct(half_shape, jnp.bfloat16)] * 2
 
     def rows_at(columns):
         return pl.BlockSpec((group * block, columns), lambda i, *_: (jnp.minimum(i, steps - 1), 0))
@@ -400,17 +401,13 @@
                 pl.BlockSpec((8, group * block), lambda i, *_: (0, jnp.minimum(i, steps - 1))),
                 whole(weights.shape),
             ],
-            out_specs=[rows_at(width), whole((blocks, LANES)), whole(keep_shape), whole(give_shape)],
-            scratch_shapes=[
-                pltpu.VMEM((blocks, block, width), jnp.bfloat16),
-                pltpu.VMEM((slots, *half), jnp.float32),
-            ],
+            out_specs=[rows_at(width), whole((blocks, LANES)), whole(half_shape), whole(half_shape)],
+            scratch_shapes=[pltpu.VMEM((blocks, block, width), jnp.bfloat16)],
         ),
         out_shape=[
             jax.ShapeDtypeStruct((rows, width), jnp.bfloat16),
             jax.ShapeDtypeStruct((blocks, LANES), jnp.float32),
-            jax.ShapeDtypeStruct(keep_shape, jnp.float32),
-            jax.ShapeDtypeStruct(give_shape, jnp.bfloat16),
+            *both_halves,
         ],
         compiler_params=params(),
         cost_estimate=cost(2 * rows * width * DEPTH + 2 * slots * block * block * width, 4 * rows * width),
@@ -421,7 +418,7 @@
         functools.partial(cross_kernel, blocks, block),
         in_specs=[smem] + [hbm] * 4 + [fixed] * 5,
         out_specs=[vmem, vmem],
-        out_shape=[jax.ShapeDtypeStruct(keep_shape, jnp.float32), jax.ShapeDtypeStruct(give_shape, jnp.bfloat16)],
+        out_shape=both_halves,
         scratch_shapes=[
             pltpu.VMEM((2 * edge, width), jnp.bfloat16),
             pltpu.VMEM((8, 2 * edge), jnp.bfloat16),
@@ -447,8 +444,8 @@
         out_specs=[vmem] * chips,
         out_shape=[own_rows] + [message] * (chips - 1),
         scratch_shapes=[
-            pltpu.VMEM(keep_shape, jnp.float32),
-            pltpu.VMEM(give_shape, jnp.bfloat16),
+            pltpu.VMEM(half_shape, jnp.bfloat16),
+            pltpu.VMEM(half_shape, jnp.bfloat16),
             pltpu.SemaphoreType.DMA((2,)),
         ],
         compiler_params=small,

time: 104 us -> 95.4 us (0.917)
  Pallas kernels: 56.5 us -> 50.2 us
  local copies, waits for them, and re-layouts: 4.32 us -> 2.85 us
    pallas_call x1, Pallas kernels: 33.8 us -> 30.7 us  [on_device(): pl.pallas_call(functools.partial(main_kernel, steps, group, block), grid_...]
    pallas_call x1, Pallas kernels: 9.98 us -> 8.41 us  [on_device(): pl.pallas_call(functools.partial(cross_kernel, blocks, block), in_specs=[...]
    unnamed x21, local copies, waits for them, and re-layouts: 4.09 us -> 2.62 us
  transfers between devices with their start and end apart: 16 -> 16, of which waited for: 3 -> 3; matrix products, arithmetic and copies ran while one was open for 0% -> 0% of each run, Pallas kernels for 50% -> 48%
where the time goes in v5:
time: 95.4 us; the launch traced here: 94.5 us
  Pallas kernels  50.2 us (53%)
  starting transfers between devices  28.2 us (30%)
  waiting for transfers between devices  11.5 us (12%)
  local copies, waits for them, and re-layouts  2.85 us (3%)
  between operations  1.58 us (2%)
    pallas_call x1, Pallas kernels, on_device(): pl.pallas_call(functools.partial(main_kernel, steps, group, block), grid_...  30.7 us
    ppermute x6, starting transfers between devices, shifted(): return lax.ppermute(value, axis, steps)  14.4 us
    ppermute x3, waiting for transfers between devices, on_device(): lax.ppermute(m, 'pix', [(i, i ^ 2 * (d + 1)) for i in range(n_pix)])  9.57 us
    pallas_call x1, Pallas kernels, on_device(): pl.pallas_call(functools.partial(cross_kernel, blocks, block), in_specs=[...  8.41 us
    ppermute x3, starting transfers between devices, on_device(): other = lax.ppermute(mine, 'pix', [(i, i ^ distance) for i in range(n_pix)])  6.67 us
    pallas_call x1, Pallas kernels, on_device(): pl.pallas_call(cut_kernel, in_specs=[hbm, vmem], out_specs=[hbm, hbm, vme...  6.06 us
    pallas_call x1, Pallas kernels, on_device(): pl.pallas_call(functools.partial(score_kernel, blocks, place_of, pixel_co...  4.7 us
    ppermute x3, starting transfers between devices, on_device(): lax.ppermute(m, 'pix', [(i, i ^ 2 * (d + 1)) for i in range(n_pix)])  3.55 us
  transfers between devices with their start and end apart: 16, of which 3 were waited for; matrix products, arithmetic and copies ran while one was open for 0% of the time, Pallas kernels for 48%

profile of v5, /device:TPU:8, one launch (start us, length us, event | category | flops | bytes accessed | tf_op | source)
XLA Modules:
  0.0 94.5 jit_solution(4876088490009744097)
XLA Ops:
  0.6 0.9 constant_dynamic-update-slice_fusion.4
  1.5 0.1 collective-permute-start
  1.6 3.0 %collective-permute-start.1 = (bf16[256,128]{1,0:T(8,128)(2,1)S(1)}, bf16[256,128]{1,0:T(8,128)(2,1)S(1)}, u32[]{:S(2)}, u32[]{:S(2)}) collective-permute-start(bf16[256,128]{1,0:T(8,128)(2,1)S(1)} %get-tuple-element.47), channel_id=1, source_target_pairs={{0,2},{1,3},{2,0},{3,1},{4,6},{5,7},{6,4},{7,5},{8,10},{9,11},{10,... | collective-permute-start | bytes 196616 | tf_op jit(solution)/shard_map/ppermute | solution.py:329
  4.6 0.5 collective-permute-start.2
  5.1 6.1 %cut_edges.1 = (bf16[384,2048]{1,0:T(8,128)(2,1)}, bf16[384,2048]{1,0:T(8,128)(2,1)}, bf16[2,5120]{1,0:T(2,128)(2,1)}, bf16[2,5120]{1,0:T(2,128)(2,1)}, bf16[8,384,256]{2,1,0:T(8,128)(2,1)}) custom-call(bf16[5120,2048]{1,0:T(8,128)(2,1)} %x_ref.1, f32[5,2048]{1,0:T(8,128)} %stencil_ref.1), custom_call_target="tpu_custom_call" | custom-call | bytes 6291456 | tf_op jit(solution)/shard_map/cut_edges/pallas_call | solution.py:333
  11.1 0.1 pad.5.clone
  11.2 1.3 %collective-permute-start.4 = (bf16[2,5120]{1,0:T(2,128)(2,1)}, bf16[2,5120]{1,0:T(2,128)(2,1)S(1)}, u32[]{:S(2)}, u32[]{:S(2)}) collective-permute-start(bf16[2,5120]{1,0:T(2,128)(2,1)} %get-tuple-element.29), channel_id=1, source_target_pairs={{0,4},{4,8},{8,12},{12,16},{16,20},{20,24},{24,28},{1,5},{5,9},{9,... | collective-permute-start | bytes 61448 | tf_op jit(solution)/shard_map/ppermute | solution.py:320
  12.5 1.3 %collective-permute-start.3 = (bf16[2,5120]{1,0:T(2,128)(2,1)}, bf16[2,5120]{1,0:T(2,128)(2,1)S(1)}, u32[]{:S(2)}, u32[]{:S(2)}) collective-permute-start(bf16[2,5120]{1,0:T(2,128)(2,1)} %get-tuple-element.28), channel_id=1, source_target_pairs={{4,0},{8,4},{12,8},{16,12},{20,16},{24,20},{28,24},{5,1},{9,5},{13... | collective-permute-start | bytes 61448 | tf_op jit(solution)/shard_map/ppermute | solution.py:320
  13.8 3.5 %collective-permute-start.5 = (bf16[384,2048]{1,0:T(8,128)(2,1)}, bf16[384,2048]{1,0:T(8,128)(2,1)S(1)}, u32[]{:S(2)}, u32[]{:S(2)}) collective-permute-start(bf16[384,2048]{1,0:T(8,128)(2,1)} %get-tuple-element.32), channel_id=1, source_target_pairs={{0,1},{1,2},{2,3},{4,5},{5,6},{6,7},{8,9},{9,10},{10,11},{12,13},{... | collective-permute-start | bytes 4718600 | tf_op jit(solution)/shard_map/ppermute | solution.py:320
  17.3 2.5 %collective-permute-start.6 = (bf16[384,2048]{1,0:T(8,128)(2,1)}, bf16[384,2048]{1,0:T(8,128)(2,1)S(1)}, u32[]{:S(2)}, u32[]{:S(2)}) collective-permute-start(bf16[384,2048]{1,0:T(8,128)(2,1)} %get-tuple-element.33), channel_id=1, source_target_pairs={{1,0},{2,1},{3,2},{5,4},{6,5},{7,6},{9,8},{10,9},{11,10},{13,12},{... | collective-permute-start | bytes 4718600 | tf_op jit(solution)/shard_map/ppermute | solution.py:320
  19.8 5.5 %collective-permute-start.13 = (bf16[1024,128]{1,0:T(8,128)(2,1)S(1)}, bf16[1024,128]{1,0:T(8,128)(2,1)S(1)}, u32[]{:S(2)}, u32[]{:S(2)}) collective-permute-start(bf16[1024,128]{1,0:T(8,128)(2,1)S(1)} %pad_maximum_fusion), channel_id=1, source_target_pairs={{0,16},{4,20},{8,24},{12,28},{16,0},{20,4},{24,8},{28,12},{1,17},{... | collective-permute-start | bytes 786440 | tf_op jit(solution)/shard_map/ppermute | solution.py:367
  25.4 0.1 pad_maximum_fusion.1.columns_ref
  25.5 3.9 %collective-permute-start.7 = (bf16[8,384]{1,0:T(8,128)(2,1)S(1)}, bf16[8,384]{1,0:T(8,128)(2,1)S(1)}, u32[]{:S(2)}, u32[]{:S(2)}) collective-permute-start(bf16[8,384]{1,0:T(8,128)(2,1)S(1)} %get-tuple-element.51), channel_id=1, source_target_pairs={{0,1},{1,2},{2,3},{4,5},{5,6},{6,7},{8,9},{9,10},{10,11},{12,13},{... | collective-permute-start | bytes 18440 | tf_op jit(solution)/shard_map/ppermute | solution.py:320
  29.4 2.0 %collective-permute-start.8 = (bf16[8,384]{1,0:T(8,128)(2,1)S(1)}, bf16[8,384]{1,0:T(8,128)(2,1)S(1)}, u32[]{:S(2)}, u32[]{:S(2)}) collective-permute-start(bf16[8,384]{1,0:T(8,128)(2,1)S(1)} %get-tuple-element.50), channel_id=1, source_target_pairs={{1,0},{2,1},{3,2},{5,4},{6,5},{7,6},{9,8},{10,9},{11,10},{13,12},{... | collective-permute-start | bytes 18440 | tf_op jit(solution)/shard_map/ppermute | solution.py:320
  31.4 0.1 constant_dynamic-update-slice_fusion
  31.4 0.7 collective-permute-start.14
  32.1 30.7 %smooth_and_gram.1 = (bf16[5120,2048]{1,0:T(8,128)(2,1)}, f32[40,128]{1,0:T(8,128)}, bf16[50,4,16,128]{3,2,1,0:T(8,128)(2,1)}, bf16[50,4,16,128]{3,2,1,0:T(8,128)(2,1)}) custom-call(s32[2,48]{1,0:T(2,128)} %bitcast.2, bf16[5120,2048]{1,0:T(8,128)(2,1)} %x_ref.1, bf16[8,5120]{1,0:T(8,128)(2,1)} %copy-done.5, bf16[8,384,256]{2,1,0:T(8,128)(2,1)} %get-tuple-element.30.w_ref.w_hbm), custom_call_target="tpu_custom_call" | custom-call | flops 11274289152 | bytes 41943040 | tf_op jit(solution)/shard_map/smooth_and_gram/pallas_call | solution.py:394
  62.8 0.5 copy-done.6
  63.4 0.6 copy-done.3
  63.9 0.5 copy-done.4
  64.5 8.4 %cross_grams.1 = (bf16[50,4,16,128]{3,2,1,0:T(8,128)(2,1)}, bf16[50,4,16,128]{3,2,1,0:T(8,128)(2,1)}) custom-call(s32[2,48]{1,0:T(2,128)} %bitcast.3, bf16[384,2048]{1,0:T(8,128)(2,1)} %copy-done.3, bf16[384,2048]{1,0:T(8,128)(2,1)} %copy-done.4, bf16[8,384]{1,0:T(8,128)(2,1)} %copy-done.6, bf16[8,384]{1,0:T(8,128)(2,1)} %copy-done.7, ...), custom_call_target="tpu_custom_call" | custom-call | flops 1207959552 | bytes 6291456 | tf_op jit(solution)/shard_map/cross_grams/pallas_call | solution.py:417
  72.9 0.1 collective-permute-start.9
  73.0 0.1 constant_dynamic-update-slice_fusion.5.refs_4_
  73.1 0.6 collective-permute-start.15
  73.7 1.9 %collective-permute-done.9.got_hbm = bf16[50,4,16,128]{3,2,1,0:T(8,128)(2,1)S(1)} collective-permute-done((bf16[50,4,16,128]{3,2,1,0:T(8,128)(2,1)}, bf16[50,4,16,128]{3,2,1,0:T(8,128)(2,1)S(1)}, u32[]{:S(2)}, u32[]{:S(2)}) %collective-permute-start.9) | collective-permute-done | bytes 819232 | tf_op jit(solution)/shard_map/ppermute | solution.py:437
  75.5 0.4 chip_sums.1
  76.0 1.5 %collective-permute-start.10 = (bf16[56,16,128]{2,1,0:T(8,128)(2,1)S(1)}, bf16[56,16,128]{2,1,0:T(8,128)(2,1)S(1)}, u32[]{:S(2)}, u32[]{:S(2)}) collective-permute-start(bf16[56,16,128]{2,1,0:T(8,128)(2,1)S(1)} %get-tuple-element.40), channel_id=1, source_target_pairs={{0,8},{4,12},{8,0},{12,4},{16,24},{20,28},{24,16},{28,20},{1,9},{5... | collective-permute-start | bytes 688136 | tf_op jit(solution)/shard_map/ppermute | solution.py:455
  77.5 0.5 collective-permute-start.11
  78.0 1.5 %collective-permute-start.12 = (bf16[56,16,128]{2,1,0:T(8,128)(2,1)S(1)}, bf16[56,16,128]{2,1,0:T(8,128)(2,1)S(1)}, u32[]{:S(2)}, u32[]{:S(2)}) collective-permute-start(bf16[56,16,128]{2,1,0:T(8,128)(2,1)S(1)} %get-tuple-element.42), channel_id=1, source_target_pairs={{0,24},{4,28},{8,16},{12,20},{16,8},{20,12},{24,0},{28,4},{1,25},{... | collective-permute-start | bytes 688136 | tf_op jit(solution)/shard_map/ppermute | solution.py:455
  80.2 4.3 %collective-permute-done.10.refs_1_ = bf16[56,16,128]{2,1,0:T(8,128)(2,1)S(1)} collective-permute-done((bf16[56,16,128]{2,1,0:T(8,128)(2,1)S(1)}, bf16[56,16,128]{2,1,0:T(8,128)(2,1)S(1)}, u32[]{:S(2)}, u32[]{:S(2)}) %collective-permute-start.10) | collective-permute-done | bytes 229408 | tf_op jit(solution)/shard_map/ppermute | solution.py:455
  84.5 5.3 %collective-permute-done.11.refs_2_ = bf16[56,16,128]{2,1,0:T(8,128)(2,1)S(1)} collective-permute-done((bf16[56,16,128]{2,1,0:T(8,128)(2,1)S(1)}, bf16[56,16,128]{2,1,0:T(8,128)(2,1)S(1)}, u32[]{:S(2)}, u32[]{:S(2)}) %collective-permute-start.11) | collective-permute-done | bytes 229408 | tf_op jit(solution)/shard_map/ppermute | solution.py:455
  89.8 4.7 %scores.1 = bf16[48,16,128]{2,1,0:T(8,128)(2,1)} custom-call(s32[2,48]{1,0:T(2,128)S(1)} %bitcast.4, s32[1]{0:T(128)S(6)} %copy.17.live_ref, s32[160]{0:T(256)S(1)} %copy-done.2, f32[52,16,128]{2,1,0:T(8,128)S(1)} %get-tuple-element.39.refs_0_, bf16[56,16,128]{2,1,0:T(8,128)(2,1)S(1)} %collective-permute-done.10.refs_1_, ...), custom_call_target="tpu_custom_call" | custom-call | tf_op jit(solution)/shard_map/scores/pallas_call | solution.py:458
  (33 shorter events, 0.2 us)
Async XLA Ops:
  1.5 9.7 %collective-permute-start = (bf16[256,128]{1,0:T(8,128)(2,1)S(1)}, bf16[256,128]{1,0:T(8,128)(2,1)S(1)}, u32[]{:S(2)}, u32[]{:S(2)}) collective-permute-start(bf16[256,128]{1,0:T(8,128)(2,1)S(1)} %get-tuple-element.47), channel_id=1, source_target_pairs={{0,1},{1,0},{2,3},{3,2},{4,5},{5,4},{6,7},{7,6},{8,9},{9,8},{10,11... | collective-permute-start | bytes 196616 | tf_op jit(solution)/shard_map/ppermute | solution.py:329
  1.6 9.6 %collective-permute-start.1 = (bf16[256,128]{1,0:T(8,128)(2,1)S(1)}, bf16[256,128]{1,0:T(8,128)(2,1)S(1)}, u32[]{:S(2)}, u32[]{:S(2)}) collective-permute-start(bf16[256,128]{1,0:T(8,128)(2,1)S(1)} %get-tuple-element.47), channel_id=1, source_target_pairs={{0,2},{1,3},{2,0},{3,1},{4,6},{5,7},{6,4},{7,5},{8,10},{9,11},{10,... | collective-permute-start | bytes 196616 | tf_op jit(solution)/shard_map/ppermute | solution.py:329
  4.6 6.6 %collective-permute-start.2 = (bf16[256,128]{1,0:T(8,128)(2,1)S(1)}, bf16[256,128]{1,0:T(8,128)(2,1)S(1)}, u32[]{:S(2)}, u32[]{:S(2)}) collective-permute-start(bf16[256,128]{1,0:T(8,128)(2,1)S(1)} %get-tuple-element.47), channel_id=1, source_target_pairs={{0,3},{1,2},{2,1},{3,0},{4,7},{5,6},{6,5},{7,4},{8,11},{9,10},{10,... | collective-permute-start | bytes 196616 | tf_op jit(solution)/shard_map/ppermute | solution.py:329
  11.2 14.1 %collective-permute-start.4 = (bf16[2,5120]{1,0:T(2,128)(2,1)}, bf16[2,5120]{1,0:T(2,128)(2,1)S(1)}, u32[]{:S(2)}, u32[]{:S(2)}) collective-permute-start(bf16[2,5120]{1,0:T(2,128)(2,1)} %get-tuple-element.29), channel_id=1, source_target_pairs={{0,4},{4,8},{8,12},{12,16},{16,20},{20,24},{24,28},{1,5},{5,9},{9,... | collective-permute-start | bytes 61448 | tf_op jit(solution)/shard_map/ppermute | solution.py:320
  12.5 12.8 %collective-permute-start.3 = (bf16[2,5120]{1,0:T(2,128)(2,1)}, bf16[2,5120]{1,0:T(2,128)(2,1)S(1)}, u32[]{:S(2)}, u32[]{:S(2)}) collective-permute-start(bf16[2,5120]{1,0:T(2,128)(2,1)} %get-tuple-element.28), channel_id=1, source_target_pairs={{4,0},{8,4},{12,8},{16,12},{20,16},{24,20},{28,24},{5,1},{9,5},{13... | collective-permute-start | bytes 61448 | tf_op jit(solution)/shard_map/ppermute | solution.py:320
  13.8 49.0 %collective-permute-start.5 = (bf16[384,2048]{1,0:T(8,128)(2,1)}, bf16[384,2048]{1,0:T(8,128)(2,1)S(1)}, u32[]{:S(2)}, u32[]{:S(2)}) collective-permute-start(bf16[384,2048]{1,0:T(8,128)(2,1)} %get-tuple-element.32), channel_id=1, source_target_pairs={{0,1},{1,2},{2,3},{4,5},{5,6},{6,7},{8,9},{9,10},{10,11},{12,13},{... | collective-permute-start | bytes 4718600 | tf_op jit(solution)/shard_map/ppermute | solution.py:320
  17.3 45.5 %collective-permute-start.6 = (bf16[384,2048]{1,0:T(8,128)(2,1)}, bf16[384,2048]{1,0:T(8,128)(2,1)S(1)}, u32[]{:S(2)}, u32[]{:S(2)}) collective-permute-start(bf16[384,2048]{1,0:T(8,128)(2,1)} %get-tuple-element.33), channel_id=1, source_target_pairs={{1,0},{2,1},{3,2},{5,4},{6,5},{7,6},{9,8},{10,9},{11,10},{13,12},{... | collective-permute-start | bytes 4718600 | tf_op jit(solution)/shard_map/ppermute | solution.py:320
  19.8 11.5 %collective-permute-start.13 = (bf16[1024,128]{1,0:T(8,128)(2,1)S(1)}, bf16[1024,128]{1,0:T(8,128)(2,1)S(1)}, u32[]{:S(2)}, u32[]{:S(2)}) collective-permute-start(bf16[1024,128]{1,0:T(8,128)(2,1)S(1)} %pad_maximum_fusion), channel_id=1, source_target_pairs={{0,16},{4,20},{8,24},{12,28},{16,0},{20,4},{24,8},{28,12},{1,17},{... | collective-permute-start | bytes 786440 | tf_op jit(solution)/shard_map/ppermute | solution.py:367
  25.5 6.6 %copy-start.5 = (bf16[8,5120]{1,0:T(8,128)(2,1)}, bf16[8,5120]{1,0:T(8,128)(2,1)S(1)}, u32[]{:S(2)}) copy-start(bf16[8,5120]{1,0:T(8,128)(2,1)S(1)} %pad_maximum_fusion.1.columns_ref) | copy-start | bytes 245764
  25.5 37.3 %collective-permute-start.7 = (bf16[8,384]{1,0:T(8,128)(2,1)S(1)}, bf16[8,384]{1,0:T(8,128)(2,1)S(1)}, u32[]{:S(2)}, u32[]{:S(2)}) collective-permute-start(bf16[8,384]{1,0:T(8,128)(2,1)S(1)} %get-tuple-element.51), channel_id=1, source_target_pairs={{0,1},{1,2},{2,3},{4,5},{5,6},{6,7},{8,9},{9,10},{10,11},{12,13},{... | collective-permute-start | bytes 18440 | tf_op jit(solution)/shard_map/ppermute | solution.py:320
  29.4 33.4 %collective-permute-start.8 = (bf16[8,384]{1,0:T(8,128)(2,1)S(1)}, bf16[8,384]{1,0:T(8,128)(2,1)S(1)}, u32[]{:S(2)}, u32[]{:S(2)}) collective-permute-start(bf16[8,384]{1,0:T(8,128)(2,1)S(1)} %get-tuple-element.50), channel_id=1, source_target_pairs={{1,0},{2,1},{3,2},{5,4},{6,5},{7,6},{9,8},{10,9},{11,10},{13,12},{... | collective-permute-start | bytes 18440 | tf_op jit(solution)/shard_map/ppermute | solution.py:320
  31.4 41.6 %collective-permute-start.14 = (bf16[2048,128]{1,0:T(8,128)(2,1)S(1)}, bf16[2048,128]{1,0:T(8,128)(2,1)S(1)}, u32[]{:S(2)}, u32[]{:S(2)}) collective-permute-start(bf16[2048,128]{1,0:T(8,128)(2,1)S(1)} %get-tuple-element.48), channel_id=1, source_target_pairs={{0,8},{4,12},{8,0},{12,4},{16,24},{20,28},{24,16},{28,20},{1,9},{5... | collective-permute-start | bytes 1572872 | tf_op jit(solution)/shard_map/ppermute | solution.py:367
  62.8 0.6 copy-start.6
  62.8 0.6 copy-start.7
  62.8 1.1 %copy-start.3 = (bf16[384,2048]{1,0:T(8,128)(2,1)}, bf16[384,2048]{1,0:T(8,128)(2,1)S(1)}, u32[]{:S(2)}) copy-start(bf16[384,2048]{1,0:T(8,128)(2,1)S(1)} %collective-permute-done.5.down_hbm) | copy-start | bytes 4718596
  62.8 1.7 %copy-start.4 = (bf16[384,2048]{1,0:T(8,128)(2,1)}, bf16[384,2048]{1,0:T(8,128)(2,1)S(1)}, u32[]{:S(2)}) copy-start(bf16[384,2048]{1,0:T(8,128)(2,1)S(1)} %collective-permute-done.6.up_hbm) | copy-start | bytes 4718596
  72.9 2.6 %copy-start = (bf16[50,4,16,128]{3,2,1,0:T(8,128)(2,1)S(1)}, bf16[50,4,16,128]{3,2,1,0:T(8,128)(2,1)}, u32[]{:S(2)}) copy-start(bf16[50,4,16,128]{3,2,1,0:T(8,128)(2,1)} %get-tuple-element.37.keep_hbm) | copy-start | bytes 2457604
  72.9 16.9 %copy-start.1 = (s32[48,2]{0,1:T(2,128)S(1)}, s32[48,2]{0,1:T(2,128)}, u32[]{:S(2)}) copy-start(s32[48,2]{0,1:T(2,128)} %param.8) | copy-start | bytes 1156
  72.9 16.8 %copy-start.2 = (s32[160]{0:T(256)S(1)}, s32[160]{0:T(256)}, u32[]{:S(2)}) copy-start(s32[160]{0:T(256)} %rules_ref.1) | copy-start | bytes 1924
  72.9 2.6 %collective-permute-start.9 = (bf16[50,4,16,128]{3,2,1,0:T(8,128)(2,1)}, bf16[50,4,16,128]{3,2,1,0:T(8,128)(2,1)S(1)}, u32[]{:S(2)}, u32[]{:S(2)}) collective-permute-start(bf16[50,4,16,128]{3,2,1,0:T(8,128)(2,1)} %get-tuple-element.38), channel_id=1, source_target_pairs={{0,4},{4,0},{8,12},{12,8},{16,20},{20,16},{24,28},{28,24},{1,5},{5... | collective-permute-start | bytes 2457608 | tf_op jit(solution)/shard_map/ppermute | solution.py:437
  73.1 7.1 %collective-permute-start.15 = (bf16[4096,128]{1,0:T(8,128)(2,1)S(1)}, bf16[4096,128]{1,0:T(8,128)(2,1)S(1)}, u32[]{:S(2)}, u32[]{:S(2)}) collective-permute-start(bf16[4096,128]{1,0:T(8,128)(2,1)S(1)} %constant_dynamic-update-slice_fusion.5.refs_4_), channel_id=1, source_target_pairs={{0,4},{4,0},{8,12},{12,8},{16,20},{20,16},{24,28},{28,24},{1,5},{5... | collective-permute-start | bytes 3145736 | tf_op jit(solution)/shard_map/ppermute | solution.py:367
  76.0 8.5 %collective-permute-start.10 = (bf16[56,16,128]{2,1,0:T(8,128)(2,1)S(1)}, bf16[56,16,128]{2,1,0:T(8,128)(2,1)S(1)}, u32[]{:S(2)}, u32[]{:S(2)}) collective-permute-start(bf16[56,16,128]{2,1,0:T(8,128)(2,1)S(1)} %get-tuple-element.40), channel_id=1, source_target_pairs={{0,8},{4,12},{8,0},{12,4},{16,24},{20,28},{24,16},{28,20},{1,9},{5... | collective-permute-start | bytes 688136 | tf_op jit(solution)/shard_map/ppermute | solution.py:455
  77.5 12.3 %collective-permute-start.11 = (bf16[56,16,128]{2,1,0:T(8,128)(2,1)S(1)}, bf16[56,16,128]{2,1,0:T(8,128)(2,1)S(1)}, u32[]{:S(2)}, u32[]{:S(2)}) collective-permute-start(bf16[56,16,128]{2,1,0:T(8,128)(2,1)S(1)} %get-tuple-element.41), channel_id=1, source_target_pairs={{0,16},{4,20},{8,24},{12,28},{16,0},{20,4},{24,8},{28,12},{1,17},{... | collective-permute-start | bytes 688136 | tf_op jit(solution)/shard_map/ppermute | solution.py:455
  78.0 11.7 %collective-permute-start.12 = (bf16[56,16,128]{2,1,0:T(8,128)(2,1)S(1)}, bf16[56,16,128]{2,1,0:T(8,128)(2,1)S(1)}, u32[]{:S(2)}, u32[]{:S(2)}) collective-permute-start(bf16[56,16,128]{2,1,0:T(8,128)(2,1)S(1)} %get-tuple-element.42), channel_id=1, source_target_pairs={{0,24},{4,28},{8,16},{12,20},{16,8},{20,12},{24,0},{28,4},{1,25},{... | collective-permute-start | bytes 688136 | tf_op jit(solution)/shard_map/ppermute | solution.py:455

commit v6 on v5

--- a/solution.py
+++ b/solution.py
@@ -13,6 +13,7 @@
 HALF = LANES // 2
 TILE = 2 * LANES
 DEPTH = 3 * LANES
+EXTRA = 16
 VMEM_BYTES = 58 * 1024 * 1024
 
 
@@ -26,6 +27,13 @@
 
 def whole(shape):
     return pl.BlockSpec(shape, lambda *_: (0,) * len(shape))
+
+
+def fetch(sources, targets, sems):
+    copies = [pltpu.make_async_copy(x, y, sems.at[k]) for k, (x, y) in enumerate(zip(sources, targets))]
+    for copy in copies:
+        copy.start()
+    return copies
 
 
 def split(values):
@@ -37,13 +45,17 @@
     rows, width = x_ref.shape
     tiles = width // TILE
     first = lax.broadcasted_iota(jnp.int32, (rows, LANES), 1) < HALF
+    last = None
     for j in range(tiles):
         own = x_ref[:, j * TILE : (j + 1) * TILE]
         before = halo if j == 0 else x_ref[:, j * TILE - LANES : j * TILE]
         after = halo if j == tiles - 1 else x_ref[:, (j + 1) * TILE : (j + 1) * TILE + LANES]
-        edge = jnp.where(first, after, before)
-        window = jnp.concatenate([own, edge], axis=1)
-        store(j, jnp.dot(window, w_ref[j], preferred_element_type=jnp.float32))
+        window = jnp.concatenate([own, jnp.where(first, after, before)], axis=1)
+        values = jnp.dot(window, w_ref[j], preferred_element_type=jnp.float32)
+        if j > 0:
+            store(j - 1, last)
+        last = values
+    store(tiles - 1, last)
 
 
 def lane_pairs(values):
@@ -84,31 +96,32 @@
             out_ref[j, k0 : k0 + rows, n0 : n0 + LANES] = w.astype(jnp.bfloat16)
 
 
-def cut_kernel(images_ref, stencil_ref, top_ref, bottom_ref, head_ref, tail_ref, w_ref, strips, bands, sems):
-    rows, width = images_ref.shape
-    edge = top_ref.shape[0]
-    reads = [
-        pltpu.make_async_copy(images_ref.at[pl.ds(0, edge)], bands.at[0], sems.at[0]),
-        pltpu.make_async_copy(images_ref.at[pl.ds(rows - edge, edge)], bands.at[1], sems.at[1]),
-        pltpu.make_async_copy(images_ref.at[:, pl.ds(0, LANES)], strips.at[0], sems.at[2]),
-        pltpu.make_async_copy(images_ref.at[:, pl.ds(width - LANES, LANES)], strips.at[1], sems.at[3]),
-    ]
-    writes = [
-        pltpu.make_async_copy(bands.at[0], top_ref, sems.at[4]),
-        pltpu.make_async_copy(bands.at[1], bottom_ref, sems.at[5]),
-    ]
-    for copy in reads:
-        copy.start()
+def columns_kernel(images_ref, stencil_ref, head_ref, tail_ref, w_ref, strips, sems):
+    width = images_ref.shape[1]
+    copies = fetch((images_ref.at[:, pl.ds(0, LANES)], images_ref.at[:, pl.ds(width - LANES, LANES)]),
+                   (strips.at[0], strips.at[1]), sems)
     write_weights(stencil_ref, w_ref)
-    for k in range(2):
-        reads[k].wait()
-        writes[k].start()
     row = lax.broadcasted_iota(jnp.int32, (8, LANES), 0)
     lane = lax.broadcasted_iota(jnp.int32, (8, LANES), 1)
     for k, (out, shift) in enumerate(((head_ref, 0), (tail_ref, LANES - 2))):
-        reads[2 + k].wait()
+        copies[k].wait()
         pick = (lane == row + shift).astype(jnp.bfloat16)
         out[...] = gram_of(pick, strips[k])[:2].astype(jnp.bfloat16)
+
+
+def message_kernel(images_ref, columns_ref, top_ref, bottom_ref, bands, sems):
+    rows = images_ref.shape[0]
+    edge = bands.shape[1] - EXTRA
+    copies = fetch((images_ref.at[pl.ds(0, edge)], images_ref.at[pl.ds(rows - edge, edge)]),
+                   (bands.at[0, pl.ds(0, edge)], bands.at[1, pl.ds(0, edge)]), sems)
+    bands[:, edge:, :] = jnp.zeros((2, EXTRA, bands.shape[2]), bands.dtype)
+    bands[0, edge : edge + 8, :edge] = columns_ref[:, :edge]
+    bands[1, edge : edge + 8, :edge] = columns_ref[:, rows - edge :]
+    writes = []
+    for k, out in enumerate((top_ref, bottom_ref)):
+        copies[k].wait()
+        writes += [pltpu.make_async_copy(bands.at[k], out, sems.at[2 + k])]
+        writes[k].start()
     for copy in writes:
         copy.wait()
 
@@ -122,25 +135,29 @@
 
 
 def main_kernel(steps, group, block, pairs_ref, x_ref, columns_ref, w_ref,
-                out_ref, energy_ref, keep_ref, give_ref, held):
+                out_hbm, energy_ref, keep_ref, give_ref, held, sems):
     step = pl.program_id(0)
     blocks = steps * group
     chips = keep_ref.shape[1]
     slots = pairs_ref.shape[1]
 
+    def copy_out(k):
+        here = pl.ds(k * group, group)
+        return pltpu.make_async_copy(held.at[here], out_hbm.at[here], sems.at[k])
+
     @pl.when(step < steps)
     def smooth():
         total = [None]
 
         def store(j, values):
             columns = slice(j * TILE, (j + 1) * TILE)
-            rounded = values.astype(jnp.bfloat16)
-            out_ref[:, columns] = rounded
-            held[pl.ds(step * group, group), :, columns] = rounded.reshape(group, block, TILE)
+            rounded = values.astype(jnp.bfloat16).reshape(group, block, TILE)
+            held[pl.ds(step * group, group), :, columns] = rounded
             squares = lane_pairs(values)
             total[0] = squares if j == 0 else total[0] + squares
 
         smooth_rows(x_ref, halo_tile(columns_ref), w_ref, store)
+        copy_out(step).start()
         for g in range(group):
             energy_ref[pl.ds(step * group + g, 1), :] = row_sums(total[0][g * block : (g + 1) * block, :])
 
@@ -156,18 +173,12 @@
             return carry
 
         lax.fori_loop(0, slots, one, 0, unroll=4)
-
-
-def fetch(sources, targets, sems):
-    copies = [pltpu.make_async_copy(x, y, sems.at[k]) for k, (x, y) in enumerate(zip(sources, targets))]
-    for copy in copies:
-        copy.start()
-    return copies
-
-
-def cross_kernel(blocks, block, pairs_ref, down_hbm, up_hbm, down_columns_hbm, up_columns_hbm, w_hbm, energy_hbm,
-                 smoothed_hbm, keep_hbm, give_hbm, keep_ref, give_ref, x_ref, columns_ref, w_ref, energy_ref, own, near,
-                 table, sems):
+        for k in range(steps):
+            copy_out(k).wait()
+
+
+def cross_kernel(blocks, block, pairs_ref, down_hbm, up_hbm, w_hbm, energy_hbm, smoothed_hbm, keep_hbm,
+                 give_hbm, keep_ref, give_ref, x_ref, columns_ref, w_ref, energy_ref, own, near, table, sems):
     core = lax.axis_index("pix") % 2
     first_block = lax.axis_index("ion") * blocks
     slots = pairs_ref.shape[1]
@@ -177,8 +188,8 @@
     rows = blocks * block
     low, high = pl.ds(0, edge), pl.ds(edge, edge)
     copies = fetch(
-        (down_hbm, up_hbm, down_columns_hbm, up_columns_hbm, w_hbm, energy_hbm, smoothed_hbm.at[low],
-         smoothed_hbm.at[pl.ds(rows - edge, edge)], keep_hbm, give_hbm),
+        (down_hbm.at[low], up_hbm.at[low], down_hbm.at[pl.ds(edge, EXTRA), low], up_hbm.at[pl.ds(edge, EXTRA), low], w_hbm,
+         energy_hbm, smoothed_hbm.at[low], smoothed_hbm.at[pl.ds(rows - edge, edge)], keep_hbm, give_hbm),
         (x_ref.at[low], x_ref.at[high], columns_ref.at[:, low], columns_ref.at[:, high], w_ref, energy_ref, own.at[low],
          own.at[high], keep_ref, give_ref),
         sems,
@@ -194,7 +205,7 @@
         squares = lane_pairs(values)
         total[0] = squares if j == 0 else total[0] + squares
 
-    smooth_rows(x_ref, halo_tile(columns_ref), w_ref, store)
+    smooth_rows(x_ref, halo_tile(columns_ref.at[:8]), w_ref, store)
     for k in range(2 * REACH):
         row = k if k < REACH else k + blocks
         table[row : row + 1, :] = row_sums(total[0][k * block : (k + 1) * block, :])
@@ -300,7 +311,7 @@
         out_ref[s] = jnp.where(s < live_ref[0], scores, 0.0).astype(jnp.bfloat16)
         return carry
 
-    lax.fori_loop(0, slots, one, 0, unroll=16)
+    lax.fori_loop(0, slots, one, 0, unroll=slots)
 
 
 def on_device(images, stencil, pairs, live, rule_of_block, adduct):
@@ -326,41 +337,49 @@
 
     part = rules_here * block // n_pix
     mine = lax.dynamic_slice_in_dim(adduct.reshape(rules_here * block, block), pix * part, part, 0)
-    turns = [lax.ppermute(mine, "ion", [(i, i ^ d) for i in range(n_ion)]) for d in range(1, n_ion)]
-
-    edge_rows = jax.ShapeDtypeStruct((edge, width), images.dtype)
+
+    def turned(value, distance):
+        other = lax.ppermute(value, "ion", [(i, i ^ distance) for i in range(n_ion)])
+        return jnp.concatenate([value, other], axis=0)
+
+    mine = turned(mine, 1)
+
     edge_columns = jax.ShapeDtypeStruct((2, rows), images.dtype)
-    top, bottom, head, tail, weights = pl.pallas_call(
-        cut_kernel,
+    head, tail, weights = pl.pallas_call(
+        columns_kernel,
         in_specs=[hbm, vmem],
-        out_specs=[hbm, hbm, vmem, vmem, vmem],
+        out_specs=[vmem, vmem, vmem],
         out_shape=[
-            edge_rows,
-            edge_rows,
             edge_columns,
             edge_columns,
             jax.ShapeDtypeStruct((width // TILE, DEPTH, TILE), jnp.bfloat16),
         ],
-        scratch_shapes=[
-            pltpu.VMEM((2, rows, LANES), images.dtype),
-            pltpu.VMEM((2, edge, width), images.dtype),
-            pltpu.SemaphoreType.DMA((6,)),
-        ],
+        scratch_shapes=[pltpu.VMEM((2, rows, LANES), images.dtype), pltpu.SemaphoreType.DMA((2,))],
+        compiler_params=params(),
+        cost_estimate=cost(0, 4 * rows * LANES),
+        name="columns",
+    )(images, stencil)
+    head, tail, mine = lax.optimization_barrier((head, tail, mine))
+    before = shifted("pix", n_pix, True, tail)
+    after = shifted("pix", n_pix, False, head)
+    for k in range(1, n_ion.bit_length() - 1):
+        mine = turned(mine, 2**k)
+    columns = jnp.concatenate([after, jnp.zeros((4, rows), images.dtype), before], axis=0)
+
+    message = jax.ShapeDtypeStruct((edge + EXTRA, width), images.dtype)
+    top, bottom = pl.pallas_call(
+        message_kernel,
+        in_specs=[hbm, vmem],
+        out_specs=[hbm, hbm],
+        out_shape=[message, message],
+        scratch_shapes=[pltpu.VMEM((2, edge + EXTRA, width), images.dtype), pltpu.SemaphoreType.DMA((4,))],
         compiler_params=params(),
         cost_estimate=cost(0, 8 * edge * width),
-        name="cut_edges",
-    )(images, stencil)
-
-    top, bottom, head, tail, *turns = lax.optimization_barrier((top, bottom, head, tail, *turns))
-    mine = jnp.concatenate([mine, *turns], axis=0)
-
+        name="edge_messages",
+    )(images, columns)
+    top, bottom, mine = lax.optimization_barrier((top, bottom, mine))
     down = shifted("ion", n_ion, True, bottom)
     up = shifted("ion", n_ion, False, top)
-    before = shifted("pix", n_pix, True, tail)
-    after = shifted("pix", n_pix, False, head)
-    columns = jnp.concatenate([after, jnp.zeros((4, rows), images.dtype), before], axis=0)
-    down_columns = shifted("ion", n_ion, True, columns[:, rows - edge :])
-    up_columns = shifted("ion", n_ion, False, columns[:, :edge])
 
     distances = [n_pix >> k for k in range(1, n_pix.bit_length())]
     for distance in distances:
@@ -401,11 +420,11 @@
                 pl.BlockSpec((8, group * block), lambda i, *_: (0, jnp.minimum(i, steps - 1))),
                 whole(weights.shape),
             ],
-            out_specs=[rows_at(width), whole((blocks, LANES)), whole(half_shape), whole(half_shape)],
-            scratch_shapes=[pltpu.VMEM((blocks, block, width), jnp.bfloat16)],
+            out_specs=[hbm, whole((blocks, LANES)), whole(half_shape), whole(half_shape)],
+            scratch_shapes=[pltpu.VMEM((blocks, block, width), jnp.bfloat16), pltpu.SemaphoreType.DMA((steps,))],
         ),
         out_shape=[
-            jax.ShapeDtypeStruct((rows, width), jnp.bfloat16),
+            jax.ShapeDtypeStruct((blocks, block, width), jnp.bfloat16),
             jax.ShapeDtypeStruct((blocks, LANES), jnp.float32),
             *both_halves,
         ],
@@ -413,15 +432,16 @@
         cost_estimate=cost(2 * rows * width * DEPTH + 2 * slots * block * block * width, 4 * rows * width),
         name="smooth_and_gram",
     )(table_pairs, images, columns, weights)
+    smoothed = smoothed.reshape(rows, width)
 
     keep, give = pl.pallas_call(
         functools.partial(cross_kernel, blocks, block),
-        in_specs=[smem] + [hbm] * 4 + [fixed] * 5,
+        in_specs=[smem] + [hbm] * 2 + [fixed] * 5,
         out_specs=[vmem, vmem],
         out_shape=both_halves,
         scratch_shapes=[
             pltpu.VMEM((2 * edge, width), jnp.bfloat16),
-            pltpu.VMEM((8, 2 * edge), jnp.bfloat16),
+            pltpu.VMEM((EXTRA, 2 * edge), jnp.bfloat16),
             pltpu.VMEM(weights.shape, jnp.bfloat16),
             pltpu.VMEM((blocks, LANES), jnp.float32),
             pltpu.VMEM((2 * edge, width), jnp.bfloat16),
@@ -432,7 +452,7 @@
         compiler_params=params(),
         cost_estimate=cost(4 * edge * width * DEPTH, 8 * edge * width),
         name="cross_grams",
-    )(table_pairs, down, up, down_columns, up_columns, weights, energy, smoothed, keep, give)
+    )(table_pairs, down, up, weights, energy, smoothed, keep, give)
 
     got = lax.ppermute(give, "pix", [(i, i ^ 1) for i in range(n_pix)])
     message = jax.ShapeDtypeStruct((slots + 2 * units * chips, share, LANES), jnp.bfloat16)

time: 95.4 us -> 97.9 us (1.026)
  waiting for transfers between devices: 11.5 us -> 18 us
  starting transfers between devices: 28.2 us -> 22.8 us
  Pallas kernels: 50.2 us -> 52.3 us
    ppermute x6 -> x4, waiting for transfers between devices: 0.02 us -> 6.44 us  [shifted(): return lax.ppermute(value, axis, steps)]
    ppermute x6 -> x4, starting transfers between devices: 14.4 us -> 8.96 us  [shifted(): return lax.ppermute(value, axis, steps)]
    pallas_call x1 -> x2, Pallas kernels: 6.06 us -> 8.35 us  [the longest x1 4.32 us: on_device(): pl.pallas_call(columns_kernel, in_specs=[hbm, vmem], out_specs=[vmem, vme...]
    pallas_call x1, Pallas kernels: 30.7 us -> 29.1 us  [on_device(): pl.pallas_call(functools.partial(main_kernel, steps, group, block), grid_...]
    pallas_call x1, Pallas kernels: 8.41 us -> 9.92 us  [on_device(): pl.pallas_call(functools.partial(cross_kernel, blocks, block), in_specs=[...]
    ppermute x3 -> x2, starting transfers between devices: 3.55 us -> 2.76 us  [turned(): lax.ppermute(value, 'ion', [(i, i ^ distance) for i in range(n_ion)])]
    unnamed x21 -> x12, local copies, waits for them, and re-layouts: 2.62 us -> 2.25 us
  transfers between devices with their start and end apart: 16 -> 13, of which waited for: 3 -> 7; matrix products, arithmetic and copies ran while one was open for 0% -> 1% of each run, Pallas kernels for 48% -> 49%
where the time goes in v6:
time: 97.9 us; the launch traced here: 97.8 us
  Pallas kernels  52.3 us (53%)
  starting transfers between devices  22.8 us (23%)
  waiting for transfers between devices  18 us (18%)
  local copies, waits for them, and re-layouts  2.41 us (2%)
  between operations  1.49 us (2%)
    pallas_call x1, Pallas kernels, on_device(): pl.pallas_call(functools.partial(main_kernel, steps, group, block), grid_...  29.1 us
    pallas_call x1, Pallas kernels, on_device(): pl.pallas_call(functools.partial(cross_kernel, blocks, block), in_specs=[...  9.92 us
    ppermute x3, waiting for transfers between devices, on_device(): lax.ppermute(m, 'pix', [(i, i ^ 2 * (d + 1)) for i in range(n_pix)])  9.29 us
    ppermute x4, starting transfers between devices, shifted(): return lax.ppermute(value, axis, steps)  8.96 us
    ppermute x3, starting transfers between devices, on_device(): other = lax.ppermute(mine, 'pix', [(i, i ^ distance) for i in range(n_pix)])  7.44 us
    ppermute x4, waiting for transfers between devices, shifted(): return lax.ppermute(value, axis, steps)  6.44 us
    pallas_call x1, Pallas kernels, on_device(): pl.pallas_call(functools.partial(score_kernel, blocks, place_of, pixel_co...  4.46 us
    pallas_call x1, Pallas kernels, on_device(): pl.pallas_call(columns_kernel, in_specs=[hbm, vmem], out_specs=[vmem, vme...  4.32 us
  transfers between devices with their start and end apart: 13, of which 7 were waited for; matrix products, arithmetic and copies ran while one was open for 1% of the time, Pallas kernels for 49%

profile of v6, /device:TPU:8, one launch (start us, length us, event | category | flops | bytes accessed | tf_op | source)
XLA Modules:
  0.0 97.8 jit_solution(7754075846647588086)
XLA Ops:
  0.6 0.0 copy-start
  0.6 1.0 %copy-done = bf16[16,128,128]{2,1,0:T(8,128)(2,1)S(1)} copy-done((bf16[16,128,128]{2,1,0:T(8,128)(2,1)S(1)}, bf16[16,128,128]{2,1,0:T(8,128)(2,1)}, u32[]{:S(2)}) %copy-start) | copy-done | bytes 524312
  1.7 4.3 %columns.1 = (bf16[2,5120]{1,0:T(2,128)(2,1)}, bf16[2,5120]{1,0:T(2,128)(2,1)}, bf16[8,384,256]{2,1,0:T(8,128)(2,1)}) custom-call(bf16[5120,2048]{1,0:T(8,128)(2,1)} %images_ref.3, f32[5,2048]{1,0:T(8,128)} %stencil_ref.1), custom_call_target="tpu_custom_call" | custom-call | bytes 2621440 | tf_op jit(solution)/shard_map/columns/pallas_call | solution.py:348
  6.0 1.7 %collective-permute-start.2 = (bf16[2,5120]{1,0:T(2,128)(2,1)}, bf16[2,5120]{1,0:T(2,128)(2,1)S(1)}, u32[]{:S(2)}, u32[]{:S(2)}) collective-permute-start(bf16[2,5120]{1,0:T(2,128)(2,1)} %get-tuple-element.26), channel_id=1, source_target_pairs={{0,4},{4,8},{8,12},{12,16},{16,20},{20,24},{24,28},{1,5},{5,9},{9,... | collective-permute-start | bytes 61448 | tf_op jit(solution)/shard_map/ppermute | solution.py:331
  7.8 1.3 %collective-permute-start.1 = (bf16[2,5120]{1,0:T(2,128)(2,1)}, bf16[2,5120]{1,0:T(2,128)(2,1)S(1)}, u32[]{:S(2)}, u32[]{:S(2)}) collective-permute-start(bf16[2,5120]{1,0:T(2,128)(2,1)} %get-tuple-element.25), channel_id=1, source_target_pairs={{4,0},{8,4},{12,8},{16,12},{20,16},{24,20},{28,24},{5,1},{9,5},{13... | collective-permute-start | bytes 61448 | tf_op jit(solution)/shard_map/ppermute | solution.py:331
  9.1 0.1 pad.5.clone
  9.2 2.8 %collective-permute-start.3 = (bf16[512,128]{1,0:T(8,128)(2,1)S(1)}, bf16[512,128]{1,0:T(8,128)(2,1)S(1)}, u32[]{:S(2)}, u32[]{:S(2)}) collective-permute-start(bf16[512,128]{1,0:T(8,128)(2,1)S(1)} %pad_maximum_fusion.2), channel_id=1, source_target_pairs={{0,2},{1,3},{2,0},{3,1},{4,6},{5,7},{6,4},{7,5},{8,10},{9,11},{10,... | collective-permute-start | bytes 393224 | tf_op jit(solution)/shard_map/ppermute | solution.py:342
  11.9 0.9 collective-permute-done.1
  12.8 0.7 pad_maximum_fusion.3.columns_ref
  13.5 4.0 %edge_messages.1 = (bf16[400,2048]{1,0:T(8,128)(2,1)}, bf16[400,2048]{1,0:T(8,128)(2,1)}) custom-call(bf16[5120,2048]{1,0:T(8,128)(2,1)} %images_ref.3, bf16[8,5120]{1,0:T(8,128)(2,1)} %pad_maximum_fusion.3.columns_ref), custom_call_target="tpu_custom_call" | custom-call | bytes 6291456 | tf_op jit(solution)/shard_map/edge_messages/pallas_call | solution.py:370
  17.6 4.4 %collective-permute-start.10 = (bf16[1024,128]{1,0:T(8,128)(2,1)S(1)}, bf16[1024,128]{1,0:T(8,128)(2,1)S(1)}, u32[]{:S(2)}, u32[]{:S(2)}) collective-permute-start(bf16[1024,128]{1,0:T(8,128)(2,1)S(1)} %pad_maximum_fusion.1), channel_id=1, source_target_pairs={{0,16},{4,20},{8,24},{12,28},{16,0},{20,4},{24,8},{28,12},{1,17},{... | collective-permute-start | bytes 786440 | tf_op jit(solution)/shard_map/ppermute | solution.py:386
  22.0 3.6 %collective-permute-start.4 = (bf16[400,2048]{1,0:T(8,128)(2,1)}, bf16[400,2048]{1,0:T(8,128)(2,1)S(1)}, u32[]{:S(2)}, u32[]{:S(2)}) collective-permute-start(bf16[400,2048]{1,0:T(8,128)(2,1)} %get-tuple-element.32), channel_id=1, source_target_pairs={{0,1},{1,2},{2,3},{4,5},{5,6},{6,7},{8,9},{9,10},{10,11},{12,13},{... | collective-permute-start | bytes 4915208 | tf_op jit(solution)/shard_map/ppermute | solution.py:331
  25.6 2.4 %collective-permute-start.5 = (bf16[400,2048]{1,0:T(8,128)(2,1)}, bf16[400,2048]{1,0:T(8,128)(2,1)}, u32[]{:S(2)}, u32[]{:S(2)}) collective-permute-start(bf16[400,2048]{1,0:T(8,128)(2,1)} %get-tuple-element.33), channel_id=1, source_target_pairs={{1,0},{2,1},{3,2},{5,4},{6,5},{7,6},{9,8},{10,9},{11,10},{13,12},{... | collective-permute-start | bytes 4915208 | tf_op jit(solution)/shard_map/ppermute | solution.py:331
  28.0 0.4 collective-permute-done.10
  28.4 2.5 %collective-permute-start.11 = (bf16[2048,128]{1,0:T(8,128)(2,1)S(1)}, bf16[2048,128]{1,0:T(8,128)(2,1)S(1)}, u32[]{:S(2)}, u32[]{:S(2)}) collective-permute-start(bf16[2048,128]{1,0:T(8,128)(2,1)S(1)} %pad_maximum_fusion), channel_id=1, source_target_pairs={{0,8},{4,12},{8,0},{12,4},{16,24},{20,28},{24,16},{28,20},{1,9},{5... | collective-permute-start | bytes 1572872 | tf_op jit(solution)/shard_map/ppermute | solution.py:386
  30.9 29.1 %smooth_and_gram.1 = (bf16[40,128,2048]{2,1,0:T(8,128)(2,1)}, f32[40,128]{1,0:T(8,128)}, bf16[50,4,16,128]{3,2,1,0:T(8,128)(2,1)}, bf16[50,4,16,128]{3,2,1,0:T(8,128)(2,1)}) custom-call(s32[2,48]{1,0:T(2,128)} %bitcast.4, bf16[5120,2048]{1,0:T(8,128)(2,1)} %images_ref.3, bf16[8,5120]{1,0:T(8,128)(2,1)} %pad_maximum_fusion.3.columns_ref, ...), custom_call_target="tpu_custom_call" | custom-call | flops 11274289152 | bytes 41943040 | tf_op jit(solution)/shard_map/smooth_and_gram/pallas_call | solution.py:413
  60.1 1.5 %collective-permute-done.4.down_hbm = bf16[400,2048]{1,0:T(8,128)(2,1)S(1)} collective-permute-done((bf16[400,2048]{1,0:T(8,128)(2,1)}, bf16[400,2048]{1,0:T(8,128)(2,1)S(1)}, u32[]{:S(2)}, u32[]{:S(2)}) %collective-permute-start.4) | collective-permute-done | bytes 1638432 | tf_op jit(solution)/shard_map/ppermute | solution.py:331
  61.6 4.1 %collective-permute-done.5.up_hbm = bf16[400,2048]{1,0:T(8,128)(2,1)} collective-permute-done((bf16[400,2048]{1,0:T(8,128)(2,1)}, bf16[400,2048]{1,0:T(8,128)(2,1)}, u32[]{:S(2)}, u32[]{:S(2)}) %collective-permute-start.5) | collective-permute-done | bytes 1638432 | tf_op jit(solution)/shard_map/ppermute | solution.py:331
  65.7 9.9 %cross_grams.1 = (bf16[50,4,16,128]{3,2,1,0:T(8,128)(2,1)}, bf16[50,4,16,128]{3,2,1,0:T(8,128)(2,1)}) custom-call(s32[2,48]{1,0:T(2,128)} %bitcast.5, bf16[400,2048]{1,0:T(8,128)(2,1)} %copy-done.4, bf16[400,2048]{1,0:T(8,128)(2,1)} %collective-permute-done.5.up_hbm, bf16[8,384,256]{2,1,0:T(8,128)(2,1)} %get-tuple-element.27.w_ref.w_hbm, ...), custom_call_target="tpu_custom_call" | custom-call | flops 1207959552 | bytes 6291456 | tf_op jit(solution)/shard_map/cross_grams/pallas_call | solution.py:437
  75.6 0.0 copy-start.2
  75.6 0.1 collective-permute-start.6
  75.7 0.1 constant_dynamic-update-slice_fusion.refs_4_
  75.8 0.6 collective-permute-start.12
  76.4 1.9 %collective-permute-done.6.got_hbm = bf16[50,4,16,128]{3,2,1,0:T(8,128)(2,1)S(1)} collective-permute-done((bf16[50,4,16,128]{3,2,1,0:T(8,128)(2,1)}, bf16[50,4,16,128]{3,2,1,0:T(8,128)(2,1)S(1)}, u32[]{:S(2)}, u32[]{:S(2)}) %collective-permute-start.6) | collective-permute-done | bytes 819232 | tf_op jit(solution)/shard_map/ppermute | solution.py:457
  78.2 1.1 %copy-done.1 = bf16[50,4,16,128]{3,2,1,0:T(8,128)(2,1)S(1)} copy-done((bf16[50,4,16,128]{3,2,1,0:T(8,128)(2,1)S(1)}, bf16[50,4,16,128]{3,2,1,0:T(8,128)(2,1)}, u32[]{:S(2)}) %copy-start.1) | copy-done | bytes 819224
  79.4 0.4 chip_sums.1
  79.8 1.2 %collective-permute-start.7 = (bf16[56,16,128]{2,1,0:T(8,128)(2,1)S(1)}, bf16[56,16,128]{2,1,0:T(8,128)(2,1)S(1)}, u32[]{:S(2)}, u32[]{:S(2)}) collective-permute-start(bf16[56,16,128]{2,1,0:T(8,128)(2,1)S(1)} %get-tuple-element.40), channel_id=1, source_target_pairs={{0,8},{4,12},{8,0},{12,4},{16,24},{20,28},{24,16},{28,20},{1,9},{5... | collective-permute-start | bytes 688136 | tf_op jit(solution)/shard_map/ppermute | solution.py:475
  81.0 1.7 %collective-permute-start.8 = (bf16[56,16,128]{2,1,0:T(8,128)(2,1)S(1)}, bf16[56,16,128]{2,1,0:T(8,128)(2,1)S(1)}, u32[]{:S(2)}, u32[]{:S(2)}) collective-permute-start(bf16[56,16,128]{2,1,0:T(8,128)(2,1)S(1)} %get-tuple-element.41), channel_id=1, source_target_pairs={{0,16},{4,20},{8,24},{12,28},{16,0},{20,4},{24,8},{28,12},{1,17},{... | collective-permute-start | bytes 688136 | tf_op jit(solution)/shard_map/ppermute | solution.py:475
  82.8 0.6 collective-permute-start.9
  84.0 4.3 %collective-permute-done.7.refs_1_ = bf16[56,16,128]{2,1,0:T(8,128)(2,1)S(1)} collective-permute-done((bf16[56,16,128]{2,1,0:T(8,128)(2,1)S(1)}, bf16[56,16,128]{2,1,0:T(8,128)(2,1)S(1)}, u32[]{:S(2)}, u32[]{:S(2)}) %collective-permute-start.7) | collective-permute-done | bytes 229408 | tf_op jit(solution)/shard_map/ppermute | solution.py:475
  88.3 5.0 %collective-permute-done.8.refs_2_ = bf16[56,16,128]{2,1,0:T(8,128)(2,1)S(1)} collective-permute-done((bf16[56,16,128]{2,1,0:T(8,128)(2,1)S(1)}, bf16[56,16,128]{2,1,0:T(8,128)(2,1)S(1)}, u32[]{:S(2)}, u32[]{:S(2)}) %collective-permute-start.8) | collective-permute-done | bytes 229408 | tf_op jit(solution)/shard_map/ppermute | solution.py:475
  93.3 4.5 %scores.1 = bf16[48,16,128]{2,1,0:T(8,128)(2,1)} custom-call(s32[2,48]{1,0:T(2,128)S(1)} %bitcast.6, s32[1]{0:T(128)S(6)} %copy.10.live_ref, s32[160]{0:T(256)S(1)} %copy-done.3, f32[52,16,128]{2,1,0:T(8,128)S(1)} %get-tuple-element.39.refs_0_, bf16[56,16,128]{2,1,0:T(8,128)(2,1)S(1)} %collective-permute-done.7.refs_1_, ...), custom_call_target="tpu_custom_call" | custom-call | tf_op jit(solution)/shard_map/scores/pallas_call | solution.py:478
  (20 shorter events, 0.2 us)
Async XLA Ops:
  0.6 1.0 %copy-start = (bf16[16,128,128]{2,1,0:T(8,128)(2,1)S(1)}, bf16[16,128,128]{2,1,0:T(8,128)(2,1)}, u32[]{:S(2)}) copy-start(bf16[16,128,128]{2,1,0:T(8,128)(2,1)} %param.11) | copy-start | bytes 1572868
  1.7 4.3 %collective-permute-start = (bf16[256,128]{1,0:T(8,128)(2,1)S(1)}, bf16[256,128]{1,0:T(8,128)(2,1)S(1)}, u32[]{:S(2)}, u32[]{:S(2)}) collective-permute-start(bf16[256,128]{1,0:T(8,128)(2,1)S(1)} %constant_dynamic-slice_fusion), channel_id=1, source_target_pairs={{0,1},{1,0},{2,3},{3,2},{4,5},{5,4},{6,7},{7,6},{8,9},{9,8},{10,11... | collective-permute-start | bytes 196616 | tf_op jit(solution)/shard_map/ppermute | solution.py:342
  6.0 5.9 %collective-permute-start.2 = (bf16[2,5120]{1,0:T(2,128)(2,1)}, bf16[2,5120]{1,0:T(2,128)(2,1)S(1)}, u32[]{:S(2)}, u32[]{:S(2)}) collective-permute-start(bf16[2,5120]{1,0:T(2,128)(2,1)} %get-tuple-element.26), channel_id=1, source_target_pairs={{0,4},{4,8},{8,12},{12,16},{16,20},{20,24},{24,28},{1,5},{5,9},{9,... | collective-permute-start | bytes 61448 | tf_op jit(solution)/shard_map/ppermute | solution.py:331
  7.8 5.0 %collective-permute-start.1 = (bf16[2,5120]{1,0:T(2,128)(2,1)}, bf16[2,5120]{1,0:T(2,128)(2,1)S(1)}, u32[]{:S(2)}, u32[]{:S(2)}) collective-permute-start(bf16[2,5120]{1,0:T(2,128)(2,1)} %get-tuple-element.25), channel_id=1, source_target_pairs={{4,0},{8,4},{12,8},{16,12},{20,16},{24,20},{28,24},{5,1},{9,5},{13... | collective-permute-start | bytes 61448 | tf_op jit(solution)/shard_map/ppermute | solution.py:331
  9.2 8.4 %collective-permute-start.3 = (bf16[512,128]{1,0:T(8,128)(2,1)S(1)}, bf16[512,128]{1,0:T(8,128)(2,1)S(1)}, u32[]{:S(2)}, u32[]{:S(2)}) collective-permute-start(bf16[512,128]{1,0:T(8,128)(2,1)S(1)} %pad_maximum_fusion.2), channel_id=1, source_target_pairs={{0,2},{1,3},{2,0},{3,1},{4,6},{5,7},{6,4},{7,5},{8,10},{9,11},{10,... | collective-permute-start | bytes 393224 | tf_op jit(solution)/shard_map/ppermute | solution.py:342
  17.6 10.8 %collective-permute-start.10 = (bf16[1024,128]{1,0:T(8,128)(2,1)S(1)}, bf16[1024,128]{1,0:T(8,128)(2,1)S(1)}, u32[]{:S(2)}, u32[]{:S(2)}) collective-permute-start(bf16[1024,128]{1,0:T(8,128)(2,1)S(1)} %pad_maximum_fusion.1), channel_id=1, source_target_pairs={{0,16},{4,20},{8,24},{12,28},{16,0},{20,4},{24,8},{28,12},{1,17},{... | collective-permute-start | bytes 786440 | tf_op jit(solution)/shard_map/ppermute | solution.py:386
  22.0 39.5 %collective-permute-start.4 = (bf16[400,2048]{1,0:T(8,128)(2,1)}, bf16[400,2048]{1,0:T(8,128)(2,1)S(1)}, u32[]{:S(2)}, u32[]{:S(2)}) collective-permute-start(bf16[400,2048]{1,0:T(8,128)(2,1)} %get-tuple-element.32), channel_id=1, source_target_pairs={{0,1},{1,2},{2,3},{4,5},{5,6},{6,7},{8,9},{9,10},{10,11},{12,13},{... | collective-permute-start | bytes 4915208 | tf_op jit(solution)/shard_map/ppermute | solution.py:331
  25.6 40.1 %collective-permute-start.5 = (bf16[400,2048]{1,0:T(8,128)(2,1)}, bf16[400,2048]{1,0:T(8,128)(2,1)}, u32[]{:S(2)}, u32[]{:S(2)}) collective-permute-start(bf16[400,2048]{1,0:T(8,128)(2,1)} %get-tuple-element.33), channel_id=1, source_target_pairs={{1,0},{2,1},{3,2},{5,4},{6,5},{7,6},{9,8},{10,9},{11,10},{13,12},{... | collective-permute-start | bytes 4915208 | tf_op jit(solution)/shard_map/ppermute | solution.py:331
  28.4 47.3 %collective-permute-start.11 = (bf16[2048,128]{1,0:T(8,128)(2,1)S(1)}, bf16[2048,128]{1,0:T(8,128)(2,1)S(1)}, u32[]{:S(2)}, u32[]{:S(2)}) collective-permute-start(bf16[2048,128]{1,0:T(8,128)(2,1)S(1)} %pad_maximum_fusion), channel_id=1, source_target_pairs={{0,8},{4,12},{8,0},{12,4},{16,24},{20,28},{24,16},{28,20},{1,9},{5... | collective-permute-start | bytes 1572872 | tf_op jit(solution)/shard_map/ppermute | solution.py:386
  61.6 4.1 %copy-start.4 = (bf16[400,2048]{1,0:T(8,128)(2,1)}, bf16[400,2048]{1,0:T(8,128)(2,1)S(1)}, u32[]{:S(2)}) copy-start(bf16[400,2048]{1,0:T(8,128)(2,1)S(1)} %collective-permute-done.4.down_hbm) | copy-start | bytes 4915204
  75.6 17.7 %copy-start.2 = (s32[48,2]{0,1:T(2,128)S(1)}, s32[48,2]{0,1:T(2,128)}, u32[]{:S(2)}) copy-start(s32[48,2]{0,1:T(2,128)} %param.8) | copy-start | bytes 1156
  75.6 17.7 %copy-start.3 = (s32[160]{0:T(256)S(1)}, s32[160]{0:T(256)}, u32[]{:S(2)}) copy-start(s32[160]{0:T(256)} %rules_ref.1) | copy-start | bytes 1924
  75.6 2.6 %collective-permute-start.6 = (bf16[50,4,16,128]{3,2,1,0:T(8,128)(2,1)}, bf16[50,4,16,128]{3,2,1,0:T(8,128)(2,1)S(1)}, u32[]{:S(2)}, u32[]{:S(2)}) collective-permute-start(bf16[50,4,16,128]{3,2,1,0:T(8,128)(2,1)} %get-tuple-element.38), channel_id=1, source_target_pairs={{0,4},{4,0},{8,12},{12,8},{16,20},{20,16},{24,28},{28,24},{1,5},{5... | collective-permute-start | bytes 2457608 | tf_op jit(solution)/shard_map/ppermute | solution.py:457
  75.8 8.2 %collective-permute-start.12 = (bf16[4096,128]{1,0:T(8,128)(2,1)S(1)}, bf16[4096,128]{1,0:T(8,128)(2,1)S(1)}, u32[]{:S(2)}, u32[]{:S(2)}) collective-permute-start(bf16[4096,128]{1,0:T(8,128)(2,1)S(1)} %constant_dynamic-update-slice_fusion.refs_4_), channel_id=1, source_target_pairs={{0,4},{4,0},{8,12},{12,8},{16,20},{20,16},{24,28},{28,24},{1,5},{5... | collective-permute-start | bytes 3145736 | tf_op jit(solution)/shard_map/ppermute | solution.py:386
  78.2 1.1 %copy-start.1 = (bf16[50,4,16,128]{3,2,1,0:T(8,128)(2,1)S(1)}, bf16[50,4,16,128]{3,2,1,0:T(8,128)(2,1)}, u32[]{:S(2)}) copy-start(bf16[50,4,16,128]{3,2,1,0:T(8,128)(2,1)} %get-tuple-element.37.keep_hbm) | copy-start | bytes 2457604
  79.8 8.5 %collective-permute-start.7 = (bf16[56,16,128]{2,1,0:T(8,128)(2,1)S(1)}, bf16[56,16,128]{2,1,0:T(8,128)(2,1)S(1)}, u32[]{:S(2)}, u32[]{:S(2)}) collective-permute-start(bf16[56,16,128]{2,1,0:T(8,128)(2,1)S(1)} %get-tuple-element.40), channel_id=1, source_target_pairs={{0,8},{4,12},{8,0},{12,4},{16,24},{20,28},{24,16},{28,20},{1,9},{5... | collective-permute-start | bytes 688136 | tf_op jit(solution)/shard_map/ppermute | solution.py:475
  81.0 12.3 %collective-permute-start.8 = (bf16[56,16,128]{2,1,0:T(8,128)(2,1)S(1)}, bf16[56,16,128]{2,1,0:T(8,128)(2,1)S(1)}, u32[]{:S(2)}, u32[]{:S(2)}) collective-permute-start(bf16[56,16,128]{2,1,0:T(8,128)(2,1)S(1)} %get-tuple-element.41), channel_id=1, source_target_pairs={{0,16},{4,20},{8,24},{12,28},{16,0},{20,4},{24,8},{28,12},{1,17},{... | collective-permute-start | bytes 688136 | tf_op jit(solution)/shard_map/ppermute | solution.py:475
  82.8 10.6 %collective-permute-start.9 = (bf16[56,16,128]{2,1,0:T(8,128)(2,1)S(1)}, bf16[56,16,128]{2,1,0:T(8,128)(2,1)S(1)}, u32[]{:S(2)}, u32[]{:S(2)}) collective-permute-start(bf16[56,16,128]{2,1,0:T(8,128)(2,1)S(1)} %get-tuple-element.42), channel_id=1, source_target_pairs={{0,24},{4,28},{8,16},{12,20},{16,8},{20,12},{24,0},{28,4},{1,25},{... | collective-permute-start | bytes 688136 | tf_op jit(solution)/shard_map/ppermute | solution.py:475

commit v7 on v6

--- a/solution.py
+++ b/solution.py
@@ -13,7 +13,6 @@
 HALF = LANES // 2
 TILE = 2 * LANES
 DEPTH = 3 * LANES
-EXTRA = 16
 VMEM_BYTES = 58 * 1024 * 1024
 
 
@@ -96,34 +95,40 @@
             out_ref[j, k0 : k0 + rows, n0 : n0 + LANES] = w.astype(jnp.bfloat16)
 
 
-def columns_kernel(images_ref, stencil_ref, head_ref, tail_ref, w_ref, strips, sems):
+def columns_kernel(images_ref, stencil_ref, near_ref, far_ref, w_ref, strips, sems):
     width = images_ref.shape[1]
     copies = fetch((images_ref.at[:, pl.ds(0, LANES)], images_ref.at[:, pl.ds(width - LANES, LANES)]),
                    (strips.at[0], strips.at[1]), sems)
     write_weights(stencil_ref, w_ref)
     row = lax.broadcasted_iota(jnp.int32, (8, LANES), 0)
     lane = lax.broadcasted_iota(jnp.int32, (8, LANES), 1)
-    for k, (out, shift) in enumerate(((head_ref, 0), (tail_ref, LANES - 2))):
+    sides = []
+    for k, shift in enumerate((0, LANES - 2)):
         copies[k].wait()
         pick = (lane == row + shift).astype(jnp.bfloat16)
-        out[...] = gram_of(pick, strips[k])[:2].astype(jnp.bfloat16)
-
-
-def message_kernel(images_ref, columns_ref, top_ref, bottom_ref, bands, sems):
-    rows = images_ref.shape[0]
-    edge = bands.shape[1] - EXTRA
-    copies = fetch((images_ref.at[pl.ds(0, edge)], images_ref.at[pl.ds(rows - edge, edge)]),
-                   (bands.at[0, pl.ds(0, edge)], bands.at[1, pl.ds(0, edge)]), sems)
-    bands[:, edge:, :] = jnp.zeros((2, EXTRA, bands.shape[2]), bands.dtype)
-    bands[0, edge : edge + 8, :edge] = columns_ref[:, :edge]
-    bands[1, edge : edge + 8, :edge] = columns_ref[:, rows - edge :]
-    writes = []
-    for k, out in enumerate((top_ref, bottom_ref)):
-        copies[k].wait()
-        writes += [pltpu.make_async_copy(bands.at[k], out, sems.at[2 + k])]
-        writes[k].start()
-    for copy in writes:
-        copy.wait()
+        sides.append(gram_of(pick, strips[k])[:2])
+    head, tail = sides
+    odd = lax.axis_index("pix") % 2 == 1
+    near_ref[...] = jnp.where(odd, head, tail).astype(jnp.bfloat16)
+    far_ref[...] = jnp.where(odd, tail, head).astype(jnp.bfloat16)
+
+
+def rows_kernel(images_ref, near_ref, far_ref, bands, sems):
+    rows, edge = images_ref.shape[0], near_ref.shape[0]
+    odd = lax.axis_index("ion") % 2
+    reads = fetch(
+        [images_ref.at[pl.ds(pl.multiple_of(k * (rows - edge), edge // REACH), edge)] for k in (1 - odd, odd)],
+        [bands.at[0], bands.at[1]],
+        sems,
+    )
+    writes = [
+        pltpu.make_async_copy(bands.at[k], out, sems.at[2 + k]) for k, out in enumerate((near_ref, far_ref))
+    ]
+    for read, write in zip(reads, writes):
+        read.wait()
+        write.start()
+    for write in writes:
+        write.wait()
 
 
 def halo_tile(columns_ref):
@@ -177,8 +182,8 @@
             copy_out(k).wait()
 
 
-def cross_kernel(blocks, block, pairs_ref, down_hbm, up_hbm, w_hbm, energy_hbm, smoothed_hbm, keep_hbm,
-                 give_hbm, keep_ref, give_ref, x_ref, columns_ref, w_ref, energy_ref, own, near, table, sems):
+def cross_kernel(blocks, block, pairs_ref, near_hbm, far_hbm, near_columns_hbm, far_columns_hbm, w_hbm, energy_hbm, smoothed_hbm, keep_hbm,
+                 give_hbm, keep_ref, give_ref, x_ref, columns_ref, w_ref, energy_ref, own, other, table, sems):
     core = lax.axis_index("pix") % 2
     first_block = lax.axis_index("ion") * blocks
     slots = pairs_ref.shape[1]
@@ -187,10 +192,12 @@
     edge = REACH * block
     rows = blocks * block
     low, high = pl.ds(0, edge), pl.ds(edge, edge)
+    odd = lax.axis_index("ion") % 2
+    near, far = (pl.ds(pl.multiple_of(k * edge, edge), edge) for k in (1 - odd, odd))
     copies = fetch(
-        (down_hbm.at[low], up_hbm.at[low], down_hbm.at[pl.ds(edge, EXTRA), low], up_hbm.at[pl.ds(edge, EXTRA), low], w_hbm,
-         energy_hbm, smoothed_hbm.at[low], smoothed_hbm.at[pl.ds(rows - edge, edge)], keep_hbm, give_hbm),
-        (x_ref.at[low], x_ref.at[high], columns_ref.at[:, low], columns_ref.at[:, high], w_ref, energy_ref, own.at[low],
+        (near_hbm, far_hbm, near_columns_hbm, far_columns_hbm, w_hbm, energy_hbm, smoothed_hbm.at[low],
+         smoothed_hbm.at[pl.ds(rows - edge, edge)], keep_hbm, give_hbm),
+        (x_ref.at[near], x_ref.at[far], columns_ref.at[:, near], columns_ref.at[:, far], w_ref, energy_ref, own.at[low],
          own.at[high], keep_ref, give_ref),
         sems,
     )
@@ -201,11 +208,11 @@
     total = [None]
 
     def store(j, values):
-        near[:, j * TILE : (j + 1) * TILE] = values.astype(jnp.bfloat16)
+        other[:, j * TILE : (j + 1) * TILE] = values.astype(jnp.bfloat16)
         squares = lane_pairs(values)
         total[0] = squares if j == 0 else total[0] + squares
 
-    smooth_rows(x_ref, halo_tile(columns_ref.at[:8]), w_ref, store)
+    smooth_rows(x_ref, halo_tile(columns_ref), w_ref, store)
     for k in range(2 * REACH):
         row = k if k < REACH else k + blocks
         table[row : row + 1, :] = row_sums(total[0][k * block : (k + 1) * block, :])
@@ -226,7 +233,7 @@
             side = (b >= 0).astype(jnp.int32)
             a_row = pl.multiple_of((a - side * (blocks - 2 * REACH)) * block, block)
             b_row = pl.multiple_of((b + REACH - side * blocks) * block, block)
-            gram = gram_of(own[pl.ds(a_row, block), :], near[pl.ds(b_row, block), :])
+            gram = gram_of(own[pl.ds(a_row, block), :], other[pl.ds(b_row, block), :])
             keep_ref[s], give_ref[s] = by_core(gram, chips, core)
 
         return carry
@@ -326,9 +333,11 @@
     core, chip = pix % 2, pix // 2
     edge = REACH * block
 
-    def shifted(axis, size, up, value):
-        steps = [(i, i + 1) if up else (i + 1, i) for i in range(size - 1)]
-        return lax.ppermute(value, axis, steps)
+    def swapped(axis, size, near, far):
+        pairs_of = [[(i, i + 1) for i in range(first, size - 1, 2)] for first in (0, 1)]
+        return [
+            lax.ppermute(value, axis, both + [(j, i) for i, j in both]) for value, both in zip((near, far), pairs_of)
+        ]
 
     vmem = pl.BlockSpec(memory_space=pltpu.VMEM)
     smem = pl.BlockSpec(memory_space=pltpu.SMEM)
@@ -337,15 +346,26 @@
 
     part = rules_here * block // n_pix
     mine = lax.dynamic_slice_in_dim(adduct.reshape(rules_here * block, block), pix * part, part, 0)
-
-    def turned(value, distance):
-        other = lax.ppermute(value, "ion", [(i, i ^ distance) for i in range(n_ion)])
-        return jnp.concatenate([value, other], axis=0)
-
-    mine = turned(mine, 1)
+    turns = [lax.ppermute(mine, "ion", [(i, i ^ d) for i in range(n_ion)]) for d in range(1, n_ion)]
+
+    edge_rows = jax.ShapeDtypeStruct((edge, width), images.dtype)
+    near, far = pl.pallas_call(
+        rows_kernel,
+        in_specs=[hbm],
+        out_specs=[hbm, hbm],
+        out_shape=[edge_rows, edge_rows],
+        scratch_shapes=[pltpu.VMEM((2, edge, width), images.dtype), pltpu.SemaphoreType.DMA((4,))],
+        compiler_params=params(),
+        cost_estimate=cost(0, 8 * edge * width),
+        name="edge_rows",
+    )(images)
+    near, far, *turns = lax.optimization_barrier((near, far, *turns))
+    near_rows, far_rows = swapped("ion", n_ion, near, far)
+    mine = jnp.concatenate([mine, *turns], axis=0)
 
     edge_columns = jax.ShapeDtypeStruct((2, rows), images.dtype)
-    head, tail, weights = pl.pallas_call(
+    images_later, near, far = lax.optimization_barrier((images, near, far))
+    near, far, weights = pl.pallas_call(
         columns_kernel,
         in_specs=[hbm, vmem],
         out_specs=[vmem, vmem, vmem],
@@ -358,28 +378,14 @@
         compiler_params=params(),
         cost_estimate=cost(0, 4 * rows * LANES),
         name="columns",
-    )(images, stencil)
-    head, tail, mine = lax.optimization_barrier((head, tail, mine))
-    before = shifted("pix", n_pix, True, tail)
-    after = shifted("pix", n_pix, False, head)
-    for k in range(1, n_ion.bit_length() - 1):
-        mine = turned(mine, 2**k)
+    )(images_later, stencil)
+    near, far = swapped("pix", n_pix, near, far)
+    odd = pix % 2 == 1
+    after, before = jnp.where(odd, far, near), jnp.where(odd, near, far)
     columns = jnp.concatenate([after, jnp.zeros((4, rows), images.dtype), before], axis=0)
-
-    message = jax.ShapeDtypeStruct((edge + EXTRA, width), images.dtype)
-    top, bottom = pl.pallas_call(
-        message_kernel,
-        in_specs=[hbm, vmem],
-        out_specs=[hbm, hbm],
-        out_shape=[message, message],
-        scratch_shapes=[pltpu.VMEM((2, edge + EXTRA, width), images.dtype), pltpu.SemaphoreType.DMA((4,))],
-        compiler_params=params(),
-        cost_estimate=cost(0, 8 * edge * width),
-        name="edge_messages",
-    )(images, columns)
-    top, bottom, mine = lax.optimization_barrier((top, bottom, mine))
-    down = shifted("ion", n_ion, True, bottom)
-    up = shifted("ion", n_ion, False, top)
+    first, last = columns[:, :edge], columns[:, rows - edge :]
+    odd = ion % 2 == 1
+    near_columns, far_columns = swapped("ion", n_ion, jnp.where(odd, first, last), jnp.where(odd, last, first))
 
     distances = [n_pix >> k for k in range(1, n_pix.bit_length())]
     for distance in distances:
@@ -436,12 +442,12 @@
 
     keep, give = pl.pallas_call(
         functools.partial(cross_kernel, blocks, block),
-        in_specs=[smem] + [hbm] * 2 + [fixed] * 5,
+        in_specs=[smem] + [hbm] * 4 + [fixed] * 5,
         out_specs=[vmem, vmem],
         out_shape=both_halves,
         scratch_shapes=[
             pltpu.VMEM((2 * edge, width), jnp.bfloat16),
-            pltpu.VMEM((EXTRA, 2 * edge), jnp.bfloat16),
+            pltpu.VMEM((8, 2 * edge), jnp.bfloat16),
             pltpu.VMEM(weights.shape, jnp.bfloat16),
             pltpu.VMEM((blocks, LANES), jnp.float32),
             pltpu.VMEM((2 * edge, width), jnp.bfloat16),
@@ -452,7 +458,7 @@
         compiler_params=params(),
         cost_estimate=cost(4 * edge * width * DEPTH, 8 * edge * width),
         name="cross_grams",
-    )(table_pairs, down, up, weights, energy, smoothed, keep, give)
+    )(table_pairs, near_rows, far_rows, near_columns, far_columns, weights, energy, smoothed, keep, give)
 
     got = lax.ppermute(give, "pix", [(i, i ^ 1) for i in range(n_pix)])
     message = jax.ShapeDtypeStruct((slots + 2 * units * chips, share, LANES), jnp.bfloat16)

time: 97.9 us -> 93 us (0.950)
  Pallas kernels: 52.3 us -> 49.6 us
  waiting for transfers between devices: 18 us -> 15.7 us
    ppermute x6 -> x9, waiting for transfers between devices: 6.45 us -> 1.83 us  [the longest x3 1.82 us: on_device(): lax.ppermute(mine, 'ion', [(i, i ^ d) for i in range(n_ion)])]
    ppermute x3, starting transfers between devices: 7.44 us -> 3.69 us  [on_device(): other = lax.ppermute(mine, 'pix', [(i, i ^ distance) for i in range(n_pix)])]
    ppermute x6 -> x9, starting transfers between devices: 11.7 us -> 15.2 us  [the longest x6 11.6 us: swapped(): lax.ppermute(value, axis, both + [(j, i) for i, j in both])]
    ppermute x3, waiting for transfers between devices: 0.42 us -> 3.31 us  [on_device(): other = lax.ppermute(mine, 'pix', [(i, i ^ distance) for i in range(n_pix)])]
    pallas_call x1, Pallas kernels: 9.92 us -> 8.12 us  [on_device(): pl.pallas_call(functools.partial(cross_kernel, blocks, block), in_specs=[...]
    unnamed x12 -> x21, local copies, waits for them, and re-layouts: 2.25 us -> 2.61 us
  transfers between devices with their start and end apart: 13 -> 16, of which waited for: 7 -> 6; matrix products, arithmetic and copies ran while one was open for 1% -> 0% of each run, Pallas kernels for 49% -> 49%
where the time goes in v7:
time: 93 us; the launch traced here: 92.4 us
  Pallas kernels  49.6 us (53%)
  starting transfers between devices  22.5 us (24%)
  waiting for transfers between devices  15.7 us (17%)
  local copies, waits for them, and re-layouts  2.84 us (3%)
  between operations  1.59 us (2%)
    pallas_call x1, Pallas kernels, on_device(): pl.pallas_call(functools.partial(main_kernel, steps, group, block), grid_...  29.2 us
    ppermute x6, starting transfers between devices, swapped(): lax.ppermute(value, axis, both + [(j, i) for i, j in both])  11.6 us
    ppermute x3, waiting for transfers between devices, on_device(): lax.ppermute(m, 'pix', [(i, i ^ 2 * (d + 1)) for i in range(n_pix)])  8.67 us
    pallas_call x1, Pallas kernels, on_device(): pl.pallas_call(functools.partial(cross_kernel, blocks, block), in_specs=[...  8.12 us
    pallas_call x1, Pallas kernels, on_device(): pl.pallas_call(functools.partial(score_kernel, blocks, place_of, pixel_co...  4.46 us
    pallas_call x1, Pallas kernels, on_device(): pl.pallas_call(columns_kernel, in_specs=[hbm, vmem], out_specs=[vmem, vme...  4.28 us
    ppermute x3, starting transfers between devices, on_device(): other = lax.ppermute(mine, 'pix', [(i, i ^ distance) for i in range(n_pix)])  3.69 us
    ppermute x3, starting transfers between devices, on_device(): lax.ppermute(m, 'pix', [(i, i ^ 2 * (d + 1)) for i in range(n_pix)])  3.55 us
  transfers between devices with their start and end apart: 16, of which 6 were waited for; matrix products, arithmetic and copies ran while one was open for 0% of the time, Pallas kernels for 49%

profile of v7, /device:TPU:8, one launch (start us, length us, event | category | flops | bytes accessed | tf_op | source)
XLA Modules:
  0.0 92.4 jit_solution(2075960577278201693)
XLA Ops:
  0.6 0.9 constant_dynamic-update-slice_fusion.4
  1.6 3.0 %collective-permute-start.1 = (bf16[256,128]{1,0:T(8,128)(2,1)S(1)}, bf16[256,128]{1,0:T(8,128)(2,1)S(1)}, u32[]{:S(2)}, u32[]{:S(2)}) collective-permute-start(bf16[256,128]{1,0:T(8,128)(2,1)S(1)} %get-tuple-element.45), channel_id=1, source_target_pairs={{0,2},{1,3},{2,0},{3,1},{4,6},{5,7},{6,4},{7,5},{8,10},{9,11},{10,... | collective-permute-start | bytes 196616 | tf_op jit(solution)/shard_map/ppermute | solution.py:349
  4.6 0.5 collective-permute-start.2
  5.1 3.1 %edge_rows.1 = (bf16[384,2048]{1,0:T(8,128)(2,1)}, bf16[384,2048]{1,0:T(8,128)(2,1)}) custom-call(bf16[5120,2048]{1,0:T(8,128)(2,1)} %x_ref.1), custom_call_target="tpu_custom_call" | custom-call | bytes 6291456 | tf_op jit(solution)/shard_map/edge_rows/pallas_call | solution.py:352
  8.2 0.1 pad.5.clone
  8.3 0.9 collective-permute-done.1
  9.2 0.9 collective-permute-done.2
  10.1 2.2 %collective-permute-start.5 = (bf16[384,2048]{1,0:T(8,128)(2,1)}, bf16[384,2048]{1,0:T(8,128)(2,1)S(1)}, u32[]{:S(2)}, u32[]{:S(2)}) collective-permute-start(bf16[384,2048]{1,0:T(8,128)(2,1)} %get-tuple-element.25), channel_id=1, source_target_pairs={{0,1},{2,3},{1,0},{3,2},{4,5},{6,7},{5,4},{7,6},{8,9},{10,11},{9,8... | collective-permute-start | bytes 4718600 | tf_op jit(solution)/shard_map/ppermute | solution.py:339
  12.3 2.8 %collective-permute-start.6 = (bf16[384,2048]{1,0:T(8,128)(2,1)}, bf16[384,2048]{1,0:T(8,128)(2,1)S(1)}, u32[]{:S(2)}, u32[]{:S(2)}) collective-permute-start(bf16[384,2048]{1,0:T(8,128)(2,1)} %get-tuple-element.26), channel_id=1, source_target_pairs={{1,2},{2,1},{5,6},{6,5},{9,10},{10,9},{13,14},{14,13},{17,18},{18,... | collective-permute-start | bytes 4718600 | tf_op jit(solution)/shard_map/ppermute | solution.py:339
  15.0 4.3 %columns.1 = (bf16[2,5120]{1,0:T(2,128)(2,1)}, bf16[2,5120]{1,0:T(2,128)(2,1)}, bf16[8,384,256]{2,1,0:T(8,128)(2,1)}) custom-call(bf16[5120,2048]{1,0:T(8,128)(2,1)} %x_ref.1, f32[5,2048]{1,0:T(8,128)} %stencil_ref.1), custom_call_target="tpu_custom_call" | custom-call | bytes 2621440 | tf_op jit(solution)/shard_map/columns/pallas_call | solution.py:368
  19.3 0.7 collective-permute-start.3
  20.0 2.9 %collective-permute-start.4 = (bf16[2,5120]{1,0:T(2,128)(2,1)}, bf16[2,5120]{1,0:T(2,128)(2,1)S(1)}, u32[]{:S(2)}, u32[]{:S(2)}) collective-permute-start(bf16[2,5120]{1,0:T(2,128)(2,1)} %get-tuple-element.29), channel_id=1, source_target_pairs={{0,4},{8,12},{16,20},{24,28},{4,0},{12,8},{20,16},{28,24},{1,5},{9... | collective-permute-start | bytes 61448 | tf_op jit(solution)/shard_map/ppermute | solution.py:339
  22.9 1.6 %collective-permute-start.13 = (bf16[1024,128]{1,0:T(8,128)(2,1)S(1)}, bf16[1024,128]{1,0:T(8,128)(2,1)S(1)}, u32[]{:S(2)}, u32[]{:S(2)}) collective-permute-start(bf16[1024,128]{1,0:T(8,128)(2,1)S(1)} %pad_maximum_fusion), channel_id=1, source_target_pairs={{0,16},{4,20},{8,24},{12,28},{16,0},{20,4},{24,8},{28,12},{1,17},{... | collective-permute-start | bytes 786440 | tf_op jit(solution)/shard_map/ppermute | solution.py:392
  24.7 0.1 pad_maximum_fusion.1.columns_ref
  24.9 3.1 %collective-permute-start.8 = (bf16[8,384]{1,0:T(8,128)(2,1)S(1)}, bf16[8,384]{1,0:T(8,128)(2,1)S(1)}, u32[]{:S(2)}, u32[]{:S(2)}) collective-permute-start(bf16[8,384]{1,0:T(8,128)(2,1)S(1)} %get-tuple-element.48), channel_id=1, source_target_pairs={{1,2},{2,1},{5,6},{6,5},{9,10},{10,9},{13,14},{14,13},{17,18},{18,... | collective-permute-start | bytes 18440 | tf_op jit(solution)/shard_map/ppermute | solution.py:339
  27.9 3.3 %collective-permute-done.13 = bf16[1024,128]{1,0:T(8,128)(2,1)S(1)} collective-permute-done((bf16[1024,128]{1,0:T(8,128)(2,1)S(1)}, bf16[1024,128]{1,0:T(8,128)(2,1)S(1)}, u32[]{:S(2)}, u32[]{:S(2)}) %collective-permute-start.13) | collective-permute-done | bytes 262176 | tf_op jit(solution)/shard_map/ppermute | solution.py:392
  31.2 0.1 constant_dynamic-update-slice_fusion
  31.3 1.6 %collective-permute-start.14 = (bf16[2048,128]{1,0:T(8,128)(2,1)S(1)}, bf16[2048,128]{1,0:T(8,128)(2,1)S(1)}, u32[]{:S(2)}, u32[]{:S(2)}) collective-permute-start(bf16[2048,128]{1,0:T(8,128)(2,1)S(1)} %get-tuple-element.46), channel_id=1, source_target_pairs={{0,8},{4,12},{8,0},{12,4},{16,24},{20,28},{24,16},{28,20},{1,9},{5... | collective-permute-start | bytes 1572872 | tf_op jit(solution)/shard_map/ppermute | solution.py:392
  32.9 29.2 %smooth_and_gram.1 = (bf16[40,128,2048]{2,1,0:T(8,128)(2,1)}, f32[40,128]{1,0:T(8,128)}, bf16[50,4,16,128]{3,2,1,0:T(8,128)(2,1)}, bf16[50,4,16,128]{3,2,1,0:T(8,128)(2,1)}) custom-call(s32[2,48]{1,0:T(2,128)} %bitcast.3, bf16[5120,2048]{1,0:T(8,128)(2,1)} %x_ref.1, bf16[8,5120]{1,0:T(8,128)(2,1)} %copy-done.5, ...), custom_call_target="tpu_custom_call" | custom-call | flops 11274289152 | bytes 41943040 | tf_op jit(solution)/shard_map/smooth_and_gram/pallas_call | solution.py:419
  62.2 0.5 copy-done.6
  62.7 0.6 copy-done.3
  63.3 0.5 copy-done.4
  63.8 8.1 %cross_grams.1 = (bf16[50,4,16,128]{3,2,1,0:T(8,128)(2,1)}, bf16[50,4,16,128]{3,2,1,0:T(8,128)(2,1)}) custom-call(s32[2,48]{1,0:T(2,128)} %bitcast.4, bf16[384,2048]{1,0:T(8,128)(2,1)} %copy-done.3, bf16[384,2048]{1,0:T(8,128)(2,1)} %copy-done.4, bf16[8,384]{1,0:T(8,128)(2,1)} %copy-done.6, bf16[8,384]{1,0:T(8,128)(2,1)} %copy-done.7, ...), custom_call_target="tpu_custom_call" | custom-call | flops 1207959552 | bytes 6291456 | tf_op jit(solution)/shard_map/cross_grams/pallas_call | solution.py:443
  72.1 0.6 collective-permute-start.15
  72.7 1.9 %collective-permute-done.9.got_hbm = bf16[50,4,16,128]{3,2,1,0:T(8,128)(2,1)S(1)} collective-permute-done((bf16[50,4,16,128]{3,2,1,0:T(8,128)(2,1)}, bf16[50,4,16,128]{3,2,1,0:T(8,128)(2,1)S(1)}, u32[]{:S(2)}, u32[]{:S(2)}) %collective-permute-start.9) | collective-permute-done | bytes 819232 | tf_op jit(solution)/shard_map/ppermute | solution.py:463
  74.6 0.4 chip_sums.1
  75.0 0.6 collective-permute-start.10
  75.6 1.5 %collective-permute-start.11 = (bf16[56,16,128]{2,1,0:T(8,128)(2,1)S(1)}, bf16[56,16,128]{2,1,0:T(8,128)(2,1)S(1)}, u32[]{:S(2)}, u32[]{:S(2)}) collective-permute-start(bf16[56,16,128]{2,1,0:T(8,128)(2,1)S(1)} %get-tuple-element.39), channel_id=1, source_target_pairs={{0,16},{4,20},{8,24},{12,28},{16,0},{20,4},{24,8},{28,12},{1,17},{... | collective-permute-start | bytes 688136 | tf_op jit(solution)/shard_map/ppermute | solution.py:481
  77.1 1.4 %collective-permute-start.12 = (bf16[56,16,128]{2,1,0:T(8,128)(2,1)S(1)}, bf16[56,16,128]{2,1,0:T(8,128)(2,1)S(1)}, u32[]{:S(2)}, u32[]{:S(2)}) collective-permute-start(bf16[56,16,128]{2,1,0:T(8,128)(2,1)S(1)} %get-tuple-element.40), channel_id=1, source_target_pairs={{0,24},{4,28},{8,16},{12,20},{16,8},{20,12},{24,0},{28,4},{1,25},{... | collective-permute-start | bytes 688136 | tf_op jit(solution)/shard_map/ppermute | solution.py:481
  79.2 4.3 %collective-permute-done.10.refs_1_ = bf16[56,16,128]{2,1,0:T(8,128)(2,1)S(1)} collective-permute-done((bf16[56,16,128]{2,1,0:T(8,128)(2,1)S(1)}, bf16[56,16,128]{2,1,0:T(8,128)(2,1)S(1)}, u32[]{:S(2)}, u32[]{:S(2)}) %collective-permute-start.10) | collective-permute-done | bytes 229408 | tf_op jit(solution)/shard_map/ppermute | solution.py:481
  83.5 4.4 %collective-permute-done.11.refs_2_ = bf16[56,16,128]{2,1,0:T(8,128)(2,1)S(1)} collective-permute-done((bf16[56,16,128]{2,1,0:T(8,128)(2,1)S(1)}, bf16[56,16,128]{2,1,0:T(8,128)(2,1)S(1)}, u32[]{:S(2)}, u32[]{:S(2)}) %collective-permute-start.11) | collective-permute-done | bytes 229408 | tf_op jit(solution)/shard_map/ppermute | solution.py:481
  87.9 4.5 %scores.1 = bf16[48,16,128]{2,1,0:T(8,128)(2,1)} custom-call(s32[2,48]{1,0:T(2,128)S(1)} %bitcast.5, s32[1]{0:T(128)S(6)} %copy.17.live_ref, s32[160]{0:T(256)S(1)} %copy-done.2, f32[52,16,128]{2,1,0:T(8,128)S(1)} %get-tuple-element.37.refs_0_, bf16[56,16,128]{2,1,0:T(8,128)(2,1)S(1)} %collective-permute-done.10.refs_1_, ...), custom_call_target="tpu_custom_call" | custom-call | tf_op jit(solution)/shard_map/scores/pallas_call | solution.py:484
  (35 shorter events, 0.5 us)
Async XLA Ops:
  1.5 6.8 %collective-permute-start = (bf16[256,128]{1,0:T(8,128)(2,1)S(1)}, bf16[256,128]{1,0:T(8,128)(2,1)S(1)}, u32[]{:S(2)}, u32[]{:S(2)}) collective-permute-start(bf16[256,128]{1,0:T(8,128)(2,1)S(1)} %get-tuple-element.45), channel_id=1, source_target_pairs={{0,1},{1,0},{2,3},{3,2},{4,5},{5,4},{6,7},{7,6},{8,9},{9,8},{10,11... | collective-permute-start | bytes 196616 | tf_op jit(solution)/shard_map/ppermute | solution.py:349
  1.6 7.6 %collective-permute-start.1 = (bf16[256,128]{1,0:T(8,128)(2,1)S(1)}, bf16[256,128]{1,0:T(8,128)(2,1)S(1)}, u32[]{:S(2)}, u32[]{:S(2)}) collective-permute-start(bf16[256,128]{1,0:T(8,128)(2,1)S(1)} %get-tuple-element.45), channel_id=1, source_target_pairs={{0,2},{1,3},{2,0},{3,1},{4,6},{5,7},{6,4},{7,5},{8,10},{9,11},{10,... | collective-permute-start | bytes 196616 | tf_op jit(solution)/shard_map/ppermute | solution.py:349
  4.6 5.5 %collective-permute-start.2 = (bf16[256,128]{1,0:T(8,128)(2,1)S(1)}, bf16[256,128]{1,0:T(8,128)(2,1)S(1)}, u32[]{:S(2)}, u32[]{:S(2)}) collective-permute-start(bf16[256,128]{1,0:T(8,128)(2,1)S(1)} %get-tuple-element.45), channel_id=1, source_target_pairs={{0,3},{1,2},{2,1},{3,0},{4,7},{5,6},{6,5},{7,4},{8,11},{9,10},{10,... | collective-permute-start | bytes 196616 | tf_op jit(solution)/shard_map/ppermute | solution.py:349
  10.1 52.0 %collective-permute-start.5 = (bf16[384,2048]{1,0:T(8,128)(2,1)}, bf16[384,2048]{1,0:T(8,128)(2,1)S(1)}, u32[]{:S(2)}, u32[]{:S(2)}) collective-permute-start(bf16[384,2048]{1,0:T(8,128)(2,1)} %get-tuple-element.25), channel_id=1, source_target_pairs={{0,1},{2,3},{1,0},{3,2},{4,5},{6,7},{5,4},{7,6},{8,9},{10,11},{9,8... | collective-permute-start | bytes 4718600 | tf_op jit(solution)/shard_map/ppermute | solution.py:339
  12.3 49.9 %collective-permute-start.6 = (bf16[384,2048]{1,0:T(8,128)(2,1)}, bf16[384,2048]{1,0:T(8,128)(2,1)S(1)}, u32[]{:S(2)}, u32[]{:S(2)}) collective-permute-start(bf16[384,2048]{1,0:T(8,128)(2,1)} %get-tuple-element.26), channel_id=1, source_target_pairs={{1,2},{2,1},{5,6},{6,5},{9,10},{10,9},{13,14},{14,13},{17,18},{18,... | collective-permute-start | bytes 4718600 | tf_op jit(solution)/shard_map/ppermute | solution.py:339
  19.3 5.3 %collective-permute-start.3 = (bf16[2,5120]{1,0:T(2,128)(2,1)}, bf16[2,5120]{1,0:T(2,128)(2,1)S(1)}, u32[]{:S(2)}, u32[]{:S(2)}) collective-permute-start(bf16[2,5120]{1,0:T(2,128)(2,1)} %get-tuple-element.28), channel_id=1, source_target_pairs={{4,8},{12,16},{20,24},{8,4},{16,12},{24,20},{5,9},{13,17},{21,25},... | collective-permute-start | bytes 61448 | tf_op jit(solution)/shard_map/ppermute | solution.py:339
  20.0 4.6 %collective-permute-start.4 = (bf16[2,5120]{1,0:T(2,128)(2,1)}, bf16[2,5120]{1,0:T(2,128)(2,1)S(1)}, u32[]{:S(2)}, u32[]{:S(2)}) collective-permute-start(bf16[2,5120]{1,0:T(2,128)(2,1)} %get-tuple-element.29), channel_id=1, source_target_pairs={{0,4},{8,12},{16,20},{24,28},{4,0},{12,8},{20,16},{28,24},{1,5},{9... | collective-permute-start | bytes 61448 | tf_op jit(solution)/shard_map/ppermute | solution.py:339
  22.9 8.3 %collective-permute-start.13 = (bf16[1024,128]{1,0:T(8,128)(2,1)S(1)}, bf16[1024,128]{1,0:T(8,128)(2,1)S(1)}, u32[]{:S(2)}, u32[]{:S(2)}) collective-permute-start(bf16[1024,128]{1,0:T(8,128)(2,1)S(1)} %pad_maximum_fusion), channel_id=1, source_target_pairs={{0,16},{4,20},{8,24},{12,28},{16,0},{20,4},{24,8},{28,12},{1,17},{... | collective-permute-start | bytes 786440 | tf_op jit(solution)/shard_map/ppermute | solution.py:392
  24.8 8.1 %copy-start.5 = (bf16[8,5120]{1,0:T(8,128)(2,1)}, bf16[8,5120]{1,0:T(8,128)(2,1)S(1)}, u32[]{:S(2)}) copy-start(bf16[8,5120]{1,0:T(8,128)(2,1)S(1)} %pad_maximum_fusion.1.columns_ref) | copy-start | bytes 245764
  24.8 37.3 %collective-permute-start.7 = (bf16[8,384]{1,0:T(8,128)(2,1)S(1)}, bf16[8,384]{1,0:T(8,128)(2,1)S(1)}, u32[]{:S(2)}, u32[]{:S(2)}) collective-permute-start(bf16[8,384]{1,0:T(8,128)(2,1)S(1)} %get-tuple-element.49), channel_id=1, source_target_pairs={{0,1},{2,3},{1,0},{3,2},{4,5},{6,7},{5,4},{7,6},{8,9},{10,11},{9,8... | collective-permute-start | bytes 18440 | tf_op jit(solution)/shard_map/ppermute | solution.py:339
  24.9 37.2 %collective-permute-start.8 = (bf16[8,384]{1,0:T(8,128)(2,1)S(1)}, bf16[8,384]{1,0:T(8,128)(2,1)S(1)}, u32[]{:S(2)}, u32[]{:S(2)}) collective-permute-start(bf16[8,384]{1,0:T(8,128)(2,1)S(1)} %get-tuple-element.48), channel_id=1, source_target_pairs={{1,2},{2,1},{5,6},{6,5},{9,10},{10,9},{13,14},{14,13},{17,18},{18,... | collective-permute-start | bytes 18440 | tf_op jit(solution)/shard_map/ppermute | solution.py:339
  31.3 40.7 %collective-permute-start.14 = (bf16[2048,128]{1,0:T(8,128)(2,1)S(1)}, bf16[2048,128]{1,0:T(8,128)(2,1)S(1)}, u32[]{:S(2)}, u32[]{:S(2)}) collective-permute-start(bf16[2048,128]{1,0:T(8,128)(2,1)S(1)} %get-tuple-element.46), channel_id=1, source_target_pairs={{0,8},{4,12},{8,0},{12,4},{16,24},{20,28},{24,16},{28,20},{1,9},{5... | collective-permute-start | bytes 1572872 | tf_op jit(solution)/shard_map/ppermute | solution.py:392
  62.1 0.6 copy-start.6
  62.1 0.6 copy-start.7
  62.1 1.1 %copy-start.3 = (bf16[384,2048]{1,0:T(8,128)(2,1)}, bf16[384,2048]{1,0:T(8,128)(2,1)S(1)}, u32[]{:S(2)}) copy-start(bf16[384,2048]{1,0:T(8,128)(2,1)S(1)} %collective-permute-done.5.near_hbm) | copy-start | bytes 4718596
  62.1 1.6 %copy-start.4 = (bf16[384,2048]{1,0:T(8,128)(2,1)}, bf16[384,2048]{1,0:T(8,128)(2,1)S(1)}, u32[]{:S(2)}) copy-start(bf16[384,2048]{1,0:T(8,128)(2,1)S(1)} %collective-permute-done.6.far_hbm) | copy-start | bytes 4718596
  71.9 2.6 %copy-start = (bf16[50,4,16,128]{3,2,1,0:T(8,128)(2,1)S(1)}, bf16[50,4,16,128]{3,2,1,0:T(8,128)(2,1)}, u32[]{:S(2)}) copy-start(bf16[50,4,16,128]{3,2,1,0:T(8,128)(2,1)} %get-tuple-element.35.keep_hbm) | copy-start | bytes 2457604
  71.9 16.0 %copy-start.1 = (s32[48,2]{0,1:T(2,128)S(1)}, s32[48,2]{0,1:T(2,128)}, u32[]{:S(2)}) copy-start(s32[48,2]{0,1:T(2,128)} %param.8) | copy-start | bytes 1156
  71.9 15.9 %copy-start.2 = (s32[160]{0:T(256)S(1)}, s32[160]{0:T(256)}, u32[]{:S(2)}) copy-start(s32[160]{0:T(256)} %rules_ref.1) | copy-start | bytes 1924
  72.0 2.6 %collective-permute-start.9 = (bf16[50,4,16,128]{3,2,1,0:T(8,128)(2,1)}, bf16[50,4,16,128]{3,2,1,0:T(8,128)(2,1)S(1)}, u32[]{:S(2)}, u32[]{:S(2)}) collective-permute-start(bf16[50,4,16,128]{3,2,1,0:T(8,128)(2,1)} %get-tuple-element.36), channel_id=1, source_target_pairs={{0,4},{4,0},{8,12},{12,8},{16,20},{20,16},{24,28},{28,24},{1,5},{5... | collective-permute-start | bytes 2457608 | tf_op jit(solution)/shard_map/ppermute | solution.py:463
  72.1 7.1 %collective-permute-start.15 = (bf16[4096,128]{1,0:T(8,128)(2,1)S(1)}, bf16[4096,128]{1,0:T(8,128)(2,1)S(1)}, u32[]{:S(2)}, u32[]{:S(2)}) collective-permute-start(bf16[4096,128]{1,0:T(8,128)(2,1)S(1)} %constant_dynamic-update-slice_fusion.5.refs_4_), channel_id=1, source_target_pairs={{0,4},{4,0},{8,12},{12,8},{16,20},{20,16},{24,28},{28,24},{1,5},{5... | collective-permute-start | bytes 3145736 | tf_op jit(solution)/shard_map/ppermute | solution.py:392
  75.0 8.5 %collective-permute-start.10 = (bf16[56,16,128]{2,1,0:T(8,128)(2,1)S(1)}, bf16[56,16,128]{2,1,0:T(8,128)(2,1)S(1)}, u32[]{:S(2)}, u32[]{:S(2)}) collective-permute-start(bf16[56,16,128]{2,1,0:T(8,128)(2,1)S(1)} %get-tuple-element.38), channel_id=1, source_target_pairs={{0,8},{4,12},{8,0},{12,4},{16,24},{20,28},{24,16},{28,20},{1,9},{5... | collective-permute-start | bytes 688136 | tf_op jit(solution)/shard_map/ppermute | solution.py:481
  75.6 12.3 %collective-permute-start.11 = (bf16[56,16,128]{2,1,0:T(8,128)(2,1)S(1)}, bf16[56,16,128]{2,1,0:T(8,128)(2,1)S(1)}, u32[]{:S(2)}, u32[]{:S(2)}) collective-permute-start(bf16[56,16,128]{2,1,0:T(8,128)(2,1)S(1)} %get-tuple-element.39), channel_id=1, source_target_pairs={{0,16},{4,20},{8,24},{12,28},{16,0},{20,4},{24,8},{28,12},{1,17},{... | collective-permute-start | bytes 688136 | tf_op jit(solution)/shard_map/ppermute | solution.py:481
  77.1 10.8 %collective-permute-start.12 = (bf16[56,16,128]{2,1,0:T(8,128)(2,1)S(1)}, bf16[56,16,128]{2,1,0:T(8,128)(2,1)S(1)}, u32[]{:S(2)}, u32[]{:S(2)}) collective-permute-start(bf16[56,16,128]{2,1,0:T(8,128)(2,1)S(1)} %get-tuple-element.40), channel_id=1, source_target_pairs={{0,24},{4,28},{8,16},{12,20},{16,8},{20,12},{24,0},{28,4},{1,25},{... | collective-permute-start | bytes 688136 | tf_op jit(solution)/shard_map/ppermute | solution.py:481

commit v8 on v7

--- a/solution.py
+++ b/solution.py
@@ -35,31 +35,28 @@
     return copies
 
 
-def split(values):
-    high = values.astype(jnp.bfloat16)
-    return high, (values - high.astype(jnp.float32)).astype(jnp.bfloat16)
-
-
 def smooth_rows(x_ref, halo, w_ref, store):
     rows, width = x_ref.shape
     tiles = width // TILE
     first = lax.broadcasted_iota(jnp.int32, (rows, LANES), 1) < HALF
-    last = None
-    for j in range(tiles):
+
+    def tile(j):
         own = x_ref[:, j * TILE : (j + 1) * TILE]
         before = halo if j == 0 else x_ref[:, j * TILE - LANES : j * TILE]
         after = halo if j == tiles - 1 else x_ref[:, (j + 1) * TILE : (j + 1) * TILE + LANES]
         window = jnp.concatenate([own, jnp.where(first, after, before)], axis=1)
-        values = jnp.dot(window, w_ref[j], preferred_element_type=jnp.float32)
-        if j > 0:
-            store(j - 1, last)
-        last = values
-    store(tiles - 1, last)
-
-
-def lane_pairs(values):
-    squares = values * values
-    return squares[:, :LANES] + squares[:, LANES:]
+        return jnp.dot(window, w_ref[j], preferred_element_type=jnp.float32)
+
+    total = None
+    for j in range(0, tiles, 2):
+        squares = None
+        for k, values in enumerate([tile(j), tile(j + 1)]):
+            store(j + k, values.astype(jnp.bfloat16))
+            values = values * values
+            values = values[:, :LANES] + values[:, LANES:]
+            squares = values if k == 0 else squares + values
+        total = squares if j == 0 else total + squares
+    return total
 
 
 def row_sums(part):
@@ -95,38 +92,35 @@
             out_ref[j, k0 : k0 + rows, n0 : n0 + LANES] = w.astype(jnp.bfloat16)
 
 
-def columns_kernel(images_ref, stencil_ref, near_ref, far_ref, w_ref, strips, sems):
-    width = images_ref.shape[1]
-    copies = fetch((images_ref.at[:, pl.ds(0, LANES)], images_ref.at[:, pl.ds(width - LANES, LANES)]),
-                   (strips.at[0], strips.at[1]), sems)
+def cut_kernel(images_ref, stencil_ref, near_rows, far_rows, near_columns, far_columns, w_ref, bands, strips, sems):
+    rows, width = images_ref.shape
+    edge = near_rows.shape[0]
+    odd = lax.axis_index("ion") % 2
+    starts = [pl.multiple_of(k * (rows - edge), edge // REACH) for k in (1 - odd, odd)]
+    reads = fetch(
+        [images_ref.at[pl.ds(start, edge)] for start in starts]
+        + [images_ref.at[:, pl.ds(start, LANES)] for start in (0, width - LANES)],
+        [bands.at[0], bands.at[1], strips.at[0], strips.at[1]],
+        sems,
+    )
+    writes = [
+        pltpu.make_async_copy(bands.at[k], out, sems.at[4 + k]) for k, out in enumerate((near_rows, far_rows))
+    ]
     write_weights(stencil_ref, w_ref)
+    for read, write in zip(reads, writes):
+        read.wait()
+        write.start()
     row = lax.broadcasted_iota(jnp.int32, (8, LANES), 0)
     lane = lax.broadcasted_iota(jnp.int32, (8, LANES), 1)
     sides = []
     for k, shift in enumerate((0, LANES - 2)):
-        copies[k].wait()
+        reads[2 + k].wait()
         pick = (lane == row + shift).astype(jnp.bfloat16)
         sides.append(gram_of(pick, strips[k])[:2])
     head, tail = sides
     odd = lax.axis_index("pix") % 2 == 1
-    near_ref[...] = jnp.where(odd, head, tail).astype(jnp.bfloat16)
-    far_ref[...] = jnp.where(odd, tail, head).astype(jnp.bfloat16)
-
-
-def rows_kernel(images_ref, near_ref, far_ref, bands, sems):
-    rows, edge = images_ref.shape[0], near_ref.shape[0]
-    odd = lax.axis_index("ion") % 2
-    reads = fetch(
-        [images_ref.at[pl.ds(pl.multiple_of(k * (rows - edge), edge // REACH), edge)] for k in (1 - odd, odd)],
-        [bands.at[0], bands.at[1]],
-        sems,
-    )
-    writes = [
-        pltpu.make_async_copy(bands.at[k], out, sems.at[2 + k]) for k, out in enumerate((near_ref, far_ref))
-    ]
-    for read, write in zip(reads, writes):
-        read.wait()
-        write.start()
+    near_columns[...] = jnp.where(odd, head, tail).astype(jnp.bfloat16)
+    far_columns[...] = jnp.where(odd, tail, head).astype(jnp.bfloat16)
     for write in writes:
         write.wait()
 
@@ -152,19 +146,13 @@
 
     @pl.when(step < steps)
     def smooth():
-        total = [None]
-
         def store(j, values):
-            columns = slice(j * TILE, (j + 1) * TILE)
-            rounded = values.astype(jnp.bfloat16).reshape(group, block, TILE)
-            held[pl.ds(step * group, group), :, columns] = rounded
-            squares = lane_pairs(values)
-            total[0] = squares if j == 0 else total[0] + squares
-
-        smooth_rows(x_ref, halo_tile(columns_ref), w_ref, store)
+            held[pl.ds(step * group, group), :, j * TILE : (j + 1) * TILE] = values.reshape(group, block, TILE)
+
+        total = smooth_rows(x_ref, halo_tile(columns_ref), w_ref, store)
         copy_out(step).start()
         for g in range(group):
-            energy_ref[pl.ds(step * group + g, 1), :] = row_sums(total[0][g * block : (g + 1) * block, :])
+            energy_ref[pl.ds(step * group + g, 1), :] = row_sums(total[g * block : (g + 1) * block, :])
 
     @pl.when(step == steps)
     def grams():
@@ -188,7 +176,7 @@
     first_block = lax.axis_index("ion") * blocks
     slots = pairs_ref.shape[1]
     chips, share = keep_ref.shape[1:3]
-    units = (keep_ref.shape[0] - slots) // 2
+    units = keep_ref.shape[0] - slots
     edge = REACH * block
     rows = blocks * block
     low, high = pl.ds(0, edge), pl.ds(edge, edge)
@@ -205,25 +193,19 @@
         copy.wait()
     table[...] = jnp.zeros_like(table)
     table[REACH : REACH + blocks, :] = energy_ref[...]
-    total = [None]
-
     def store(j, values):
-        other[:, j * TILE : (j + 1) * TILE] = values.astype(jnp.bfloat16)
-        squares = lane_pairs(values)
-        total[0] = squares if j == 0 else total[0] + squares
-
-    smooth_rows(x_ref, halo_tile(columns_ref), w_ref, store)
+        other[:, j * TILE : (j + 1) * TILE] = values
+
+    total = smooth_rows(x_ref, halo_tile(columns_ref), w_ref, store)
     for k in range(2 * REACH):
         row = k if k < REACH else k + blocks
-        table[row : row + 1, :] = row_sums(total[0][k * block : (k + 1) * block, :])
+        table[row : row + 1, :] = row_sums(total[k * block : (k + 1) * block, :])
     for copy in copies[6:]:
         copy.wait()
 
     shape = (units, chips, share, LANES)
-    upper, lower = split(table[...].reshape(shape))
     for ref in (keep_ref, give_ref):
-        ref[slots : slots + units] = upper
-        ref[slots + units :] = lower
+        ref[slots:] = table[...].reshape(shape).astype(jnp.bfloat16)
 
     def one(s, carry):
         a, b = pairs_ref[0, s] - first_block, pairs_ref[1, s] - first_block
@@ -248,22 +230,16 @@
     shape = (units * chips, share, LANES)
     for copy in fetch((keep_hbm, got_hbm), (keep_ref, got_ref), sems):
         copy.wait()
-    energies = 0.0
-    for ref in (keep_ref, got_ref):
-        energies = energies + (
-            ref[slots : slots + units].astype(jnp.float32) + ref[slots + units :].astype(jnp.float32)
-        )
-    high, low = split(energies)
+    energies = (keep_ref[slots:].astype(jnp.float32) + got_ref[slots:].astype(jnp.float32)).reshape(shape)
     for d in range(chips):
         total = keep_ref[:slots, chip ^ d].astype(jnp.float32) + got_ref[:slots, chip ^ d].astype(jnp.float32)
         if d == 0:
             own_ref[:slots] = total
-            own_ref[slots:] = energies.reshape(shape)
+            own_ref[slots:] = energies
         else:
             out = out_refs[d - 1]
             out[:slots] = total.astype(jnp.bfloat16)
-            out[slots : slots + units * chips] = high.reshape(shape)
-            out[slots + units * chips :] = low.reshape(shape)
+            out[slots:] = energies.astype(jnp.bfloat16)
 
 
 def score_kernel(blocks, place_of, pixel_count, pairs_ref, live_ref, rules_ref, *refs):
@@ -271,7 +247,6 @@
     sources, out_ref, own_ref = refs[: chips + 2], refs[chips + 2], refs[chips + 3]
     got_refs, (table_ref, inverse, left, right, coloc, place, sems) = refs[chips + 4 : -7], refs[-7:]
     slots, share, block = out_ref.shape
-    e_units = inverse.shape[0] // share
     half = table_ref.shape[0] // 2
     targets = (own_ref, *got_refs, table_ref.at[pl.ds(0, half)], table_ref.at[pl.ds(half, half)])
     copies = fetch(sources, targets, sems)
@@ -291,9 +266,7 @@
     energies = own_ref[slots:]
     for got in got_refs:
         gram = gram + got[:slots].astype(jnp.float32)
-        energies = energies + (
-            got[slots : slots + e_units].astype(jnp.float32) + got[slots + e_units :].astype(jnp.float32)
-        )
+        energies = energies + got[slots:].astype(jnp.float32)
     inverse[...] = (1.0 / jnp.sqrt(energies / pixel_count + 1e-06)).reshape(inverse.shape)
 
     def pick(s, carry):
@@ -349,49 +322,41 @@
     turns = [lax.ppermute(mine, "ion", [(i, i ^ d) for i in range(n_ion)]) for d in range(1, n_ion)]
 
     edge_rows = jax.ShapeDtypeStruct((edge, width), images.dtype)
-    near, far = pl.pallas_call(
-        rows_kernel,
-        in_specs=[hbm],
-        out_specs=[hbm, hbm],
-        out_shape=[edge_rows, edge_rows],
-        scratch_shapes=[pltpu.VMEM((2, edge, width), images.dtype), pltpu.SemaphoreType.DMA((4,))],
-        compiler_params=params(),
-        cost_estimate=cost(0, 8 * edge * width),
-        name="edge_rows",
-    )(images)
-    near, far, *turns = lax.optimization_barrier((near, far, *turns))
-    near_rows, far_rows = swapped("ion", n_ion, near, far)
-    mine = jnp.concatenate([mine, *turns], axis=0)
-
     edge_columns = jax.ShapeDtypeStruct((2, rows), images.dtype)
-    images_later, near, far = lax.optimization_barrier((images, near, far))
-    near, far, weights = pl.pallas_call(
-        columns_kernel,
+    near_rows, far_rows, near, far, weights = pl.pallas_call(
+        cut_kernel,
         in_specs=[hbm, vmem],
-        out_specs=[vmem, vmem, vmem],
+        out_specs=[hbm, hbm, vmem, vmem, vmem],
         out_shape=[
+            edge_rows,
+            edge_rows,
             edge_columns,
             edge_columns,
             jax.ShapeDtypeStruct((width // TILE, DEPTH, TILE), jnp.bfloat16),
         ],
-        scratch_shapes=[pltpu.VMEM((2, rows, LANES), images.dtype), pltpu.SemaphoreType.DMA((2,))],
+        scratch_shapes=[
+            pltpu.VMEM((2, edge, width), images.dtype),
+            pltpu.VMEM((2, rows, LANES), images.dtype),
+            pltpu.SemaphoreType.DMA((6,)),
+        ],
         compiler_params=params(),
-        cost_estimate=cost(0, 4 * rows * LANES),
-        name="columns",
-    )(images_later, stencil)
+        cost_estimate=cost(0, 8 * edge * width),
+        name="cut_edges",
+    )(images, stencil)
+    near_rows, far_rows = swapped("ion", n_ion, near_rows, far_rows)
+    near, far, *turns = lax.optimization_barrier((near, far, *turns))
+    mine = jnp.concatenate([mine, *turns], axis=0)
     near, far = swapped("pix", n_pix, near, far)
     odd = pix % 2 == 1
     after, before = jnp.where(odd, far, near), jnp.where(odd, near, far)
     columns = jnp.concatenate([after, jnp.zeros((4, rows), images.dtype), before], axis=0)
-    first, last = columns[:, :edge], columns[:, rows - edge :]
-    odd = ion % 2 == 1
-    near_columns, far_columns = swapped("ion", n_ion, jnp.where(odd, first, last), jnp.where(odd, last, first))
 
     distances = [n_pix >> k for k in range(1, n_pix.bit_length())]
-    for distance in distances:
-        other = lax.ppermute(mine, "pix", [(i, i ^ distance) for i in range(n_pix)])
-        if distance > 1:
-            mine = jnp.concatenate([mine, other], axis=0)
+
+    def exchange(value, distance):
+        return lax.ppermute(value, "pix", [(i, i ^ distance) for i in range(n_pix)])
+
+    mine = jnp.concatenate([mine, exchange(mine, distances[0])], axis=0)
 
     def place_of(rule):
         row = (rule & (rules_here - 1)) * block
@@ -410,7 +375,7 @@
     steps = blocks // group
     units = -(-2 * (blocks + 2 * REACH) // block)
     half = (chips, share, LANES)
-    half_shape = (slots + 2 * units, *half)
+    half_shape = (slots + units, *half)
     both_halves = [jax.ShapeDtypeStruct(half_shape, jnp.bfloat16)] * 2
 
     def rows_at(columns):
@@ -440,6 +405,13 @@
     )(table_pairs, images, columns, weights)
     smoothed = smoothed.reshape(rows, width)
 
+    energy, columns, mine = lax.optimization_barrier((energy, columns, mine))
+    first, last = columns[:, :edge], columns[:, rows - edge :]
+    odd = ion % 2 == 1
+    near_columns, far_columns = swapped("ion", n_ion, jnp.where(odd, first, last), jnp.where(odd, last, first))
+    for distance in distances[1:-1]:
+        mine = jnp.concatenate([mine, exchange(mine, distance)], axis=0)
+
     keep, give = pl.pallas_call(
         functools.partial(cross_kernel, blocks, block),
         in_specs=[smem] + [hbm] * 4 + [fixed] * 5,
@@ -461,7 +433,7 @@
     )(table_pairs, near_rows, far_rows, near_columns, far_columns, weights, energy, smoothed, keep, give)
 
     got = lax.ppermute(give, "pix", [(i, i ^ 1) for i in range(n_pix)])
-    message = jax.ShapeDtypeStruct((slots + 2 * units * chips, share, LANES), jnp.bfloat16)
+    message = jax.ShapeDtypeStruct((slots + units * chips, share, LANES), jnp.bfloat16)
     own_rows = jax.ShapeDtypeStruct((slots + units * chips, share, LANES), jnp.float32)
     small = pltpu.CompilerParams(vmem_limit_bytes=16 * 1024 * 1024)
     own, *messages = pl.pallas_call(
@@ -477,6 +449,8 @@
         compiler_params=small,
         name="chip_sums",
     )(keep, got)
+    own, mine = lax.optimization_barrier((own, mine))
+    other = exchange(mine, distances[-1])
     received = [
         lax.ppermute(m, "pix", [(i, i ^ (2 * (d + 1))) for i in range(n_pix)]) for d, m in enumerate(messages)
     ]

time: 93 us -> 93.5 us (level)
  local copies, waits for them, and re-layouts: 2.84 us -> 5.17 us
  starting transfers between devices: 22.5 us -> 20.4 us
  other arithmetic: 0.15 us -> 1.56 us
  Pallas kernels: 49.6 us -> 48.2 us
    ppermute x6, waiting for transfers between devices: 0.02 us -> 3.62 us  [swapped(): lax.ppermute(value, axis, both + [(j, i) for i, j in both])]
    ppermute x3, waiting for transfers between devices: 3.31 us -> 0.01 us  [exchange(): return lax.ppermute(value, 'pix', [(i, i ^ distance) for i in range(n_pix)])]
    unnamed x21 -> x20, local copies, waits for them, and re-layouts: 2.61 us -> 5.06 us
    ppermute x3, starting transfers between devices: 3.69 us -> 1.79 us  [exchange(): return lax.ppermute(value, 'pix', [(i, i ^ distance) for i in range(n_pix)])]
    ppermute x3, waiting for transfers between devices: 1.82 us -> 0.01 us  [on_device(): lax.ppermute(mine, 'ion', [(i, i ^ d) for i in range(n_ion)])]
    pallas_call x2 -> x1, Pallas kernels: 7.39 us -> 6.09 us  [on_device(): pl.pallas_call(cut_kernel, in_specs=[hbm, vmem], out_specs=[hbm, hbm, vme...]
    ppermute x3, waiting for transfers between devices: 8.67 us -> 9.67 us  [on_device(): lax.ppermute(m, 'pix', [(i, i ^ 2 * (d + 1)) for i in range(n_pix)])]
  transfers between devices with their start and end apart: 16 -> 16, of which waited for: 6 -> 5; matrix products, arithmetic and copies ran while one was open for 0% -> 4% of each run, Pallas kernels for 49% -> 47%
where the time goes in v8:
time: 93.5 us; the launch traced here: 92.7 us
  Pallas kernels  48.2 us (52%)
  starting transfers between devices  20.4 us (22%)
  waiting for transfers between devices  15.7 us (17%)
  local copies, waits for them, and re-layouts  5.17 us (6%)
  other arithmetic  1.56 us (2%)
  between operations  1.52 us (2%)
    pallas_call x1, Pallas kernels, on_device(): pl.pallas_call(functools.partial(main_kernel, steps, group, block), grid_...  29.3 us
    ppermute x6, starting transfers between devices, swapped(): lax.ppermute(value, axis, both + [(j, i) for i, j in both])  11 us
    ppermute x3, waiting for transfers between devices, on_device(): lax.ppermute(m, 'pix', [(i, i ^ 2 * (d + 1)) for i in range(n_pix)])  9.67 us
    pallas_call x1, Pallas kernels, on_device(): pl.pallas_call(functools.partial(cross_kernel, blocks, block), in_specs=[...  8.08 us
    pallas_call x1, Pallas kernels, on_device(): pl.pallas_call(cut_kernel, in_specs=[hbm, vmem], out_specs=[hbm, hbm, vme...  6.09 us
    unnamed x20, local copies, waits for them, and re-layouts  5.06 us
    pallas_call x1, Pallas kernels, on_device(): pl.pallas_call(functools.partial(score_kernel, blocks, place_of, pixel_co...  4.39 us
    ppermute x3, starting transfers between devices, on_device(): lax.ppermute(mine, 'ion', [(i, i ^ d) for i in range(n_ion)])  4.05 us
  transfers between devices with their start and end apart: 16, of which 5 were waited for; matrix products, arithmetic and copies ran while one was open for 4% of the time, Pallas kernels for 47%

profile of v8, /device:TPU:8, one launch (start us, length us, event | category | flops | bytes accessed | tf_op | source)
XLA Modules:
  0.0 92.7 jit_solution(11560980094503508013)
XLA Ops:
  0.6 1.5 %constant_dynamic-update-slice_fusion.4 = (bf16[2048,128]{1,0:T(8,128)(2,1)}, bf16[256,128]{1,0:T(8,128)(2,1)S(1)}) fusion(bf16[2048,128]{1,0:T(8,128)(2,1)} %bitcast.8, s32[]{:T(128)S(6)} %select_n.40), kind=kLoop, calls=%fused_computation.9 | loop fusion | bytes 196612
  2.1 1.6 %collective-permute-start.2 = (bf16[256,128]{1,0:T(8,128)(2,1)S(1)}, bf16[256,128]{1,0:T(8,128)(2,1)S(1)}, u32[]{:S(2)}, u32[]{:S(2)}) collective-permute-start(bf16[256,128]{1,0:T(8,128)(2,1)S(1)} %get-tuple-element.53), channel_id=1, source_target_pairs={{0,3},{1,2},{2,1},{3,0},{4,7},{5,6},{6,5},{7,4},{8,11},{9,10},{10,... | collective-permute-start | bytes 196616 | tf_op jit(solution)/shard_map/ppermute | solution.py:322
  3.7 1.0 %collective-permute-start.1 = (bf16[256,128]{1,0:T(8,128)(2,1)S(1)}, bf16[256,128]{1,0:T(8,128)(2,1)S(1)}, u32[]{:S(2)}, u32[]{:S(2)}) collective-permute-start(bf16[256,128]{1,0:T(8,128)(2,1)S(1)} %get-tuple-element.53), channel_id=1, source_target_pairs={{0,2},{1,3},{2,0},{3,1},{4,6},{5,7},{6,4},{7,5},{8,10},{9,11},{10,... | collective-permute-start | bytes 196616 | tf_op jit(solution)/shard_map/ppermute | solution.py:322
  4.7 1.5 %collective-permute-start = (bf16[256,128]{1,0:T(8,128)(2,1)S(1)}, bf16[256,128]{1,0:T(8,128)(2,1)S(1)}, u32[]{:S(2)}, u32[]{:S(2)}) collective-permute-start(bf16[256,128]{1,0:T(8,128)(2,1)S(1)} %get-tuple-element.53), channel_id=1, source_target_pairs={{0,1},{1,0},{2,3},{3,2},{4,5},{5,4},{6,7},{7,6},{8,9},{9,8},{10,11... | collective-permute-start | bytes 196616 | tf_op jit(solution)/shard_map/ppermute | solution.py:322
  6.2 6.1 %cut_edges.1 = (bf16[384,2048]{1,0:T(8,128)(2,1)}, bf16[384,2048]{1,0:T(8,128)(2,1)}, bf16[2,5120]{1,0:T(2,128)(2,1)}, bf16[2,5120]{1,0:T(2,128)(2,1)}, bf16[8,384,256]{2,1,0:T(8,128)(2,1)}) custom-call(bf16[5120,2048]{1,0:T(8,128)(2,1)} %x_ref.1, f32[5,2048]{1,0:T(8,128)} %stencil_ref.1), custom_call_target="tpu_custom_call" | custom-call | bytes 6291456 | tf_op jit(solution)/shard_map/cut_edges/pallas_call | solution.py:326
  12.3 0.6 collective-permute-start.5
  12.9 4.8 %collective-permute-start.6 = (bf16[384,2048]{1,0:T(8,128)(2,1)}, bf16[384,2048]{1,0:T(8,128)(2,1)S(1)}, u32[]{:S(2)}, u32[]{:S(2)}) collective-permute-start(bf16[384,2048]{1,0:T(8,128)(2,1)} %get-tuple-element.34), channel_id=1, source_target_pairs={{1,2},{2,1},{5,6},{6,5},{9,10},{10,9},{13,14},{14,13},{17,18},{18,... | collective-permute-start | bytes 4718600 | tf_op jit(solution)/shard_map/ppermute | solution.py:312
  17.9 0.7 collective-permute-start.3
  18.5 2.9 %collective-permute-start.4 = (bf16[2,5120]{1,0:T(2,128)(2,1)}, bf16[2,5120]{1,0:T(2,128)(2,1)S(1)}, u32[]{:S(2)}, u32[]{:S(2)}) collective-permute-start(bf16[2,5120]{1,0:T(2,128)(2,1)} %get-tuple-element.30), channel_id=1, source_target_pairs={{0,4},{8,12},{16,20},{24,28},{4,0},{12,8},{20,16},{28,24},{1,5},{9... | collective-permute-start | bytes 61448 | tf_op jit(solution)/shard_map/ppermute | solution.py:312
  21.4 0.6 constant_dynamic-update-slice_fusion.3
  22.1 0.6 constant_dynamic-update-slice_fusion.2
  22.7 0.6 constant_dynamic-update-slice_fusion.1
  23.4 1.5 %collective-permute-start.7 = (bf16[1024,128]{1,0:T(8,128)(2,1)S(1)}, bf16[1024,128]{1,0:T(8,128)(2,1)S(1)}, u32[]{:S(2)}, u32[]{:S(2)}) collective-permute-start(bf16[1024,128]{1,0:T(8,128)(2,1)S(1)} %pad_maximum_fusion.1), channel_id=1, source_target_pairs={{0,16},{4,20},{8,24},{12,28},{16,0},{20,4},{24,8},{28,12},{1,17},{... | collective-permute-start | bytes 786440 | tf_op jit(solution)/shard_map/ppermute | solution.py:357
  24.9 0.7 pad_maximum_fusion.2.columns_ref
  25.7 29.3 %smooth_and_gram.1 = (bf16[40,128,2048]{2,1,0:T(8,128)(2,1)}, f32[40,128]{1,0:T(8,128)}, bf16[49,4,16,128]{3,2,1,0:T(8,128)(2,1)}, bf16[49,4,16,128]{3,2,1,0:T(8,128)(2,1)}) custom-call(s32[2,48]{1,0:T(2,128)} %bitcast.3, bf16[5120,2048]{1,0:T(8,128)(2,1)} %x_ref.1, bf16[8,5120]{1,0:T(8,128)(2,1)} %pad_maximum_fusion.2.columns_ref, ...), custom_call_target="tpu_custom_call" | custom-call | flops 11274289152 | bytes 41943040 | tf_op jit(solution)/shard_map/smooth_and_gram/pallas_call | solution.py:384
  55.1 0.7 broadcast_select_fusion.2
  55.8 1.9 %collective-permute-start.9 = (bf16[8,384]{1,0:T(8,128)(2,1)S(1)}, bf16[8,384]{1,0:T(8,128)(2,1)S(1)}, u32[]{:S(2)}, u32[]{:S(2)}) collective-permute-start(bf16[8,384]{1,0:T(8,128)(2,1)S(1)} %get-tuple-element.54), channel_id=1, source_target_pairs={{1,2},{2,1},{5,6},{6,5},{9,10},{10,9},{13,14},{14,13},{17,18},{18,... | collective-permute-start | bytes 18440 | tf_op jit(solution)/shard_map/ppermute | solution.py:312
  57.8 3.5 %collective-permute-done.9.far_columns_hbm = bf16[8,384]{1,0:T(8,128)(2,1)S(1)} collective-permute-done((bf16[8,384]{1,0:T(8,128)(2,1)S(1)}, bf16[8,384]{1,0:T(8,128)(2,1)S(1)}, u32[]{:S(2)}, u32[]{:S(2)}) %collective-permute-start.9) | collective-permute-done | bytes 6176 | tf_op jit(solution)/shard_map/ppermute | solution.py:312
  61.5 0.5 copy-done.6
  61.9 0.1 copy-done.7
  62.0 0.6 copy-done.3
  62.6 0.5 copy-done.4
  63.1 8.1 %cross_grams.1 = (bf16[49,4,16,128]{3,2,1,0:T(8,128)(2,1)}, bf16[49,4,16,128]{3,2,1,0:T(8,128)(2,1)}) custom-call(s32[2,48]{1,0:T(2,128)} %bitcast.4, bf16[384,2048]{1,0:T(8,128)(2,1)} %copy-done.3, bf16[384,2048]{1,0:T(8,128)(2,1)} %copy-done.4, bf16[8,384]{1,0:T(8,128)(2,1)} %copy-done.7, bf16[8,384]{1,0:T(8,128)(2,1)} %copy-done.6, ...), custom_call_target="tpu_custom_call" | custom-call | flops 1207959552 | bytes 6291456 | tf_op jit(solution)/shard_map/cross_grams/pallas_call | solution.py:415
  71.4 2.4 %collective-permute-done.10.got_hbm = bf16[49,4,16,128]{3,2,1,0:T(8,128)(2,1)S(1)} collective-permute-done((bf16[49,4,16,128]{3,2,1,0:T(8,128)(2,1)}, bf16[49,4,16,128]{3,2,1,0:T(8,128)(2,1)S(1)}, u32[]{:S(2)}, u32[]{:S(2)}) %collective-permute-start.10) | collective-permute-done | bytes 802848 | tf_op jit(solution)/shard_map/ppermute | solution.py:435
  73.8 0.4 chip_sums.1
  74.2 0.2 collective-permute-start.15
  74.4 2.0 %collective-permute-start.12 = (bf16[52,16,128]{2,1,0:T(8,128)(2,1)S(1)}, bf16[52,16,128]{2,1,0:T(8,128)(2,1)S(1)}, u32[]{:S(2)}, u32[]{:S(2)}) collective-permute-start(bf16[52,16,128]{2,1,0:T(8,128)(2,1)S(1)} %get-tuple-element.48), channel_id=1, source_target_pairs={{0,8},{4,12},{8,0},{12,4},{16,24},{20,28},{24,16},{28,20},{1,9},{5... | collective-permute-start | bytes 638984 | tf_op jit(solution)/shard_map/ppermute | solution.py:455
  76.4 0.7 collective-permute-start.13
  77.1 0.8 collective-permute-start.14
  78.6 4.0 %collective-permute-done.12.refs_1_ = bf16[52,16,128]{2,1,0:T(8,128)(2,1)S(1)} collective-permute-done((bf16[52,16,128]{2,1,0:T(8,128)(2,1)S(1)}, bf16[52,16,128]{2,1,0:T(8,128)(2,1)S(1)}, u32[]{:S(2)}, u32[]{:S(2)}) %collective-permute-start.12) | collective-permute-done | bytes 213024 | tf_op jit(solution)/shard_map/ppermute | solution.py:455
  82.5 5.7 %collective-permute-done.13.refs_2_ = bf16[52,16,128]{2,1,0:T(8,128)(2,1)S(1)} collective-permute-done((bf16[52,16,128]{2,1,0:T(8,128)(2,1)S(1)}, bf16[52,16,128]{2,1,0:T(8,128)(2,1)S(1)}, u32[]{:S(2)}, u32[]{:S(2)}) %collective-permute-start.13) | collective-permute-done | bytes 213024 | tf_op jit(solution)/shard_map/ppermute | solution.py:455
  88.3 4.4 %scores.1 = bf16[48,16,128]{2,1,0:T(8,128)(2,1)} custom-call(s32[2,48]{1,0:T(2,128)S(1)} %bitcast.5, s32[1]{0:T(128)S(6)} %copy.12.live_ref, s32[160]{0:T(256)S(1)} %copy-done.2, f32[52,16,128]{2,1,0:T(8,128)S(1)} %get-tuple-element.47.refs_0_, bf16[52,16,128]{2,1,0:T(8,128)(2,1)S(1)} %collective-permute-done.12.refs_1_, ...), custom_call_target="tpu_custom_call" | custom-call | tf_op jit(solution)/shard_map/scores/pallas_call | solution.py:458
  (33 shorter events, 0.6 us)
Async XLA Ops:
  2.1 15.7 %collective-permute-start.2 = (bf16[256,128]{1,0:T(8,128)(2,1)S(1)}, bf16[256,128]{1,0:T(8,128)(2,1)S(1)}, u32[]{:S(2)}, u32[]{:S(2)}) collective-permute-start(bf16[256,128]{1,0:T(8,128)(2,1)S(1)} %get-tuple-element.53), channel_id=1, source_target_pairs={{0,3},{1,2},{2,1},{3,0},{4,7},{5,6},{6,5},{7,4},{8,11},{9,10},{10,... | collective-permute-start | bytes 196616 | tf_op jit(solution)/shard_map/ppermute | solution.py:322
  3.7 14.1 %collective-permute-start.1 = (bf16[256,128]{1,0:T(8,128)(2,1)S(1)}, bf16[256,128]{1,0:T(8,128)(2,1)S(1)}, u32[]{:S(2)}, u32[]{:S(2)}) collective-permute-start(bf16[256,128]{1,0:T(8,128)(2,1)S(1)} %get-tuple-element.53), channel_id=1, source_target_pairs={{0,2},{1,3},{2,0},{3,1},{4,6},{5,7},{6,4},{7,5},{8,10},{9,11},{10,... | collective-permute-start | bytes 196616 | tf_op jit(solution)/shard_map/ppermute | solution.py:322
  4.7 13.1 %collective-permute-start = (bf16[256,128]{1,0:T(8,128)(2,1)S(1)}, bf16[256,128]{1,0:T(8,128)(2,1)S(1)}, u32[]{:S(2)}, u32[]{:S(2)}) collective-permute-start(bf16[256,128]{1,0:T(8,128)(2,1)S(1)} %get-tuple-element.53), channel_id=1, source_target_pairs={{0,1},{1,0},{2,3},{3,2},{4,5},{5,4},{6,7},{7,6},{8,9},{9,8},{10,11... | collective-permute-start | bytes 196616 | tf_op jit(solution)/shard_map/ppermute | solution.py:322
  12.3 49.2 %collective-permute-start.5 = (bf16[384,2048]{1,0:T(8,128)(2,1)}, bf16[384,2048]{1,0:T(8,128)(2,1)S(1)}, u32[]{:S(2)}, u32[]{:S(2)}) collective-permute-start(bf16[384,2048]{1,0:T(8,128)(2,1)} %get-tuple-element.33), channel_id=1, source_target_pairs={{0,1},{2,3},{1,0},{3,2},{4,5},{6,7},{5,4},{7,6},{8,9},{10,11},{9,8... | collective-permute-start | bytes 4718600 | tf_op jit(solution)/shard_map/ppermute | solution.py:312
  12.9 48.6 %collective-permute-start.6 = (bf16[384,2048]{1,0:T(8,128)(2,1)}, bf16[384,2048]{1,0:T(8,128)(2,1)S(1)}, u32[]{:S(2)}, u32[]{:S(2)}) collective-permute-start(bf16[384,2048]{1,0:T(8,128)(2,1)} %get-tuple-element.34), channel_id=1, source_target_pairs={{1,2},{2,1},{5,6},{6,5},{9,10},{10,9},{13,14},{14,13},{17,18},{18,... | collective-permute-start | bytes 4718600 | tf_op jit(solution)/shard_map/ppermute | solution.py:312
  17.9 7.0 %collective-permute-start.3 = (bf16[2,5120]{1,0:T(2,128)(2,1)}, bf16[2,5120]{1,0:T(2,128)(2,1)S(1)}, u32[]{:S(2)}, u32[]{:S(2)}) collective-permute-start(bf16[2,5120]{1,0:T(2,128)(2,1)} %get-tuple-element.29), channel_id=1, source_target_pairs={{4,8},{12,16},{20,24},{8,4},{16,12},{24,20},{5,9},{13,17},{21,25},... | collective-permute-start | bytes 61448 | tf_op jit(solution)/shard_map/ppermute | solution.py:312
  18.5 6.4 %collective-permute-start.4 = (bf16[2,5120]{1,0:T(2,128)(2,1)}, bf16[2,5120]{1,0:T(2,128)(2,1)S(1)}, u32[]{:S(2)}, u32[]{:S(2)}) collective-permute-start(bf16[2,5120]{1,0:T(2,128)(2,1)} %get-tuple-element.30), channel_id=1, source_target_pairs={{0,4},{8,12},{16,20},{24,28},{4,0},{12,8},{20,16},{28,24},{1,5},{9... | collective-permute-start | bytes 61448 | tf_op jit(solution)/shard_map/ppermute | solution.py:312
  23.4 31.6 %collective-permute-start.7 = (bf16[1024,128]{1,0:T(8,128)(2,1)S(1)}, bf16[1024,128]{1,0:T(8,128)(2,1)S(1)}, u32[]{:S(2)}, u32[]{:S(2)}) collective-permute-start(bf16[1024,128]{1,0:T(8,128)(2,1)S(1)} %pad_maximum_fusion.1), channel_id=1, source_target_pairs={{0,16},{4,20},{8,24},{12,28},{16,0},{20,4},{24,8},{28,12},{1,17},{... | collective-permute-start | bytes 786440 | tf_op jit(solution)/shard_map/ppermute | solution.py:357
  25.7 29.3 %copy-start.5 = (bf16[2048,128]{1,0:T(8,128)(2,1)S(1)}, bf16[2048,128]{1,0:T(8,128)(2,1)}, u32[]{:S(2)}) copy-start(bf16[2048,128]{1,0:T(8,128)(2,1)} %constant_dynamic-update-slice_fusion.1) | copy-start | bytes 1572868
  55.0 16.3 %collective-permute-start.11 = (bf16[2048,128]{1,0:T(8,128)(2,1)S(1)}, bf16[2048,128]{1,0:T(8,128)(2,1)S(1)}, u32[]{:S(2)}, u32[]{:S(2)}) collective-permute-start(bf16[2048,128]{1,0:T(8,128)(2,1)S(1)} %constant_dynamic-update-slice_fusion), channel_id=1, source_target_pairs={{0,8},{4,12},{8,0},{12,4},{16,24},{20,28},{24,16},{28,20},{1,9},{5... | collective-permute-start | bytes 1572872 | tf_op jit(solution)/shard_map/ppermute | solution.py:357
  55.8 5.5 %collective-permute-start.9 = (bf16[8,384]{1,0:T(8,128)(2,1)S(1)}, bf16[8,384]{1,0:T(8,128)(2,1)S(1)}, u32[]{:S(2)}, u32[]{:S(2)}) collective-permute-start(bf16[8,384]{1,0:T(8,128)(2,1)S(1)} %get-tuple-element.54), channel_id=1, source_target_pairs={{1,2},{2,1},{5,6},{6,5},{9,10},{10,9},{13,14},{14,13},{17,18},{18,... | collective-permute-start | bytes 18440 | tf_op jit(solution)/shard_map/ppermute | solution.py:312
  57.8 3.7 %collective-permute-start.8 = (bf16[8,384]{1,0:T(8,128)(2,1)S(1)}, bf16[8,384]{1,0:T(8,128)(2,1)S(1)}, u32[]{:S(2)}, u32[]{:S(2)}) collective-permute-start(bf16[8,384]{1,0:T(8,128)(2,1)S(1)} %get-tuple-element.55), channel_id=1, source_target_pairs={{0,1},{2,3},{1,0},{3,2},{4,5},{6,7},{5,4},{7,6},{8,9},{10,11},{9,8... | collective-permute-start | bytes 18440 | tf_op jit(solution)/shard_map/ppermute | solution.py:312
  61.4 0.6 copy-start.6
  61.5 0.6 copy-start.7
  61.5 1.2 %copy-start.3 = (bf16[384,2048]{1,0:T(8,128)(2,1)}, bf16[384,2048]{1,0:T(8,128)(2,1)S(1)}, u32[]{:S(2)}) copy-start(bf16[384,2048]{1,0:T(8,128)(2,1)S(1)} %collective-permute-done.5.near_hbm) | copy-start | bytes 4718596
  61.5 1.6 %copy-start.4 = (bf16[384,2048]{1,0:T(8,128)(2,1)}, bf16[384,2048]{1,0:T(8,128)(2,1)S(1)}, u32[]{:S(2)}) copy-start(bf16[384,2048]{1,0:T(8,128)(2,1)S(1)} %collective-permute-done.6.far_hbm) | copy-start | bytes 4718596
  71.2 2.6 %copy-start = (bf16[49,4,16,128]{3,2,1,0:T(8,128)(2,1)S(1)}, bf16[49,4,16,128]{3,2,1,0:T(8,128)(2,1)}, u32[]{:S(2)}) copy-start(bf16[49,4,16,128]{3,2,1,0:T(8,128)(2,1)} %get-tuple-element.43.keep_hbm) | copy-start | bytes 2408452
  71.2 17.0 %copy-start.1 = (s32[48,2]{0,1:T(2,128)S(1)}, s32[48,2]{0,1:T(2,128)}, u32[]{:S(2)}) copy-start(s32[48,2]{0,1:T(2,128)} %param.8) | copy-start | bytes 1156
  71.2 17.0 %copy-start.2 = (s32[160]{0:T(256)S(1)}, s32[160]{0:T(256)}, u32[]{:S(2)}) copy-start(s32[160]{0:T(256)} %rules_ref.1) | copy-start | bytes 1924
  71.2 2.6 %collective-permute-start.10 = (bf16[49,4,16,128]{3,2,1,0:T(8,128)(2,1)}, bf16[49,4,16,128]{3,2,1,0:T(8,128)(2,1)S(1)}, u32[]{:S(2)}, u32[]{:S(2)}) collective-permute-start(bf16[49,4,16,128]{3,2,1,0:T(8,128)(2,1)} %get-tuple-element.44), channel_id=1, source_target_pairs={{0,4},{4,0},{8,12},{12,8},{16,20},{20,16},{24,28},{28,24},{1,5},{5... | collective-permute-start | bytes 2408456 | tf_op jit(solution)/shard_map/ppermute | solution.py:435
  74.2 14.0 %collective-permute-start.15 = (bf16[4096,128]{1,0:T(8,128)(2,1)S(1)}, bf16[4096,128]{1,0:T(8,128)(2,1)S(1)}, u32[]{:S(2)}, u32[]{:S(2)}) collective-permute-start(bf16[4096,128]{1,0:T(8,128)(2,1)S(1)} %pad_maximum_fusion.refs_4_), channel_id=1, source_target_pairs={{0,4},{4,0},{8,12},{12,8},{16,20},{20,16},{24,28},{28,24},{1,5},{5... | collective-permute-start | bytes 3145736 | tf_op jit(solution)/shard_map/ppermute | solution.py:357
  74.4 8.1 %collective-permute-start.12 = (bf16[52,16,128]{2,1,0:T(8,128)(2,1)S(1)}, bf16[52,16,128]{2,1,0:T(8,128)(2,1)S(1)}, u32[]{:S(2)}, u32[]{:S(2)}) collective-permute-start(bf16[52,16,128]{2,1,0:T(8,128)(2,1)S(1)} %get-tuple-element.48), channel_id=1, source_target_pairs={{0,8},{4,12},{8,0},{12,4},{16,24},{20,28},{24,16},{28,20},{1,9},{5... | collective-permute-start | bytes 638984 | tf_op jit(solution)/shard_map/ppermute | solution.py:455
  76.4 11.8 %collective-permute-start.13 = (bf16[52,16,128]{2,1,0:T(8,128)(2,1)S(1)}, bf16[52,16,128]{2,1,0:T(8,128)(2,1)S(1)}, u32[]{:S(2)}, u32[]{:S(2)}) collective-permute-start(bf16[52,16,128]{2,1,0:T(8,128)(2,1)S(1)} %get-tuple-element.49), channel_id=1, source_target_pairs={{0,16},{4,20},{8,24},{12,28},{16,0},{20,4},{24,8},{28,12},{1,17},{... | collective-permute-start | bytes 638984 | tf_op jit(solution)/shard_map/ppermute | solution.py:455
  77.1 11.1 %collective-permute-start.14 = (bf16[52,16,128]{2,1,0:T(8,128)(2,1)S(1)}, bf16[52,16,128]{2,1,0:T(8,128)(2,1)S(1)}, u32[]{:S(2)}, u32[]{:S(2)}) collective-permute-start(bf16[52,16,128]{2,1,0:T(8,128)(2,1)S(1)} %get-tuple-element.50), channel_id=1, source_target_pairs={{0,24},{4,28},{8,16},{12,20},{16,8},{20,12},{24,0},{28,4},{1,25},{... | collective-permute-start | bytes 638984 | tf_op jit(solution)/shard_map/ppermute | solution.py:455

commit v9 on v8

--- a/solution.py
+++ b/solution.py
@@ -8,11 +8,11 @@
 from jax.sharding import PartitionSpec as P
 
 REACH = 3
+OUTER = REACH - 1
 TAPS = 5
 LANES = 128
 HALF = LANES // 2
-TILE = 2 * LANES
-DEPTH = 3 * LANES
+DEPTH = 2 * LANES
 VMEM_BYTES = 58 * 1024 * 1024
 
 
@@ -37,25 +37,24 @@
 
 def smooth_rows(x_ref, halo, w_ref, store):
     rows, width = x_ref.shape
-    tiles = width // TILE
+    tiles = width // LANES
     first = lax.broadcasted_iota(jnp.int32, (rows, LANES), 1) < HALF
-
-    def tile(j):
-        own = x_ref[:, j * TILE : (j + 1) * TILE]
-        before = halo if j == 0 else x_ref[:, j * TILE - LANES : j * TILE]
-        after = halo if j == tiles - 1 else x_ref[:, (j + 1) * TILE : (j + 1) * TILE + LANES]
-        window = jnp.concatenate([own, jnp.where(first, after, before)], axis=1)
-        return jnp.dot(window, w_ref[j], preferred_element_type=jnp.float32)
-
-    total = None
-    for j in range(0, tiles, 2):
-        squares = None
-        for k, values in enumerate([tile(j), tile(j + 1)]):
-            store(j + k, values.astype(jnp.bfloat16))
-            values = values * values
-            values = values[:, :LANES] + values[:, LANES:]
-            squares = values if k == 0 else squares + values
-        total = squares if j == 0 else total + squares
+    before, total, squares = None, None, None
+    for j in range(-1, tiles):
+        if j < 0:
+            window = jnp.concatenate([halo, x_ref[:, :LANES]], axis=1)
+        elif j == tiles - 1:
+            window = jnp.concatenate([x_ref[:, j * LANES :], halo], axis=1)
+        else:
+            window = x_ref[:, j * LANES : (j + 2) * LANES]
+        now = jnp.dot(window, w_ref[j + 1], preferred_element_type=jnp.float32)
+        if j >= 0:
+            values = jnp.where(first, before, now)
+            store(j, values.astype(jnp.bfloat16))
+            squares = values * values if j % 2 == 0 else squares + values * values
+            if j % 2 == 1:
+                total = squares if total is None else total + squares
+        before = now
     return total
 
 
@@ -76,27 +75,29 @@
 
 
 def write_weights(stencil_ref, out_ref):
+    tiles = stencil_ref.shape[1] // LANES
     out_ref[...] = jnp.zeros_like(out_ref)
-    strip = 16
-    places = [(0, LANES, 0, 2), (LANES, LANES, LANES, 2)]
-    places += [(LANES - strip, strip, LANES, 2), (LANES, strip, 0, 2)]
-    places += [(TILE + LANES - strip, strip, 0, 2 - LANES - TILE), (TILE, strip, LANES, 2)]
-    for k0, rows, n0, shift in places:
-        k = lax.broadcasted_iota(jnp.int32, (rows, LANES), 0) + k0
-        tap = k - lax.broadcasted_iota(jnp.int32, (rows, LANES), 1) - n0 + shift
-        for j in range(out_ref.shape[0]):
-            taps = stencil_ref[:, j * TILE + n0 : j * TILE + n0 + LANES]
-            w = jnp.zeros((rows, LANES), jnp.float32)
-            for t in range(TAPS):
-                w = jnp.where(tap == t, taps[t : t + 1, :], w)
-            out_ref[j, k0 : k0 + rows, n0 : n0 + LANES] = w.astype(jnp.bfloat16)
+    k0, rows = 3 * LANES // 8, 5 * LANES // 4
+    k = lax.broadcasted_iota(jnp.int32, (rows, LANES), 0) + k0
+    lane = lax.broadcasted_iota(jnp.int32, (rows, LANES), 1)
+    tap = k - lane + jnp.where(lane < HALF, 2 - LANES, 2)
+    early = lax.broadcasted_iota(jnp.int32, (TAPS, LANES), 1) < HALF
+    zeros = jnp.zeros((TAPS, LANES), jnp.float32)
+    for j in range(-1, tiles):
+        here = stencil_ref[:, j * LANES : (j + 1) * LANES] if j >= 0 else zeros
+        after = stencil_ref[:, (j + 1) * LANES : (j + 2) * LANES] if j + 1 < tiles else zeros
+        taps = jnp.where(early, after, here)
+        w = jnp.zeros((rows, LANES), jnp.float32)
+        for t in range(TAPS):
+            w = jnp.where(tap == t, taps[t : t + 1, :], w)
+        out_ref[j + 1, k0 : k0 + rows] = w.astype(jnp.bfloat16)
 
 
 def cut_kernel(images_ref, stencil_ref, near_rows, far_rows, near_columns, far_columns, w_ref, bands, strips, sems):
     rows, width = images_ref.shape
     edge = near_rows.shape[0]
     odd = lax.axis_index("ion") % 2
-    starts = [pl.multiple_of(k * (rows - edge), edge // REACH) for k in (1 - odd, odd)]
+    starts = [pl.multiple_of(k * (rows - edge), edge // OUTER) for k in (1 - odd, odd)]
     reads = fetch(
         [images_ref.at[pl.ds(start, edge)] for start in starts]
         + [images_ref.at[:, pl.ds(start, LANES)] for start in (0, width - LANES)],
@@ -147,7 +148,7 @@
     @pl.when(step < steps)
     def smooth():
         def store(j, values):
-            held[pl.ds(step * group, group), :, j * TILE : (j + 1) * TILE] = values.reshape(group, block, TILE)
+            held[pl.ds(step * group, group), :, j * LANES : (j + 1) * LANES] = values.reshape(group, block, LANES)
 
         total = smooth_rows(x_ref, halo_tile(columns_ref), w_ref, store)
         copy_out(step).start()
@@ -170,36 +171,40 @@
             copy_out(k).wait()
 
 
-def cross_kernel(blocks, block, pairs_ref, near_hbm, far_hbm, near_columns_hbm, far_columns_hbm, w_hbm, energy_hbm, smoothed_hbm, keep_hbm,
-                 give_hbm, keep_ref, give_ref, x_ref, columns_ref, w_ref, energy_ref, own, other, table, sems):
+def cross_kernel(blocks, block, pairs_ref, near_hbm, far_hbm, near_edge_hbm, far_edge_hbm, w_hbm, energy_hbm,
+                 smoothed_hbm, keep_hbm, give_hbm, keep_ref, give_ref, near_same, near_cross, far_same, far_cross,
+                 x_ref, edge_ref, w_ref, energy_ref, own, other, table, sems):
     core = lax.axis_index("pix") % 2
     first_block = lax.axis_index("ion") * blocks
     slots = pairs_ref.shape[1]
     chips, share = keep_ref.shape[1:3]
     units = keep_ref.shape[0] - slots
-    edge = REACH * block
+    edge = OUTER * block
+    reach = REACH * block
     rows = blocks * block
-    low, high = pl.ds(0, edge), pl.ds(edge, edge)
     odd = lax.axis_index("ion") % 2
     near, far = (pl.ds(pl.multiple_of(k * edge, edge), edge) for k in (1 - odd, odd))
     copies = fetch(
-        (near_hbm, far_hbm, near_columns_hbm, far_columns_hbm, w_hbm, energy_hbm, smoothed_hbm.at[low],
-         smoothed_hbm.at[pl.ds(rows - edge, edge)], keep_hbm, give_hbm),
-        (x_ref.at[near], x_ref.at[far], columns_ref.at[:, near], columns_ref.at[:, far], w_ref, energy_ref, own.at[low],
-         own.at[high], keep_ref, give_ref),
+        (near_hbm, far_hbm, near_edge_hbm, far_edge_hbm, w_hbm, energy_hbm, smoothed_hbm.at[pl.ds(0, reach)],
+         smoothed_hbm.at[pl.ds(rows - reach, reach)], keep_hbm, give_hbm),
+        (x_ref.at[near], x_ref.at[far], edge_ref.at[:, near], edge_ref.at[:, far], w_ref, energy_ref,
+         own.at[pl.ds(0, reach)], own.at[pl.ds(reach, reach)], keep_ref, give_ref),
         sems,
     )
     for copy in copies[:6]:
         copy.wait()
     table[...] = jnp.zeros_like(table)
     table[REACH : REACH + blocks, :] = energy_ref[...]
+
     def store(j, values):
-        other[:, j * TILE : (j + 1) * TILE] = values
-
-    total = smooth_rows(x_ref, halo_tile(columns_ref), w_ref, store)
-    for k in range(2 * REACH):
-        row = k if k < REACH else k + blocks
+        other[:, j * LANES : (j + 1) * LANES] = values
+
+    total = smooth_rows(x_ref, halo_tile(edge_ref.at[:8]), w_ref, store)
+    for k in range(2 * OUTER):
+        row = k + 1 if k < OUTER else k + 1 + blocks
         table[row : row + 1, :] = row_sums(total[k * block : (k + 1) * block, :])
+    for row, lane in ((0, 0), (2 * REACH + blocks - 1, edge)):
+        table[row : row + 1, :] = edge_ref[8:, lane : lane + LANES].astype(jnp.float32)[:1]
     for copy in copies[6:]:
         copy.wait()
 
@@ -210,11 +215,11 @@
     def one(s, carry):
         a, b = pairs_ref[0, s] - first_block, pairs_ref[1, s] - first_block
 
-        @pl.when((b < 0) | (b >= blocks))
+        @pl.when(((b < 0) & (b >= -OUTER)) | ((b >= blocks) & (b < blocks + OUTER)))
         def crossing():
             side = (b >= 0).astype(jnp.int32)
             a_row = pl.multiple_of((a - side * (blocks - 2 * REACH)) * block, block)
-            b_row = pl.multiple_of((b + REACH - side * blocks) * block, block)
+            b_row = pl.multiple_of((b + OUTER - side * blocks) * block, block)
             gram = gram_of(own[pl.ds(a_row, block), :], other[pl.ds(b_row, block), :])
             keep_ref[s], give_ref[s] = by_core(gram, chips, core)
 
@@ -222,14 +227,40 @@
 
     lax.fori_loop(0, slots, one, 0)
 
-
-def chip_kernel(slots, units, keep_hbm, got_hbm, own_ref, *refs):
-    out_refs, (keep_ref, got_ref, sems) = refs[:-3], refs[-3:]
+    def piece(ref, k):
+        return ref[k * block : (k + 1) * block, :]
+
+    above = by_core(gram_of(piece(other, OUTER), piece(own, REACH)), chips, core)
+    below = by_core(gram_of(piece(other, OUTER - 1), piece(own, REACH - 1)), chips, core)
+    for k, (near_ref, far_ref) in enumerate(((near_same, far_same), (near_cross, far_cross))):
+        near_ref[...] = jnp.where(odd == 1, below[k], above[k])
+        far_ref[...] = jnp.where(odd == 1, above[k], below[k])
+
+
+def chip_kernel(blocks, slots, units, pairs_ref, keep_hbm, got_hbm, *refs):
+    third_hbm, own_ref, out_refs, (keep_ref, got_ref, third, sems) = refs[:4], refs[4], refs[5:-4], refs[-4:]
     chip = lax.axis_index("pix") // 2
+    first_block = lax.axis_index("ion") * blocks
+    odd = lax.axis_index("ion") % 2
     chips, share = keep_ref.shape[1:3]
     shape = (units * chips, share, LANES)
-    for copy in fetch((keep_hbm, got_hbm), (keep_ref, got_ref), sems):
+    targets = [keep_ref, got_ref] + [third.at[k] for k in range(4)]
+    for copy in fetch((keep_hbm, got_hbm, *third_hbm), targets, sems):
         copy.wait()
+
+    def one(s, carry):
+        b = pairs_ref[1, s] - first_block
+
+        @pl.when((b == -REACH) | (b == blocks + REACH - 1))
+        def returned():
+            above = (b > 0).astype(jnp.int32)
+            place = jnp.where(above + odd == 1, 0, 2)
+            keep_ref[s] = third[place]
+            got_ref[s] = third[place + 1]
+
+        return carry
+
+    lax.fori_loop(0, slots, one, 0)
     energies = (keep_ref[slots:].astype(jnp.float32) + got_ref[slots:].astype(jnp.float32)).reshape(shape)
     for d in range(chips):
         total = keep_ref[:slots, chip ^ d].astype(jnp.float32) + got_ref[:slots, chip ^ d].astype(jnp.float32)
@@ -304,7 +335,7 @@
     pixel_count = width * n_pix
     chips, share = n_pix // 2, block // n_pix
     core, chip = pix % 2, pix // 2
-    edge = REACH * block
+    edge = OUTER * block
 
     def swapped(axis, size, near, far):
         pairs_of = [[(i, i + 1) for i in range(first, size - 1, 2)] for first in (0, 1)]
@@ -332,7 +363,7 @@
             edge_rows,
             edge_columns,
             edge_columns,
-            jax.ShapeDtypeStruct((width // TILE, DEPTH, TILE), jnp.bfloat16),
+            jax.ShapeDtypeStruct((width // LANES + 1, DEPTH, LANES), jnp.bfloat16),
         ],
         scratch_shapes=[
             pltpu.VMEM((2, edge, width), images.dtype),
@@ -406,23 +437,26 @@
     smoothed = smoothed.reshape(rows, width)
 
     energy, columns, mine = lax.optimization_barrier((energy, columns, mine))
-    first, last = columns[:, :edge], columns[:, rows - edge :]
+    third = jnp.pad(energy.astype(jnp.bfloat16), ((0, 0), (0, edge - LANES)))
+    rest = jnp.zeros((7, edge), images.dtype)
+    first = jnp.concatenate([columns[:, :edge], third[REACH - 1 : REACH], rest], axis=0)
+    last = jnp.concatenate([columns[:, rows - edge :], third[blocks - REACH : blocks - REACH + 1], rest], axis=0)
     odd = ion % 2 == 1
-    near_columns, far_columns = swapped("ion", n_ion, jnp.where(odd, first, last), jnp.where(odd, last, first))
+    near_edge, far_edge = swapped("ion", n_ion, jnp.where(odd, first, last), jnp.where(odd, last, first))
     for distance in distances[1:-1]:
         mine = jnp.concatenate([mine, exchange(mine, distance)], axis=0)
 
-    keep, give = pl.pallas_call(
+    keep, give, *third = pl.pallas_call(
         functools.partial(cross_kernel, blocks, block),
         in_specs=[smem] + [hbm] * 4 + [fixed] * 5,
-        out_specs=[vmem, vmem],
-        out_shape=both_halves,
+        out_specs=[vmem] * 6,
+        out_shape=both_halves + [jax.ShapeDtypeStruct(half, jnp.bfloat16)] * 4,
         scratch_shapes=[
             pltpu.VMEM((2 * edge, width), jnp.bfloat16),
-            pltpu.VMEM((8, 2 * edge), jnp.bfloat16),
+            pltpu.VMEM((16, 2 * edge), jnp.bfloat16),
             pltpu.VMEM(weights.shape, jnp.bfloat16),
             pltpu.VMEM((blocks, LANES), jnp.float32),
-            pltpu.VMEM((2 * edge, width), jnp.bfloat16),
+            pltpu.VMEM((2 * REACH * block, width), jnp.bfloat16),
             pltpu.VMEM((2 * edge, width), jnp.bfloat16),
             pltpu.VMEM((units * block // 2, LANES), jnp.float32),
             pltpu.SemaphoreType.DMA((10,)),
@@ -430,25 +464,34 @@
         compiler_params=params(),
         cost_estimate=cost(4 * edge * width * DEPTH, 8 * edge * width),
         name="cross_grams",
-    )(table_pairs, near_rows, far_rows, near_columns, far_columns, weights, energy, smoothed, keep, give)
+    )(table_pairs, near_rows, far_rows, near_edge, far_edge, weights, energy, smoothed, keep, give)
 
     got = lax.ppermute(give, "pix", [(i, i ^ 1) for i in range(n_pix)])
+
+    def both_cores(same, cross, first):
+        both = [(i, i + 1) for i in range(first, n_ion - 1, 2)]
+        both += [(j, i) for i, j in both]
+        crossing = [(p * n_ion + i, (p ^ 1) * n_ion + j) for p in range(n_pix) for i, j in both]
+        return lax.ppermute(same, "ion", both), lax.ppermute(cross, ("pix", "ion"), crossing)
+
+    third = both_cores(*third[:2], 0) + both_cores(*third[2:], 1)
     message = jax.ShapeDtypeStruct((slots + units * chips, share, LANES), jnp.bfloat16)
     own_rows = jax.ShapeDtypeStruct((slots + units * chips, share, LANES), jnp.float32)
     small = pltpu.CompilerParams(vmem_limit_bytes=16 * 1024 * 1024)
     own, *messages = pl.pallas_call(
-        functools.partial(chip_kernel, slots, units),
-        in_specs=[fixed, hbm],
+        functools.partial(chip_kernel, blocks, slots, units),
+        in_specs=[smem, fixed] + [hbm] * 5,
         out_specs=[vmem] * chips,
         out_shape=[own_rows] + [message] * (chips - 1),
         scratch_shapes=[
             pltpu.VMEM(half_shape, jnp.bfloat16),
             pltpu.VMEM(half_shape, jnp.bfloat16),
-            pltpu.SemaphoreType.DMA((2,)),
+            pltpu.VMEM((4, *half), jnp.bfloat16),
+            pltpu.SemaphoreType.DMA((6,)),
         ],
         compiler_params=small,
         name="chip_sums",
-    )(keep, got)
+    )(table_pairs, keep, got, *third)
     own, mine = lax.optimization_barrier((own, mine))
     other = exchange(mine, distances[-1])
     received = [

time: 93.5 us -> 99.8 us (1.067)
  starting transfers between devices: 20.4 us -> 30.3 us
  local copies, waits for them, and re-layouts: 5.17 us -> 3.12 us
  Pallas kernels: 48.2 us -> 47 us
    ppermute x0 -> x4, starting transfers between devices: none -> 8.29 us  [the longest x2 4.59 us: both_cores(): lax.ppermute(same, 'ion', both)]
    ppermute x0 -> x4, waiting for transfers between devices: none -> 3.24 us  [the longest x2 3.23 us: both_cores(): lax.ppermute(cross, ('pix', 'ion'), crossing)]
    unnamed x20 -> x18, local copies, waits for them, and re-layouts: 5.06 us -> 2.21 us
    ppermute x1, waiting for transfers between devices: 2.42 us -> 0.01 us  [on_device(): got = lax.ppermute(give, 'pix', [(i, i ^ 1) for i in range(n_pix)])]
    pallas_call x1, Pallas kernels: 8.08 us -> 6.49 us  [on_device(): pl.pallas_call(functools.partial(cross_kernel, blocks, block), in_specs=[...]
    pallas_call x1, Pallas kernels: 0.37 us -> 1.91 us  [on_device(): pl.pallas_call(functools.partial(chip_kernel, blocks, slots, units), in_s...]
    ppermute x3, starting transfers between devices: 1.79 us -> 3.31 us  [exchange(): return lax.ppermute(value, 'pix', [(i, i ^ distance) for i in range(n_pix)])]
  transfers between devices with their start and end apart: 16 -> 20, of which waited for: 5 -> 6; matrix products, arithmetic and copies ran while one was open for 4% -> 3% of each run, Pallas kernels for 47% -> 41%
where the time goes in v9:
time: 99.8 us; the launch traced here: 99.4 us
  Pallas kernels  47 us (47%)
  starting transfers between devices  30.3 us (30%)
  waiting for transfers between devices  15.8 us (16%)
  local copies, waits for them, and re-layouts  3.12 us (3%)
  other arithmetic  1.66 us (2%)
  between operations  1.56 us (2%)
    pallas_call x1, Pallas kernels, on_device(): pl.pallas_call(functools.partial(main_kernel, steps, group, block), grid_...  28.9 us
    ppermute x6, starting transfers between devices, swapped(): lax.ppermute(value, axis, both + [(j, i) for i, j in both])  11 us
    ppermute x3, waiting for transfers between devices, on_device(): lax.ppermute(m, 'pix', [(i, i ^ 2 * (d + 1)) for i in range(n_pix)])  8.9 us
    pallas_call x1, Pallas kernels, on_device(): pl.pallas_call(functools.partial(cross_kernel, blocks, block), in_specs=[...  6.49 us
    pallas_call x1, Pallas kernels, on_device(): pl.pallas_call(cut_kernel, in_specs=[hbm, vmem], out_specs=[hbm, hbm, vme...  5.27 us
    ppermute x2, starting transfers between devices, both_cores(): lax.ppermute(same, 'ion', both)  4.59 us
    pallas_call x1, Pallas kernels, on_device(): pl.pallas_call(functools.partial(score_kernel, blocks, place_of, pixel_co...  4.39 us
    ppermute x3, starting transfers between devices, on_device(): lax.ppermute(mine, 'ion', [(i, i ^ d) for i in range(n_ion)])  4.12 us
  transfers between devices with their start and end apart: 20, of which 6 were waited for; matrix products, arithmetic and copies ran while one was open for 3% of the time, Pallas kernels for 41%

profile of v9, /device:TPU:8, one launch (start us, length us, event | category | flops | bytes accessed | tf_op | source)
XLA Modules:
  0.0 99.4 jit_solution(10190122475334340089)
XLA Ops:
  0.6 0.9 constant_dynamic-update-slice_fusion.4
  1.5 1.6 %collective-permute-start.2 = (bf16[256,128]{1,0:T(8,128)(2,1)S(1)}, bf16[256,128]{1,0:T(8,128)(2,1)S(1)}, u32[]{:S(2)}, u32[]{:S(2)}) collective-permute-start(bf16[256,128]{1,0:T(8,128)(2,1)S(1)} %get-tuple-element.61), channel_id=1, source_target_pairs={{0,3},{1,2},{2,1},{3,0},{4,7},{5,6},{6,5},{7,4},{8,11},{9,10},{10,... | collective-permute-start | bytes 196616 | tf_op jit(solution)/shard_map/ppermute | solution.py:353
  3.1 1.1 %collective-permute-start.1 = (bf16[256,128]{1,0:T(8,128)(2,1)S(1)}, bf16[256,128]{1,0:T(8,128)(2,1)S(1)}, u32[]{:S(2)}, u32[]{:S(2)}) collective-permute-start(bf16[256,128]{1,0:T(8,128)(2,1)S(1)} %get-tuple-element.61), channel_id=1, source_target_pairs={{0,2},{1,3},{2,0},{3,1},{4,6},{5,7},{6,4},{7,5},{8,10},{9,11},{10,... | collective-permute-start | bytes 196616 | tf_op jit(solution)/shard_map/ppermute | solution.py:353
  4.2 1.4 %collective-permute-start = (bf16[256,128]{1,0:T(8,128)(2,1)S(1)}, bf16[256,128]{1,0:T(8,128)(2,1)S(1)}, u32[]{:S(2)}, u32[]{:S(2)}) collective-permute-start(bf16[256,128]{1,0:T(8,128)(2,1)S(1)} %get-tuple-element.61), channel_id=1, source_target_pairs={{0,1},{1,0},{2,3},{3,2},{4,5},{5,4},{6,7},{7,6},{8,9},{9,8},{10,11... | collective-permute-start | bytes 196616 | tf_op jit(solution)/shard_map/ppermute | solution.py:353
  5.6 5.3 %cut_edges.1 = (bf16[256,2048]{1,0:T(8,128)(2,1)}, bf16[256,2048]{1,0:T(8,128)(2,1)}, bf16[2,5120]{1,0:T(2,128)(2,1)}, bf16[2,5120]{1,0:T(2,128)(2,1)}, bf16[17,256,128]{2,1,0:T(8,128)(2,1)}) custom-call(bf16[5120,2048]{1,0:T(8,128)(2,1)} %x_ref.1, f32[5,2048]{1,0:T(8,128)} %stencil_ref.1), custom_call_target="tpu_custom_call" | custom-call | bytes 4194304 | tf_op jit(solution)/shard_map/cut_edges/pallas_call | solution.py:357
  10.9 0.7 collective-permute-start.5
  11.6 4.7 %collective-permute-start.6 = (bf16[256,2048]{1,0:T(8,128)(2,1)}, bf16[256,2048]{1,0:T(8,128)(2,1)S(1)}, u32[]{:S(2)}, u32[]{:S(2)}) collective-permute-start(bf16[256,2048]{1,0:T(8,128)(2,1)} %get-tuple-element.38), channel_id=1, source_target_pairs={{1,2},{2,1},{5,6},{6,5},{9,10},{10,9},{13,14},{14,13},{17,18},{18,... | collective-permute-start | bytes 3145736 | tf_op jit(solution)/shard_map/ppermute | solution.py:343
  16.6 0.7 collective-permute-start.3
  17.2 2.9 %collective-permute-start.4 = (bf16[2,5120]{1,0:T(2,128)(2,1)}, bf16[2,5120]{1,0:T(2,128)(2,1)S(1)}, u32[]{:S(2)}, u32[]{:S(2)}) collective-permute-start(bf16[2,5120]{1,0:T(2,128)(2,1)} %get-tuple-element.34), channel_id=1, source_target_pairs={{0,4},{8,12},{16,20},{24,28},{4,0},{12,8},{20,16},{28,24},{1,5},{9... | collective-permute-start | bytes 61448 | tf_op jit(solution)/shard_map/ppermute | solution.py:343
  20.2 1.6 %collective-permute-start.7 = (bf16[1024,128]{1,0:T(8,128)(2,1)S(1)}, bf16[1024,128]{1,0:T(8,128)(2,1)S(1)}, u32[]{:S(2)}, u32[]{:S(2)}) collective-permute-start(bf16[1024,128]{1,0:T(8,128)(2,1)S(1)} %pad_maximum_fusion.1), channel_id=1, source_target_pairs={{0,16},{4,20},{8,24},{12,28},{16,0},{20,4},{24,8},{28,12},{1,17},{... | collective-permute-start | bytes 786440 | tf_op jit(solution)/shard_map/ppermute | solution.py:388
  21.9 0.7 pad_maximum_fusion.2.columns_ref
  22.6 28.9 %smooth_and_gram.1 = (bf16[40,128,2048]{2,1,0:T(8,128)(2,1)}, f32[40,128]{1,0:T(8,128)}, bf16[49,4,16,128]{3,2,1,0:T(8,128)(2,1)}, bf16[49,4,16,128]{3,2,1,0:T(8,128)(2,1)}) custom-call(s32[2,48]{1,0:T(2,128)} %bitcast.3, bf16[5120,2048]{1,0:T(8,128)(2,1)} %x_ref.1, bf16[8,5120]{1,0:T(8,128)(2,1)} %pad_maximum_fusion.2.columns_ref, ...), custom_call_target="tpu_custom_call" | custom-call | flops 8589934592 | bytes 41943040 | tf_op jit(solution)/shard_map/smooth_and_gram/pallas_call | solution.py:415
  51.6 0.7 convert_element_type.5
  52.3 1.5 %collective-permute-start.15 = (bf16[2048,128]{1,0:T(8,128)(2,1)S(1)}, bf16[2048,128]{1,0:T(8,128)(2,1)S(1)}, u32[]{:S(2)}, u32[]{:S(2)}) collective-permute-start(bf16[2048,128]{1,0:T(8,128)(2,1)S(1)} %constant_dynamic-update-slice_fusion), channel_id=1, source_target_pairs={{0,8},{4,12},{8,0},{12,4},{16,24},{20,28},{24,16},{28,20},{1,9},{5... | collective-permute-start | bytes 1572872 | tf_op jit(solution)/shard_map/ppermute | solution.py:388
  53.9 0.7 fusion
  54.6 1.9 %collective-permute-start.9 = (bf16[16,256]{1,0:T(8,128)(2,1)S(1)}, bf16[16,256]{1,0:T(8,128)(2,1)S(1)}, u32[]{:S(2)}, u32[]{:S(2)}) collective-permute-start(bf16[16,256]{1,0:T(8,128)(2,1)S(1)} %get-tuple-element.66), channel_id=1, source_target_pairs={{1,2},{2,1},{5,6},{6,5},{9,10},{10,9},{13,14},{14,13},{17,18},{18,... | collective-permute-start | bytes 24584 | tf_op jit(solution)/shard_map/ppermute | solution.py:343
  56.6 3.5 %collective-permute-done.9.far_edge_hbm = bf16[16,256]{1,0:T(8,128)(2,1)S(1)} collective-permute-done((bf16[16,256]{1,0:T(8,128)(2,1)S(1)}, bf16[16,256]{1,0:T(8,128)(2,1)S(1)}, u32[]{:S(2)}, u32[]{:S(2)}) %collective-permute-start.9) | collective-permute-done | bytes 8224 | tf_op jit(solution)/shard_map/ppermute | solution.py:343
  60.3 0.5 copy-done.5
  60.9 0.4 copy-done.3
  61.6 6.5 %cross_grams.1 = (bf16[49,4,16,128]{3,2,1,0:T(8,128)(2,1)}, bf16[49,4,16,128]{3,2,1,0:T(8,128)(2,1)}, bf16[4,16,128]{2,1,0:T(8,128)(2,1)}, bf16[4,16,128]{2,1,0:...) custom-call(s32[2,48]{1,0:T(2,128)} %bitcast.4, bf16[256,2048]{1,0:T(8,128)(2,1)} %copy-done.3, ...), custom_call_target="tpu_custom_call" | custom-call | flops 536870912 | bytes 4194304 | tf_op jit(solution)/shard_map/cross_grams/pallas_call | solution.py:449
  68.3 1.8 %collective-permute-start.12 = (bf16[4,16,128]{2,1,0:T(8,128)(2,1)}, bf16[4,16,128]{2,1,0:T(8,128)(2,1)S(1)}, u32[]{:S(2)}, u32[]{:S(2)}) collective-permute-start(bf16[4,16,128]{2,1,0:T(8,128)(2,1)} %get-tuple-element.50), channel_id=1, source_target_pairs={{0,5},{2,7},{1,4},{3,6},{4,1},{6,3},{5,0},{7,2},{8,13},{10,15},{9,... | collective-permute-start | bytes 49160 | tf_op jit(solution)/shard_map/ppermute | solution.py:475
  70.1 4.5 %collective-permute-start.13 = (bf16[4,16,128]{2,1,0:T(8,128)(2,1)}, bf16[4,16,128]{2,1,0:T(8,128)(2,1)S(1)}, u32[]{:S(2)}, u32[]{:S(2)}) collective-permute-start(bf16[4,16,128]{2,1,0:T(8,128)(2,1)} %get-tuple-element.51), channel_id=1, source_target_pairs={{1,2},{2,1},{5,6},{6,5},{9,10},{10,9},{13,14},{14,13},{17,18},{18,... | collective-permute-start | bytes 49160 | tf_op jit(solution)/shard_map/ppermute | solution.py:475
  74.6 1.9 %collective-permute-start.14 = (bf16[4,16,128]{2,1,0:T(8,128)(2,1)}, bf16[4,16,128]{2,1,0:T(8,128)(2,1)S(1)}, u32[]{:S(2)}, u32[]{:S(2)}) collective-permute-start(bf16[4,16,128]{2,1,0:T(8,128)(2,1)} %get-tuple-element.52), channel_id=1, source_target_pairs={{1,6},{2,5},{5,2},{6,1},{9,14},{10,13},{13,10},{14,9},{17,22},{18,... | collective-permute-start | bytes 49160 | tf_op jit(solution)/shard_map/ppermute | solution.py:475
  76.6 3.2 %collective-permute-done.14.refs_3_ = bf16[4,16,128]{2,1,0:T(8,128)(2,1)S(1)} collective-permute-done((bf16[4,16,128]{2,1,0:T(8,128)(2,1)}, bf16[4,16,128]{2,1,0:T(8,128)(2,1)S(1)}, u32[]{:S(2)}, u32[]{:S(2)}) %collective-permute-start.14) | collective-permute-done | bytes 16416 | tf_op jit(solution)/shard_map/ppermute | solution.py:475
  79.9 1.9 %chip_sums.1 = (f32[52,16,128]{2,1,0:T(8,128)S(1)}, bf16[52,16,128]{2,1,0:T(8,128)(2,1)S(1)}, bf16[52,16,128]{2,1,0:T(8,128)(2,1)S(1)}, bf16[52,16,128]{2,1,0:T(8,128)(2,1)S(1)}) custom-call(s32[2,48]{1,0:T(2,128)S(1)} %bitcast.5, bf16[49,4,16,128]{3,2,1,0:T(8,128)(2,1)S(1)} %copy-done, bf16[49,4,16,128]{3,2,1,0:T(8,128)(2,1)S(1)} %collective-permute-done.10.got_hbm, ...), custom_call_target="tpu_custom_call" | custom-call | tf_op jit(solution)/shard_map/chip_sums/pallas_call | solution.py:481
  82.0 0.5 collective-permute-start.16
  82.5 2.5 %collective-permute-start.17 = (bf16[52,16,128]{2,1,0:T(8,128)(2,1)S(1)}, bf16[52,16,128]{2,1,0:T(8,128)(2,1)S(1)}, u32[]{:S(2)}, u32[]{:S(2)}) collective-permute-start(bf16[52,16,128]{2,1,0:T(8,128)(2,1)S(1)} %get-tuple-element.57), channel_id=1, source_target_pairs={{0,16},{4,20},{8,24},{12,28},{16,0},{20,4},{24,8},{28,12},{1,17},{... | collective-permute-start | bytes 638984 | tf_op jit(solution)/shard_map/ppermute | solution.py:498
  85.0 0.5 collective-permute-start.18
  86.2 3.9 %collective-permute-done.16.refs_1_ = bf16[52,16,128]{2,1,0:T(8,128)(2,1)S(1)} collective-permute-done((bf16[52,16,128]{2,1,0:T(8,128)(2,1)S(1)}, bf16[52,16,128]{2,1,0:T(8,128)(2,1)S(1)}, u32[]{:S(2)}, u32[]{:S(2)}) %collective-permute-start.16) | collective-permute-done | bytes 213024 | tf_op jit(solution)/shard_map/ppermute | solution.py:498
  90.1 4.2 %collective-permute-done.17.refs_2_ = bf16[52,16,128]{2,1,0:T(8,128)(2,1)S(1)} collective-permute-done((bf16[52,16,128]{2,1,0:T(8,128)(2,1)S(1)}, bf16[52,16,128]{2,1,0:T(8,128)(2,1)S(1)}, u32[]{:S(2)}, u32[]{:S(2)}) %collective-permute-start.17) | collective-permute-done | bytes 213024 | tf_op jit(solution)/shard_map/ppermute | solution.py:498
  94.3 0.8 collective-permute-done.18.refs_3_
  95.1 4.4 %scores.1 = bf16[48,16,128]{2,1,0:T(8,128)(2,1)} custom-call(s32[2,48]{1,0:T(2,128)S(1)} %bitcast.6, s32[1]{0:T(128)S(6)} %copy.12.live_ref, s32[160]{0:T(256)S(1)} %copy-done.2, f32[52,16,128]{2,1,0:T(8,128)S(1)} %get-tuple-element.55.refs_0_, bf16[52,16,128]{2,1,0:T(8,128)(2,1)S(1)} %collective-permute-done.16.refs_1_, ...), custom_call_target="tpu_custom_call" | custom-call | tf_op jit(solution)/shard_map/scores/pallas_call | solution.py:501
  (44 shorter events, 1.4 us)
Async XLA Ops:
  1.5 15.1 %collective-permute-start.2 = (bf16[256,128]{1,0:T(8,128)(2,1)S(1)}, bf16[256,128]{1,0:T(8,128)(2,1)S(1)}, u32[]{:S(2)}, u32[]{:S(2)}) collective-permute-start(bf16[256,128]{1,0:T(8,128)(2,1)S(1)} %get-tuple-element.61), channel_id=1, source_target_pairs={{0,3},{1,2},{2,1},{3,0},{4,7},{5,6},{6,5},{7,4},{8,11},{9,10},{10,... | collective-permute-start | bytes 196616 | tf_op jit(solution)/shard_map/ppermute | solution.py:353
  3.1 13.4 %collective-permute-start.1 = (bf16[256,128]{1,0:T(8,128)(2,1)S(1)}, bf16[256,128]{1,0:T(8,128)(2,1)S(1)}, u32[]{:S(2)}, u32[]{:S(2)}) collective-permute-start(bf16[256,128]{1,0:T(8,128)(2,1)S(1)} %get-tuple-element.61), channel_id=1, source_target_pairs={{0,2},{1,3},{2,0},{3,1},{4,6},{5,7},{6,4},{7,5},{8,10},{9,11},{10,... | collective-permute-start | bytes 196616 | tf_op jit(solution)/shard_map/ppermute | solution.py:353
  4.2 12.3 %collective-permute-start = (bf16[256,128]{1,0:T(8,128)(2,1)S(1)}, bf16[256,128]{1,0:T(8,128)(2,1)S(1)}, u32[]{:S(2)}, u32[]{:S(2)}) collective-permute-start(bf16[256,128]{1,0:T(8,128)(2,1)S(1)} %get-tuple-element.61), channel_id=1, source_target_pairs={{0,1},{1,0},{2,3},{3,2},{4,5},{5,4},{6,7},{7,6},{8,9},{9,8},{10,11... | collective-permute-start | bytes 196616 | tf_op jit(solution)/shard_map/ppermute | solution.py:353
  10.9 49.4 %collective-permute-start.5 = (bf16[256,2048]{1,0:T(8,128)(2,1)}, bf16[256,2048]{1,0:T(8,128)(2,1)S(1)}, u32[]{:S(2)}, u32[]{:S(2)}) collective-permute-start(bf16[256,2048]{1,0:T(8,128)(2,1)} %get-tuple-element.37), channel_id=1, source_target_pairs={{0,1},{2,3},{1,0},{3,2},{4,5},{6,7},{5,4},{7,6},{8,9},{10,11},{9,8... | collective-permute-start | bytes 3145736 | tf_op jit(solution)/shard_map/ppermute | solution.py:343
  11.6 48.7 %collective-permute-start.6 = (bf16[256,2048]{1,0:T(8,128)(2,1)}, bf16[256,2048]{1,0:T(8,128)(2,1)S(1)}, u32[]{:S(2)}, u32[]{:S(2)}) collective-permute-start(bf16[256,2048]{1,0:T(8,128)(2,1)} %get-tuple-element.38), channel_id=1, source_target_pairs={{1,2},{2,1},{5,6},{6,5},{9,10},{10,9},{13,14},{14,13},{17,18},{18,... | collective-permute-start | bytes 3145736 | tf_op jit(solution)/shard_map/ppermute | solution.py:343
  16.6 5.3 %collective-permute-start.3 = (bf16[2,5120]{1,0:T(2,128)(2,1)}, bf16[2,5120]{1,0:T(2,128)(2,1)S(1)}, u32[]{:S(2)}, u32[]{:S(2)}) collective-permute-start(bf16[2,5120]{1,0:T(2,128)(2,1)} %get-tuple-element.33), channel_id=1, source_target_pairs={{4,8},{12,16},{20,24},{8,4},{16,12},{24,20},{5,9},{13,17},{21,25},... | collective-permute-start | bytes 61448 | tf_op jit(solution)/shard_map/ppermute | solution.py:343
  17.2 4.6 %collective-permute-start.4 = (bf16[2,5120]{1,0:T(2,128)(2,1)}, bf16[2,5120]{1,0:T(2,128)(2,1)S(1)}, u32[]{:S(2)}, u32[]{:S(2)}) collective-permute-start(bf16[2,5120]{1,0:T(2,128)(2,1)} %get-tuple-element.34), channel_id=1, source_target_pairs={{0,4},{8,12},{16,20},{24,28},{4,0},{12,8},{20,16},{28,24},{1,5},{9... | collective-permute-start | bytes 61448 | tf_op jit(solution)/shard_map/ppermute | solution.py:343
  20.2 31.3 %collective-permute-start.7 = (bf16[1024,128]{1,0:T(8,128)(2,1)S(1)}, bf16[1024,128]{1,0:T(8,128)(2,1)S(1)}, u32[]{:S(2)}, u32[]{:S(2)}) collective-permute-start(bf16[1024,128]{1,0:T(8,128)(2,1)S(1)} %pad_maximum_fusion.1), channel_id=1, source_target_pairs={{0,16},{4,20},{8,24},{12,28},{16,0},{20,4},{24,8},{28,12},{1,17},{... | collective-permute-start | bytes 786440 | tf_op jit(solution)/shard_map/ppermute | solution.py:388
  52.3 22.3 %collective-permute-start.15 = (bf16[2048,128]{1,0:T(8,128)(2,1)S(1)}, bf16[2048,128]{1,0:T(8,128)(2,1)S(1)}, u32[]{:S(2)}, u32[]{:S(2)}) collective-permute-start(bf16[2048,128]{1,0:T(8,128)(2,1)S(1)} %constant_dynamic-update-slice_fusion), channel_id=1, source_target_pairs={{0,8},{4,12},{8,0},{12,4},{16,24},{20,28},{24,16},{28,20},{1,9},{5... | collective-permute-start | bytes 1572872 | tf_op jit(solution)/shard_map/ppermute | solution.py:388
  54.6 5.5 %collective-permute-start.9 = (bf16[16,256]{1,0:T(8,128)(2,1)S(1)}, bf16[16,256]{1,0:T(8,128)(2,1)S(1)}, u32[]{:S(2)}, u32[]{:S(2)}) collective-permute-start(bf16[16,256]{1,0:T(8,128)(2,1)S(1)} %get-tuple-element.66), channel_id=1, source_target_pairs={{1,2},{2,1},{5,6},{6,5},{9,10},{10,9},{13,14},{14,13},{17,18},{18,... | collective-permute-start | bytes 24584 | tf_op jit(solution)/shard_map/ppermute | solution.py:343
  56.6 3.7 %collective-permute-start.8 = (bf16[16,256]{1,0:T(8,128)(2,1)S(1)}, bf16[16,256]{1,0:T(8,128)(2,1)S(1)}, u32[]{:S(2)}, u32[]{:S(2)}) collective-permute-start(bf16[16,256]{1,0:T(8,128)(2,1)S(1)} %get-tuple-element.67), channel_id=1, source_target_pairs={{0,1},{2,3},{1,0},{3,2},{4,5},{6,7},{5,4},{7,6},{8,9},{10,11},{9,8... | collective-permute-start | bytes 24584 | tf_op jit(solution)/shard_map/ppermute | solution.py:343
  60.2 0.6 copy-start.5
  60.3 0.6 copy-start.6
  60.3 1.0 copy-start.3
  60.3 1.3 %copy-start.4 = (bf16[256,2048]{1,0:T(8,128)(2,1)}, bf16[256,2048]{1,0:T(8,128)(2,1)S(1)}, u32[]{:S(2)}) copy-start(bf16[256,2048]{1,0:T(8,128)(2,1)S(1)} %collective-permute-done.6.far_hbm) | copy-start | bytes 3145732
  68.1 11.8 %copy-start = (bf16[49,4,16,128]{3,2,1,0:T(8,128)(2,1)S(1)}, bf16[49,4,16,128]{3,2,1,0:T(8,128)(2,1)}, u32[]{:S(2)}) copy-start(bf16[49,4,16,128]{3,2,1,0:T(8,128)(2,1)} %get-tuple-element.47.keep_hbm) | copy-start | bytes 2408452
  68.1 11.8 %copy-start.1 = (s32[48,2]{0,1:T(2,128)S(1)}, s32[48,2]{0,1:T(2,128)}, u32[]{:S(2)}) copy-start(s32[48,2]{0,1:T(2,128)} %param.8) | copy-start | bytes 1156
  68.1 26.9 %copy-start.2 = (s32[160]{0:T(256)S(1)}, s32[160]{0:T(256)}, u32[]{:S(2)}) copy-start(s32[160]{0:T(256)} %rules_ref.1) | copy-start | bytes 1924
  68.1 11.7 %collective-permute-start.10 = (bf16[49,4,16,128]{3,2,1,0:T(8,128)(2,1)}, bf16[49,4,16,128]{3,2,1,0:T(8,128)(2,1)S(1)}, u32[]{:S(2)}, u32[]{:S(2)}) collective-permute-start(bf16[49,4,16,128]{3,2,1,0:T(8,128)(2,1)} %get-tuple-element.48), channel_id=1, source_target_pairs={{0,4},{4,0},{8,12},{12,8},{16,20},{20,16},{24,28},{28,24},{1,5},{5... | collective-permute-start | bytes 2408456 | tf_op jit(solution)/shard_map/ppermute | solution.py:469
  68.2 8.4 %collective-permute-start.11 = (bf16[4,16,128]{2,1,0:T(8,128)(2,1)}, bf16[4,16,128]{2,1,0:T(8,128)(2,1)S(1)}, u32[]{:S(2)}, u32[]{:S(2)}) collective-permute-start(bf16[4,16,128]{2,1,0:T(8,128)(2,1)} %get-tuple-element.49), channel_id=1, source_target_pairs={{0,1},{2,3},{1,0},{3,2},{4,5},{6,7},{5,4},{7,6},{8,9},{10,11},{9,8... | collective-permute-start | bytes 49160 | tf_op jit(solution)/shard_map/ppermute | solution.py:475
  68.3 8.3 %collective-permute-start.12 = (bf16[4,16,128]{2,1,0:T(8,128)(2,1)}, bf16[4,16,128]{2,1,0:T(8,128)(2,1)S(1)}, u32[]{:S(2)}, u32[]{:S(2)}) collective-permute-start(bf16[4,16,128]{2,1,0:T(8,128)(2,1)} %get-tuple-element.50), channel_id=1, source_target_pairs={{0,5},{2,7},{1,4},{3,6},{4,1},{6,3},{5,0},{7,2},{8,13},{10,15},{9,... | collective-permute-start | bytes 49160 | tf_op jit(solution)/shard_map/ppermute | solution.py:475
  70.1 6.6 %collective-permute-start.13 = (bf16[4,16,128]{2,1,0:T(8,128)(2,1)}, bf16[4,16,128]{2,1,0:T(8,128)(2,1)S(1)}, u32[]{:S(2)}, u32[]{:S(2)}) collective-permute-start(bf16[4,16,128]{2,1,0:T(8,128)(2,1)} %get-tuple-element.51), channel_id=1, source_target_pairs={{1,2},{2,1},{5,6},{6,5},{9,10},{10,9},{13,14},{14,13},{17,18},{18,... | collective-permute-start | bytes 49160 | tf_op jit(solution)/shard_map/ppermute | solution.py:475
  74.6 5.3 %collective-permute-start.14 = (bf16[4,16,128]{2,1,0:T(8,128)(2,1)}, bf16[4,16,128]{2,1,0:T(8,128)(2,1)S(1)}, u32[]{:S(2)}, u32[]{:S(2)}) collective-permute-start(bf16[4,16,128]{2,1,0:T(8,128)(2,1)} %get-tuple-element.52), channel_id=1, source_target_pairs={{1,6},{2,5},{5,2},{6,1},{9,14},{10,13},{13,10},{14,9},{17,22},{18,... | collective-permute-start | bytes 49160 | tf_op jit(solution)/shard_map/ppermute | solution.py:475
  81.8 13.3 %collective-permute-start.19 = (bf16[4096,128]{1,0:T(8,128)(2,1)S(1)}, bf16[4096,128]{1,0:T(8,128)(2,1)S(1)}, u32[]{:S(2)}, u32[]{:S(2)}) collective-permute-start(bf16[4096,128]{1,0:T(8,128)(2,1)S(1)} %pad_maximum_fusion.refs_4_), channel_id=1, source_target_pairs={{0,4},{4,0},{8,12},{12,8},{16,20},{20,16},{24,28},{28,24},{1,5},{5... | collective-permute-start | bytes 3145736 | tf_op jit(solution)/shard_map/ppermute | solution.py:388
  82.0 8.1 %collective-permute-start.16 = (bf16[52,16,128]{2,1,0:T(8,128)(2,1)S(1)}, bf16[52,16,128]{2,1,0:T(8,128)(2,1)S(1)}, u32[]{:S(2)}, u32[]{:S(2)}) collective-permute-start(bf16[52,16,128]{2,1,0:T(8,128)(2,1)S(1)} %get-tuple-element.56), channel_id=1, source_target_pairs={{0,8},{4,12},{8,0},{12,4},{16,24},{20,28},{24,16},{28,20},{1,9},{5... | collective-permute-start | bytes 638984 | tf_op jit(solution)/shard_map/ppermute | solution.py:498
  82.5 11.8 %collective-permute-start.17 = (bf16[52,16,128]{2,1,0:T(8,128)(2,1)S(1)}, bf16[52,16,128]{2,1,0:T(8,128)(2,1)S(1)}, u32[]{:S(2)}, u32[]{:S(2)}) collective-permute-start(bf16[52,16,128]{2,1,0:T(8,128)(2,1)S(1)} %get-tuple-element.57), channel_id=1, source_target_pairs={{0,16},{4,20},{8,24},{12,28},{16,0},{20,4},{24,8},{28,12},{1,17},{... | collective-permute-start | bytes 638984 | tf_op jit(solution)/shard_map/ppermute | solution.py:498
  85.0 10.1 %collective-permute-start.18 = (bf16[52,16,128]{2,1,0:T(8,128)(2,1)S(1)}, bf16[52,16,128]{2,1,0:T(8,128)(2,1)S(1)}, u32[]{:S(2)}, u32[]{:S(2)}) collective-permute-start(bf16[52,16,128]{2,1,0:T(8,128)(2,1)S(1)} %get-tuple-element.58), channel_id=1, source_target_pairs={{0,24},{4,28},{8,16},{12,20},{16,8},{20,12},{24,0},{28,4},{1,25},{... | collective-permute-start | bytes 638984 | tf_op jit(solution)/shard_map/ppermute | solution.py:498

commit v10 on v8

--- a/solution.py
+++ b/solution.py
@@ -11,8 +11,7 @@
 TAPS = 5
 LANES = 128
 HALF = LANES // 2
-TILE = 2 * LANES
-DEPTH = 3 * LANES
+DEPTH = 2 * LANES
 VMEM_BYTES = 58 * 1024 * 1024
 
 
@@ -37,25 +36,24 @@
 
 def smooth_rows(x_ref, halo, w_ref, store):
     rows, width = x_ref.shape
-    tiles = width // TILE
+    tiles = width // LANES
     first = lax.broadcasted_iota(jnp.int32, (rows, LANES), 1) < HALF
-
-    def tile(j):
-        own = x_ref[:, j * TILE : (j + 1) * TILE]
-        before = halo if j == 0 else x_ref[:, j * TILE - LANES : j * TILE]
-        after = halo if j == tiles - 1 else x_ref[:, (j + 1) * TILE : (j + 1) * TILE + LANES]
-        window = jnp.concatenate([own, jnp.where(first, after, before)], axis=1)
-        return jnp.dot(window, w_ref[j], preferred_element_type=jnp.float32)
-
-    total = None
-    for j in range(0, tiles, 2):
-        squares = None
-        for k, values in enumerate([tile(j), tile(j + 1)]):
-            store(j + k, values.astype(jnp.bfloat16))
-            values = values * values
-            values = values[:, :LANES] + values[:, LANES:]
-            squares = values if k == 0 else squares + values
-        total = squares if j == 0 else total + squares
+    before, total, squares = None, None, None
+    for j in range(-1, tiles):
+        if j < 0:
+            window = jnp.concatenate([halo, x_ref[:, :LANES]], axis=1)
+        elif j == tiles - 1:
+            window = jnp.concatenate([x_ref[:, j * LANES :], halo], axis=1)
+        else:
+            window = x_ref[:, j * LANES : (j + 2) * LANES]
+        now = jnp.dot(window, w_ref[j + 1], preferred_element_type=jnp.float32)
+        if j >= 0:
+            values = jnp.where(first, before, now)
+            store(j, values.astype(jnp.bfloat16))
+            squares = values * values if j % 2 == 0 else squares + values * values
+            if j % 2 == 1:
+                total = squares if total is None else total + squares
+        before = now
     return total
 
 
@@ -76,20 +74,22 @@
 
 
 def write_weights(stencil_ref, out_ref):
+    tiles = stencil_ref.shape[1] // LANES
     out_ref[...] = jnp.zeros_like(out_ref)
-    strip = 16
-    places = [(0, LANES, 0, 2), (LANES, LANES, LANES, 2)]
-    places += [(LANES - strip, strip, LANES, 2), (LANES, strip, 0, 2)]
-    places += [(TILE + LANES - strip, strip, 0, 2 - LANES - TILE), (TILE, strip, LANES, 2)]
-    for k0, rows, n0, shift in places:
-        k = lax.broadcasted_iota(jnp.int32, (rows, LANES), 0) + k0
-        tap = k - lax.broadcasted_iota(jnp.int32, (rows, LANES), 1) - n0 + shift
-        for j in range(out_ref.shape[0]):
-            taps = stencil_ref[:, j * TILE + n0 : j * TILE + n0 + LANES]
-            w = jnp.zeros((rows, LANES), jnp.float32)
-            for t in range(TAPS):
-                w = jnp.where(tap == t, taps[t : t + 1, :], w)
-            out_ref[j, k0 : k0 + rows, n0 : n0 + LANES] = w.astype(jnp.bfloat16)
+    k0, rows = 3 * LANES // 8, 5 * LANES // 4
+    k = lax.broadcasted_iota(jnp.int32, (rows, LANES), 0) + k0
+    lane = lax.broadcasted_iota(jnp.int32, (rows, LANES), 1)
+    tap = k - lane + jnp.where(lane < HALF, 2 - LANES, 2)
+    early = lax.broadcasted_iota(jnp.int32, (TAPS, LANES), 1) < HALF
+    zeros = jnp.zeros((TAPS, LANES), jnp.float32)
+    for j in range(-1, tiles):
+        here = stencil_ref[:, j * LANES : (j + 1) * LANES] if j >= 0 else zeros
+        after = stencil_ref[:, (j + 1) * LANES : (j + 2) * LANES] if j + 1 < tiles else zeros
+        taps = jnp.where(early, after, here)
+        w = jnp.zeros((rows, LANES), jnp.float32)
+        for t in range(TAPS):
+            w = jnp.where(tap == t, taps[t : t + 1, :], w)
+        out_ref[j + 1, k0 : k0 + rows] = w.astype(jnp.bfloat16)
 
 
 def cut_kernel(images_ref, stencil_ref, near_rows, far_rows, near_columns, far_columns, w_ref, bands, strips, sems):
@@ -147,15 +147,16 @@
     @pl.when(step < steps)
     def smooth():
         def store(j, values):
-            held[pl.ds(step * group, group), :, j * TILE : (j + 1) * TILE] = values.reshape(group, block, TILE)
+            held[pl.ds(step * group, group), :, j * LANES : (j + 1) * LANES] = values.reshape(group, block, LANES)
 
         total = smooth_rows(x_ref, halo_tile(columns_ref), w_ref, store)
-        copy_out(step).start()
         for g in range(group):
             energy_ref[pl.ds(step * group + g, 1), :] = row_sums(total[g * block : (g + 1) * block, :])
 
     @pl.when(step == steps)
     def grams():
+        for k in range(steps):
+            copy_out(k).start()
         core = lax.axis_index("pix") % 2
         first = lax.axis_index("ion") * blocks
 
@@ -194,7 +195,7 @@
     table[...] = jnp.zeros_like(table)
     table[REACH : REACH + blocks, :] = energy_ref[...]
     def store(j, values):
-        other[:, j * TILE : (j + 1) * TILE] = values
+        other[:, j * LANES : (j + 1) * LANES] = values
 
     total = smooth_rows(x_ref, halo_tile(columns_ref), w_ref, store)
     for k in range(2 * REACH):
@@ -332,7 +333,7 @@
             edge_rows,
             edge_columns,
             edge_columns,
-            jax.ShapeDtypeStruct((width // TILE, DEPTH, TILE), jnp.bfloat16),
+            jax.ShapeDtypeStruct((width // LANES + 1, DEPTH, LANES), jnp.bfloat16),
         ],
         scratch_shapes=[
             pltpu.VMEM((2, edge, width), images.dtype),
@@ -350,6 +351,10 @@
     odd = pix % 2 == 1
     after, before = jnp.where(odd, far, near), jnp.where(odd, near, far)
     columns = jnp.concatenate([after, jnp.zeros((4, rows), images.dtype), before], axis=0)
+    first, last = columns[:, :edge], columns[:, rows - edge :]
+    odd = ion % 2 == 1
+    near_columns, far_columns = swapped("ion", n_ion, jnp.where(odd, first, last), jnp.where(odd, last, first))
+    columns, near_columns, far_columns = lax.optimization_barrier((columns, near_columns, far_columns))
 
     distances = [n_pix >> k for k in range(1, n_pix.bit_length())]
 
@@ -405,10 +410,7 @@
     )(table_pairs, images, columns, weights)
     smoothed = smoothed.reshape(rows, width)
 
-    energy, columns, mine = lax.optimization_barrier((energy, columns, mine))
-    first, last = columns[:, :edge], columns[:, rows - edge :]
-    odd = ion % 2 == 1
-    near_columns, far_columns = swapped("ion", n_ion, jnp.where(odd, first, last), jnp.where(odd, last, first))
+    energy, mine = lax.optimization_barrier((energy, mine))
     for distance in distances[1:-1]:
         mine = jnp.concatenate([mine, exchange(mine, distance)], axis=0)
 

time: 93.5 us -> 112 us (1.20)
  waiting for transfers between devices: 15.7 us -> 34.3 us
  starting transfers between devices: 20.4 us -> 23.3 us
  other arithmetic: 1.56 us -> 0.22 us
  Pallas kernels: 48.2 us -> 47 us
    ppermute x6, waiting for transfers between devices: 3.62 us -> 23 us  [swapped(): lax.ppermute(value, axis, both + [(j, i) for i, j in both])]
    ppermute x3, starting transfers between devices: 1.79 us -> 4.63 us  [exchange(): return lax.ppermute(value, 'pix', [(i, i ^ distance) for i in range(n_pix)])]
    pallas_call x1, Pallas kernels: 29.3 us -> 27.6 us  [on_device(): pl.pallas_call(functools.partial(main_kernel, steps, group, block), grid_...]
    unnamed x20 -> x22, local copies, waits for them, and re-layouts: 5.06 us -> 5.05 us
  transfers between devices with their start and end apart: 16 -> 16, of which waited for: 5 -> 5; matrix products, arithmetic and copies ran while one was open for 4% -> 2% of each run, Pallas kernels for 47% -> 38%
where the time goes in v10:
time: 112 us; the launch traced here: 111 us
  Pallas kernels  47 us (42%)
  waiting for transfers between devices  34.3 us (31%)
  starting transfers between devices  23.3 us (21%)
  local copies, waits for them, and re-layouts  5.16 us (5%)
  between operations  1.54 us (1%)
    pallas_call x1, Pallas kernels, on_device(): pl.pallas_call(functools.partial(main_kernel, steps, group, block), grid_...  27.6 us
    ppermute x6, waiting for transfers between devices, swapped(): lax.ppermute(value, axis, both + [(j, i) for i, j in both])  23 us
    ppermute x6, starting transfers between devices, swapped(): lax.ppermute(value, axis, both + [(j, i) for i, j in both])  11 us
    ppermute x3, waiting for transfers between devices, on_device(): lax.ppermute(m, 'pix', [(i, i ^ 2 * (d + 1)) for i in range(n_pix)])  8.9 us
    pallas_call x1, Pallas kernels, on_device(): pl.pallas_call(functools.partial(cross_kernel, blocks, block), in_specs=[...  8.77 us
    pallas_call x1, Pallas kernels, on_device(): pl.pallas_call(cut_kernel, in_specs=[hbm, vmem], out_specs=[hbm, hbm, vme...  5.89 us
    unnamed x22, local copies, waits for them, and re-layouts  5.05 us
    ppermute x3, starting transfers between devices, exchange(): return lax.ppermute(value, 'pix', [(i, i ^ distance) for i in range(n_pix)])  4.63 us
  transfers between devices with their start and end apart: 16, of which 5 were waited for; matrix products, arithmetic and copies ran while one was open for 2% of the time, Pallas kernels for 38%

profile of v10, /device:TPU:8, one launch (start us, length us, event | category | flops | bytes accessed | tf_op | source)
XLA Modules:
  0.0 111.5 jit_solution(756089536174364194)
XLA Ops:
  0.6 1.5 %constant_dynamic-update-slice_fusion.4 = (bf16[2048,128]{1,0:T(8,128)(2,1)}, bf16[256,128]{1,0:T(8,128)(2,1)S(1)}) fusion(bf16[2048,128]{1,0:T(8,128)(2,1)} %bitcast.8, s32[]{:T(128)S(6)} %select_n.40), kind=kLoop, calls=%fused_computation.9 | loop fusion | bytes 196612
  2.1 1.6 %collective-permute-start.2 = (bf16[256,128]{1,0:T(8,128)(2,1)S(1)}, bf16[256,128]{1,0:T(8,128)(2,1)S(1)}, u32[]{:S(2)}, u32[]{:S(2)}) collective-permute-start(bf16[256,128]{1,0:T(8,128)(2,1)S(1)} %get-tuple-element.57), channel_id=1, source_target_pairs={{0,3},{1,2},{2,1},{3,0},{4,7},{5,6},{6,5},{7,4},{8,11},{9,10},{10,... | collective-permute-start | bytes 196616 | tf_op jit(solution)/shard_map/ppermute | solution.py:323
  3.7 1.0 collective-permute-start.1
  4.7 1.5 %collective-permute-start = (bf16[256,128]{1,0:T(8,128)(2,1)S(1)}, bf16[256,128]{1,0:T(8,128)(2,1)S(1)}, u32[]{:S(2)}, u32[]{:S(2)}) collective-permute-start(bf16[256,128]{1,0:T(8,128)(2,1)S(1)} %get-tuple-element.57), channel_id=1, source_target_pairs={{0,1},{1,0},{2,3},{3,2},{4,5},{5,4},{6,7},{7,6},{8,9},{9,8},{10,11... | collective-permute-start | bytes 196616 | tf_op jit(solution)/shard_map/ppermute | solution.py:323
  6.2 5.9 %cut_edges.1 = (bf16[384,2048]{1,0:T(8,128)(2,1)}, bf16[384,2048]{1,0:T(8,128)(2,1)}, bf16[2,5120]{1,0:T(2,128)(2,1)}, bf16[2,5120]{1,0:T(2,128)(2,1)}, bf16[17,256,128]{2,1,0:T(8,128)(2,1)}) custom-call(bf16[5120,2048]{1,0:T(8,128)(2,1)} %x_ref.1, f32[5,2048]{1,0:T(8,128)} %stencil_ref.1), custom_call_target="tpu_custom_call" | custom-call | bytes 6291456 | tf_op jit(solution)/shard_map/cut_edges/pallas_call | solution.py:327
  12.1 0.6 collective-permute-start.7
  12.7 4.8 %collective-permute-start.8 = (bf16[384,2048]{1,0:T(8,128)(2,1)}, bf16[384,2048]{1,0:T(8,128)(2,1)S(1)}, u32[]{:S(2)}, u32[]{:S(2)}) collective-permute-start(bf16[384,2048]{1,0:T(8,128)(2,1)} %get-tuple-element.37), channel_id=1, source_target_pairs={{1,2},{2,1},{5,6},{6,5},{9,10},{10,9},{13,14},{14,13},{17,18},{18,... | collective-permute-start | bytes 4718600 | tf_op jit(solution)/shard_map/ppermute | solution.py:313
  17.6 0.1 pad.7.clone
  17.7 0.7 collective-permute-start.3
  18.3 2.9 %collective-permute-start.4 = (bf16[2,5120]{1,0:T(2,128)(2,1)}, bf16[2,5120]{1,0:T(2,128)(2,1)S(1)}, u32[]{:S(2)}, u32[]{:S(2)}) collective-permute-start(bf16[2,5120]{1,0:T(2,128)(2,1)} %get-tuple-element.32), channel_id=1, source_target_pairs={{0,4},{8,12},{16,20},{24,28},{4,0},{12,8},{20,16},{28,24},{1,5},{9... | collective-permute-start | bytes 61448 | tf_op jit(solution)/shard_map/ppermute | solution.py:313
  21.2 0.6 constant_dynamic-update-slice_fusion.3
  21.9 0.6 constant_dynamic-update-slice_fusion.2
  22.6 0.1 pad_maximum_fusion.2.columns_ref
  22.7 1.9 %collective-permute-start.6 = (bf16[8,384]{1,0:T(8,128)(2,1)S(1)}, bf16[8,384]{1,0:T(8,128)(2,1)S(1)}, u32[]{:S(2)}, u32[]{:S(2)}) collective-permute-start(bf16[8,384]{1,0:T(8,128)(2,1)S(1)} %get-tuple-element.58), channel_id=1, source_target_pairs={{1,2},{2,1},{5,6},{6,5},{9,10},{10,9},{13,14},{14,13},{17,18},{18,... | collective-permute-start | bytes 18440 | tf_op jit(solution)/shard_map/ppermute | solution.py:313
  24.7 0.6 constant_dynamic-update-slice_fusion.1
  25.3 2.9 %collective-permute-start.9 = (bf16[1024,128]{1,0:T(8,128)(2,1)S(1)}, bf16[1024,128]{1,0:T(8,128)(2,1)S(1)}, u32[]{:S(2)}, u32[]{:S(2)}) collective-permute-start(bf16[1024,128]{1,0:T(8,128)(2,1)S(1)} %pad_maximum_fusion.1), channel_id=1, source_target_pairs={{0,16},{4,20},{8,24},{12,28},{16,0},{20,4},{24,8},{28,12},{1,17},{... | collective-permute-start | bytes 786440 | tf_op jit(solution)/shard_map/ppermute | solution.py:362
  28.2 22.9 %collective-permute-done.6.far_columns_hbm = bf16[8,384]{1,0:T(8,128)(2,1)S(1)} collective-permute-done((bf16[8,384]{1,0:T(8,128)(2,1)S(1)}, bf16[8,384]{1,0:T(8,128)(2,1)S(1)}, u32[]{:S(2)}, u32[]{:S(2)}) %collective-permute-start.6) | collective-permute-done | bytes 6176 | tf_op jit(solution)/shard_map/ppermute | solution.py:313
  51.2 27.6 %smooth_and_gram.1 = (bf16[40,128,2048]{2,1,0:T(8,128)(2,1)}, f32[40,128]{1,0:T(8,128)}, bf16[49,4,16,128]{3,2,1,0:T(8,128)(2,1)}, bf16[49,4,16,128]{3,2,1,0:T(8,128)(2,1)}) custom-call(s32[2,48]{1,0:T(2,128)} %bitcast.3, bf16[5120,2048]{1,0:T(8,128)(2,1)} %x_ref.1, bf16[8,5120]{1,0:T(8,128)(2,1)} %copy-done.6, ...), custom_call_target="tpu_custom_call" | custom-call | flops 8589934592 | bytes 41943040 | tf_op jit(solution)/shard_map/smooth_and_gram/pallas_call | solution.py:389
  78.8 1.6 %collective-permute-start.11 = (bf16[2048,128]{1,0:T(8,128)(2,1)S(1)}, bf16[2048,128]{1,0:T(8,128)(2,1)S(1)}, u32[]{:S(2)}, u32[]{:S(2)}) collective-permute-start(bf16[2048,128]{1,0:T(8,128)(2,1)S(1)} %constant_dynamic-update-slice_fusion), channel_id=1, source_target_pairs={{0,8},{4,12},{8,0},{12,4},{16,24},{20,28},{24,16},{28,20},{1,9},{5... | collective-permute-start | bytes 1572872 | tf_op jit(solution)/shard_map/ppermute | solution.py:362
  80.4 1.1 %copy-done.3 = bf16[384,2048]{1,0:T(8,128)(2,1)} copy-done((bf16[384,2048]{1,0:T(8,128)(2,1)}, bf16[384,2048]{1,0:T(8,128)(2,1)S(1)}, u32[]{:S(2)}) %copy-start.3) | copy-done | bytes 1572888
  81.5 0.5 copy-done.4
  82.0 8.8 %cross_grams.1 = (bf16[49,4,16,128]{3,2,1,0:T(8,128)(2,1)}, bf16[49,4,16,128]{3,2,1,0:T(8,128)(2,1)}) custom-call(s32[2,48]{1,0:T(2,128)} %bitcast.4, bf16[384,2048]{1,0:T(8,128)(2,1)} %copy-done.3, bf16[384,2048]{1,0:T(8,128)(2,1)} %copy-done.4, bf16[8,384]{1,0:T(8,128)(2,1)} %copy-done.8, bf16[8,384]{1,0:T(8,128)(2,1)} %copy-done.7, ...), custom_call_target="tpu_custom_call" | custom-call | flops 805306368 | bytes 6291456 | tf_op jit(solution)/shard_map/cross_grams/pallas_call | solution.py:417
  91.0 2.4 %collective-permute-done.10.got_hbm = bf16[49,4,16,128]{3,2,1,0:T(8,128)(2,1)S(1)} collective-permute-done((bf16[49,4,16,128]{3,2,1,0:T(8,128)(2,1)}, bf16[49,4,16,128]{3,2,1,0:T(8,128)(2,1)S(1)}, u32[]{:S(2)}, u32[]{:S(2)}) %collective-permute-start.10) | collective-permute-done | bytes 802848 | tf_op jit(solution)/shard_map/ppermute | solution.py:437
  93.4 0.4 chip_sums.1
  93.8 0.2 collective-permute-start.15
  94.0 0.6 collective-permute-start.12
  94.6 1.5 %collective-permute-start.13 = (bf16[52,16,128]{2,1,0:T(8,128)(2,1)S(1)}, bf16[52,16,128]{2,1,0:T(8,128)(2,1)S(1)}, u32[]{:S(2)}, u32[]{:S(2)}) collective-permute-start(bf16[52,16,128]{2,1,0:T(8,128)(2,1)S(1)} %get-tuple-element.53), channel_id=1, source_target_pairs={{0,16},{4,20},{8,24},{12,28},{16,0},{20,4},{24,8},{28,12},{1,17},{... | collective-permute-start | bytes 638984 | tf_op jit(solution)/shard_map/ppermute | solution.py:457
  96.1 1.4 %collective-permute-start.14 = (bf16[52,16,128]{2,1,0:T(8,128)(2,1)S(1)}, bf16[52,16,128]{2,1,0:T(8,128)(2,1)S(1)}, u32[]{:S(2)}, u32[]{:S(2)}) collective-permute-start(bf16[52,16,128]{2,1,0:T(8,128)(2,1)S(1)} %get-tuple-element.54), channel_id=1, source_target_pairs={{0,24},{4,28},{8,16},{12,20},{16,8},{20,12},{24,0},{28,4},{1,25},{... | collective-permute-start | bytes 638984 | tf_op jit(solution)/shard_map/ppermute | solution.py:457
  98.2 3.9 %collective-permute-done.12.refs_1_ = bf16[52,16,128]{2,1,0:T(8,128)(2,1)S(1)} collective-permute-done((bf16[52,16,128]{2,1,0:T(8,128)(2,1)S(1)}, bf16[52,16,128]{2,1,0:T(8,128)(2,1)S(1)}, u32[]{:S(2)}, u32[]{:S(2)}) %collective-permute-start.12) | collective-permute-done | bytes 213024 | tf_op jit(solution)/shard_map/ppermute | solution.py:457
  102.1 3.3 %collective-permute-done.13.refs_2_ = bf16[52,16,128]{2,1,0:T(8,128)(2,1)S(1)} collective-permute-done((bf16[52,16,128]{2,1,0:T(8,128)(2,1)S(1)}, bf16[52,16,128]{2,1,0:T(8,128)(2,1)S(1)}, u32[]{:S(2)}, u32[]{:S(2)}) %collective-permute-start.13) | collective-permute-done | bytes 213024 | tf_op jit(solution)/shard_map/ppermute | solution.py:457
  105.4 1.6 %collective-permute-done.14.refs_3_ = bf16[52,16,128]{2,1,0:T(8,128)(2,1)S(1)} collective-permute-done((bf16[52,16,128]{2,1,0:T(8,128)(2,1)S(1)}, bf16[52,16,128]{2,1,0:T(8,128)(2,1)S(1)}, u32[]{:S(2)}, u32[]{:S(2)}) %collective-permute-start.14) | collective-permute-done | bytes 213024 | tf_op jit(solution)/shard_map/ppermute | solution.py:457
  107.1 4.4 %scores.1 = bf16[48,16,128]{2,1,0:T(8,128)(2,1)} custom-call(s32[2,48]{1,0:T(2,128)S(1)} %bitcast.5, s32[1]{0:T(128)S(6)} %copy.12.live_ref, s32[160]{0:T(256)S(1)} %copy-done.2, f32[52,16,128]{2,1,0:T(8,128)S(1)} %get-tuple-element.51.refs_0_, bf16[52,16,128]{2,1,0:T(8,128)(2,1)S(1)} %collective-permute-done.12.refs_1_, ...), custom_call_target="tpu_custom_call" | custom-call | tf_op jit(solution)/shard_map/scores/pallas_call | solution.py:460
  (35 shorter events, 0.4 us)
Async XLA Ops:
  2.1 15.5 %collective-permute-start.2 = (bf16[256,128]{1,0:T(8,128)(2,1)S(1)}, bf16[256,128]{1,0:T(8,128)(2,1)S(1)}, u32[]{:S(2)}, u32[]{:S(2)}) collective-permute-start(bf16[256,128]{1,0:T(8,128)(2,1)S(1)} %get-tuple-element.57), channel_id=1, source_target_pairs={{0,3},{1,2},{2,1},{3,0},{4,7},{5,6},{6,5},{7,4},{8,11},{9,10},{10,... | collective-permute-start | bytes 196616 | tf_op jit(solution)/shard_map/ppermute | solution.py:323
  3.7 14.0 %collective-permute-start.1 = (bf16[256,128]{1,0:T(8,128)(2,1)S(1)}, bf16[256,128]{1,0:T(8,128)(2,1)S(1)}, u32[]{:S(2)}, u32[]{:S(2)}) collective-permute-start(bf16[256,128]{1,0:T(8,128)(2,1)S(1)} %get-tuple-element.57), channel_id=1, source_target_pairs={{0,2},{1,3},{2,0},{3,1},{4,6},{5,7},{6,4},{7,5},{8,10},{9,11},{10,... | collective-permute-start | bytes 196616 | tf_op jit(solution)/shard_map/ppermute | solution.py:323
  4.7 12.9 %collective-permute-start = (bf16[256,128]{1,0:T(8,128)(2,1)S(1)}, bf16[256,128]{1,0:T(8,128)(2,1)S(1)}, u32[]{:S(2)}, u32[]{:S(2)}) collective-permute-start(bf16[256,128]{1,0:T(8,128)(2,1)S(1)} %get-tuple-element.57), channel_id=1, source_target_pairs={{0,1},{1,0},{2,3},{3,2},{4,5},{5,4},{6,7},{7,6},{8,9},{9,8},{10,11... | collective-permute-start | bytes 196616 | tf_op jit(solution)/shard_map/ppermute | solution.py:323
  12.1 68.3 %collective-permute-start.7 = (bf16[384,2048]{1,0:T(8,128)(2,1)}, bf16[384,2048]{1,0:T(8,128)(2,1)S(1)}, u32[]{:S(2)}, u32[]{:S(2)}) collective-permute-start(bf16[384,2048]{1,0:T(8,128)(2,1)} %get-tuple-element.36), channel_id=1, source_target_pairs={{0,1},{2,3},{1,0},{3,2},{4,5},{6,7},{5,4},{7,6},{8,9},{10,11},{9,8... | collective-permute-start | bytes 4718600 | tf_op jit(solution)/shard_map/ppermute | solution.py:313
  12.7 67.7 %collective-permute-start.8 = (bf16[384,2048]{1,0:T(8,128)(2,1)}, bf16[384,2048]{1,0:T(8,128)(2,1)S(1)}, u32[]{:S(2)}, u32[]{:S(2)}) collective-permute-start(bf16[384,2048]{1,0:T(8,128)(2,1)} %get-tuple-element.37), channel_id=1, source_target_pairs={{1,2},{2,1},{5,6},{6,5},{9,10},{10,9},{13,14},{14,13},{17,18},{18,... | collective-permute-start | bytes 4718600 | tf_op jit(solution)/shard_map/ppermute | solution.py:313
  17.7 4.9 %collective-permute-start.3 = (bf16[2,5120]{1,0:T(2,128)(2,1)}, bf16[2,5120]{1,0:T(2,128)(2,1)S(1)}, u32[]{:S(2)}, u32[]{:S(2)}) collective-permute-start(bf16[2,5120]{1,0:T(2,128)(2,1)} %get-tuple-element.31), channel_id=1, source_target_pairs={{4,8},{12,16},{20,24},{8,4},{16,12},{24,20},{5,9},{13,17},{21,25},... | collective-permute-start | bytes 61448 | tf_op jit(solution)/shard_map/ppermute | solution.py:313
  18.3 4.2 %collective-permute-start.4 = (bf16[2,5120]{1,0:T(2,128)(2,1)}, bf16[2,5120]{1,0:T(2,128)(2,1)S(1)}, u32[]{:S(2)}, u32[]{:S(2)}) collective-permute-start(bf16[2,5120]{1,0:T(2,128)(2,1)} %get-tuple-element.32), channel_id=1, source_target_pairs={{0,4},{8,12},{16,20},{24,28},{4,0},{12,8},{20,16},{28,24},{1,5},{9... | collective-permute-start | bytes 61448 | tf_op jit(solution)/shard_map/ppermute | solution.py:313
  22.7 28.5 %copy-start.6 = (bf16[8,5120]{1,0:T(8,128)(2,1)}, bf16[8,5120]{1,0:T(8,128)(2,1)S(1)}, u32[]{:S(2)}) copy-start(bf16[8,5120]{1,0:T(8,128)(2,1)S(1)} %pad_maximum_fusion.2.columns_ref) | copy-start | bytes 245764
  22.7 28.5 %collective-permute-start.6 = (bf16[8,384]{1,0:T(8,128)(2,1)S(1)}, bf16[8,384]{1,0:T(8,128)(2,1)S(1)}, u32[]{:S(2)}, u32[]{:S(2)}) collective-permute-start(bf16[8,384]{1,0:T(8,128)(2,1)S(1)} %get-tuple-element.58), channel_id=1, source_target_pairs={{1,2},{2,1},{5,6},{6,5},{9,10},{10,9},{13,14},{14,13},{17,18},{18,... | collective-permute-start | bytes 18440 | tf_op jit(solution)/shard_map/ppermute | solution.py:313
  24.6 26.5 %collective-permute-start.5 = (bf16[8,384]{1,0:T(8,128)(2,1)S(1)}, bf16[8,384]{1,0:T(8,128)(2,1)S(1)}, u32[]{:S(2)}, u32[]{:S(2)}) collective-permute-start(bf16[8,384]{1,0:T(8,128)(2,1)S(1)} %get-tuple-element.59), channel_id=1, source_target_pairs={{0,1},{2,3},{1,0},{3,2},{4,5},{6,7},{5,4},{7,6},{8,9},{10,11},{9,8... | collective-permute-start | bytes 18440 | tf_op jit(solution)/shard_map/ppermute | solution.py:313
  25.3 53.4 %collective-permute-start.9 = (bf16[1024,128]{1,0:T(8,128)(2,1)S(1)}, bf16[1024,128]{1,0:T(8,128)(2,1)S(1)}, u32[]{:S(2)}, u32[]{:S(2)}) collective-permute-start(bf16[1024,128]{1,0:T(8,128)(2,1)S(1)} %pad_maximum_fusion.1), channel_id=1, source_target_pairs={{0,16},{4,20},{8,24},{12,28},{16,0},{20,4},{24,8},{28,12},{1,17},{... | collective-permute-start | bytes 786440 | tf_op jit(solution)/shard_map/ppermute | solution.py:362
  51.1 27.6 %copy-start.7 = (bf16[8,384]{1,0:T(8,128)(2,1)}, bf16[8,384]{1,0:T(8,128)(2,1)S(1)}, u32[]{:S(2)}) copy-start(bf16[8,384]{1,0:T(8,128)(2,1)S(1)} %collective-permute-done.6.far_columns_hbm) | copy-start | bytes 18436
  51.1 27.6 %copy-start.8 = (bf16[8,384]{1,0:T(8,128)(2,1)}, bf16[8,384]{1,0:T(8,128)(2,1)S(1)}, u32[]{:S(2)}) copy-start(bf16[8,384]{1,0:T(8,128)(2,1)S(1)} %collective-permute-done.5.near_columns_hbm) | copy-start | bytes 18436
  51.1 27.6 %copy-start.5 = (bf16[2048,128]{1,0:T(8,128)(2,1)S(1)}, bf16[2048,128]{1,0:T(8,128)(2,1)}, u32[]{:S(2)}) copy-start(bf16[2048,128]{1,0:T(8,128)(2,1)} %constant_dynamic-update-slice_fusion.1) | copy-start | bytes 1572868
  78.8 12.1 %collective-permute-start.11 = (bf16[2048,128]{1,0:T(8,128)(2,1)S(1)}, bf16[2048,128]{1,0:T(8,128)(2,1)S(1)}, u32[]{:S(2)}, u32[]{:S(2)}) collective-permute-start(bf16[2048,128]{1,0:T(8,128)(2,1)S(1)} %constant_dynamic-update-slice_fusion), channel_id=1, source_target_pairs={{0,8},{4,12},{8,0},{12,4},{16,24},{20,28},{24,16},{28,20},{1,9},{5... | collective-permute-start | bytes 1572872 | tf_op jit(solution)/shard_map/ppermute | solution.py:362
  80.4 1.2 %copy-start.3 = (bf16[384,2048]{1,0:T(8,128)(2,1)}, bf16[384,2048]{1,0:T(8,128)(2,1)S(1)}, u32[]{:S(2)}) copy-start(bf16[384,2048]{1,0:T(8,128)(2,1)S(1)} %collective-permute-done.7.near_hbm) | copy-start | bytes 4718596
  80.4 1.7 %copy-start.4 = (bf16[384,2048]{1,0:T(8,128)(2,1)}, bf16[384,2048]{1,0:T(8,128)(2,1)S(1)}, u32[]{:S(2)}) copy-start(bf16[384,2048]{1,0:T(8,128)(2,1)S(1)} %collective-permute-done.8.far_hbm) | copy-start | bytes 4718596
  90.8 2.6 %copy-start = (bf16[49,4,16,128]{3,2,1,0:T(8,128)(2,1)S(1)}, bf16[49,4,16,128]{3,2,1,0:T(8,128)(2,1)}, u32[]{:S(2)}) copy-start(bf16[49,4,16,128]{3,2,1,0:T(8,128)(2,1)} %get-tuple-element.47.keep_hbm) | copy-start | bytes 2408452
  90.8 16.3 %copy-start.1 = (s32[48,2]{0,1:T(2,128)S(1)}, s32[48,2]{0,1:T(2,128)}, u32[]{:S(2)}) copy-start(s32[48,2]{0,1:T(2,128)} %param.8) | copy-start | bytes 1156
  90.8 16.2 %copy-start.2 = (s32[160]{0:T(256)S(1)}, s32[160]{0:T(256)}, u32[]{:S(2)}) copy-start(s32[160]{0:T(256)} %rules_ref.1) | copy-start | bytes 1924
  90.8 2.6 %collective-permute-start.10 = (bf16[49,4,16,128]{3,2,1,0:T(8,128)(2,1)}, bf16[49,4,16,128]{3,2,1,0:T(8,128)(2,1)S(1)}, u32[]{:S(2)}, u32[]{:S(2)}) collective-permute-start(bf16[49,4,16,128]{3,2,1,0:T(8,128)(2,1)} %get-tuple-element.48), channel_id=1, source_target_pairs={{0,4},{4,0},{8,12},{12,8},{16,20},{20,16},{24,28},{28,24},{1,5},{5... | collective-permute-start | bytes 2408456 | tf_op jit(solution)/shard_map/ppermute | solution.py:437
  93.8 13.3 %collective-permute-start.15 = (bf16[4096,128]{1,0:T(8,128)(2,1)S(1)}, bf16[4096,128]{1,0:T(8,128)(2,1)S(1)}, u32[]{:S(2)}, u32[]{:S(2)}) collective-permute-start(bf16[4096,128]{1,0:T(8,128)(2,1)S(1)} %pad_maximum_fusion.refs_4_), channel_id=1, source_target_pairs={{0,4},{4,0},{8,12},{12,8},{16,20},{20,16},{24,28},{28,24},{1,5},{5... | collective-permute-start | bytes 3145736 | tf_op jit(solution)/shard_map/ppermute | solution.py:362
  94.0 8.1 %collective-permute-start.12 = (bf16[52,16,128]{2,1,0:T(8,128)(2,1)S(1)}, bf16[52,16,128]{2,1,0:T(8,128)(2,1)S(1)}, u32[]{:S(2)}, u32[]{:S(2)}) collective-permute-start(bf16[52,16,128]{2,1,0:T(8,128)(2,1)S(1)} %get-tuple-element.52), channel_id=1, source_target_pairs={{0,8},{4,12},{8,0},{12,4},{16,24},{20,28},{24,16},{28,20},{1,9},{5... | collective-permute-start | bytes 638984 | tf_op jit(solution)/shard_map/ppermute | solution.py:457
  94.6 10.9 %collective-permute-start.13 = (bf16[52,16,128]{2,1,0:T(8,128)(2,1)S(1)}, bf16[52,16,128]{2,1,0:T(8,128)(2,1)S(1)}, u32[]{:S(2)}, u32[]{:S(2)}) collective-permute-start(bf16[52,16,128]{2,1,0:T(8,128)(2,1)S(1)} %get-tuple-element.53), channel_id=1, source_target_pairs={{0,16},{4,20},{8,24},{12,28},{16,0},{20,4},{24,8},{28,12},{1,17},{... | collective-permute-start | bytes 638984 | tf_op jit(solution)/shard_map/ppermute | solution.py:457
  96.1 11.0 %collective-permute-start.14 = (bf16[52,16,128]{2,1,0:T(8,128)(2,1)S(1)}, bf16[52,16,128]{2,1,0:T(8,128)(2,1)S(1)}, u32[]{:S(2)}, u32[]{:S(2)}) collective-permute-start(bf16[52,16,128]{2,1,0:T(8,128)(2,1)S(1)} %get-tuple-element.54), channel_id=1, source_target_pairs={{0,24},{4,28},{8,16},{12,20},{16,8},{20,12},{24,0},{28,4},{1,25},{... | collective-permute-start | bytes 638984 | tf_op jit(solution)/shard_map/ppermute | solution.py:457

commit v11 on v10

--- a/solution.py
+++ b/solution.py
@@ -347,6 +347,7 @@
     near_rows, far_rows = swapped("ion", n_ion, near_rows, far_rows)
     near, far, *turns = lax.optimization_barrier((near, far, *turns))
     mine = jnp.concatenate([mine, *turns], axis=0)
+    near, far, mine = lax.optimization_barrier((near, far, mine))
     near, far = swapped("pix", n_pix, near, far)
     odd = pix % 2 == 1
     after, before = jnp.where(odd, far, near), jnp.where(odd, near, far)
@@ -354,14 +355,14 @@
     first, last = columns[:, :edge], columns[:, rows - edge :]
     odd = ion % 2 == 1
     near_columns, far_columns = swapped("ion", n_ion, jnp.where(odd, first, last), jnp.where(odd, last, first))
-    columns, near_columns, far_columns = lax.optimization_barrier((columns, near_columns, far_columns))
 
     distances = [n_pix >> k for k in range(1, n_pix.bit_length())]
 
     def exchange(value, distance):
         return lax.ppermute(value, "pix", [(i, i ^ distance) for i in range(n_pix)])
 
-    mine = jnp.concatenate([mine, exchange(mine, distances[0])], axis=0)
+    for distance in distances[:-1]:
+        mine = jnp.concatenate([mine, exchange(mine, distance)], axis=0)
 
     def place_of(rule):
         row = (rule & (rules_here - 1)) * block
@@ -410,9 +411,6 @@
     )(table_pairs, images, columns, weights)
     smoothed = smoothed.reshape(rows, width)
 
-    energy, mine = lax.optimization_barrier((energy, mine))
-    for distance in distances[1:-1]:
-        mine = jnp.concatenate([mine, exchange(mine, distance)], axis=0)
 
     keep, give = pl.pallas_call(
         functools.partial(cross_kernel, blocks, block),

time: 112 us -> 87.2 us (0.78)
  waiting for transfers between devices: 34.3 us -> 14.7 us
  local copies, waits for them, and re-layouts: 5.16 us -> 2.29 us
  starting transfers between devices: 23.3 us -> 21.9 us
    ppermute x6, waiting for transfers between devices: 23 us -> 0.02 us  [swapped(): lax.ppermute(value, axis, both + [(j, i) for i, j in both])]
    ppermute x3, waiting for transfers between devices: 0.01 us -> 4.04 us  [exchange(): return lax.ppermute(value, 'pix', [(i, i ^ distance) for i in range(n_pix)])]
    unnamed x22 -> x16, local copies, waits for them, and re-layouts: 5.05 us -> 2.2 us
    ppermute x3, starting transfers between devices: 4.63 us -> 3.28 us  [exchange(): return lax.ppermute(value, 'pix', [(i, i ^ distance) for i in range(n_pix)])]
  transfers between devices with their start and end apart: 16 -> 16, of which waited for: 5 -> 4; matrix products, arithmetic and copies ran while one was open for 2% -> 0% of each run, Pallas kernels for 38% -> 48%
where the time goes in v11:
time: 87.2 us; the launch traced here: 86.6 us
  Pallas kernels  46 us (53%)
  starting transfers between devices  21.9 us (25%)
  waiting for transfers between devices  14.7 us (17%)
  local copies, waits for them, and re-layouts  2.29 us (3%)
  between operations  1.58 us (2%)
    pallas_call x1, Pallas kernels, on_device(): pl.pallas_call(functools.partial(main_kernel, steps, group, block), grid_...  27.4 us
    ppermute x6, starting transfers between devices, swapped(): lax.ppermute(value, axis, both + [(j, i) for i, j in both])  11.5 us
    ppermute x3, waiting for transfers between devices, on_device(): lax.ppermute(m, 'pix', [(i, i ^ 2 * (d + 1)) for i in range(n_pix)])  8.19 us
    pallas_call x1, Pallas kernels, on_device(): pl.pallas_call(functools.partial(cross_kernel, blocks, block), in_specs=[...  7.85 us
    pallas_call x1, Pallas kernels, on_device(): pl.pallas_call(cut_kernel, in_specs=[hbm, vmem], out_specs=[hbm, hbm, vme...  5.91 us
    pallas_call x1, Pallas kernels, on_device(): pl.pallas_call(functools.partial(score_kernel, blocks, place_of, pixel_co...  4.39 us
    ppermute x3, waiting for transfers between devices, exchange(): return lax.ppermute(value, 'pix', [(i, i ^ distance) for i in range(n_pix)])  4.04 us
    ppermute x3, starting transfers between devices, on_device(): lax.ppermute(m, 'pix', [(i, i ^ 2 * (d + 1)) for i in range(n_pix)])  3.5 us
  transfers between devices with their start and end apart: 16, of which 4 were waited for; matrix products, arithmetic and copies ran while one was open for 0% of the time, Pallas kernels for 48%

profile of v11, /device:TPU:8, one launch (start us, length us, event | category | flops | bytes accessed | tf_op | source)
XLA Modules:
  0.0 86.6 jit_solution(8563795517949794829)
XLA Ops:
  0.6 0.0 copy-start
  0.7 1.0 %copy-done = bf16[16,128,128]{2,1,0:T(8,128)(2,1)S(1)} copy-done((bf16[16,128,128]{2,1,0:T(8,128)(2,1)S(1)}, bf16[16,128,128]{2,1,0:T(8,128)(2,1)}, u32[]{:S(2)}) %copy-start) | copy-done | bytes 524312
  1.7 3.0 %collective-permute-start.1 = (bf16[256,128]{1,0:T(8,128)(2,1)S(1)}, bf16[256,128]{1,0:T(8,128)(2,1)S(1)}, u32[]{:S(2)}, u32[]{:S(2)}) collective-permute-start(bf16[256,128]{1,0:T(8,128)(2,1)S(1)} %constant_dynamic-slice_fusion), channel_id=1, source_target_pairs={{0,2},{1,3},{2,0},{3,1},{4,6},{5,7},{6,4},{7,5},{8,10},{9,11},{10,... | collective-permute-start | bytes 196616 | tf_op jit(solution)/shard_map/ppermute | solution.py:323
  4.7 0.5 collective-permute-start.2
  5.2 5.9 %cut_edges.1 = (bf16[384,2048]{1,0:T(8,128)(2,1)}, bf16[384,2048]{1,0:T(8,128)(2,1)}, bf16[2,5120]{1,0:T(2,128)(2,1)}, bf16[2,5120]{1,0:T(2,128)(2,1)}, bf16[17,256,128]{2,1,0:T(8,128)(2,1)}) custom-call(bf16[5120,2048]{1,0:T(8,128)(2,1)} %x_ref.1, f32[5,2048]{1,0:T(8,128)} %stencil_ref.1), custom_call_target="tpu_custom_call" | custom-call | bytes 6291456 | tf_op jit(solution)/shard_map/cut_edges/pallas_call | solution.py:327
  11.1 0.7 collective-permute-start.3
  11.8 2.9 %collective-permute-start.4 = (bf16[2,5120]{1,0:T(2,128)(2,1)}, bf16[2,5120]{1,0:T(2,128)(2,1)S(1)}, u32[]{:S(2)}, u32[]{:S(2)}) collective-permute-start(bf16[2,5120]{1,0:T(2,128)(2,1)} %get-tuple-element.35), channel_id=1, source_target_pairs={{0,4},{8,12},{16,20},{24,28},{4,0},{12,8},{20,16},{28,24},{1,5},{9... | collective-permute-start | bytes 61448 | tf_op jit(solution)/shard_map/ppermute | solution.py:313
  14.7 1.3 %collective-permute-start.5 = (bf16[384,2048]{1,0:T(8,128)(2,1)}, bf16[384,2048]{1,0:T(8,128)(2,1)S(1)}, u32[]{:S(2)}, u32[]{:S(2)}) collective-permute-start(bf16[384,2048]{1,0:T(8,128)(2,1)} %get-tuple-element.38), channel_id=1, source_target_pairs={{0,1},{2,3},{1,0},{3,2},{4,5},{6,7},{5,4},{7,6},{8,9},{10,11},{9,8... | collective-permute-start | bytes 4718600 | tf_op jit(solution)/shard_map/ppermute | solution.py:313
  16.1 4.6 %collective-permute-start.6 = (bf16[384,2048]{1,0:T(8,128)(2,1)}, bf16[384,2048]{1,0:T(8,128)(2,1)}, u32[]{:S(2)}, u32[]{:S(2)}) collective-permute-start(bf16[384,2048]{1,0:T(8,128)(2,1)} %get-tuple-element.39), channel_id=1, source_target_pairs={{1,2},{2,1},{5,6},{6,5},{9,10},{10,9},{13,14},{14,13},{17,18},{18,... | collective-permute-start | bytes 4718600 | tf_op jit(solution)/shard_map/ppermute | solution.py:313
  20.7 0.1 pad.6.clone
  20.8 1.5 %collective-permute-start.10 = (bf16[1024,128]{1,0:T(8,128)(2,1)S(1)}, bf16[1024,128]{1,0:T(8,128)(2,1)S(1)}, u32[]{:S(2)}, u32[]{:S(2)}) collective-permute-start(bf16[1024,128]{1,0:T(8,128)(2,1)S(1)} %pad_maximum_fusion.2), channel_id=1, source_target_pairs={{0,16},{4,20},{8,24},{12,28},{16,0},{20,4},{24,8},{28,12},{1,17},{... | collective-permute-start | bytes 786440 | tf_op jit(solution)/shard_map/ppermute | solution.py:362
  22.4 0.1 pad_maximum_fusion.3.columns_ref
  22.5 0.1 collective-permute-start.7
  22.6 1.9 %collective-permute-start.8 = (bf16[8,384]{1,0:T(8,128)(2,1)S(1)}, bf16[8,384]{1,0:T(8,128)(2,1)S(1)}, u32[]{:S(2)}, u32[]{:S(2)}) collective-permute-start(bf16[8,384]{1,0:T(8,128)(2,1)S(1)} %get-tuple-element.52), channel_id=1, source_target_pairs={{1,2},{2,1},{5,6},{6,5},{9,10},{10,9},{13,14},{14,13},{17,18},{18,... | collective-permute-start | bytes 18440 | tf_op jit(solution)/shard_map/ppermute | solution.py:313
  24.5 4.0 %collective-permute-done.10 = bf16[1024,128]{1,0:T(8,128)(2,1)S(1)} collective-permute-done((bf16[1024,128]{1,0:T(8,128)(2,1)S(1)}, bf16[1024,128]{1,0:T(8,128)(2,1)S(1)}, u32[]{:S(2)}, u32[]{:S(2)}) %collective-permute-start.10) | collective-permute-done | bytes 262176 | tf_op jit(solution)/shard_map/ppermute | solution.py:362
  28.6 1.6 %collective-permute-start.11 = (bf16[2048,128]{1,0:T(8,128)(2,1)S(1)}, bf16[2048,128]{1,0:T(8,128)(2,1)S(1)}, u32[]{:S(2)}, u32[]{:S(2)}) collective-permute-start(bf16[2048,128]{1,0:T(8,128)(2,1)S(1)} %pad_maximum_fusion.1), channel_id=1, source_target_pairs={{0,8},{4,12},{8,0},{12,4},{16,24},{20,28},{24,16},{28,20},{1,9},{5... | collective-permute-start | bytes 1572872 | tf_op jit(solution)/shard_map/ppermute | solution.py:362
  30.1 27.4 %smooth_and_gram.1 = (bf16[40,128,2048]{2,1,0:T(8,128)(2,1)}, f32[40,128]{1,0:T(8,128)}, bf16[49,4,16,128]{3,2,1,0:T(8,128)(2,1)}, bf16[49,4,16,128]{3,2,1,0:T(8,128)(2,1)}) custom-call(s32[2,48]{1,0:T(2,128)} %bitcast.4, bf16[5120,2048]{1,0:T(8,128)(2,1)} %x_ref.1, bf16[8,5120]{1,0:T(8,128)(2,1)} %copy-done.5, ...), custom_call_target="tpu_custom_call" | custom-call | flops 8589934592 | bytes 41943040 | tf_op jit(solution)/shard_map/smooth_and_gram/pallas_call | solution.py:390
  57.6 0.5 copy-done.6
  58.2 0.0 copy-done.7
  58.2 0.6 copy-done.4
  58.8 7.8 %cross_grams.1 = (bf16[49,4,16,128]{3,2,1,0:T(8,128)(2,1)}, bf16[49,4,16,128]{3,2,1,0:T(8,128)(2,1)}) custom-call(s32[2,48]{1,0:T(2,128)} %bitcast.5, bf16[384,2048]{1,0:T(8,128)(2,1)} %copy-done.4, bf16[384,2048]{1,0:T(8,128)(2,1)} %collective-permute-done.6.far_hbm, bf16[8,384]{1,0:T(8,128)(2,1)} %copy-done.6, bf16[8,384]{1,0:T(8,128)(2,1)} %copy-done.7, ...), custom_call_target="tpu_custom_call" | custom-call | flops 805306368 | bytes 6291456 | tf_op jit(solution)/shard_map/cross_grams/pallas_call | solution.py:415
  66.7 0.1 collective-permute-start.9
  66.8 0.1 pad_maximum_fusion.refs_4_
  66.8 2.4 %collective-permute-done.9.got_hbm = bf16[49,4,16,128]{3,2,1,0:T(8,128)(2,1)S(1)} collective-permute-done((bf16[49,4,16,128]{3,2,1,0:T(8,128)(2,1)}, bf16[49,4,16,128]{3,2,1,0:T(8,128)(2,1)S(1)}, u32[]{:S(2)}, u32[]{:S(2)}) %collective-permute-start.9) | collective-permute-done | bytes 802848 | tf_op jit(solution)/shard_map/ppermute | solution.py:435
  69.3 0.4 chip_sums.1
  69.6 0.2 collective-permute-start.15
  69.8 0.5 collective-permute-start.12
  70.4 1.5 %collective-permute-start.13 = (bf16[52,16,128]{2,1,0:T(8,128)(2,1)S(1)}, bf16[52,16,128]{2,1,0:T(8,128)(2,1)S(1)}, u32[]{:S(2)}, u32[]{:S(2)}) collective-permute-start(bf16[52,16,128]{2,1,0:T(8,128)(2,1)S(1)} %get-tuple-element.49), channel_id=1, source_target_pairs={{0,16},{4,20},{8,24},{12,28},{16,0},{20,4},{24,8},{28,12},{1,17},{... | collective-permute-start | bytes 638984 | tf_op jit(solution)/shard_map/ppermute | solution.py:455
  71.9 1.4 %collective-permute-start.14 = (bf16[52,16,128]{2,1,0:T(8,128)(2,1)S(1)}, bf16[52,16,128]{2,1,0:T(8,128)(2,1)S(1)}, u32[]{:S(2)}, u32[]{:S(2)}) collective-permute-start(bf16[52,16,128]{2,1,0:T(8,128)(2,1)S(1)} %get-tuple-element.50), channel_id=1, source_target_pairs={{0,24},{4,28},{8,16},{12,20},{16,8},{20,12},{24,0},{28,4},{1,25},{... | collective-permute-start | bytes 638984 | tf_op jit(solution)/shard_map/ppermute | solution.py:455
  74.0 3.9 %collective-permute-done.12.refs_1_ = bf16[52,16,128]{2,1,0:T(8,128)(2,1)S(1)} collective-permute-done((bf16[52,16,128]{2,1,0:T(8,128)(2,1)S(1)}, bf16[52,16,128]{2,1,0:T(8,128)(2,1)S(1)}, u32[]{:S(2)}, u32[]{:S(2)}) %collective-permute-start.12) | collective-permute-done | bytes 213024 | tf_op jit(solution)/shard_map/ppermute | solution.py:455
  77.9 4.3 %collective-permute-done.13.refs_2_ = bf16[52,16,128]{2,1,0:T(8,128)(2,1)S(1)} collective-permute-done((bf16[52,16,128]{2,1,0:T(8,128)(2,1)S(1)}, bf16[52,16,128]{2,1,0:T(8,128)(2,1)S(1)}, u32[]{:S(2)}, u32[]{:S(2)}) %collective-permute-start.13) | collective-permute-done | bytes 213024 | tf_op jit(solution)/shard_map/ppermute | solution.py:455
  82.2 4.4 %scores.1 = bf16[48,16,128]{2,1,0:T(8,128)(2,1)} custom-call(s32[2,48]{1,0:T(2,128)S(1)} %bitcast.6, s32[1]{0:T(128)S(6)} %copy.8.live_ref, s32[160]{0:T(256)S(1)} %copy-done.3, f32[52,16,128]{2,1,0:T(8,128)S(1)} %get-tuple-element.47.refs_0_, bf16[52,16,128]{2,1,0:T(8,128)(2,1)S(1)} %collective-permute-done.12.refs_1_, ...), custom_call_target="tpu_custom_call" | custom-call | tf_op jit(solution)/shard_map/scores/pallas_call | solution.py:458
  (30 shorter events, 0.2 us)
Async XLA Ops:
  0.6 1.0 %copy-start = (bf16[16,128,128]{2,1,0:T(8,128)(2,1)S(1)}, bf16[16,128,128]{2,1,0:T(8,128)(2,1)}, u32[]{:S(2)}) copy-start(bf16[16,128,128]{2,1,0:T(8,128)(2,1)} %param.11) | copy-start | bytes 1572868
  1.7 9.4 %collective-permute-start = (bf16[256,128]{1,0:T(8,128)(2,1)S(1)}, bf16[256,128]{1,0:T(8,128)(2,1)S(1)}, u32[]{:S(2)}, u32[]{:S(2)}) collective-permute-start(bf16[256,128]{1,0:T(8,128)(2,1)S(1)} %constant_dynamic-slice_fusion), channel_id=1, source_target_pairs={{0,1},{1,0},{2,3},{3,2},{4,5},{5,4},{6,7},{7,6},{8,9},{9,8},{10,11... | collective-permute-start | bytes 196616 | tf_op jit(solution)/shard_map/ppermute | solution.py:323
  1.7 9.4 %collective-permute-start.1 = (bf16[256,128]{1,0:T(8,128)(2,1)S(1)}, bf16[256,128]{1,0:T(8,128)(2,1)S(1)}, u32[]{:S(2)}, u32[]{:S(2)}) collective-permute-start(bf16[256,128]{1,0:T(8,128)(2,1)S(1)} %constant_dynamic-slice_fusion), channel_id=1, source_target_pairs={{0,2},{1,3},{2,0},{3,1},{4,6},{5,7},{6,4},{7,5},{8,10},{9,11},{10,... | collective-permute-start | bytes 196616 | tf_op jit(solution)/shard_map/ppermute | solution.py:323
  4.7 6.4 %collective-permute-start.2 = (bf16[256,128]{1,0:T(8,128)(2,1)S(1)}, bf16[256,128]{1,0:T(8,128)(2,1)S(1)}, u32[]{:S(2)}, u32[]{:S(2)}) collective-permute-start(bf16[256,128]{1,0:T(8,128)(2,1)S(1)} %constant_dynamic-slice_fusion), channel_id=1, source_target_pairs={{0,3},{1,2},{2,1},{3,0},{4,7},{5,6},{6,5},{7,4},{8,11},{9,10},{10,... | collective-permute-start | bytes 196616 | tf_op jit(solution)/shard_map/ppermute | solution.py:323
  11.1 11.2 %collective-permute-start.3 = (bf16[2,5120]{1,0:T(2,128)(2,1)}, bf16[2,5120]{1,0:T(2,128)(2,1)S(1)}, u32[]{:S(2)}, u32[]{:S(2)}) collective-permute-start(bf16[2,5120]{1,0:T(2,128)(2,1)} %get-tuple-element.34), channel_id=1, source_target_pairs={{4,8},{12,16},{20,24},{8,4},{16,12},{24,20},{5,9},{13,17},{21,25},... | collective-permute-start | bytes 61448 | tf_op jit(solution)/shard_map/ppermute | solution.py:313
  11.8 10.5 %collective-permute-start.4 = (bf16[2,5120]{1,0:T(2,128)(2,1)}, bf16[2,5120]{1,0:T(2,128)(2,1)S(1)}, u32[]{:S(2)}, u32[]{:S(2)}) collective-permute-start(bf16[2,5120]{1,0:T(2,128)(2,1)} %get-tuple-element.35), channel_id=1, source_target_pairs={{0,4},{8,12},{16,20},{24,28},{4,0},{12,8},{20,16},{28,24},{1,5},{9... | collective-permute-start | bytes 61448 | tf_op jit(solution)/shard_map/ppermute | solution.py:313
  14.7 42.9 %collective-permute-start.5 = (bf16[384,2048]{1,0:T(8,128)(2,1)}, bf16[384,2048]{1,0:T(8,128)(2,1)S(1)}, u32[]{:S(2)}, u32[]{:S(2)}) collective-permute-start(bf16[384,2048]{1,0:T(8,128)(2,1)} %get-tuple-element.38), channel_id=1, source_target_pairs={{0,1},{2,3},{1,0},{3,2},{4,5},{6,7},{5,4},{7,6},{8,9},{10,11},{9,8... | collective-permute-start | bytes 4718600 | tf_op jit(solution)/shard_map/ppermute | solution.py:313
  16.1 41.6 %collective-permute-start.6 = (bf16[384,2048]{1,0:T(8,128)(2,1)}, bf16[384,2048]{1,0:T(8,128)(2,1)}, u32[]{:S(2)}, u32[]{:S(2)}) collective-permute-start(bf16[384,2048]{1,0:T(8,128)(2,1)} %get-tuple-element.39), channel_id=1, source_target_pairs={{1,2},{2,1},{5,6},{6,5},{9,10},{10,9},{13,14},{14,13},{17,18},{18,... | collective-permute-start | bytes 4718600 | tf_op jit(solution)/shard_map/ppermute | solution.py:313
  20.8 7.7 %collective-permute-start.10 = (bf16[1024,128]{1,0:T(8,128)(2,1)S(1)}, bf16[1024,128]{1,0:T(8,128)(2,1)S(1)}, u32[]{:S(2)}, u32[]{:S(2)}) collective-permute-start(bf16[1024,128]{1,0:T(8,128)(2,1)S(1)} %pad_maximum_fusion.2), channel_id=1, source_target_pairs={{0,16},{4,20},{8,24},{12,28},{16,0},{20,4},{24,8},{28,12},{1,17},{... | collective-permute-start | bytes 786440 | tf_op jit(solution)/shard_map/ppermute | solution.py:362
  22.5 7.7 %copy-start.5 = (bf16[8,5120]{1,0:T(8,128)(2,1)}, bf16[8,5120]{1,0:T(8,128)(2,1)S(1)}, u32[]{:S(2)}) copy-start(bf16[8,5120]{1,0:T(8,128)(2,1)S(1)} %pad_maximum_fusion.3.columns_ref) | copy-start | bytes 245764
  22.5 35.1 %collective-permute-start.7 = (bf16[8,384]{1,0:T(8,128)(2,1)S(1)}, bf16[8,384]{1,0:T(8,128)(2,1)S(1)}, u32[]{:S(2)}, u32[]{:S(2)}) collective-permute-start(bf16[8,384]{1,0:T(8,128)(2,1)S(1)} %get-tuple-element.53), channel_id=1, source_target_pairs={{0,1},{2,3},{1,0},{3,2},{4,5},{6,7},{5,4},{7,6},{8,9},{10,11},{9,8... | collective-permute-start | bytes 18440 | tf_op jit(solution)/shard_map/ppermute | solution.py:313
  22.6 35.0 %collective-permute-start.8 = (bf16[8,384]{1,0:T(8,128)(2,1)S(1)}, bf16[8,384]{1,0:T(8,128)(2,1)S(1)}, u32[]{:S(2)}, u32[]{:S(2)}) collective-permute-start(bf16[8,384]{1,0:T(8,128)(2,1)S(1)} %get-tuple-element.52), channel_id=1, source_target_pairs={{1,2},{2,1},{5,6},{6,5},{9,10},{10,9},{13,14},{14,13},{17,18},{18,... | collective-permute-start | bytes 18440 | tf_op jit(solution)/shard_map/ppermute | solution.py:313
  28.6 38.2 %collective-permute-start.11 = (bf16[2048,128]{1,0:T(8,128)(2,1)S(1)}, bf16[2048,128]{1,0:T(8,128)(2,1)S(1)}, u32[]{:S(2)}, u32[]{:S(2)}) collective-permute-start(bf16[2048,128]{1,0:T(8,128)(2,1)S(1)} %pad_maximum_fusion.1), channel_id=1, source_target_pairs={{0,8},{4,12},{8,0},{12,4},{16,24},{20,28},{24,16},{28,20},{1,9},{5... | collective-permute-start | bytes 1572872 | tf_op jit(solution)/shard_map/ppermute | solution.py:362
  57.6 0.6 copy-start.6
  57.6 0.6 copy-start.7
  57.6 1.2 %copy-start.4 = (bf16[384,2048]{1,0:T(8,128)(2,1)}, bf16[384,2048]{1,0:T(8,128)(2,1)S(1)}, u32[]{:S(2)}) copy-start(bf16[384,2048]{1,0:T(8,128)(2,1)S(1)} %collective-permute-done.5.near_hbm) | copy-start | bytes 4718596
  66.6 2.6 %copy-start.1 = (bf16[49,4,16,128]{3,2,1,0:T(8,128)(2,1)S(1)}, bf16[49,4,16,128]{3,2,1,0:T(8,128)(2,1)}, u32[]{:S(2)}) copy-start(bf16[49,4,16,128]{3,2,1,0:T(8,128)(2,1)} %get-tuple-element.43.keep_hbm) | copy-start | bytes 2408452
  66.7 15.6 %copy-start.2 = (s32[48,2]{0,1:T(2,128)S(1)}, s32[48,2]{0,1:T(2,128)}, u32[]{:S(2)}) copy-start(s32[48,2]{0,1:T(2,128)} %param.8) | copy-start | bytes 1156
  66.7 15.5 %copy-start.3 = (s32[160]{0:T(256)S(1)}, s32[160]{0:T(256)}, u32[]{:S(2)}) copy-start(s32[160]{0:T(256)} %rules_ref.1) | copy-start | bytes 1924
  66.7 2.6 %collective-permute-start.9 = (bf16[49,4,16,128]{3,2,1,0:T(8,128)(2,1)}, bf16[49,4,16,128]{3,2,1,0:T(8,128)(2,1)S(1)}, u32[]{:S(2)}, u32[]{:S(2)}) collective-permute-start(bf16[49,4,16,128]{3,2,1,0:T(8,128)(2,1)} %get-tuple-element.44), channel_id=1, source_target_pairs={{0,4},{4,0},{8,12},{12,8},{16,20},{20,16},{24,28},{28,24},{1,5},{5... | collective-permute-start | bytes 2408456 | tf_op jit(solution)/shard_map/ppermute | solution.py:435
  69.6 12.6 %collective-permute-start.15 = (bf16[4096,128]{1,0:T(8,128)(2,1)S(1)}, bf16[4096,128]{1,0:T(8,128)(2,1)S(1)}, u32[]{:S(2)}, u32[]{:S(2)}) collective-permute-start(bf16[4096,128]{1,0:T(8,128)(2,1)S(1)} %pad_maximum_fusion.refs_4_), channel_id=1, source_target_pairs={{0,4},{4,0},{8,12},{12,8},{16,20},{20,16},{24,28},{28,24},{1,5},{5... | collective-permute-start | bytes 3145736 | tf_op jit(solution)/shard_map/ppermute | solution.py:362
  69.8 8.1 %collective-permute-start.12 = (bf16[52,16,128]{2,1,0:T(8,128)(2,1)S(1)}, bf16[52,16,128]{2,1,0:T(8,128)(2,1)S(1)}, u32[]{:S(2)}, u32[]{:S(2)}) collective-permute-start(bf16[52,16,128]{2,1,0:T(8,128)(2,1)S(1)} %get-tuple-element.48), channel_id=1, source_target_pairs={{0,8},{4,12},{8,0},{12,4},{16,24},{20,28},{24,16},{28,20},{1,9},{5... | collective-permute-start | bytes 638984 | tf_op jit(solution)/shard_map/ppermute | solution.py:455
  70.4 11.8 %collective-permute-start.13 = (bf16[52,16,128]{2,1,0:T(8,128)(2,1)S(1)}, bf16[52,16,128]{2,1,0:T(8,128)(2,1)S(1)}, u32[]{:S(2)}, u32[]{:S(2)}) collective-permute-start(bf16[52,16,128]{2,1,0:T(8,128)(2,1)S(1)} %get-tuple-element.49), channel_id=1, source_target_pairs={{0,16},{4,20},{8,24},{12,28},{16,0},{20,4},{24,8},{28,12},{1,17},{... | collective-permute-start | bytes 638984 | tf_op jit(solution)/shard_map/ppermute | solution.py:455
  71.9 10.3 %collective-permute-start.14 = (bf16[52,16,128]{2,1,0:T(8,128)(2,1)S(1)}, bf16[52,16,128]{2,1,0:T(8,128)(2,1)S(1)}, u32[]{:S(2)}, u32[]{:S(2)}) collective-permute-start(bf16[52,16,128]{2,1,0:T(8,128)(2,1)S(1)} %get-tuple-element.50), channel_id=1, source_target_pairs={{0,24},{4,28},{8,16},{12,20},{16,8},{20,12},{24,0},{28,4},{1,25},{... | collective-permute-start | bytes 638984 | tf_op jit(solution)/shard_map/ppermute | solution.py:455

commit v12 on v10

--- a/solution.py
+++ b/solution.py
@@ -13,6 +13,7 @@
 HALF = LANES // 2
 DEPTH = 2 * LANES
 VMEM_BYTES = 58 * 1024 * 1024
+MAIN_VMEM_BYTES = 125 * 1024 * 512
 
 
 def params():
@@ -283,16 +284,17 @@
     for copy in copies[-2:]:
         copy.wait()
 
-    def one(s, carry):
-        scores = jnp.zeros((share, block), jnp.float32)
-        for k in range(pieces):
-            matrix = table_ref[pl.ds(pl.multiple_of(place[k, s], depth), depth), :]
-            part = coloc[s, :, k * depth : (k + 1) * depth]
-            scores = scores + jnp.dot(part, matrix, preferred_element_type=jnp.float32)
-        out_ref[s] = jnp.where(s < live_ref[0], scores, 0.0).astype(jnp.bfloat16)
-        return carry
-
-    lax.fori_loop(0, slots, one, 0, unroll=slots)
+    def matrix(s):
+        rows = [table_ref[pl.ds(pl.multiple_of(place[k, s], depth), depth), :] for k in range(pieces)]
+        return jnp.concatenate(rows, axis=0)
+
+    for s in range(0, slots, 2):
+        both = jnp.concatenate([matrix(s), matrix(s + 1)], axis=1)
+        rows = coloc[s : s + 2].reshape(2 * share, block)
+        scores = jnp.dot(rows, both, preferred_element_type=jnp.float32)
+        for k in range(2):
+            part = scores[k * share : (k + 1) * share, k * block : (k + 1) * block]
+            out_ref[s + k] = jnp.where(s + k < live_ref[0], part, 0.0).astype(jnp.bfloat16)
 
 
 def on_device(images, stencil, pairs, live, rule_of_block, adduct):
@@ -347,6 +349,7 @@
     near_rows, far_rows = swapped("ion", n_ion, near_rows, far_rows)
     near, far, *turns = lax.optimization_barrier((near, far, *turns))
     mine = jnp.concatenate([mine, *turns], axis=0)
+    near, far, mine = lax.optimization_barrier((near, far, mine))
     near, far = swapped("pix", n_pix, near, far)
     odd = pix % 2 == 1
     after, before = jnp.where(odd, far, near), jnp.where(odd, near, far)
@@ -354,7 +357,6 @@
     first, last = columns[:, :edge], columns[:, rows - edge :]
     odd = ion % 2 == 1
     near_columns, far_columns = swapped("ion", n_ion, jnp.where(odd, first, last), jnp.where(odd, last, first))
-    columns, near_columns, far_columns = lax.optimization_barrier((columns, near_columns, far_columns))
 
     distances = [n_pix >> k for k in range(1, n_pix.bit_length())]
 
@@ -404,13 +406,13 @@
             jax.ShapeDtypeStruct((blocks, LANES), jnp.float32),
             *both_halves,
         ],
-        compiler_params=params(),
+        compiler_params=pltpu.CompilerParams(vmem_limit_bytes=MAIN_VMEM_BYTES),
         cost_estimate=cost(2 * rows * width * DEPTH + 2 * slots * block * block * width, 4 * rows * width),
         name="smooth_and_gram",
     )(table_pairs, images, columns, weights)
     smoothed = smoothed.reshape(rows, width)
-
-    energy, mine = lax.optimization_barrier((energy, mine))
+    received = (near_rows, far_rows, near_columns, far_columns)
+    energy, mine, *received = lax.optimization_barrier((energy, mine, *received))
     for distance in distances[1:-1]:
         mine = jnp.concatenate([mine, exchange(mine, distance)], axis=0)
 
@@ -432,7 +434,7 @@
         compiler_params=params(),
         cost_estimate=cost(4 * edge * width * DEPTH, 8 * edge * width),
         name="cross_grams",
-    )(table_pairs, near_rows, far_rows, near_columns, far_columns, weights, energy, smoothed, keep, give)
+    )(table_pairs, *received, weights, energy, smoothed, keep, give)
 
     got = lax.ppermute(give, "pix", [(i, i ^ 1) for i in range(n_pix)])
     message = jax.ShapeDtypeStruct((slots + units * chips, share, LANES), jnp.bfloat16)

time: 112 us -> 87.2 us (0.78)
  waiting for transfers between devices: 34.3 us -> 15.6 us
  local copies, waits for them, and re-layouts: 5.16 us -> 1.15 us
  starting transfers between devices: 23.3 us -> 21.8 us
    ppermute x6, waiting for transfers between devices: 23 us -> 3.36 us  [swapped(): lax.ppermute(value, axis, both + [(j, i) for i, j in both])]
    unnamed x22 -> x14, local copies, waits for them, and re-layouts: 5.05 us -> 1.06 us
    ppermute x3, waiting for transfers between devices: 0.01 us -> 3.03 us  [exchange(): return lax.ppermute(value, 'pix', [(i, i ^ distance) for i in range(n_pix)])]
    ppermute x1, waiting for transfers between devices: 2.42 us -> 0.01 us  [on_device(): got = lax.ppermute(give, 'pix', [(i, i ^ 1) for i in range(n_pix)])]
    ppermute x3, starting transfers between devices: 4.63 us -> 3.15 us  [exchange(): return lax.ppermute(value, 'pix', [(i, i ^ distance) for i in range(n_pix)])]
  transfers between devices with their start and end apart: 16 -> 16, of which waited for: 5 -> 4; matrix products, arithmetic and copies ran while one was open for 2% -> 0% of each run, Pallas kernels for 38% -> 48%
where the time goes in v12:
time: 87.2 us; the launch traced here: 86.9 us
  Pallas kernels  46.5 us (53%)
  starting transfers between devices  21.8 us (25%)
  waiting for transfers between devices  15.6 us (18%)
  between operations  1.56 us (2%)
  local copies, waits for them, and re-layouts  1.15 us (1%)
    pallas_call x1, Pallas kernels, on_device(): pl.pallas_call(functools.partial(main_kernel, steps, group, block), grid_...  27.5 us
    ppermute x6, starting transfers between devices, swapped(): lax.ppermute(value, axis, both + [(j, i) for i, j in both])  11 us
    ppermute x3, waiting for transfers between devices, on_device(): lax.ppermute(m, 'pix', [(i, i ^ 2 * (d + 1)) for i in range(n_pix)])  9.24 us
    pallas_call x1, Pallas kernels, on_device(): pl.pallas_call(functools.partial(cross_kernel, blocks, block), in_specs=[...  8.49 us
    pallas_call x1, Pallas kernels, on_device(): pl.pallas_call(cut_kernel, in_specs=[hbm, vmem], out_specs=[hbm, hbm, vme...  5.88 us
    pallas_call x1, Pallas kernels, on_device(): pl.pallas_call(functools.partial(score_kernel, blocks, place_of, pixel_co...  4.22 us
    ppermute x3, starting transfers between devices, on_device(): lax.ppermute(mine, 'ion', [(i, i ^ d) for i in range(n_ion)])  4.05 us
    ppermute x3, starting transfers between devices, on_device(): lax.ppermute(m, 'pix', [(i, i ^ 2 * (d + 1)) for i in range(n_pix)])  3.55 us
  transfers between devices with their start and end apart: 16, of which 4 were waited for; matrix products, arithmetic and copies ran while one was open for 0% of the time, Pallas kernels for 48%

profile of v12, /device:TPU:8, one launch (start us, length us, event | category | flops | bytes accessed | tf_op | source)
XLA Modules:
  0.0 86.9 jit_solution(14691611022325160638)
XLA Ops:
  0.6 0.0 copy-start
  0.7 1.0 %copy-done = bf16[16,128,128]{2,1,0:T(8,128)(2,1)S(1)} copy-done((bf16[16,128,128]{2,1,0:T(8,128)(2,1)S(1)}, bf16[16,128,128]{2,1,0:T(8,128)(2,1)}, u32[]{:S(2)}) %copy-start) | copy-done | bytes 524312
  1.7 1.6 %collective-permute-start.2 = (bf16[256,128]{1,0:T(8,128)(2,1)S(1)}, bf16[256,128]{1,0:T(8,128)(2,1)S(1)}, u32[]{:S(2)}, u32[]{:S(2)}) collective-permute-start(bf16[256,128]{1,0:T(8,128)(2,1)S(1)} %constant_dynamic-slice_fusion), channel_id=1, source_target_pairs={{0,3},{1,2},{2,1},{3,0},{4,7},{5,6},{6,5},{7,4},{8,11},{9,10},{10,... | collective-permute-start | bytes 196616 | tf_op jit(solution)/shard_map/ppermute | solution.py:325
  3.3 1.1 %collective-permute-start.1 = (bf16[256,128]{1,0:T(8,128)(2,1)S(1)}, bf16[256,128]{1,0:T(8,128)(2,1)S(1)}, u32[]{:S(2)}, u32[]{:S(2)}) collective-permute-start(bf16[256,128]{1,0:T(8,128)(2,1)S(1)} %constant_dynamic-slice_fusion), channel_id=1, source_target_pairs={{0,2},{1,3},{2,0},{3,1},{4,6},{5,7},{6,4},{7,5},{8,10},{9,11},{10,... | collective-permute-start | bytes 196616 | tf_op jit(solution)/shard_map/ppermute | solution.py:325
  4.3 1.4 %collective-permute-start = (bf16[256,128]{1,0:T(8,128)(2,1)S(1)}, bf16[256,128]{1,0:T(8,128)(2,1)S(1)}, u32[]{:S(2)}, u32[]{:S(2)}) collective-permute-start(bf16[256,128]{1,0:T(8,128)(2,1)S(1)} %constant_dynamic-slice_fusion), channel_id=1, source_target_pairs={{0,1},{1,0},{2,3},{3,2},{4,5},{5,4},{6,7},{7,6},{8,9},{9,8},{10,11... | collective-permute-start | bytes 196616 | tf_op jit(solution)/shard_map/ppermute | solution.py:325
  5.7 5.9 %cut_edges.1 = (bf16[384,2048]{1,0:T(8,128)(2,1)}, bf16[384,2048]{1,0:T(8,128)(2,1)}, bf16[2,5120]{1,0:T(2,128)(2,1)}, bf16[2,5120]{1,0:T(2,128)(2,1)}, bf16[17,256,128]{2,1,0:T(8,128)(2,1)}) custom-call(bf16[5120,2048]{1,0:T(8,128)(2,1)} %x_ref.1, f32[5,2048]{1,0:T(8,128)} %stencil_ref.1), custom_call_target="tpu_custom_call" | custom-call | bytes 6291456 | tf_op jit(solution)/shard_map/cut_edges/pallas_call | solution.py:329
  11.7 0.7 collective-permute-start.3
  12.4 2.9 %collective-permute-start.4 = (bf16[2,5120]{1,0:T(2,128)(2,1)}, bf16[2,5120]{1,0:T(2,128)(2,1)S(1)}, u32[]{:S(2)}, u32[]{:S(2)}) collective-permute-start(bf16[2,5120]{1,0:T(2,128)(2,1)} %get-tuple-element.41), channel_id=1, source_target_pairs={{0,4},{8,12},{16,20},{24,28},{4,0},{12,8},{20,16},{28,24},{1,5},{9... | collective-permute-start | bytes 61448 | tf_op jit(solution)/shard_map/ppermute | solution.py:315
  15.3 0.8 collective-permute-start.6
  16.1 4.6 %collective-permute-start.7 = (bf16[384,2048]{1,0:T(8,128)(2,1)}, bf16[384,2048]{1,0:T(8,128)(2,1)}, u32[]{:S(2)}, u32[]{:S(2)}) collective-permute-start(bf16[384,2048]{1,0:T(8,128)(2,1)} %get-tuple-element.47), channel_id=1, source_target_pairs={{1,2},{2,1},{5,6},{6,5},{9,10},{10,9},{13,14},{14,13},{17,18},{18,... | collective-permute-start | bytes 4718600 | tf_op jit(solution)/shard_map/ppermute | solution.py:315
  20.7 0.1 pad.5.clone
  20.8 1.5 %collective-permute-start.5 = (bf16[1024,128]{1,0:T(8,128)(2,1)S(1)}, bf16[1024,128]{1,0:T(8,128)(2,1)S(1)}, u32[]{:S(2)}, u32[]{:S(2)}) collective-permute-start(bf16[1024,128]{1,0:T(8,128)(2,1)S(1)} %pad_maximum_fusion.2), channel_id=1, source_target_pairs={{0,16},{4,20},{8,24},{12,28},{16,0},{20,4},{24,8},{28,12},{1,17},{... | collective-permute-start | bytes 786440 | tf_op jit(solution)/shard_map/ppermute | solution.py:364
  22.3 0.1 pad_maximum_fusion.3.columns_ref
  22.4 0.0 copy-start.4
  22.5 1.9 %collective-permute-start.9 = (bf16[8,384]{1,0:T(8,128)(2,1)S(1)}, bf16[8,384]{1,0:T(8,128)(2,1)S(1)}, u32[]{:S(2)}, u32[]{:S(2)}) collective-permute-start(bf16[8,384]{1,0:T(8,128)(2,1)S(1)} %get-tuple-element.64), channel_id=1, source_target_pairs={{1,2},{2,1},{5,6},{6,5},{9,10},{10,9},{13,14},{14,13},{17,18},{18,... | collective-permute-start | bytes 18440 | tf_op jit(solution)/shard_map/ppermute | solution.py:315
  24.4 0.1 collective-permute-start.8
  24.5 27.5 %smooth_and_gram.1 = (bf16[40,128,2048]{2,1,0:T(8,128)(2,1)}, f32[40,128]{1,0:T(8,128)}, bf16[49,4,16,128]{3,2,1,0:T(8,128)(2,1)}, bf16[49,4,16,128]{3,2,1,0:T(8,128)(2,1)}) custom-call(s32[2,48]{1,0:T(2,128)} %bitcast.4, bf16[5120,2048]{1,0:T(8,128)(2,1)} %x_ref.1, bf16[8,5120]{1,0:T(8,128)(2,1)} %copy-done.4, ...), custom_call_target="tpu_custom_call" | custom-call | flops 8589934592 | bytes 41943040 | tf_op jit(solution)/shard_map/smooth_and_gram/pallas_call | solution.py:391
  52.0 3.3 %collective-permute-done.9.far_columns_hbm = bf16[8,384]{1,0:T(8,128)(2,1)S(1)} collective-permute-done((bf16[8,384]{1,0:T(8,128)(2,1)S(1)}, bf16[8,384]{1,0:T(8,128)(2,1)S(1)}, u32[]{:S(2)}, u32[]{:S(2)}) %collective-permute-start.9) | collective-permute-done | bytes 6176 | tf_op jit(solution)/shard_map/ppermute | solution.py:315
  55.4 1.6 %collective-permute-start.11 = (bf16[2048,128]{1,0:T(8,128)(2,1)S(1)}, bf16[2048,128]{1,0:T(8,128)(2,1)S(1)}, u32[]{:S(2)}, u32[]{:S(2)}) collective-permute-start(bf16[2048,128]{1,0:T(8,128)(2,1)S(1)} %pad_maximum_fusion.1), channel_id=1, source_target_pairs={{0,8},{4,12},{8,0},{12,4},{16,24},{20,28},{24,16},{28,20},{1,9},{5... | collective-permute-start | bytes 1572872 | tf_op jit(solution)/shard_map/ppermute | solution.py:364
  57.0 8.5 %cross_grams.1 = (bf16[49,4,16,128]{3,2,1,0:T(8,128)(2,1)}, bf16[49,4,16,128]{3,2,1,0:T(8,128)(2,1)}) custom-call(s32[2,48]{1,0:T(2,128)} %bitcast.5, bf16[384,2048]{1,0:T(8,128)(2,1)} %collective-permute-done.6.near_hbm, bf16[384,2048]{1,0:T(8,128)(2,1)} %collective-permute-done.7.far_hbm, bf16[8,384]{1,0:T(8,128)(2,1)} %copy-done.6, ...), custom_call_target="tpu_custom_call" | custom-call | flops 805306368 | bytes 6291456 | tf_op jit(solution)/shard_map/cross_grams/pallas_call | solution.py:419
  65.5 0.0 copy-start.2
  65.5 0.1 collective-permute-start.10
  65.6 3.0 %collective-permute-done.11 = bf16[2048,128]{1,0:T(8,128)(2,1)S(1)} collective-permute-done((bf16[2048,128]{1,0:T(8,128)(2,1)S(1)}, bf16[2048,128]{1,0:T(8,128)(2,1)S(1)}, u32[]{:S(2)}, u32[]{:S(2)}) %collective-permute-start.11) | collective-permute-done | bytes 524320 | tf_op jit(solution)/shard_map/ppermute | solution.py:364
  68.6 0.1 pad_maximum_fusion.refs_4_
  68.7 0.4 chip_sums.1
  69.1 0.1 collective-permute-start.15
  69.2 1.6 %collective-permute-start.12 = (bf16[52,16,128]{2,1,0:T(8,128)(2,1)S(1)}, bf16[52,16,128]{2,1,0:T(8,128)(2,1)S(1)}, u32[]{:S(2)}, u32[]{:S(2)}) collective-permute-start(bf16[52,16,128]{2,1,0:T(8,128)(2,1)S(1)} %get-tuple-element.60), channel_id=1, source_target_pairs={{0,8},{4,12},{8,0},{12,4},{16,24},{20,28},{24,16},{28,20},{1,9},{5... | collective-permute-start | bytes 638984 | tf_op jit(solution)/shard_map/ppermute | solution.py:459
  70.7 0.8 collective-permute-start.13
  71.5 1.2 %collective-permute-start.14 = (bf16[52,16,128]{2,1,0:T(8,128)(2,1)S(1)}, bf16[52,16,128]{2,1,0:T(8,128)(2,1)S(1)}, u32[]{:S(2)}, u32[]{:S(2)}) collective-permute-start(bf16[52,16,128]{2,1,0:T(8,128)(2,1)S(1)} %get-tuple-element.62), channel_id=1, source_target_pairs={{0,24},{4,28},{8,16},{12,20},{16,8},{20,12},{24,0},{28,4},{1,25},{... | collective-permute-start | bytes 638984 | tf_op jit(solution)/shard_map/ppermute | solution.py:459
  73.4 3.9 %collective-permute-done.12.refs_1_ = bf16[52,16,128]{2,1,0:T(8,128)(2,1)S(1)} collective-permute-done((bf16[52,16,128]{2,1,0:T(8,128)(2,1)S(1)}, bf16[52,16,128]{2,1,0:T(8,128)(2,1)S(1)}, u32[]{:S(2)}, u32[]{:S(2)}) %collective-permute-start.12) | collective-permute-done | bytes 213024 | tf_op jit(solution)/shard_map/ppermute | solution.py:459
  77.3 5.3 %collective-permute-done.13.refs_2_ = bf16[52,16,128]{2,1,0:T(8,128)(2,1)S(1)} collective-permute-done((bf16[52,16,128]{2,1,0:T(8,128)(2,1)S(1)}, bf16[52,16,128]{2,1,0:T(8,128)(2,1)S(1)}, u32[]{:S(2)}, u32[]{:S(2)}) %collective-permute-start.13) | collective-permute-done | bytes 213024 | tf_op jit(solution)/shard_map/ppermute | solution.py:459
  82.7 4.2 %scores.1 = bf16[48,16,128]{2,1,0:T(8,128)(2,1)} custom-call(s32[2,48]{1,0:T(2,128)S(1)} %bitcast.6, s32[1]{0:T(128)S(6)} %copy.8.live_ref, s32[160]{0:T(256)S(1)} %copy-done.3, f32[52,16,128]{2,1,0:T(8,128)S(1)} %get-tuple-element.59.refs_0_, bf16[52,16,128]{2,1,0:T(8,128)(2,1)S(1)} %collective-permute-done.12.refs_1_, ...), custom_call_target="tpu_custom_call" | custom-call | tf_op jit(solution)/shard_map/scores/pallas_call | solution.py:462
  (28 shorter events, 0.2 us)
Async XLA Ops:
  0.6 1.0 %copy-start = (bf16[16,128,128]{2,1,0:T(8,128)(2,1)S(1)}, bf16[16,128,128]{2,1,0:T(8,128)(2,1)}, u32[]{:S(2)}) copy-start(bf16[16,128,128]{2,1,0:T(8,128)(2,1)} %param.11) | copy-start | bytes 1572868
  1.7 9.9 %collective-permute-start.2 = (bf16[256,128]{1,0:T(8,128)(2,1)S(1)}, bf16[256,128]{1,0:T(8,128)(2,1)S(1)}, u32[]{:S(2)}, u32[]{:S(2)}) collective-permute-start(bf16[256,128]{1,0:T(8,128)(2,1)S(1)} %constant_dynamic-slice_fusion), channel_id=1, source_target_pairs={{0,3},{1,2},{2,1},{3,0},{4,7},{5,6},{6,5},{7,4},{8,11},{9,10},{10,... | collective-permute-start | bytes 196616 | tf_op jit(solution)/shard_map/ppermute | solution.py:325
  3.3 8.4 %collective-permute-start.1 = (bf16[256,128]{1,0:T(8,128)(2,1)S(1)}, bf16[256,128]{1,0:T(8,128)(2,1)S(1)}, u32[]{:S(2)}, u32[]{:S(2)}) collective-permute-start(bf16[256,128]{1,0:T(8,128)(2,1)S(1)} %constant_dynamic-slice_fusion), channel_id=1, source_target_pairs={{0,2},{1,3},{2,0},{3,1},{4,6},{5,7},{6,4},{7,5},{8,10},{9,11},{10,... | collective-permute-start | bytes 196616 | tf_op jit(solution)/shard_map/ppermute | solution.py:325
  4.3 7.3 %collective-permute-start = (bf16[256,128]{1,0:T(8,128)(2,1)S(1)}, bf16[256,128]{1,0:T(8,128)(2,1)S(1)}, u32[]{:S(2)}, u32[]{:S(2)}) collective-permute-start(bf16[256,128]{1,0:T(8,128)(2,1)S(1)} %constant_dynamic-slice_fusion), channel_id=1, source_target_pairs={{0,1},{1,0},{2,3},{3,2},{4,5},{5,4},{6,7},{7,6},{8,9},{9,8},{10,11... | collective-permute-start | bytes 196616 | tf_op jit(solution)/shard_map/ppermute | solution.py:325
  11.7 10.6 %collective-permute-start.3 = (bf16[2,5120]{1,0:T(2,128)(2,1)}, bf16[2,5120]{1,0:T(2,128)(2,1)S(1)}, u32[]{:S(2)}, u32[]{:S(2)}) collective-permute-start(bf16[2,5120]{1,0:T(2,128)(2,1)} %get-tuple-element.40), channel_id=1, source_target_pairs={{4,8},{12,16},{20,24},{8,4},{16,12},{24,20},{5,9},{13,17},{21,25},... | collective-permute-start | bytes 61448 | tf_op jit(solution)/shard_map/ppermute | solution.py:315
  12.4 10.0 %collective-permute-start.4 = (bf16[2,5120]{1,0:T(2,128)(2,1)}, bf16[2,5120]{1,0:T(2,128)(2,1)S(1)}, u32[]{:S(2)}, u32[]{:S(2)}) collective-permute-start(bf16[2,5120]{1,0:T(2,128)(2,1)} %get-tuple-element.41), channel_id=1, source_target_pairs={{0,4},{8,12},{16,20},{24,28},{4,0},{12,8},{20,16},{28,24},{1,5},{9... | collective-permute-start | bytes 61448 | tf_op jit(solution)/shard_map/ppermute | solution.py:315
  15.3 40.1 %collective-permute-start.6 = (bf16[384,2048]{1,0:T(8,128)(2,1)}, bf16[384,2048]{1,0:T(8,128)(2,1)}, u32[]{:S(2)}, u32[]{:S(2)}) collective-permute-start(bf16[384,2048]{1,0:T(8,128)(2,1)} %get-tuple-element.46), channel_id=1, source_target_pairs={{0,1},{2,3},{1,0},{3,2},{4,5},{6,7},{5,4},{7,6},{8,9},{10,11},{9,8... | collective-permute-start | bytes 4718600 | tf_op jit(solution)/shard_map/ppermute | solution.py:315
  16.1 39.3 %collective-permute-start.7 = (bf16[384,2048]{1,0:T(8,128)(2,1)}, bf16[384,2048]{1,0:T(8,128)(2,1)}, u32[]{:S(2)}, u32[]{:S(2)}) collective-permute-start(bf16[384,2048]{1,0:T(8,128)(2,1)} %get-tuple-element.47), channel_id=1, source_target_pairs={{1,2},{2,1},{5,6},{6,5},{9,10},{10,9},{13,14},{14,13},{17,18},{18,... | collective-permute-start | bytes 4718600 | tf_op jit(solution)/shard_map/ppermute | solution.py:315
  20.8 31.2 %collective-permute-start.5 = (bf16[1024,128]{1,0:T(8,128)(2,1)S(1)}, bf16[1024,128]{1,0:T(8,128)(2,1)S(1)}, u32[]{:S(2)}, u32[]{:S(2)}) collective-permute-start(bf16[1024,128]{1,0:T(8,128)(2,1)S(1)} %pad_maximum_fusion.2), channel_id=1, source_target_pairs={{0,16},{4,20},{8,24},{12,28},{16,0},{20,4},{24,8},{28,12},{1,17},{... | collective-permute-start | bytes 786440 | tf_op jit(solution)/shard_map/ppermute | solution.py:364
  22.4 2.0 %copy-start.4 = (bf16[8,5120]{1,0:T(8,128)(2,1)}, bf16[8,5120]{1,0:T(8,128)(2,1)S(1)}, u32[]{:S(2)}) copy-start(bf16[8,5120]{1,0:T(8,128)(2,1)S(1)} %pad_maximum_fusion.3.columns_ref) | copy-start | bytes 245764
  22.5 32.9 %collective-permute-start.9 = (bf16[8,384]{1,0:T(8,128)(2,1)S(1)}, bf16[8,384]{1,0:T(8,128)(2,1)S(1)}, u32[]{:S(2)}, u32[]{:S(2)}) collective-permute-start(bf16[8,384]{1,0:T(8,128)(2,1)S(1)} %get-tuple-element.64), channel_id=1, source_target_pairs={{1,2},{2,1},{5,6},{6,5},{9,10},{10,9},{13,14},{14,13},{17,18},{18,... | collective-permute-start | bytes 18440 | tf_op jit(solution)/shard_map/ppermute | solution.py:315
  24.4 31.0 %collective-permute-start.8 = (bf16[8,384]{1,0:T(8,128)(2,1)S(1)}, bf16[8,384]{1,0:T(8,128)(2,1)S(1)}, u32[]{:S(2)}, u32[]{:S(2)}) collective-permute-start(bf16[8,384]{1,0:T(8,128)(2,1)S(1)} %get-tuple-element.65), channel_id=1, source_target_pairs={{0,1},{2,3},{1,0},{3,2},{4,5},{6,7},{5,4},{7,6},{8,9},{10,11},{9,8... | collective-permute-start | bytes 18440 | tf_op jit(solution)/shard_map/ppermute | solution.py:315
  55.4 1.6 %copy-start.5 = (bf16[8,384]{1,0:T(8,128)(2,1)}, bf16[8,384]{1,0:T(8,128)(2,1)S(1)}, u32[]{:S(2)}) copy-start(bf16[8,384]{1,0:T(8,128)(2,1)S(1)} %collective-permute-done.9.far_columns_hbm) | copy-start | bytes 18436
  55.4 1.6 %copy-start.6 = (bf16[8,384]{1,0:T(8,128)(2,1)}, bf16[8,384]{1,0:T(8,128)(2,1)S(1)}, u32[]{:S(2)}) copy-start(bf16[8,384]{1,0:T(8,128)(2,1)S(1)} %collective-permute-done.8.near_columns_hbm) | copy-start | bytes 18436
  55.4 13.2 %collective-permute-start.11 = (bf16[2048,128]{1,0:T(8,128)(2,1)S(1)}, bf16[2048,128]{1,0:T(8,128)(2,1)S(1)}, u32[]{:S(2)}, u32[]{:S(2)}) collective-permute-start(bf16[2048,128]{1,0:T(8,128)(2,1)S(1)} %pad_maximum_fusion.1), channel_id=1, source_target_pairs={{0,8},{4,12},{8,0},{12,4},{16,24},{20,28},{24,16},{28,20},{1,9},{5... | collective-permute-start | bytes 1572872 | tf_op jit(solution)/shard_map/ppermute | solution.py:364
  65.5 3.2 %copy-start.1 = (bf16[49,4,16,128]{3,2,1,0:T(8,128)(2,1)S(1)}, bf16[49,4,16,128]{3,2,1,0:T(8,128)(2,1)}, u32[]{:S(2)}) copy-start(bf16[49,4,16,128]{3,2,1,0:T(8,128)(2,1)} %get-tuple-element.55.keep_hbm) | copy-start | bytes 2408452
  65.5 17.2 %copy-start.2 = (s32[48,2]{0,1:T(2,128)S(1)}, s32[48,2]{0,1:T(2,128)}, u32[]{:S(2)}) copy-start(s32[48,2]{0,1:T(2,128)} %param.8) | copy-start | bytes 1156
  65.5 17.1 %copy-start.3 = (s32[160]{0:T(256)S(1)}, s32[160]{0:T(256)}, u32[]{:S(2)}) copy-start(s32[160]{0:T(256)} %rules_ref.1) | copy-start | bytes 1924
  65.5 3.2 %collective-permute-start.10 = (bf16[49,4,16,128]{3,2,1,0:T(8,128)(2,1)}, bf16[49,4,16,128]{3,2,1,0:T(8,128)(2,1)S(1)}, u32[]{:S(2)}, u32[]{:S(2)}) collective-permute-start(bf16[49,4,16,128]{3,2,1,0:T(8,128)(2,1)} %get-tuple-element.56), channel_id=1, source_target_pairs={{0,4},{4,0},{8,12},{12,8},{16,20},{20,16},{24,28},{28,24},{1,5},{5... | collective-permute-start | bytes 2408456 | tf_op jit(solution)/shard_map/ppermute | solution.py:439
  69.1 13.5 %collective-permute-start.15 = (bf16[4096,128]{1,0:T(8,128)(2,1)S(1)}, bf16[4096,128]{1,0:T(8,128)(2,1)S(1)}, u32[]{:S(2)}, u32[]{:S(2)}) collective-permute-start(bf16[4096,128]{1,0:T(8,128)(2,1)S(1)} %pad_maximum_fusion.refs_4_), channel_id=1, source_target_pairs={{0,4},{4,0},{8,12},{12,8},{16,20},{20,16},{24,28},{28,24},{1,5},{5... | collective-permute-start | bytes 3145736 | tf_op jit(solution)/shard_map/ppermute | solution.py:364
  69.2 8.1 %collective-permute-start.12 = (bf16[52,16,128]{2,1,0:T(8,128)(2,1)S(1)}, bf16[52,16,128]{2,1,0:T(8,128)(2,1)S(1)}, u32[]{:S(2)}, u32[]{:S(2)}) collective-permute-start(bf16[52,16,128]{2,1,0:T(8,128)(2,1)S(1)} %get-tuple-element.60), channel_id=1, source_target_pairs={{0,8},{4,12},{8,0},{12,4},{16,24},{20,28},{24,16},{28,20},{1,9},{5... | collective-permute-start | bytes 638984 | tf_op jit(solution)/shard_map/ppermute | solution.py:459
  70.7 11.9 %collective-permute-start.13 = (bf16[52,16,128]{2,1,0:T(8,128)(2,1)S(1)}, bf16[52,16,128]{2,1,0:T(8,128)(2,1)S(1)}, u32[]{:S(2)}, u32[]{:S(2)}) collective-permute-start(bf16[52,16,128]{2,1,0:T(8,128)(2,1)S(1)} %get-tuple-element.61), channel_id=1, source_target_pairs={{0,16},{4,20},{8,24},{12,28},{16,0},{20,4},{24,8},{28,12},{1,17},{... | collective-permute-start | bytes 638984 | tf_op jit(solution)/shard_map/ppermute | solution.py:459
  71.5 11.1 %collective-permute-start.14 = (bf16[52,16,128]{2,1,0:T(8,128)(2,1)S(1)}, bf16[52,16,128]{2,1,0:T(8,128)(2,1)S(1)}, u32[]{:S(2)}, u32[]{:S(2)}) collective-permute-start(bf16[52,16,128]{2,1,0:T(8,128)(2,1)S(1)} %get-tuple-element.62), channel_id=1, source_target_pairs={{0,24},{4,28},{8,16},{12,20},{16,8},{20,12},{24,0},{28,4},{1,25},{... | collective-permute-start | bytes 638984 | tf_op jit(solution)/shard_map/ppermute | solution.py:459

commit v13 on v12

--- a/solution.py
+++ b/solution.py
@@ -167,7 +167,7 @@
             keep_ref[s], give_ref[s] = by_core(gram_of(held[a], held[b]), chips, core)
             return carry
 
-        lax.fori_loop(0, slots, one, 0, unroll=4)
+        lax.fori_loop(0, slots, one, 0, unroll=12)
         for k in range(steps):
             copy_out(k).wait()
 
@@ -185,14 +185,17 @@
     odd = lax.axis_index("ion") % 2
     near, far = (pl.ds(pl.multiple_of(k * edge, edge), edge) for k in (1 - odd, odd))
     copies = fetch(
-        (near_hbm, far_hbm, near_columns_hbm, far_columns_hbm, w_hbm, energy_hbm, smoothed_hbm.at[low],
-         smoothed_hbm.at[pl.ds(rows - edge, edge)], keep_hbm, give_hbm),
-        (x_ref.at[near], x_ref.at[far], columns_ref.at[:, near], columns_ref.at[:, far], w_ref, energy_ref, own.at[low],
-         own.at[high], keep_ref, give_ref),
+        (near_hbm, far_hbm, near_columns_hbm, far_columns_hbm, w_hbm, energy_hbm),
+        (x_ref.at[near], x_ref.at[far], columns_ref.at[:, near], columns_ref.at[:, far], w_ref, energy_ref),
         sems,
     )
-    for copy in copies[:6]:
+    for copy in copies:
         copy.wait()
+    copies = fetch(
+        (smoothed_hbm.at[low], smoothed_hbm.at[pl.ds(rows - edge, edge)], keep_hbm, give_hbm),
+        (own.at[low], own.at[high], keep_ref, give_ref),
+        sems,
+    )
     table[...] = jnp.zeros_like(table)
     table[REACH : REACH + blocks, :] = energy_ref[...]
     def store(j, values):
@@ -202,7 +205,7 @@
     for k in range(2 * REACH):
         row = k if k < REACH else k + blocks
         table[row : row + 1, :] = row_sums(total[k * block : (k + 1) * block, :])
-    for copy in copies[6:]:
+    for copy in copies:
         copy.wait()
 
     shape = (units, chips, share, LANES)

time: 87.2 us -> 87.2 us (level)
  waiting for transfers between devices: 15.6 us -> 17 us
  Pallas kernels: 46.5 us -> 45.1 us
    ppermute x6, waiting for transfers between devices: 3.36 us -> 4.75 us  [swapped(): lax.ppermute(value, axis, both + [(j, i) for i, j in both])]
    pallas_call x1, Pallas kernels: 27.5 us -> 26.1 us  [on_device(): pl.pallas_call(functools.partial(main_kernel, steps, group, block), grid_...]
  transfers between devices with their start and end apart: 16 -> 16, of which waited for: 4 -> 4; matrix products, arithmetic and copies ran while one was open for 0% -> 0% of each run, Pallas kernels for 48% -> 47%
where the time goes in v13:
time: 87.2 us; the launch traced here: 86.9 us
  Pallas kernels  45.1 us (52%)
  starting transfers between devices  21.8 us (25%)
  waiting for transfers between devices  17 us (19%)
  between operations  1.56 us (2%)
  local copies, waits for them, and re-layouts  1.15 us (1%)
    pallas_call x1, Pallas kernels, on_device(): pl.pallas_call(functools.partial(main_kernel, steps, group, block), grid_...  26.1 us
    ppermute x6, starting transfers between devices, swapped(): lax.ppermute(value, axis, both + [(j, i) for i, j in both])  11 us
    ppermute x3, waiting for transfers between devices, on_device(): lax.ppermute(m, 'pix', [(i, i ^ 2 * (d + 1)) for i in range(n_pix)])  9.24 us
    pallas_call x1, Pallas kernels, on_device(): pl.pallas_call(functools.partial(cross_kernel, blocks, block), in_specs=[...  8.55 us
    pallas_call x1, Pallas kernels, on_device(): pl.pallas_call(cut_kernel, in_specs=[hbm, vmem], out_specs=[hbm, hbm, vme...  5.88 us
    ppermute x6, waiting for transfers between devices, swapped(): lax.ppermute(value, axis, both + [(j, i) for i, j in both])  4.75 us
    pallas_call x1, Pallas kernels, on_device(): pl.pallas_call(functools.partial(score_kernel, blocks, place_of, pixel_co...  4.22 us
    ppermute x3, starting transfers between devices, on_device(): lax.ppermute(mine, 'ion', [(i, i ^ d) for i in range(n_ion)])  4.05 us
  transfers between devices with their start and end apart: 16, of which 4 were waited for; matrix products, arithmetic and copies ran while one was open for 0% of the time, Pallas kernels for 47%

profile of v13, /device:TPU:8, one launch (start us, length us, event | category | flops | bytes accessed | tf_op | source)
XLA Modules:
  0.0 86.9 jit_solution(14925676784174923574)
XLA Ops:
  0.6 0.0 copy-start
  0.7 1.0 %copy-done = bf16[16,128,128]{2,1,0:T(8,128)(2,1)S(1)} copy-done((bf16[16,128,128]{2,1,0:T(8,128)(2,1)S(1)}, bf16[16,128,128]{2,1,0:T(8,128)(2,1)}, u32[]{:S(2)}) %copy-start) | copy-done | bytes 524312
  1.7 1.6 %collective-permute-start.2 = (bf16[256,128]{1,0:T(8,128)(2,1)S(1)}, bf16[256,128]{1,0:T(8,128)(2,1)S(1)}, u32[]{:S(2)}, u32[]{:S(2)}) collective-permute-start(bf16[256,128]{1,0:T(8,128)(2,1)S(1)} %constant_dynamic-slice_fusion), channel_id=1, source_target_pairs={{0,3},{1,2},{2,1},{3,0},{4,7},{5,6},{6,5},{7,4},{8,11},{9,10},{10,... | collective-permute-start | bytes 196616 | tf_op jit(solution)/shard_map/ppermute | solution.py:328
  3.3 1.1 %collective-permute-start.1 = (bf16[256,128]{1,0:T(8,128)(2,1)S(1)}, bf16[256,128]{1,0:T(8,128)(2,1)S(1)}, u32[]{:S(2)}, u32[]{:S(2)}) collective-permute-start(bf16[256,128]{1,0:T(8,128)(2,1)S(1)} %constant_dynamic-slice_fusion), channel_id=1, source_target_pairs={{0,2},{1,3},{2,0},{3,1},{4,6},{5,7},{6,4},{7,5},{8,10},{9,11},{10,... | collective-permute-start | bytes 196616 | tf_op jit(solution)/shard_map/ppermute | solution.py:328
  4.3 1.4 %collective-permute-start = (bf16[256,128]{1,0:T(8,128)(2,1)S(1)}, bf16[256,128]{1,0:T(8,128)(2,1)S(1)}, u32[]{:S(2)}, u32[]{:S(2)}) collective-permute-start(bf16[256,128]{1,0:T(8,128)(2,1)S(1)} %constant_dynamic-slice_fusion), channel_id=1, source_target_pairs={{0,1},{1,0},{2,3},{3,2},{4,5},{5,4},{6,7},{7,6},{8,9},{9,8},{10,11... | collective-permute-start | bytes 196616 | tf_op jit(solution)/shard_map/ppermute | solution.py:328
  5.7 5.9 %cut_edges.1 = (bf16[384,2048]{1,0:T(8,128)(2,1)}, bf16[384,2048]{1,0:T(8,128)(2,1)}, bf16[2,5120]{1,0:T(2,128)(2,1)}, bf16[2,5120]{1,0:T(2,128)(2,1)}, bf16[17,256,128]{2,1,0:T(8,128)(2,1)}) custom-call(bf16[5120,2048]{1,0:T(8,128)(2,1)} %x_ref.1, f32[5,2048]{1,0:T(8,128)} %stencil_ref.1), custom_call_target="tpu_custom_call" | custom-call | bytes 6291456 | tf_op jit(solution)/shard_map/cut_edges/pallas_call | solution.py:332
  11.7 0.7 collective-permute-start.3
  12.4 2.9 %collective-permute-start.4 = (bf16[2,5120]{1,0:T(2,128)(2,1)}, bf16[2,5120]{1,0:T(2,128)(2,1)S(1)}, u32[]{:S(2)}, u32[]{:S(2)}) collective-permute-start(bf16[2,5120]{1,0:T(2,128)(2,1)} %get-tuple-element.41), channel_id=1, source_target_pairs={{0,4},{8,12},{16,20},{24,28},{4,0},{12,8},{20,16},{28,24},{1,5},{9... | collective-permute-start | bytes 61448 | tf_op jit(solution)/shard_map/ppermute | solution.py:318
  15.3 0.8 collective-permute-start.6
  16.1 4.6 %collective-permute-start.7 = (bf16[384,2048]{1,0:T(8,128)(2,1)}, bf16[384,2048]{1,0:T(8,128)(2,1)}, u32[]{:S(2)}, u32[]{:S(2)}) collective-permute-start(bf16[384,2048]{1,0:T(8,128)(2,1)} %get-tuple-element.47), channel_id=1, source_target_pairs={{1,2},{2,1},{5,6},{6,5},{9,10},{10,9},{13,14},{14,13},{17,18},{18,... | collective-permute-start | bytes 4718600 | tf_op jit(solution)/shard_map/ppermute | solution.py:318
  20.7 0.1 pad.5.clone
  20.8 1.5 %collective-permute-start.5 = (bf16[1024,128]{1,0:T(8,128)(2,1)S(1)}, bf16[1024,128]{1,0:T(8,128)(2,1)S(1)}, u32[]{:S(2)}, u32[]{:S(2)}) collective-permute-start(bf16[1024,128]{1,0:T(8,128)(2,1)S(1)} %pad_maximum_fusion.2), channel_id=1, source_target_pairs={{0,16},{4,20},{8,24},{12,28},{16,0},{20,4},{24,8},{28,12},{1,17},{... | collective-permute-start | bytes 786440 | tf_op jit(solution)/shard_map/ppermute | solution.py:367
  22.3 0.1 pad_maximum_fusion.3.columns_ref
  22.4 0.0 copy-start.4
  22.5 1.9 %collective-permute-start.9 = (bf16[8,384]{1,0:T(8,128)(2,1)S(1)}, bf16[8,384]{1,0:T(8,128)(2,1)S(1)}, u32[]{:S(2)}, u32[]{:S(2)}) collective-permute-start(bf16[8,384]{1,0:T(8,128)(2,1)S(1)} %get-tuple-element.64), channel_id=1, source_target_pairs={{1,2},{2,1},{5,6},{6,5},{9,10},{10,9},{13,14},{14,13},{17,18},{18,... | collective-permute-start | bytes 18440 | tf_op jit(solution)/shard_map/ppermute | solution.py:318
  24.4 0.1 collective-permute-start.8
  24.5 26.1 %smooth_and_gram.1 = (bf16[40,128,2048]{2,1,0:T(8,128)(2,1)}, f32[40,128]{1,0:T(8,128)}, bf16[49,4,16,128]{3,2,1,0:T(8,128)(2,1)}, bf16[49,4,16,128]{3,2,1,0:T(8,128)(2,1)}) custom-call(s32[2,48]{1,0:T(2,128)} %bitcast.4, bf16[5120,2048]{1,0:T(8,128)(2,1)} %x_ref.1, bf16[8,5120]{1,0:T(8,128)(2,1)} %copy-done.4, ...), custom_call_target="tpu_custom_call" | custom-call | flops 8589934592 | bytes 41943040 | tf_op jit(solution)/shard_map/smooth_and_gram/pallas_call | solution.py:394
  50.6 4.7 %collective-permute-done.9.far_columns_hbm = bf16[8,384]{1,0:T(8,128)(2,1)S(1)} collective-permute-done((bf16[8,384]{1,0:T(8,128)(2,1)S(1)}, bf16[8,384]{1,0:T(8,128)(2,1)S(1)}, u32[]{:S(2)}, u32[]{:S(2)}) %collective-permute-start.9) | collective-permute-done | bytes 6176 | tf_op jit(solution)/shard_map/ppermute | solution.py:318
  55.4 1.6 %collective-permute-start.11 = (bf16[2048,128]{1,0:T(8,128)(2,1)S(1)}, bf16[2048,128]{1,0:T(8,128)(2,1)S(1)}, u32[]{:S(2)}, u32[]{:S(2)}) collective-permute-start(bf16[2048,128]{1,0:T(8,128)(2,1)S(1)} %pad_maximum_fusion.1), channel_id=1, source_target_pairs={{0,8},{4,12},{8,0},{12,4},{16,24},{20,28},{24,16},{28,20},{1,9},{5... | collective-permute-start | bytes 1572872 | tf_op jit(solution)/shard_map/ppermute | solution.py:367
  57.0 8.5 %cross_grams.1 = (bf16[49,4,16,128]{3,2,1,0:T(8,128)(2,1)}, bf16[49,4,16,128]{3,2,1,0:T(8,128)(2,1)}) custom-call(s32[2,48]{1,0:T(2,128)} %bitcast.5, bf16[384,2048]{1,0:T(8,128)(2,1)} %collective-permute-done.6.near_hbm, bf16[384,2048]{1,0:T(8,128)(2,1)} %collective-permute-done.7.far_hbm, bf16[8,384]{1,0:T(8,128)(2,1)} %copy-done.6, ...), custom_call_target="tpu_custom_call" | custom-call | flops 805306368 | bytes 6291456 | tf_op jit(solution)/shard_map/cross_grams/pallas_call | solution.py:422
  65.6 0.0 copy-start.3
  65.6 0.1 collective-permute-start.10
  65.6 3.0 %collective-permute-done.11 = bf16[2048,128]{1,0:T(8,128)(2,1)S(1)} collective-permute-done((bf16[2048,128]{1,0:T(8,128)(2,1)S(1)}, bf16[2048,128]{1,0:T(8,128)(2,1)S(1)}, u32[]{:S(2)}, u32[]{:S(2)}) %collective-permute-start.11) | collective-permute-done | bytes 524320 | tf_op jit(solution)/shard_map/ppermute | solution.py:367
  68.6 0.1 pad_maximum_fusion.refs_4_
  68.7 0.4 chip_sums.1
  69.1 0.1 collective-permute-start.15
  69.2 1.6 %collective-permute-start.12 = (bf16[52,16,128]{2,1,0:T(8,128)(2,1)S(1)}, bf16[52,16,128]{2,1,0:T(8,128)(2,1)S(1)}, u32[]{:S(2)}, u32[]{:S(2)}) collective-permute-start(bf16[52,16,128]{2,1,0:T(8,128)(2,1)S(1)} %get-tuple-element.60), channel_id=1, source_target_pairs={{0,8},{4,12},{8,0},{12,4},{16,24},{20,28},{24,16},{28,20},{1,9},{5... | collective-permute-start | bytes 638984 | tf_op jit(solution)/shard_map/ppermute | solution.py:462
  70.7 0.8 collective-permute-start.13
  71.5 1.2 %collective-permute-start.14 = (bf16[52,16,128]{2,1,0:T(8,128)(2,1)S(1)}, bf16[52,16,128]{2,1,0:T(8,128)(2,1)S(1)}, u32[]{:S(2)}, u32[]{:S(2)}) collective-permute-start(bf16[52,16,128]{2,1,0:T(8,128)(2,1)S(1)} %get-tuple-element.62), channel_id=1, source_target_pairs={{0,24},{4,28},{8,16},{12,20},{16,8},{20,12},{24,0},{28,4},{1,25},{... | collective-permute-start | bytes 638984 | tf_op jit(solution)/shard_map/ppermute | solution.py:462
  73.4 3.9 %collective-permute-done.12.refs_1_ = bf16[52,16,128]{2,1,0:T(8,128)(2,1)S(1)} collective-permute-done((bf16[52,16,128]{2,1,0:T(8,128)(2,1)S(1)}, bf16[52,16,128]{2,1,0:T(8,128)(2,1)S(1)}, u32[]{:S(2)}, u32[]{:S(2)}) %collective-permute-start.12) | collective-permute-done | bytes 213024 | tf_op jit(solution)/shard_map/ppermute | solution.py:462
  77.3 5.3 %collective-permute-done.13.refs_2_ = bf16[52,16,128]{2,1,0:T(8,128)(2,1)S(1)} collective-permute-done((bf16[52,16,128]{2,1,0:T(8,128)(2,1)S(1)}, bf16[52,16,128]{2,1,0:T(8,128)(2,1)S(1)}, u32[]{:S(2)}, u32[]{:S(2)}) %collective-permute-start.13) | collective-permute-done | bytes 213024 | tf_op jit(solution)/shard_map/ppermute | solution.py:462
  82.7 4.2 %scores.1 = bf16[48,16,128]{2,1,0:T(8,128)(2,1)} custom-call(s32[2,48]{1,0:T(2,128)S(1)} %bitcast.6, s32[1]{0:T(128)S(6)} %copy.8.live_ref, s32[160]{0:T(256)S(1)} %copy-done.3, f32[52,16,128]{2,1,0:T(8,128)S(1)} %get-tuple-element.59.refs_0_, bf16[52,16,128]{2,1,0:T(8,128)(2,1)S(1)} %collective-permute-done.12.refs_1_, ...), custom_call_target="tpu_custom_call" | custom-call | tf_op jit(solution)/shard_map/scores/pallas_call | solution.py:465
  (28 shorter events, 0.2 us)
Async XLA Ops:
  0.6 1.0 %copy-start = (bf16[16,128,128]{2,1,0:T(8,128)(2,1)S(1)}, bf16[16,128,128]{2,1,0:T(8,128)(2,1)}, u32[]{:S(2)}) copy-start(bf16[16,128,128]{2,1,0:T(8,128)(2,1)} %param.11) | copy-start | bytes 1572868
  1.7 9.9 %collective-permute-start.2 = (bf16[256,128]{1,0:T(8,128)(2,1)S(1)}, bf16[256,128]{1,0:T(8,128)(2,1)S(1)}, u32[]{:S(2)}, u32[]{:S(2)}) collective-permute-start(bf16[256,128]{1,0:T(8,128)(2,1)S(1)} %constant_dynamic-slice_fusion), channel_id=1, source_target_pairs={{0,3},{1,2},{2,1},{3,0},{4,7},{5,6},{6,5},{7,4},{8,11},{9,10},{10,... | collective-permute-start | bytes 196616 | tf_op jit(solution)/shard_map/ppermute | solution.py:328
  3.3 8.4 %collective-permute-start.1 = (bf16[256,128]{1,0:T(8,128)(2,1)S(1)}, bf16[256,128]{1,0:T(8,128)(2,1)S(1)}, u32[]{:S(2)}, u32[]{:S(2)}) collective-permute-start(bf16[256,128]{1,0:T(8,128)(2,1)S(1)} %constant_dynamic-slice_fusion), channel_id=1, source_target_pairs={{0,2},{1,3},{2,0},{3,1},{4,6},{5,7},{6,4},{7,5},{8,10},{9,11},{10,... | collective-permute-start | bytes 196616 | tf_op jit(solution)/shard_map/ppermute | solution.py:328
  4.3 7.3 %collective-permute-start = (bf16[256,128]{1,0:T(8,128)(2,1)S(1)}, bf16[256,128]{1,0:T(8,128)(2,1)S(1)}, u32[]{:S(2)}, u32[]{:S(2)}) collective-permute-start(bf16[256,128]{1,0:T(8,128)(2,1)S(1)} %constant_dynamic-slice_fusion), channel_id=1, source_target_pairs={{0,1},{1,0},{2,3},{3,2},{4,5},{5,4},{6,7},{7,6},{8,9},{9,8},{10,11... | collective-permute-start | bytes 196616 | tf_op jit(solution)/shard_map/ppermute | solution.py:328
  11.7 10.6 %collective-permute-start.3 = (bf16[2,5120]{1,0:T(2,128)(2,1)}, bf16[2,5120]{1,0:T(2,128)(2,1)S(1)}, u32[]{:S(2)}, u32[]{:S(2)}) collective-permute-start(bf16[2,5120]{1,0:T(2,128)(2,1)} %get-tuple-element.40), channel_id=1, source_target_pairs={{4,8},{12,16},{20,24},{8,4},{16,12},{24,20},{5,9},{13,17},{21,25},... | collective-permute-start | bytes 61448 | tf_op jit(solution)/shard_map/ppermute | solution.py:318
  12.4 10.0 %collective-permute-start.4 = (bf16[2,5120]{1,0:T(2,128)(2,1)}, bf16[2,5120]{1,0:T(2,128)(2,1)S(1)}, u32[]{:S(2)}, u32[]{:S(2)}) collective-permute-start(bf16[2,5120]{1,0:T(2,128)(2,1)} %get-tuple-element.41), channel_id=1, source_target_pairs={{0,4},{8,12},{16,20},{24,28},{4,0},{12,8},{20,16},{28,24},{1,5},{9... | collective-permute-start | bytes 61448 | tf_op jit(solution)/shard_map/ppermute | solution.py:318
  15.3 40.1 %collective-permute-start.6 = (bf16[384,2048]{1,0:T(8,128)(2,1)}, bf16[384,2048]{1,0:T(8,128)(2,1)}, u32[]{:S(2)}, u32[]{:S(2)}) collective-permute-start(bf16[384,2048]{1,0:T(8,128)(2,1)} %get-tuple-element.46), channel_id=1, source_target_pairs={{0,1},{2,3},{1,0},{3,2},{4,5},{6,7},{5,4},{7,6},{8,9},{10,11},{9,8... | collective-permute-start | bytes 4718600 | tf_op jit(solution)/shard_map/ppermute | solution.py:318
  16.1 39.3 %collective-permute-start.7 = (bf16[384,2048]{1,0:T(8,128)(2,1)}, bf16[384,2048]{1,0:T(8,128)(2,1)}, u32[]{:S(2)}, u32[]{:S(2)}) collective-permute-start(bf16[384,2048]{1,0:T(8,128)(2,1)} %get-tuple-element.47), channel_id=1, source_target_pairs={{1,2},{2,1},{5,6},{6,5},{9,10},{10,9},{13,14},{14,13},{17,18},{18,... | collective-permute-start | bytes 4718600 | tf_op jit(solution)/shard_map/ppermute | solution.py:318
  20.8 29.8 %collective-permute-start.5 = (bf16[1024,128]{1,0:T(8,128)(2,1)S(1)}, bf16[1024,128]{1,0:T(8,128)(2,1)S(1)}, u32[]{:S(2)}, u32[]{:S(2)}) collective-permute-start(bf16[1024,128]{1,0:T(8,128)(2,1)S(1)} %pad_maximum_fusion.2), channel_id=1, source_target_pairs={{0,16},{4,20},{8,24},{12,28},{16,0},{20,4},{24,8},{28,12},{1,17},{... | collective-permute-start | bytes 786440 | tf_op jit(solution)/shard_map/ppermute | solution.py:367
  22.4 2.0 %copy-start.4 = (bf16[8,5120]{1,0:T(8,128)(2,1)}, bf16[8,5120]{1,0:T(8,128)(2,1)S(1)}, u32[]{:S(2)}) copy-start(bf16[8,5120]{1,0:T(8,128)(2,1)S(1)} %pad_maximum_fusion.3.columns_ref) | copy-start | bytes 245764
  22.5 32.9 %collective-permute-start.9 = (bf16[8,384]{1,0:T(8,128)(2,1)S(1)}, bf16[8,384]{1,0:T(8,128)(2,1)S(1)}, u32[]{:S(2)}, u32[]{:S(2)}) collective-permute-start(bf16[8,384]{1,0:T(8,128)(2,1)S(1)} %get-tuple-element.64), channel_id=1, source_target_pairs={{1,2},{2,1},{5,6},{6,5},{9,10},{10,9},{13,14},{14,13},{17,18},{18,... | collective-permute-start | bytes 18440 | tf_op jit(solution)/shard_map/ppermute | solution.py:318
  24.4 31.0 %collective-permute-start.8 = (bf16[8,384]{1,0:T(8,128)(2,1)S(1)}, bf16[8,384]{1,0:T(8,128)(2,1)S(1)}, u32[]{:S(2)}, u32[]{:S(2)}) collective-permute-start(bf16[8,384]{1,0:T(8,128)(2,1)S(1)} %get-tuple-element.65), channel_id=1, source_target_pairs={{0,1},{2,3},{1,0},{3,2},{4,5},{6,7},{5,4},{7,6},{8,9},{10,11},{9,8... | collective-permute-start | bytes 18440 | tf_op jit(solution)/shard_map/ppermute | solution.py:318
  55.4 1.6 %copy-start.5 = (bf16[8,384]{1,0:T(8,128)(2,1)}, bf16[8,384]{1,0:T(8,128)(2,1)S(1)}, u32[]{:S(2)}) copy-start(bf16[8,384]{1,0:T(8,128)(2,1)S(1)} %collective-permute-done.9.far_columns_hbm) | copy-start | bytes 18436
  55.4 1.6 %copy-start.6 = (bf16[8,384]{1,0:T(8,128)(2,1)}, bf16[8,384]{1,0:T(8,128)(2,1)S(1)}, u32[]{:S(2)}) copy-start(bf16[8,384]{1,0:T(8,128)(2,1)S(1)} %collective-permute-done.8.near_columns_hbm) | copy-start | bytes 18436
  55.4 13.2 %collective-permute-start.11 = (bf16[2048,128]{1,0:T(8,128)(2,1)S(1)}, bf16[2048,128]{1,0:T(8,128)(2,1)S(1)}, u32[]{:S(2)}, u32[]{:S(2)}) collective-permute-start(bf16[2048,128]{1,0:T(8,128)(2,1)S(1)} %pad_maximum_fusion.1), channel_id=1, source_target_pairs={{0,8},{4,12},{8,0},{12,4},{16,24},{20,28},{24,16},{28,20},{1,9},{5... | collective-permute-start | bytes 1572872 | tf_op jit(solution)/shard_map/ppermute | solution.py:367
  65.5 3.2 %copy-start.1 = (bf16[49,4,16,128]{3,2,1,0:T(8,128)(2,1)S(1)}, bf16[49,4,16,128]{3,2,1,0:T(8,128)(2,1)}, u32[]{:S(2)}) copy-start(bf16[49,4,16,128]{3,2,1,0:T(8,128)(2,1)} %get-tuple-element.55.keep_hbm) | copy-start | bytes 2408452
  65.5 17.1 %copy-start.2 = (s32[48,2]{0,1:T(2,128)S(1)}, s32[48,2]{0,1:T(2,128)}, u32[]{:S(2)}) copy-start(s32[48,2]{0,1:T(2,128)} %param.8) | copy-start | bytes 1156
  65.6 17.1 %copy-start.3 = (s32[160]{0:T(256)S(1)}, s32[160]{0:T(256)}, u32[]{:S(2)}) copy-start(s32[160]{0:T(256)} %rules_ref.1) | copy-start | bytes 1924
  65.6 3.1 %collective-permute-start.10 = (bf16[49,4,16,128]{3,2,1,0:T(8,128)(2,1)}, bf16[49,4,16,128]{3,2,1,0:T(8,128)(2,1)S(1)}, u32[]{:S(2)}, u32[]{:S(2)}) collective-permute-start(bf16[49,4,16,128]{3,2,1,0:T(8,128)(2,1)} %get-tuple-element.56), channel_id=1, source_target_pairs={{0,4},{4,0},{8,12},{12,8},{16,20},{20,16},{24,28},{28,24},{1,5},{5... | collective-permute-start | bytes 2408456 | tf_op jit(solution)/shard_map/ppermute | solution.py:442
  69.1 13.5 %collective-permute-start.15 = (bf16[4096,128]{1,0:T(8,128)(2,1)S(1)}, bf16[4096,128]{1,0:T(8,128)(2,1)S(1)}, u32[]{:S(2)}, u32[]{:S(2)}) collective-permute-start(bf16[4096,128]{1,0:T(8,128)(2,1)S(1)} %pad_maximum_fusion.refs_4_), channel_id=1, source_target_pairs={{0,4},{4,0},{8,12},{12,8},{16,20},{20,16},{24,28},{28,24},{1,5},{5... | collective-permute-start | bytes 3145736 | tf_op jit(solution)/shard_map/ppermute | solution.py:367
  69.2 8.1 %collective-permute-start.12 = (bf16[52,16,128]{2,1,0:T(8,128)(2,1)S(1)}, bf16[52,16,128]{2,1,0:T(8,128)(2,1)S(1)}, u32[]{:S(2)}, u32[]{:S(2)}) collective-permute-start(bf16[52,16,128]{2,1,0:T(8,128)(2,1)S(1)} %get-tuple-element.60), channel_id=1, source_target_pairs={{0,8},{4,12},{8,0},{12,4},{16,24},{20,28},{24,16},{28,20},{1,9},{5... | collective-permute-start | bytes 638984 | tf_op jit(solution)/shard_map/ppermute | solution.py:462
  70.7 11.9 %collective-permute-start.13 = (bf16[52,16,128]{2,1,0:T(8,128)(2,1)S(1)}, bf16[52,16,128]{2,1,0:T(8,128)(2,1)S(1)}, u32[]{:S(2)}, u32[]{:S(2)}) collective-permute-start(bf16[52,16,128]{2,1,0:T(8,128)(2,1)S(1)} %get-tuple-element.61), channel_id=1, source_target_pairs={{0,16},{4,20},{8,24},{12,28},{16,0},{20,4},{24,8},{28,12},{1,17},{... | collective-permute-start | bytes 638984 | tf_op jit(solution)/shard_map/ppermute | solution.py:462
  71.5 11.1 %collective-permute-start.14 = (bf16[52,16,128]{2,1,0:T(8,128)(2,1)S(1)}, bf16[52,16,128]{2,1,0:T(8,128)(2,1)S(1)}, u32[]{:S(2)}, u32[]{:S(2)}) collective-permute-start(bf16[52,16,128]{2,1,0:T(8,128)(2,1)S(1)} %get-tuple-element.62), channel_id=1, source_target_pairs={{0,24},{4,28},{8,16},{12,20},{16,8},{20,12},{24,0},{28,4},{1,25},{... | collective-permute-start | bytes 638984 | tf_op jit(solution)/shard_map/ppermute | solution.py:462

commit v14 on v13

--- a/solution.py
+++ b/solution.py
@@ -366,7 +366,8 @@
     def exchange(value, distance):
         return lax.ppermute(value, "pix", [(i, i ^ distance) for i in range(n_pix)])
 
-    mine = jnp.concatenate([mine, exchange(mine, distances[0])], axis=0)
+    for distance in distances[:-1]:
+        mine = jnp.concatenate([mine, exchange(mine, distance)], axis=0)
 
     def place_of(rule):
         row = (rule & (rules_here - 1)) * block
@@ -414,11 +415,6 @@
         name="smooth_and_gram",
     )(table_pairs, images, columns, weights)
     smoothed = smoothed.reshape(rows, width)
-    received = (near_rows, far_rows, near_columns, far_columns)
-    energy, mine, *received = lax.optimization_barrier((energy, mine, *received))
-    for distance in distances[1:-1]:
-        mine = jnp.concatenate([mine, exchange(mine, distance)], axis=0)
-
     keep, give = pl.pallas_call(
         functools.partial(cross_kernel, blocks, block),
         in_specs=[smem] + [hbm] * 4 + [fixed] * 5,
@@ -437,7 +433,7 @@
         compiler_params=params(),
         cost_estimate=cost(4 * edge * width * DEPTH, 8 * edge * width),
         name="cross_grams",
-    )(table_pairs, *received, weights, energy, smoothed, keep, give)
+    )(table_pairs, near_rows, far_rows, near_columns, far_columns, weights, energy, smoothed, keep, give)
 
     got = lax.ppermute(give, "pix", [(i, i ^ 1) for i in range(n_pix)])
     message = jax.ShapeDtypeStruct((slots + units * chips, share, LANES), jnp.bfloat16)

time: 87.2 us -> 86 us (0.986)
  waiting for transfers between devices: 17 us -> 13.6 us
  other arithmetic: 0.26 us -> 2.15 us
    ppermute x6, waiting for transfers between devices: 4.75 us -> 0.02 us  [swapped(): lax.ppermute(value, axis, both + [(j, i) for i, j in both])]
    concatenate x1 -> x2, other arithmetic: 0.07 us -> 2 us  [on_device(): mine = jnp.concatenate([mine, exchange(mine, distance)], axis=0)]
    ppermute x1, waiting for transfers between devices: 0.01 us -> 1.32 us  [on_device(): got = lax.ppermute(give, 'pix', [(i, i ^ 1) for i in range(n_pix)])]
    ppermute x3, waiting for transfers between devices: 2.97 us -> 4.04 us  [exchange(): return lax.ppermute(value, 'pix', [(i, i ^ distance) for i in range(n_pix)])]
    ppermute x3, waiting for transfers between devices: 9.24 us -> 8.19 us  [on_device(): lax.ppermute(m, 'pix', [(i, i ^ 2 * (d + 1)) for i in range(n_pix)])]
  transfers between devices with their start and end apart: 16 -> 16, of which waited for: 4 -> 4; matrix products, arithmetic and copies ran while one was open for 0% -> 3% of each run, Pallas kernels for 47% -> 47%
where the time goes in v14:
time: 86 us; the launch traced here: 85.6 us
  Pallas kernels  44.8 us (52%)
  starting transfers between devices  21.8 us (25%)
  waiting for transfers between devices  13.6 us (16%)
  other arithmetic  2.15 us (2%)
  local copies, waits for them, and re-layouts  1.71 us (2%)
  between operations  1.56 us (2%)
    pallas_call x1, Pallas kernels, on_device(): pl.pallas_call(functools.partial(main_kernel, steps, group, block), grid_...  26.1 us
    ppermute x6, starting transfers between devices, swapped(): lax.ppermute(value, axis, both + [(j, i) for i, j in both])  11.5 us
    pallas_call x1, Pallas kernels, on_device(): pl.pallas_call(functools.partial(cross_kernel, blocks, block), in_specs=[...  8.25 us
    ppermute x3, waiting for transfers between devices, on_device(): lax.ppermute(m, 'pix', [(i, i ^ 2 * (d + 1)) for i in range(n_pix)])  8.19 us
    pallas_call x1, Pallas kernels, on_device(): pl.pallas_call(cut_kernel, in_specs=[hbm, vmem], out_specs=[hbm, hbm, vme...  5.88 us
    pallas_call x1, Pallas kernels, on_device(): pl.pallas_call(functools.partial(score_kernel, blocks, place_of, pixel_co...  4.22 us
    ppermute x3, waiting for transfers between devices, exchange(): return lax.ppermute(value, 'pix', [(i, i ^ distance) for i in range(n_pix)])  4.04 us
    ppermute x3, starting transfers between devices, on_device(): lax.ppermute(m, 'pix', [(i, i ^ 2 * (d + 1)) for i in range(n_pix)])  3.5 us
  transfers between devices with their start and end apart: 16, of which 4 were waited for; matrix products, arithmetic and copies ran while one was open for 3% of the time, Pallas kernels for 47%

profile of v14, /device:TPU:8, one launch (start us, length us, event | category | flops | bytes accessed | tf_op | source)
XLA Modules:
  0.0 85.6 jit_solution(9229505960436615129)
XLA Ops:
  0.6 0.0 copy-start
  0.7 1.0 %copy-done = bf16[16,128,128]{2,1,0:T(8,128)(2,1)S(1)} copy-done((bf16[16,128,128]{2,1,0:T(8,128)(2,1)S(1)}, bf16[16,128,128]{2,1,0:T(8,128)(2,1)}, u32[]{:S(2)}) %copy-start) | copy-done | bytes 524312
  1.7 3.0 %collective-permute-start.1 = (bf16[256,128]{1,0:T(8,128)(2,1)S(1)}, bf16[256,128]{1,0:T(8,128)(2,1)S(1)}, u32[]{:S(2)}, u32[]{:S(2)}) collective-permute-start(bf16[256,128]{1,0:T(8,128)(2,1)S(1)} %constant_dynamic-slice_fusion), channel_id=1, source_target_pairs={{0,2},{1,3},{2,0},{3,1},{4,6},{5,7},{6,4},{7,5},{8,10},{9,11},{10,... | collective-permute-start | bytes 196616 | tf_op jit(solution)/shard_map/ppermute | solution.py:328
  4.7 0.5 collective-permute-start.2
  5.2 5.9 %cut_edges.1 = (bf16[384,2048]{1,0:T(8,128)(2,1)}, bf16[384,2048]{1,0:T(8,128)(2,1)}, bf16[2,5120]{1,0:T(2,128)(2,1)}, bf16[2,5120]{1,0:T(2,128)(2,1)}, bf16[17,256,128]{2,1,0:T(8,128)(2,1)}) custom-call(bf16[5120,2048]{1,0:T(8,128)(2,1)} %x_ref.1, f32[5,2048]{1,0:T(8,128)} %stencil_ref.1), custom_call_target="tpu_custom_call" | custom-call | bytes 6291456 | tf_op jit(solution)/shard_map/cut_edges/pallas_call | solution.py:332
  11.1 0.7 collective-permute-start.3
  11.8 2.9 %collective-permute-start.4 = (bf16[2,5120]{1,0:T(2,128)(2,1)}, bf16[2,5120]{1,0:T(2,128)(2,1)S(1)}, u32[]{:S(2)}, u32[]{:S(2)}) collective-permute-start(bf16[2,5120]{1,0:T(2,128)(2,1)} %get-tuple-element.35), channel_id=1, source_target_pairs={{0,4},{8,12},{16,20},{24,28},{4,0},{12,8},{20,16},{28,24},{1,5},{9... | collective-permute-start | bytes 61448 | tf_op jit(solution)/shard_map/ppermute | solution.py:318
  14.7 1.3 %collective-permute-start.5 = (bf16[384,2048]{1,0:T(8,128)(2,1)}, bf16[384,2048]{1,0:T(8,128)(2,1)}, u32[]{:S(2)}, u32[]{:S(2)}) collective-permute-start(bf16[384,2048]{1,0:T(8,128)(2,1)} %get-tuple-element.38), channel_id=1, source_target_pairs={{0,1},{2,3},{1,0},{3,2},{4,5},{6,7},{5,4},{7,6},{8,9},{10,11},{9,8... | collective-permute-start | bytes 4718600 | tf_op jit(solution)/shard_map/ppermute | solution.py:318
  16.1 4.6 %collective-permute-start.6 = (bf16[384,2048]{1,0:T(8,128)(2,1)}, bf16[384,2048]{1,0:T(8,128)(2,1)}, u32[]{:S(2)}, u32[]{:S(2)}) collective-permute-start(bf16[384,2048]{1,0:T(8,128)(2,1)} %get-tuple-element.39), channel_id=1, source_target_pairs={{1,2},{2,1},{5,6},{6,5},{9,10},{10,9},{13,14},{14,13},{17,18},{18,... | collective-permute-start | bytes 4718600 | tf_op jit(solution)/shard_map/ppermute | solution.py:318
  20.7 0.1 pad.6.clone
  20.8 1.5 %collective-permute-start.10 = (bf16[1024,128]{1,0:T(8,128)(2,1)S(1)}, bf16[1024,128]{1,0:T(8,128)(2,1)S(1)}, u32[]{:S(2)}, u32[]{:S(2)}) collective-permute-start(bf16[1024,128]{1,0:T(8,128)(2,1)S(1)} %pad_maximum_fusion.2), channel_id=1, source_target_pairs={{0,16},{4,20},{8,24},{12,28},{16,0},{20,4},{24,8},{28,12},{1,17},{... | collective-permute-start | bytes 786440 | tf_op jit(solution)/shard_map/ppermute | solution.py:367
  22.3 0.1 pad_maximum_fusion.3.columns_ref
  22.5 0.1 collective-permute-start.7
  22.5 1.9 %collective-permute-start.8 = (bf16[8,384]{1,0:T(8,128)(2,1)S(1)}, bf16[8,384]{1,0:T(8,128)(2,1)S(1)}, u32[]{:S(2)}, u32[]{:S(2)}) collective-permute-start(bf16[8,384]{1,0:T(8,128)(2,1)S(1)} %get-tuple-element.52), channel_id=1, source_target_pairs={{1,2},{2,1},{5,6},{6,5},{9,10},{10,9},{13,14},{14,13},{17,18},{18,... | collective-permute-start | bytes 18440 | tf_op jit(solution)/shard_map/ppermute | solution.py:318
  24.5 4.0 %collective-permute-done.10 = bf16[1024,128]{1,0:T(8,128)(2,1)S(1)} collective-permute-done((bf16[1024,128]{1,0:T(8,128)(2,1)S(1)}, bf16[1024,128]{1,0:T(8,128)(2,1)S(1)}, u32[]{:S(2)}, u32[]{:S(2)}) %collective-permute-start.10) | collective-permute-done | bytes 262176 | tf_op jit(solution)/shard_map/ppermute | solution.py:367
  28.5 0.8 pad_maximum_fusion.1
  29.3 1.5 %collective-permute-start.11 = (bf16[2048,128]{1,0:T(8,128)(2,1)}, bf16[2048,128]{1,0:T(8,128)(2,1)}, u32[]{:S(2)}, u32[]{:S(2)}) collective-permute-start(bf16[2048,128]{1,0:T(8,128)(2,1)} %pad_maximum_fusion.1), channel_id=1, source_target_pairs={{0,8},{4,12},{8,0},{12,4},{16,24},{20,28},{24,16},{28,20},{1,9},{5... | collective-permute-start | bytes 1572872 | tf_op jit(solution)/shard_map/ppermute | solution.py:367
  30.8 26.1 %smooth_and_gram.1 = (bf16[40,128,2048]{2,1,0:T(8,128)(2,1)}, f32[40,128]{1,0:T(8,128)}, bf16[49,4,16,128]{3,2,1,0:T(8,128)(2,1)}, bf16[49,4,16,128]{3,2,1,0:T(8,128)(2,1)}) custom-call(s32[2,48]{1,0:T(2,128)} %bitcast.4, bf16[5120,2048]{1,0:T(8,128)(2,1)} %x_ref.1, bf16[8,5120]{1,0:T(8,128)(2,1)} %copy-done.4, ...), custom_call_target="tpu_custom_call" | custom-call | flops 8589934592 | bytes 41943040 | tf_op jit(solution)/shard_map/smooth_and_gram/pallas_call | solution.py:395
  57.0 0.5 copy-done.5
  57.6 0.0 copy-done.6
  57.6 8.3 %cross_grams.1 = (bf16[49,4,16,128]{3,2,1,0:T(8,128)(2,1)}, bf16[49,4,16,128]{3,2,1,0:T(8,128)(2,1)}) custom-call(s32[2,48]{1,0:T(2,128)} %bitcast.5, bf16[384,2048]{1,0:T(8,128)(2,1)} %collective-permute-done.5.near_hbm, bf16[384,2048]{1,0:T(8,128)(2,1)} %collective-permute-done.6.far_hbm, bf16[8,384]{1,0:T(8,128)(2,1)} %copy-done.5, ...), custom_call_target="tpu_custom_call" | custom-call | flops 805306368 | bytes 6291456 | tf_op jit(solution)/shard_map/cross_grams/pallas_call | solution.py:418
  65.9 0.1 collective-permute-start.9
  66.0 1.2 %pad_maximum_fusion.refs_4_ = bf16[4096,128]{1,0:T(8,128)(2,1)S(1)} fusion(bf16[2048,128]{1,0:T(8,128)(2,1)} %collective-permute-done.11, bf16[1024,128]{1,0:T(8,128)(2,1)S(1)} %collective-permute-done.10, bf16[1024,128]{1,0:T(8,128)(2,1)S(1)} %pad_maximum_fusion.2), kind=kLoop, calls=%fused_computation | loop fusion | flops 3145728 | bytes 2097152 | tf_op jit(solution)/shard_map/concatenate | solution.py:370
  67.1 1.3 %collective-permute-done.9.got_hbm = bf16[49,4,16,128]{3,2,1,0:T(8,128)(2,1)S(1)} collective-permute-done((bf16[49,4,16,128]{3,2,1,0:T(8,128)(2,1)}, bf16[49,4,16,128]{3,2,1,0:T(8,128)(2,1)S(1)}, u32[]{:S(2)}, u32[]{:S(2)}) %collective-permute-start.9) | collective-permute-done | bytes 802848 | tf_op jit(solution)/shard_map/ppermute | solution.py:438
  68.5 0.4 chip_sums.1
  68.8 0.2 collective-permute-start.15
  69.0 0.5 collective-permute-start.12
  69.6 1.5 %collective-permute-start.13 = (bf16[52,16,128]{2,1,0:T(8,128)(2,1)S(1)}, bf16[52,16,128]{2,1,0:T(8,128)(2,1)S(1)}, u32[]{:S(2)}, u32[]{:S(2)}) collective-permute-start(bf16[52,16,128]{2,1,0:T(8,128)(2,1)S(1)} %get-tuple-element.49), channel_id=1, source_target_pairs={{0,16},{4,20},{8,24},{12,28},{16,0},{20,4},{24,8},{28,12},{1,17},{... | collective-permute-start | bytes 638984 | tf_op jit(solution)/shard_map/ppermute | solution.py:458
  71.1 1.4 %collective-permute-start.14 = (bf16[52,16,128]{2,1,0:T(8,128)(2,1)S(1)}, bf16[52,16,128]{2,1,0:T(8,128)(2,1)S(1)}, u32[]{:S(2)}, u32[]{:S(2)}) collective-permute-start(bf16[52,16,128]{2,1,0:T(8,128)(2,1)S(1)} %get-tuple-element.50), channel_id=1, source_target_pairs={{0,24},{4,28},{8,16},{12,20},{16,8},{20,12},{24,0},{28,4},{1,25},{... | collective-permute-start | bytes 638984 | tf_op jit(solution)/shard_map/ppermute | solution.py:458
  73.2 3.9 %collective-permute-done.12.refs_1_ = bf16[52,16,128]{2,1,0:T(8,128)(2,1)S(1)} collective-permute-done((bf16[52,16,128]{2,1,0:T(8,128)(2,1)S(1)}, bf16[52,16,128]{2,1,0:T(8,128)(2,1)S(1)}, u32[]{:S(2)}, u32[]{:S(2)}) %collective-permute-start.12) | collective-permute-done | bytes 213024 | tf_op jit(solution)/shard_map/ppermute | solution.py:458
  77.1 4.3 %collective-permute-done.13.refs_2_ = bf16[52,16,128]{2,1,0:T(8,128)(2,1)S(1)} collective-permute-done((bf16[52,16,128]{2,1,0:T(8,128)(2,1)S(1)}, bf16[52,16,128]{2,1,0:T(8,128)(2,1)S(1)}, u32[]{:S(2)}, u32[]{:S(2)}) %collective-permute-start.13) | collective-permute-done | bytes 213024 | tf_op jit(solution)/shard_map/ppermute | solution.py:458
  81.4 4.2 %scores.1 = bf16[48,16,128]{2,1,0:T(8,128)(2,1)} custom-call(s32[2,48]{1,0:T(2,128)S(1)} %bitcast.6, s32[1]{0:T(128)S(6)} %copy.8.live_ref, s32[160]{0:T(256)S(1)} %copy-done.3, f32[52,16,128]{2,1,0:T(8,128)S(1)} %get-tuple-element.47.refs_0_, bf16[52,16,128]{2,1,0:T(8,128)(2,1)S(1)} %collective-permute-done.12.refs_1_, ...), custom_call_target="tpu_custom_call" | custom-call | tf_op jit(solution)/shard_map/scores/pallas_call | solution.py:461
  (28 shorter events, 0.1 us)
Async XLA Ops:
  0.6 1.0 %copy-start = (bf16[16,128,128]{2,1,0:T(8,128)(2,1)S(1)}, bf16[16,128,128]{2,1,0:T(8,128)(2,1)}, u32[]{:S(2)}) copy-start(bf16[16,128,128]{2,1,0:T(8,128)(2,1)} %param.11) | copy-start | bytes 1572868
  1.7 9.4 %collective-permute-start = (bf16[256,128]{1,0:T(8,128)(2,1)S(1)}, bf16[256,128]{1,0:T(8,128)(2,1)S(1)}, u32[]{:S(2)}, u32[]{:S(2)}) collective-permute-start(bf16[256,128]{1,0:T(8,128)(2,1)S(1)} %constant_dynamic-slice_fusion), channel_id=1, source_target_pairs={{0,1},{1,0},{2,3},{3,2},{4,5},{5,4},{6,7},{7,6},{8,9},{9,8},{10,11... | collective-permute-start | bytes 196616 | tf_op jit(solution)/shard_map/ppermute | solution.py:328
  1.7 9.4 %collective-permute-start.1 = (bf16[256,128]{1,0:T(8,128)(2,1)S(1)}, bf16[256,128]{1,0:T(8,128)(2,1)S(1)}, u32[]{:S(2)}, u32[]{:S(2)}) collective-permute-start(bf16[256,128]{1,0:T(8,128)(2,1)S(1)} %constant_dynamic-slice_fusion), channel_id=1, source_target_pairs={{0,2},{1,3},{2,0},{3,1},{4,6},{5,7},{6,4},{7,5},{8,10},{9,11},{10,... | collective-permute-start | bytes 196616 | tf_op jit(solution)/shard_map/ppermute | solution.py:328
  4.7 6.4 %collective-permute-start.2 = (bf16[256,128]{1,0:T(8,128)(2,1)S(1)}, bf16[256,128]{1,0:T(8,128)(2,1)S(1)}, u32[]{:S(2)}, u32[]{:S(2)}) collective-permute-start(bf16[256,128]{1,0:T(8,128)(2,1)S(1)} %constant_dynamic-slice_fusion), channel_id=1, source_target_pairs={{0,3},{1,2},{2,1},{3,0},{4,7},{5,6},{6,5},{7,4},{8,11},{9,10},{10,... | collective-permute-start | bytes 196616 | tf_op jit(solution)/shard_map/ppermute | solution.py:328
  11.1 11.2 %collective-permute-start.3 = (bf16[2,5120]{1,0:T(2,128)(2,1)}, bf16[2,5120]{1,0:T(2,128)(2,1)S(1)}, u32[]{:S(2)}, u32[]{:S(2)}) collective-permute-start(bf16[2,5120]{1,0:T(2,128)(2,1)} %get-tuple-element.34), channel_id=1, source_target_pairs={{4,8},{12,16},{20,24},{8,4},{16,12},{24,20},{5,9},{13,17},{21,25},... | collective-permute-start | bytes 61448 | tf_op jit(solution)/shard_map/ppermute | solution.py:318
  11.8 10.5 %collective-permute-start.4 = (bf16[2,5120]{1,0:T(2,128)(2,1)}, bf16[2,5120]{1,0:T(2,128)(2,1)S(1)}, u32[]{:S(2)}, u32[]{:S(2)}) collective-permute-start(bf16[2,5120]{1,0:T(2,128)(2,1)} %get-tuple-element.35), channel_id=1, source_target_pairs={{0,4},{8,12},{16,20},{24,28},{4,0},{12,8},{20,16},{28,24},{1,5},{9... | collective-permute-start | bytes 61448 | tf_op jit(solution)/shard_map/ppermute | solution.py:318
  14.7 42.3 %collective-permute-start.5 = (bf16[384,2048]{1,0:T(8,128)(2,1)}, bf16[384,2048]{1,0:T(8,128)(2,1)}, u32[]{:S(2)}, u32[]{:S(2)}) collective-permute-start(bf16[384,2048]{1,0:T(8,128)(2,1)} %get-tuple-element.38), channel_id=1, source_target_pairs={{0,1},{2,3},{1,0},{3,2},{4,5},{6,7},{5,4},{7,6},{8,9},{10,11},{9,8... | collective-permute-start | bytes 4718600 | tf_op jit(solution)/shard_map/ppermute | solution.py:318
  16.1 40.9 %collective-permute-start.6 = (bf16[384,2048]{1,0:T(8,128)(2,1)}, bf16[384,2048]{1,0:T(8,128)(2,1)}, u32[]{:S(2)}, u32[]{:S(2)}) collective-permute-start(bf16[384,2048]{1,0:T(8,128)(2,1)} %get-tuple-element.39), channel_id=1, source_target_pairs={{1,2},{2,1},{5,6},{6,5},{9,10},{10,9},{13,14},{14,13},{17,18},{18,... | collective-permute-start | bytes 4718600 | tf_op jit(solution)/shard_map/ppermute | solution.py:318
  20.8 7.7 %collective-permute-start.10 = (bf16[1024,128]{1,0:T(8,128)(2,1)S(1)}, bf16[1024,128]{1,0:T(8,128)(2,1)S(1)}, u32[]{:S(2)}, u32[]{:S(2)}) collective-permute-start(bf16[1024,128]{1,0:T(8,128)(2,1)S(1)} %pad_maximum_fusion.2), channel_id=1, source_target_pairs={{0,16},{4,20},{8,24},{12,28},{16,0},{20,4},{24,8},{28,12},{1,17},{... | collective-permute-start | bytes 786440 | tf_op jit(solution)/shard_map/ppermute | solution.py:367
  22.4 8.4 %copy-start.4 = (bf16[8,5120]{1,0:T(8,128)(2,1)}, bf16[8,5120]{1,0:T(8,128)(2,1)S(1)}, u32[]{:S(2)}) copy-start(bf16[8,5120]{1,0:T(8,128)(2,1)S(1)} %pad_maximum_fusion.3.columns_ref) | copy-start | bytes 245764
  22.5 34.5 %collective-permute-start.7 = (bf16[8,384]{1,0:T(8,128)(2,1)S(1)}, bf16[8,384]{1,0:T(8,128)(2,1)S(1)}, u32[]{:S(2)}, u32[]{:S(2)}) collective-permute-start(bf16[8,384]{1,0:T(8,128)(2,1)S(1)} %get-tuple-element.53), channel_id=1, source_target_pairs={{0,1},{2,3},{1,0},{3,2},{4,5},{6,7},{5,4},{7,6},{8,9},{10,11},{9,8... | collective-permute-start | bytes 18440 | tf_op jit(solution)/shard_map/ppermute | solution.py:318
  22.5 34.4 %collective-permute-start.8 = (bf16[8,384]{1,0:T(8,128)(2,1)S(1)}, bf16[8,384]{1,0:T(8,128)(2,1)S(1)}, u32[]{:S(2)}, u32[]{:S(2)}) collective-permute-start(bf16[8,384]{1,0:T(8,128)(2,1)S(1)} %get-tuple-element.52), channel_id=1, source_target_pairs={{1,2},{2,1},{5,6},{6,5},{9,10},{10,9},{13,14},{14,13},{17,18},{18,... | collective-permute-start | bytes 18440 | tf_op jit(solution)/shard_map/ppermute | solution.py:318
  29.3 36.6 %collective-permute-start.11 = (bf16[2048,128]{1,0:T(8,128)(2,1)}, bf16[2048,128]{1,0:T(8,128)(2,1)}, u32[]{:S(2)}, u32[]{:S(2)}) collective-permute-start(bf16[2048,128]{1,0:T(8,128)(2,1)} %pad_maximum_fusion.1), channel_id=1, source_target_pairs={{0,8},{4,12},{8,0},{12,4},{16,24},{20,28},{24,16},{28,20},{1,9},{5... | collective-permute-start | bytes 1572872 | tf_op jit(solution)/shard_map/ppermute | solution.py:367
  57.0 0.6 copy-start.5
  57.0 0.6 copy-start.6
  65.8 2.6 %copy-start.1 = (bf16[49,4,16,128]{3,2,1,0:T(8,128)(2,1)S(1)}, bf16[49,4,16,128]{3,2,1,0:T(8,128)(2,1)}, u32[]{:S(2)}) copy-start(bf16[49,4,16,128]{3,2,1,0:T(8,128)(2,1)} %get-tuple-element.43.keep_hbm) | copy-start | bytes 2408452
  65.8 15.6 %copy-start.2 = (s32[48,2]{0,1:T(2,128)S(1)}, s32[48,2]{0,1:T(2,128)}, u32[]{:S(2)}) copy-start(s32[48,2]{0,1:T(2,128)} %param.8) | copy-start | bytes 1156
  65.9 15.5 %copy-start.3 = (s32[160]{0:T(256)S(1)}, s32[160]{0:T(256)}, u32[]{:S(2)}) copy-start(s32[160]{0:T(256)} %rules_ref.1) | copy-start | bytes 1924
  65.9 2.6 %collective-permute-start.9 = (bf16[49,4,16,128]{3,2,1,0:T(8,128)(2,1)}, bf16[49,4,16,128]{3,2,1,0:T(8,128)(2,1)S(1)}, u32[]{:S(2)}, u32[]{:S(2)}) collective-permute-start(bf16[49,4,16,128]{3,2,1,0:T(8,128)(2,1)} %get-tuple-element.44), channel_id=1, source_target_pairs={{0,4},{4,0},{8,12},{12,8},{16,20},{20,16},{24,28},{28,24},{1,5},{5... | collective-permute-start | bytes 2408456 | tf_op jit(solution)/shard_map/ppermute | solution.py:438
  68.8 12.6 %collective-permute-start.15 = (bf16[4096,128]{1,0:T(8,128)(2,1)S(1)}, bf16[4096,128]{1,0:T(8,128)(2,1)S(1)}, u32[]{:S(2)}, u32[]{:S(2)}) collective-permute-start(bf16[4096,128]{1,0:T(8,128)(2,1)S(1)} %pad_maximum_fusion.refs_4_), channel_id=1, source_target_pairs={{0,4},{4,0},{8,12},{12,8},{16,20},{20,16},{24,28},{28,24},{1,5},{5... | collective-permute-start | bytes 3145736 | tf_op jit(solution)/shard_map/ppermute | solution.py:367
  69.0 8.1 %collective-permute-start.12 = (bf16[52,16,128]{2,1,0:T(8,128)(2,1)S(1)}, bf16[52,16,128]{2,1,0:T(8,128)(2,1)S(1)}, u32[]{:S(2)}, u32[]{:S(2)}) collective-permute-start(bf16[52,16,128]{2,1,0:T(8,128)(2,1)S(1)} %get-tuple-element.48), channel_id=1, source_target_pairs={{0,8},{4,12},{8,0},{12,4},{16,24},{20,28},{24,16},{28,20},{1,9},{5... | collective-permute-start | bytes 638984 | tf_op jit(solution)/shard_map/ppermute | solution.py:458
  69.6 11.8 %collective-permute-start.13 = (bf16[52,16,128]{2,1,0:T(8,128)(2,1)S(1)}, bf16[52,16,128]{2,1,0:T(8,128)(2,1)S(1)}, u32[]{:S(2)}, u32[]{:S(2)}) collective-permute-start(bf16[52,16,128]{2,1,0:T(8,128)(2,1)S(1)} %get-tuple-element.49), channel_id=1, source_target_pairs={{0,16},{4,20},{8,24},{12,28},{16,0},{20,4},{24,8},{28,12},{1,17},{... | collective-permute-start | bytes 638984 | tf_op jit(solution)/shard_map/ppermute | solution.py:458
  71.1 10.3 %collective-permute-start.14 = (bf16[52,16,128]{2,1,0:T(8,128)(2,1)S(1)}, bf16[52,16,128]{2,1,0:T(8,128)(2,1)S(1)}, u32[]{:S(2)}, u32[]{:S(2)}) collective-permute-start(bf16[52,16,128]{2,1,0:T(8,128)(2,1)S(1)} %get-tuple-element.50), channel_id=1, source_target_pairs={{0,24},{4,28},{8,16},{12,20},{16,8},{20,12},{24,0},{28,4},{1,25},{... | collective-permute-start | bytes 638984 | tf_op jit(solution)/shard_map/ppermute | solution.py:458

commit v15 on v14

--- a/solution.py
+++ b/solution.py
@@ -167,13 +167,13 @@
             keep_ref[s], give_ref[s] = by_core(gram_of(held[a], held[b]), chips, core)
             return carry
 
-        lax.fori_loop(0, slots, one, 0, unroll=12)
+        lax.fori_loop(0, slots, one, 0, unroll=24)
         for k in range(steps):
             copy_out(k).wait()
 
 
 def cross_kernel(blocks, block, pairs_ref, near_hbm, far_hbm, near_columns_hbm, far_columns_hbm, w_hbm, energy_hbm, smoothed_hbm, keep_hbm,
-                 give_hbm, keep_ref, give_ref, x_ref, columns_ref, w_ref, energy_ref, own, other, table, sems):
+                 give_hbm, keep_ref, give_ref, x_ref, columns_ref, w_ref, energy_ref, own, other, table, found, sems):
     core = lax.axis_index("pix") % 2
     first_block = lax.axis_index("ion") * blocks
     slots = pairs_ref.shape[1]
@@ -212,20 +212,25 @@
     for ref in (keep_ref, give_ref):
         ref[slots:] = table[...].reshape(shape).astype(jnp.bfloat16)
 
-    def one(s, carry):
-        a, b = pairs_ref[0, s] - first_block, pairs_ref[1, s] - first_block
-
-        @pl.when((b < 0) | (b >= blocks))
-        def crossing():
+    def gather(s, count):
+        b = pairs_ref[1, s] - first_block
+        found[count] = s
+        return count + ((b < 0) | (b >= blocks)).astype(jnp.int32)
+
+    count = lax.fori_loop(0, slots, gather, 0)
+
+    def four(k, carry):
+        for i in range(4):
+            s = found[jnp.minimum(4 * k + i, count - 1)]
+            a, b = pairs_ref[0, s] - first_block, pairs_ref[1, s] - first_block
             side = (b >= 0).astype(jnp.int32)
             a_row = pl.multiple_of((a - side * (blocks - 2 * REACH)) * block, block)
             b_row = pl.multiple_of((b + REACH - side * blocks) * block, block)
             gram = gram_of(own[pl.ds(a_row, block), :], other[pl.ds(b_row, block), :])
             keep_ref[s], give_ref[s] = by_core(gram, chips, core)
-
         return carry
 
-    lax.fori_loop(0, slots, one, 0)
+    lax.fori_loop(0, (count + 3) // 4, four, 0)
 
 
 def chip_kernel(slots, units, keep_hbm, got_hbm, own_ref, *refs):
@@ -264,7 +269,7 @@
             place[k, s] = at
         return carry
 
-    lax.fori_loop(0, slots, find, 0)
+    lax.fori_loop(0, slots, find, 0, unroll=8)
     for copy in copies[:-2]:
         copy.wait()
     gram = own_ref[:slots]
@@ -428,6 +433,7 @@
             pltpu.VMEM((2 * edge, width), jnp.bfloat16),
             pltpu.VMEM((2 * edge, width), jnp.bfloat16),
             pltpu.VMEM((units * block // 2, LANES), jnp.float32),
+            pltpu.SMEM((slots + 1,), jnp.int32),
             pltpu.SemaphoreType.DMA((10,)),
         ],
         compiler_params=params(),

time: 86 us -> 85 us (0.988)
  Pallas kernels: 44.8 us -> 43.8 us
where the time goes in v15:
time: 85 us; the launch traced here: 84.6 us
  Pallas kernels  43.8 us (52%)
  starting transfers between devices  21.8 us (26%)
  waiting for transfers between devices  13.6 us (16%)
  other arithmetic  2.15 us (3%)
  local copies, waits for them, and re-layouts  1.71 us (2%)
  between operations  1.56 us (2%)
    pallas_call x1, Pallas kernels, on_device(): pl.pallas_call(functools.partial(main_kernel, steps, group, block), grid_...  26 us
    ppermute x6, starting transfers between devices, swapped(): lax.ppermute(value, axis, both + [(j, i) for i, j in both])  11.5 us
    ppermute x3, waiting for transfers between devices, on_device(): lax.ppermute(m, 'pix', [(i, i ^ 2 * (d + 1)) for i in range(n_pix)])  8.2 us
    pallas_call x1, Pallas kernels, on_device(): pl.pallas_call(functools.partial(cross_kernel, blocks, block), in_specs=[...  7.67 us
    pallas_call x1, Pallas kernels, on_device(): pl.pallas_call(cut_kernel, in_specs=[hbm, vmem], out_specs=[hbm, hbm, vme...  5.88 us
    ppermute x3, waiting for transfers between devices, exchange(): return lax.ppermute(value, 'pix', [(i, i ^ distance) for i in range(n_pix)])  4.04 us
    pallas_call x1, Pallas kernels, on_device(): pl.pallas_call(functools.partial(score_kernel, blocks, place_of, pixel_co...  3.84 us
    ppermute x3, starting transfers between devices, on_device(): lax.ppermute(m, 'pix', [(i, i ^ 2 * (d + 1)) for i in range(n_pix)])  3.5 us
  transfers between devices with their start and end apart: 16, of which 4 were waited for; matrix products, arithmetic and copies ran while one was open for 3% of the time, Pallas kernels for 47%

profile of v15, /device:TPU:8, one launch (start us, length us, event | category | flops | bytes accessed | tf_op | source)
XLA Modules:
  0.0 84.6 jit_solution(17760710105128127353)
XLA Ops:
  0.6 0.0 copy-start
  0.7 1.0 %copy-done = bf16[16,128,128]{2,1,0:T(8,128)(2,1)S(1)} copy-done((bf16[16,128,128]{2,1,0:T(8,128)(2,1)S(1)}, bf16[16,128,128]{2,1,0:T(8,128)(2,1)}, u32[]{:S(2)}) %copy-start) | copy-done | bytes 524312
  1.7 3.0 %collective-permute-start.1 = (bf16[256,128]{1,0:T(8,128)(2,1)S(1)}, bf16[256,128]{1,0:T(8,128)(2,1)S(1)}, u32[]{:S(2)}, u32[]{:S(2)}) collective-permute-start(bf16[256,128]{1,0:T(8,128)(2,1)S(1)} %constant_dynamic-slice_fusion), channel_id=1, source_target_pairs={{0,2},{1,3},{2,0},{3,1},{4,6},{5,7},{6,4},{7,5},{8,10},{9,11},{10,... | collective-permute-start | bytes 196616 | tf_op jit(solution)/shard_map/ppermute | solution.py:333
  4.7 0.5 collective-permute-start.2
  5.2 5.9 %cut_edges.1 = (bf16[384,2048]{1,0:T(8,128)(2,1)}, bf16[384,2048]{1,0:T(8,128)(2,1)}, bf16[2,5120]{1,0:T(2,128)(2,1)}, bf16[2,5120]{1,0:T(2,128)(2,1)}, bf16[17,256,128]{2,1,0:T(8,128)(2,1)}) custom-call(bf16[5120,2048]{1,0:T(8,128)(2,1)} %x_ref.1, f32[5,2048]{1,0:T(8,128)} %stencil_ref.1), custom_call_target="tpu_custom_call" | custom-call | bytes 6291456 | tf_op jit(solution)/shard_map/cut_edges/pallas_call | solution.py:337
  11.1 0.7 collective-permute-start.3
  11.8 2.9 %collective-permute-start.4 = (bf16[2,5120]{1,0:T(2,128)(2,1)}, bf16[2,5120]{1,0:T(2,128)(2,1)S(1)}, u32[]{:S(2)}, u32[]{:S(2)}) collective-permute-start(bf16[2,5120]{1,0:T(2,128)(2,1)} %get-tuple-element.35), channel_id=1, source_target_pairs={{0,4},{8,12},{16,20},{24,28},{4,0},{12,8},{20,16},{28,24},{1,5},{9... | collective-permute-start | bytes 61448 | tf_op jit(solution)/shard_map/ppermute | solution.py:323
  14.7 1.3 %collective-permute-start.5 = (bf16[384,2048]{1,0:T(8,128)(2,1)}, bf16[384,2048]{1,0:T(8,128)(2,1)}, u32[]{:S(2)}, u32[]{:S(2)}) collective-permute-start(bf16[384,2048]{1,0:T(8,128)(2,1)} %get-tuple-element.38), channel_id=1, source_target_pairs={{0,1},{2,3},{1,0},{3,2},{4,5},{6,7},{5,4},{7,6},{8,9},{10,11},{9,8... | collective-permute-start | bytes 4718600 | tf_op jit(solution)/shard_map/ppermute | solution.py:323
  16.1 4.6 %collective-permute-start.6 = (bf16[384,2048]{1,0:T(8,128)(2,1)}, bf16[384,2048]{1,0:T(8,128)(2,1)}, u32[]{:S(2)}, u32[]{:S(2)}) collective-permute-start(bf16[384,2048]{1,0:T(8,128)(2,1)} %get-tuple-element.39), channel_id=1, source_target_pairs={{1,2},{2,1},{5,6},{6,5},{9,10},{10,9},{13,14},{14,13},{17,18},{18,... | collective-permute-start | bytes 4718600 | tf_op jit(solution)/shard_map/ppermute | solution.py:323
  20.7 0.1 pad.6.clone
  20.8 1.5 %collective-permute-start.10 = (bf16[1024,128]{1,0:T(8,128)(2,1)S(1)}, bf16[1024,128]{1,0:T(8,128)(2,1)S(1)}, u32[]{:S(2)}, u32[]{:S(2)}) collective-permute-start(bf16[1024,128]{1,0:T(8,128)(2,1)S(1)} %pad_maximum_fusion.2), channel_id=1, source_target_pairs={{0,16},{4,20},{8,24},{12,28},{16,0},{20,4},{24,8},{28,12},{1,17},{... | collective-permute-start | bytes 786440 | tf_op jit(solution)/shard_map/ppermute | solution.py:372
  22.3 0.1 pad_maximum_fusion.3.columns_ref
  22.5 0.1 collective-permute-start.7
  22.5 1.9 %collective-permute-start.8 = (bf16[8,384]{1,0:T(8,128)(2,1)S(1)}, bf16[8,384]{1,0:T(8,128)(2,1)S(1)}, u32[]{:S(2)}, u32[]{:S(2)}) collective-permute-start(bf16[8,384]{1,0:T(8,128)(2,1)S(1)} %get-tuple-element.52), channel_id=1, source_target_pairs={{1,2},{2,1},{5,6},{6,5},{9,10},{10,9},{13,14},{14,13},{17,18},{18,... | collective-permute-start | bytes 18440 | tf_op jit(solution)/shard_map/ppermute | solution.py:323
  24.5 4.0 %collective-permute-done.10 = bf16[1024,128]{1,0:T(8,128)(2,1)S(1)} collective-permute-done((bf16[1024,128]{1,0:T(8,128)(2,1)S(1)}, bf16[1024,128]{1,0:T(8,128)(2,1)S(1)}, u32[]{:S(2)}, u32[]{:S(2)}) %collective-permute-start.10) | collective-permute-done | bytes 262176 | tf_op jit(solution)/shard_map/ppermute | solution.py:372
  28.5 0.8 pad_maximum_fusion.1
  29.3 1.5 %collective-permute-start.11 = (bf16[2048,128]{1,0:T(8,128)(2,1)}, bf16[2048,128]{1,0:T(8,128)(2,1)}, u32[]{:S(2)}, u32[]{:S(2)}) collective-permute-start(bf16[2048,128]{1,0:T(8,128)(2,1)} %pad_maximum_fusion.1), channel_id=1, source_target_pairs={{0,8},{4,12},{8,0},{12,4},{16,24},{20,28},{24,16},{28,20},{1,9},{5... | collective-permute-start | bytes 1572872 | tf_op jit(solution)/shard_map/ppermute | solution.py:372
  30.8 26.0 %smooth_and_gram.1 = (bf16[40,128,2048]{2,1,0:T(8,128)(2,1)}, f32[40,128]{1,0:T(8,128)}, bf16[49,4,16,128]{3,2,1,0:T(8,128)(2,1)}, bf16[49,4,16,128]{3,2,1,0:T(8,128)(2,1)}) custom-call(s32[2,48]{1,0:T(2,128)} %bitcast.4, bf16[5120,2048]{1,0:T(8,128)(2,1)} %x_ref.1, bf16[8,5120]{1,0:T(8,128)(2,1)} %copy-done.4, ...), custom_call_target="tpu_custom_call" | custom-call | flops 8589934592 | bytes 41943040 | tf_op jit(solution)/shard_map/smooth_and_gram/pallas_call | solution.py:400
  56.9 0.5 copy-done.5
  57.5 0.0 copy-done.6
  57.5 7.7 %cross_grams.1 = (bf16[49,4,16,128]{3,2,1,0:T(8,128)(2,1)}, bf16[49,4,16,128]{3,2,1,0:T(8,128)(2,1)}) custom-call(s32[2,48]{1,0:T(2,128)} %bitcast.5, bf16[384,2048]{1,0:T(8,128)(2,1)} %collective-permute-done.5.near_hbm, bf16[384,2048]{1,0:T(8,128)(2,1)} %collective-permute-done.6.far_hbm, bf16[8,384]{1,0:T(8,128)(2,1)} %copy-done.5, ...), custom_call_target="tpu_custom_call" | custom-call | flops 805306368 | bytes 6291456 | tf_op jit(solution)/shard_map/cross_grams/pallas_call | solution.py:423
  65.2 0.1 collective-permute-start.9
  65.3 1.2 %pad_maximum_fusion.refs_4_ = bf16[4096,128]{1,0:T(8,128)(2,1)S(1)} fusion(bf16[2048,128]{1,0:T(8,128)(2,1)} %collective-permute-done.11, bf16[1024,128]{1,0:T(8,128)(2,1)S(1)} %collective-permute-done.10, bf16[1024,128]{1,0:T(8,128)(2,1)S(1)} %pad_maximum_fusion.2), kind=kLoop, calls=%fused_computation | loop fusion | flops 3145728 | bytes 2097152 | tf_op jit(solution)/shard_map/concatenate | solution.py:375
  66.5 1.3 %collective-permute-done.9.got_hbm = bf16[49,4,16,128]{3,2,1,0:T(8,128)(2,1)S(1)} collective-permute-done((bf16[49,4,16,128]{3,2,1,0:T(8,128)(2,1)}, bf16[49,4,16,128]{3,2,1,0:T(8,128)(2,1)S(1)}, u32[]{:S(2)}, u32[]{:S(2)}) %collective-permute-start.9) | collective-permute-done | bytes 802848 | tf_op jit(solution)/shard_map/ppermute | solution.py:444
  67.8 0.4 chip_sums.1
  68.2 0.2 collective-permute-start.15
  68.4 0.6 collective-permute-start.12
  68.9 1.5 %collective-permute-start.13 = (bf16[52,16,128]{2,1,0:T(8,128)(2,1)S(1)}, bf16[52,16,128]{2,1,0:T(8,128)(2,1)S(1)}, u32[]{:S(2)}, u32[]{:S(2)}) collective-permute-start(bf16[52,16,128]{2,1,0:T(8,128)(2,1)S(1)} %get-tuple-element.49), channel_id=1, source_target_pairs={{0,16},{4,20},{8,24},{12,28},{16,0},{20,4},{24,8},{28,12},{1,17},{... | collective-permute-start | bytes 638984 | tf_op jit(solution)/shard_map/ppermute | solution.py:464
  70.5 1.4 %collective-permute-start.14 = (bf16[52,16,128]{2,1,0:T(8,128)(2,1)S(1)}, bf16[52,16,128]{2,1,0:T(8,128)(2,1)S(1)}, u32[]{:S(2)}, u32[]{:S(2)}) collective-permute-start(bf16[52,16,128]{2,1,0:T(8,128)(2,1)S(1)} %get-tuple-element.50), channel_id=1, source_target_pairs={{0,24},{4,28},{8,16},{12,20},{16,8},{20,12},{24,0},{28,4},{1,25},{... | collective-permute-start | bytes 638984 | tf_op jit(solution)/shard_map/ppermute | solution.py:464
  72.5 3.9 %collective-permute-done.12.refs_1_ = bf16[52,16,128]{2,1,0:T(8,128)(2,1)S(1)} collective-permute-done((bf16[52,16,128]{2,1,0:T(8,128)(2,1)S(1)}, bf16[52,16,128]{2,1,0:T(8,128)(2,1)S(1)}, u32[]{:S(2)}, u32[]{:S(2)}) %collective-permute-start.12) | collective-permute-done | bytes 213024 | tf_op jit(solution)/shard_map/ppermute | solution.py:464
  76.5 4.3 %collective-permute-done.13.refs_2_ = bf16[52,16,128]{2,1,0:T(8,128)(2,1)S(1)} collective-permute-done((bf16[52,16,128]{2,1,0:T(8,128)(2,1)S(1)}, bf16[52,16,128]{2,1,0:T(8,128)(2,1)S(1)}, u32[]{:S(2)}, u32[]{:S(2)}) %collective-permute-start.13) | collective-permute-done | bytes 213024 | tf_op jit(solution)/shard_map/ppermute | solution.py:464
  80.8 3.8 %scores.1 = bf16[48,16,128]{2,1,0:T(8,128)(2,1)} custom-call(s32[2,48]{1,0:T(2,128)S(1)} %bitcast.6, s32[1]{0:T(128)S(6)} %copy.8.live_ref, s32[160]{0:T(256)S(1)} %copy-done.3, f32[52,16,128]{2,1,0:T(8,128)S(1)} %get-tuple-element.47.refs_0_, bf16[52,16,128]{2,1,0:T(8,128)(2,1)S(1)} %collective-permute-done.12.refs_1_, ...), custom_call_target="tpu_custom_call" | custom-call | tf_op jit(solution)/shard_map/scores/pallas_call | solution.py:467
  (28 shorter events, 0.1 us)
Async XLA Ops:
  0.6 1.0 %copy-start = (bf16[16,128,128]{2,1,0:T(8,128)(2,1)S(1)}, bf16[16,128,128]{2,1,0:T(8,128)(2,1)}, u32[]{:S(2)}) copy-start(bf16[16,128,128]{2,1,0:T(8,128)(2,1)} %param.11) | copy-start | bytes 1572868
  1.7 9.4 %collective-permute-start = (bf16[256,128]{1,0:T(8,128)(2,1)S(1)}, bf16[256,128]{1,0:T(8,128)(2,1)S(1)}, u32[]{:S(2)}, u32[]{:S(2)}) collective-permute-start(bf16[256,128]{1,0:T(8,128)(2,1)S(1)} %constant_dynamic-slice_fusion), channel_id=1, source_target_pairs={{0,1},{1,0},{2,3},{3,2},{4,5},{5,4},{6,7},{7,6},{8,9},{9,8},{10,11... | collective-permute-start | bytes 196616 | tf_op jit(solution)/shard_map/ppermute | solution.py:333
  1.7 9.4 %collective-permute-start.1 = (bf16[256,128]{1,0:T(8,128)(2,1)S(1)}, bf16[256,128]{1,0:T(8,128)(2,1)S(1)}, u32[]{:S(2)}, u32[]{:S(2)}) collective-permute-start(bf16[256,128]{1,0:T(8,128)(2,1)S(1)} %constant_dynamic-slice_fusion), channel_id=1, source_target_pairs={{0,2},{1,3},{2,0},{3,1},{4,6},{5,7},{6,4},{7,5},{8,10},{9,11},{10,... | collective-permute-start | bytes 196616 | tf_op jit(solution)/shard_map/ppermute | solution.py:333
  4.7 6.4 %collective-permute-start.2 = (bf16[256,128]{1,0:T(8,128)(2,1)S(1)}, bf16[256,128]{1,0:T(8,128)(2,1)S(1)}, u32[]{:S(2)}, u32[]{:S(2)}) collective-permute-start(bf16[256,128]{1,0:T(8,128)(2,1)S(1)} %constant_dynamic-slice_fusion), channel_id=1, source_target_pairs={{0,3},{1,2},{2,1},{3,0},{4,7},{5,6},{6,5},{7,4},{8,11},{9,10},{10,... | collective-permute-start | bytes 196616 | tf_op jit(solution)/shard_map/ppermute | solution.py:333
  11.1 11.2 %collective-permute-start.3 = (bf16[2,5120]{1,0:T(2,128)(2,1)}, bf16[2,5120]{1,0:T(2,128)(2,1)S(1)}, u32[]{:S(2)}, u32[]{:S(2)}) collective-permute-start(bf16[2,5120]{1,0:T(2,128)(2,1)} %get-tuple-element.34), channel_id=1, source_target_pairs={{4,8},{12,16},{20,24},{8,4},{16,12},{24,20},{5,9},{13,17},{21,25},... | collective-permute-start | bytes 61448 | tf_op jit(solution)/shard_map/ppermute | solution.py:323
  11.8 10.5 %collective-permute-start.4 = (bf16[2,5120]{1,0:T(2,128)(2,1)}, bf16[2,5120]{1,0:T(2,128)(2,1)S(1)}, u32[]{:S(2)}, u32[]{:S(2)}) collective-permute-start(bf16[2,5120]{1,0:T(2,128)(2,1)} %get-tuple-element.35), channel_id=1, source_target_pairs={{0,4},{8,12},{16,20},{24,28},{4,0},{12,8},{20,16},{28,24},{1,5},{9... | collective-permute-start | bytes 61448 | tf_op jit(solution)/shard_map/ppermute | solution.py:323
  14.7 42.2 %collective-permute-start.5 = (bf16[384,2048]{1,0:T(8,128)(2,1)}, bf16[384,2048]{1,0:T(8,128)(2,1)}, u32[]{:S(2)}, u32[]{:S(2)}) collective-permute-start(bf16[384,2048]{1,0:T(8,128)(2,1)} %get-tuple-element.38), channel_id=1, source_target_pairs={{0,1},{2,3},{1,0},{3,2},{4,5},{6,7},{5,4},{7,6},{8,9},{10,11},{9,8... | collective-permute-start | bytes 4718600 | tf_op jit(solution)/shard_map/ppermute | solution.py:323
  16.1 40.9 %collective-permute-start.6 = (bf16[384,2048]{1,0:T(8,128)(2,1)}, bf16[384,2048]{1,0:T(8,128)(2,1)}, u32[]{:S(2)}, u32[]{:S(2)}) collective-permute-start(bf16[384,2048]{1,0:T(8,128)(2,1)} %get-tuple-element.39), channel_id=1, source_target_pairs={{1,2},{2,1},{5,6},{6,5},{9,10},{10,9},{13,14},{14,13},{17,18},{18,... | collective-permute-start | bytes 4718600 | tf_op jit(solution)/shard_map/ppermute | solution.py:323
  20.8 7.7 %collective-permute-start.10 = (bf16[1024,128]{1,0:T(8,128)(2,1)S(1)}, bf16[1024,128]{1,0:T(8,128)(2,1)S(1)}, u32[]{:S(2)}, u32[]{:S(2)}) collective-permute-start(bf16[1024,128]{1,0:T(8,128)(2,1)S(1)} %pad_maximum_fusion.2), channel_id=1, source_target_pairs={{0,16},{4,20},{8,24},{12,28},{16,0},{20,4},{24,8},{28,12},{1,17},{... | collective-permute-start | bytes 786440 | tf_op jit(solution)/shard_map/ppermute | solution.py:372
  22.4 8.4 %copy-start.4 = (bf16[8,5120]{1,0:T(8,128)(2,1)}, bf16[8,5120]{1,0:T(8,128)(2,1)S(1)}, u32[]{:S(2)}) copy-start(bf16[8,5120]{1,0:T(8,128)(2,1)S(1)} %pad_maximum_fusion.3.columns_ref) | copy-start | bytes 245764
  22.5 34.4 %collective-permute-start.7 = (bf16[8,384]{1,0:T(8,128)(2,1)S(1)}, bf16[8,384]{1,0:T(8,128)(2,1)S(1)}, u32[]{:S(2)}, u32[]{:S(2)}) collective-permute-start(bf16[8,384]{1,0:T(8,128)(2,1)S(1)} %get-tuple-element.53), channel_id=1, source_target_pairs={{0,1},{2,3},{1,0},{3,2},{4,5},{6,7},{5,4},{7,6},{8,9},{10,11},{9,8... | collective-permute-start | bytes 18440 | tf_op jit(solution)/shard_map/ppermute | solution.py:323
  22.5 34.4 %collective-permute-start.8 = (bf16[8,384]{1,0:T(8,128)(2,1)S(1)}, bf16[8,384]{1,0:T(8,128)(2,1)S(1)}, u32[]{:S(2)}, u32[]{:S(2)}) collective-permute-start(bf16[8,384]{1,0:T(8,128)(2,1)S(1)} %get-tuple-element.52), channel_id=1, source_target_pairs={{1,2},{2,1},{5,6},{6,5},{9,10},{10,9},{13,14},{14,13},{17,18},{18,... | collective-permute-start | bytes 18440 | tf_op jit(solution)/shard_map/ppermute | solution.py:323
  29.3 36.0 %collective-permute-start.11 = (bf16[2048,128]{1,0:T(8,128)(2,1)}, bf16[2048,128]{1,0:T(8,128)(2,1)}, u32[]{:S(2)}, u32[]{:S(2)}) collective-permute-start(bf16[2048,128]{1,0:T(8,128)(2,1)} %pad_maximum_fusion.1), channel_id=1, source_target_pairs={{0,8},{4,12},{8,0},{12,4},{16,24},{20,28},{24,16},{28,20},{1,9},{5... | collective-permute-start | bytes 1572872 | tf_op jit(solution)/shard_map/ppermute | solution.py:372
  56.9 0.6 copy-start.5
  56.9 0.6 copy-start.6
  65.2 2.6 %copy-start.1 = (bf16[49,4,16,128]{3,2,1,0:T(8,128)(2,1)S(1)}, bf16[49,4,16,128]{3,2,1,0:T(8,128)(2,1)}, u32[]{:S(2)}) copy-start(bf16[49,4,16,128]{3,2,1,0:T(8,128)(2,1)} %get-tuple-element.43.keep_hbm) | copy-start | bytes 2408452
  65.2 15.6 %copy-start.2 = (s32[48,2]{0,1:T(2,128)S(1)}, s32[48,2]{0,1:T(2,128)}, u32[]{:S(2)}) copy-start(s32[48,2]{0,1:T(2,128)} %param.8) | copy-start | bytes 1156
  65.2 15.6 %copy-start.3 = (s32[160]{0:T(256)S(1)}, s32[160]{0:T(256)}, u32[]{:S(2)}) copy-start(s32[160]{0:T(256)} %rules_ref.1) | copy-start | bytes 1924
  65.2 2.6 %collective-permute-start.9 = (bf16[49,4,16,128]{3,2,1,0:T(8,128)(2,1)}, bf16[49,4,16,128]{3,2,1,0:T(8,128)(2,1)S(1)}, u32[]{:S(2)}, u32[]{:S(2)}) collective-permute-start(bf16[49,4,16,128]{3,2,1,0:T(8,128)(2,1)} %get-tuple-element.44), channel_id=1, source_target_pairs={{0,4},{4,0},{8,12},{12,8},{16,20},{20,16},{24,28},{28,24},{1,5},{5... | collective-permute-start | bytes 2408456 | tf_op jit(solution)/shard_map/ppermute | solution.py:444
  68.2 12.6 %collective-permute-start.15 = (bf16[4096,128]{1,0:T(8,128)(2,1)S(1)}, bf16[4096,128]{1,0:T(8,128)(2,1)S(1)}, u32[]{:S(2)}, u32[]{:S(2)}) collective-permute-start(bf16[4096,128]{1,0:T(8,128)(2,1)S(1)} %pad_maximum_fusion.refs_4_), channel_id=1, source_target_pairs={{0,4},{4,0},{8,12},{12,8},{16,20},{20,16},{24,28},{28,24},{1,5},{5... | collective-permute-start | bytes 3145736 | tf_op jit(solution)/shard_map/ppermute | solution.py:372
  68.4 8.1 %collective-permute-start.12 = (bf16[52,16,128]{2,1,0:T(8,128)(2,1)S(1)}, bf16[52,16,128]{2,1,0:T(8,128)(2,1)S(1)}, u32[]{:S(2)}, u32[]{:S(2)}) collective-permute-start(bf16[52,16,128]{2,1,0:T(8,128)(2,1)S(1)} %get-tuple-element.48), channel_id=1, source_target_pairs={{0,8},{4,12},{8,0},{12,4},{16,24},{20,28},{24,16},{28,20},{1,9},{5... | collective-permute-start | bytes 638984 | tf_op jit(solution)/shard_map/ppermute | solution.py:464
  68.9 11.8 %collective-permute-start.13 = (bf16[52,16,128]{2,1,0:T(8,128)(2,1)S(1)}, bf16[52,16,128]{2,1,0:T(8,128)(2,1)S(1)}, u32[]{:S(2)}, u32[]{:S(2)}) collective-permute-start(bf16[52,16,128]{2,1,0:T(8,128)(2,1)S(1)} %get-tuple-element.49), channel_id=1, source_target_pairs={{0,16},{4,20},{8,24},{12,28},{16,0},{20,4},{24,8},{28,12},{1,17},{... | collective-permute-start | bytes 638984 | tf_op jit(solution)/shard_map/ppermute | solution.py:464
  70.5 10.3 %collective-permute-start.14 = (bf16[52,16,128]{2,1,0:T(8,128)(2,1)S(1)}, bf16[52,16,128]{2,1,0:T(8,128)(2,1)S(1)}, u32[]{:S(2)}, u32[]{:S(2)}) collective-permute-start(bf16[52,16,128]{2,1,0:T(8,128)(2,1)S(1)} %get-tuple-element.50), channel_id=1, source_target_pairs={{0,24},{4,28},{8,16},{12,20},{16,8},{20,12},{24,0},{28,4},{1,25},{... | collective-permute-start | bytes 638984 | tf_op jit(solution)/shard_map/ppermute | solution.py:464
